TPU v7x, 32 devices: a whole 2x2x4 slice. The times are simulated.
32 devices in a mesh: shard: 4 (over z), replica: 8 (over y, x, core).
Axes of the slice: x: 2, y: 2, z: 4, core: 2. Of those that a mesh axis runs over, the one named last changes fastest.
Arguments:
- tokens: bfloat16 [8192, 1024], P(('shard', 'replica')), may hold values from -6 to 6
- segment_ids: int32 [32, 256], P(('shard', 'replica')), may hold values from 0 to 5, never falling along the last dimension, each value on 1 to 128 neighbouring positions
- attn_gain: float32 [1024], replicated, may hold values from 0.25 to 1.75
- w_query: bfloat16 [1024, 2048], P('shard'), may hold values from -0.1875 to 0.1875
- w_key: bfloat16 [1024, 1024], P('shard'), may hold values from -0.1875 to 0.1875
- w_value: bfloat16 [1024, 1024], P('shard'), may hold values from -0.1875 to 0.1875
- query_gain: float32 [128], replicated, may hold values from 0.1 to 1.9
- key_gain: float32 [128], replicated, may hold values from 0.1 to 1.9
- w_out: bfloat16 [2048, 1024], P('shard'), may hold values from -0.5 to 0.5
- mlp_gain: float32 [1024], replicated, may hold values from 0.25 to 1.75
- w_gate: bfloat16 [1024, 3072], P('shard'), may hold values from -0.1875 to 0.1875
- w_up: bfloat16 [1024, 3072], P('shard'), may hold values from -0.1875 to 0.1875
- w_down: bfloat16 [3072, 1024], P('shard'), may hold values from -0.21875 to 0.21875
- cotangent: bfloat16 [8192, 1024], P(('shard', 'replica')), may hold values from -6 to 6
Outputs:
- activations: bfloat16 [8192, 1024], P(('shard', 'replica'))
- input_grad: bfloat16 [8192, 1024], P(('shard', 'replica'))
- attn_gain_grad: float32 [1024], replicated
- w_query_grad: float32 [1024, 2048], P('shard')
- w_key_grad: float32 [1024, 1024], P('shard')
- w_value_grad: float32 [1024, 1024], P('shard')
- query_gain_grad: float32 [128], replicated
- key_gain_grad: float32 [128], replicated
- w_out_grad: float32 [2048, 1024], P('shard')
- mlp_gain_grad: float32 [1024], replicated
- w_gate_grad: float32 [1024, 3072], P('shard')
- w_up_grad: float32 [1024, 3072], P('shard')
- w_down_grad: float32 [3072, 1024], P('shard')
Inputs may be any that keep to these rules, and one draw needn't show every extreme that they name: `segment_ids`: document numbers never fall along a sequence; every number from 0 to 5 is used; each document has 1 to 128 tokens, and one has exactly that many.
All inputs are finite; a program needn't handle non-finite values.
Results may differ from a plain program's by a relative error of at most 0.02.
Values may be sent and summed in bfloat16 or wider, within the bound.
No kernel may reach another device: no remote copies, remote signals or barrier semaphores. Data moves between devices by JAX's collectives and lax.ppermute only.
A program may use at most 256 MiB of HBM per device.

v0:
```python
import jax
import jax.numpy as jnp
from jax import lax
from jax.sharding import PartitionSpec as P

HEADS = 16
KV_HEADS = 8
HEAD = 128


epsilon = 1e-06
rope_base = 1000000.0
masked_score = -1e30


def norm_rows(values, gain):
    return values * lax.rsqrt(jnp.mean(values * values, axis=-1, keepdims=True) + epsilon) * gain


def positions(segment_row):
    index_row = jnp.arange(segment_row.shape[0], dtype=jnp.int32)
    change = jnp.concatenate([jnp.ones((1,), dtype=jnp.bool_), segment_row[1:] != segment_row[:-1]])
    starting = lax.cummax(jnp.where(change, index_row, jnp.zeros_like(index_row)), axis=0)
    return index_row - starting


def rotary_tables(segment_row):
    half_dim = HEAD // 2
    freqs = rope_base ** (-2.0 * jnp.arange(half_dim, dtype=jnp.float32) / HEAD)
    angles = positions(segment_row).astype(jnp.float32)[:, None] * freqs[None, :]
    return (jnp.cos(angles), jnp.sin(angles))


def apply_rotary(values, cosine, sine):
    half_dim = values.shape[-1] // 2
    first_half = values[..., :half_dim]
    second_half = values[..., half_dim:]
    return jnp.concatenate(
        [first_half * cosine - second_half * sine, second_half * cosine + first_half * sine],
        axis=-1,
    )


def causal_mask(segment_row):
    index_row = jnp.arange(segment_row.shape[0], dtype=jnp.int32)
    return (index_row[None, :] <= index_row[:, None]) & (
        segment_row[:, None] == segment_row[None, :]
    )


def swiglu(gate, up_rows):
    return jax.nn.silu(gate) * up_rows


def forward_dot(left, right):
    return jnp.dot(left, right, preferred_element_type=jnp.float32)


def back_product(grad_rows, weight):
    return lax.dot_general(
        grad_rows, weight, (((1,), (1,)), ((), ())), preferred_element_type=jnp.float32
    )


def column_term(inputs, grad_rows):
    return lax.dot_general(
        inputs, grad_rows, (((0,), (0,)), ((), ())), preferred_element_type=jnp.float32
    )


def score_block(queries, key_rows, mask_all):
    raw_scores = jnp.einsum(
        "sqkgd,stkd->skgqt", queries, key_rows, preferred_element_type=jnp.float32
    )
    return jnp.where(mask_all[:, None, None], raw_scores * HEAD ** (-0.5), masked_score)


def body(
    tokens,
    segment_ids,
    attn_gain,
    w_query,
    w_key,
    w_value,
    query_gain,
    key_gain,
    w_out,
    mlp_gain,
    w_gate,
    w_up,
    w_down,
    cotangent,
):
    gathered = (
        lax.all_gather(w_query, "shard", axis=0, tiled=True),
        lax.all_gather(w_key, "shard", axis=0, tiled=True),
        lax.all_gather(w_value, "shard", axis=0, tiled=True),
        lax.all_gather(w_out, "shard", axis=0, tiled=True),
        lax.all_gather(w_gate, "shard", axis=0, tiled=True),
        lax.all_gather(w_up, "shard", axis=0, tiled=True),
        lax.all_gather(w_down, "shard", axis=0, tiled=True),
    )
    full_q, full_k, full_v, full_o, full_g, full_u, full_d = gathered
    seq_count, length = segment_ids.shape
    rows = tokens.shape[0]
    groups = HEADS // KV_HEADS
    inputs = tokens.astype(jnp.float32)
    normed32, pull_first = jax.vjp(norm_rows, inputs, attn_gain)
    normed_in = normed32.astype(jnp.bfloat16)
    q_lin = forward_dot(normed_in, full_q)
    k_lin = forward_dot(normed_in, full_k)
    value_rows = (
        forward_dot(normed_in, full_v)
        .astype(jnp.bfloat16)
        .reshape(seq_count, length, KV_HEADS, HEAD)
    )
    cosine, sine = jax.vmap(rotary_tables)(segment_ids)
    cosine = cosine[:, :, None, :]
    sine = sine[:, :, None, :]
    mask_all = jax.vmap(causal_mask)(segment_ids)

    def prepare(q_part, k_part, q_gain, k_gain):
        q_heads = apply_rotary(
            norm_rows(q_part.reshape(seq_count, length, HEADS, HEAD), q_gain), cosine, sine
        )
        k_heads = apply_rotary(
            norm_rows(k_part.reshape(seq_count, length, KV_HEADS, HEAD), k_gain), cosine, sine
        )
        return (q_heads, k_heads)

    (q_heads, k_heads), pull_heads = jax.vjp(prepare, q_lin, k_lin, query_gain, key_gain)
    queries = q_heads.astype(jnp.bfloat16).reshape(seq_count, length, KV_HEADS, groups, HEAD)
    key_rows = k_heads.astype(jnp.bfloat16)
    scores = score_block(queries, key_rows, mask_all)
    row_max = jnp.max(scores, axis=-1, keepdims=True)
    exponent = jnp.exp(scores - row_max)
    row_total = jnp.sum(exponent, axis=-1, keepdims=True)
    attention = (exponent / row_total).astype(jnp.bfloat16)
    mixed = jnp.einsum(
        "skgqt,stkd->sqkgd", attention, value_rows, preferred_element_type=jnp.float32
    )
    mixed = mixed.reshape(rows, HEADS * HEAD).astype(jnp.bfloat16)
    hidden = inputs + forward_dot(mixed, full_o)
    mid32, pull_mid = jax.vjp(norm_rows, hidden, mlp_gain)
    normed_mid = mid32.astype(jnp.bfloat16)
    gate = forward_dot(normed_mid, full_g)
    up_rows = forward_dot(normed_mid, full_u)
    prod32, pull_swiglu = jax.vjp(swiglu, gate, up_rows)
    product = prod32.astype(jnp.bfloat16)
    activations = (hidden + forward_dot(product, full_d)).astype(jnp.bfloat16)
    full_q, full_k, full_v, full_o, full_g, full_u, full_d = (
        lax.all_gather(w_query, "shard", axis=0, tiled=True),
        lax.all_gather(w_key, "shard", axis=0, tiled=True),
        lax.all_gather(w_value, "shard", axis=0, tiled=True),
        lax.all_gather(w_out, "shard", axis=0, tiled=True),
        lax.all_gather(w_gate, "shard", axis=0, tiled=True),
        lax.all_gather(w_up, "shard", axis=0, tiled=True),
        lax.all_gather(w_down, "shard", axis=0, tiled=True),
    )
    grad_out_rows = cotangent.astype(jnp.float32)
    w_down_grad = lax.psum_scatter(
        column_term(product, cotangent).astype(jnp.bfloat16),
        "shard",
        scatter_dimension=0,
        tiled=True,
    ).astype(jnp.float32)
    d_product = back_product(cotangent, full_d)
    d_gate32, d_up32 = pull_swiglu(d_product)
    d_gate = d_gate32.astype(jnp.bfloat16)
    d_up = d_up32.astype(jnp.bfloat16)
    w_gate_grad = lax.psum_scatter(
        column_term(normed_mid, d_gate).astype(jnp.bfloat16),
        "shard",
        scatter_dimension=0,
        tiled=True,
    ).astype(jnp.float32)
    w_up_grad = lax.psum_scatter(
        column_term(normed_mid, d_up).astype(jnp.bfloat16), "shard", scatter_dimension=0, tiled=True
    ).astype(jnp.float32)
    d_mid = back_product(d_gate, full_g) + back_product(d_up, full_u)
    d_hidden_norm, mlp_gain_grad = pull_mid(d_mid)
    d_hidden = grad_out_rows + d_hidden_norm
    d_hidden_low = d_hidden.astype(jnp.bfloat16)
    w_out_grad = lax.psum_scatter(
        column_term(mixed, d_hidden_low).astype(jnp.bfloat16),
        "shard",
        scatter_dimension=0,
        tiled=True,
    ).astype(jnp.float32)
    d_mixed = (
        back_product(d_hidden_low, full_o)
        .astype(jnp.bfloat16)
        .reshape(seq_count, length, KV_HEADS, groups, HEAD)
    )
    again = score_block(queries, key_rows, mask_all)
    soft_again = jnp.exp(again - row_max) / row_total
    soft_low = soft_again.astype(jnp.bfloat16)
    d_attention = jnp.einsum(
        "sqkgd,stkd->skgqt", d_mixed, value_rows, preferred_element_type=jnp.float32
    )
    d_value = jnp.einsum("skgqt,sqkgd->stkd", soft_low, d_mixed, preferred_element_type=jnp.float32)
    d_value = d_value.reshape(rows, KV_HEADS * HEAD).astype(jnp.bfloat16)
    d_scores = soft_again * (
        d_attention - jnp.sum(soft_again * d_attention, axis=-1, keepdims=True)
    )
    d_scores = d_scores.astype(jnp.bfloat16)
    d_queries = jnp.einsum(
        "skgqt,stkd->sqkgd", d_scores, key_rows, preferred_element_type=jnp.float32
    ) * HEAD ** (-0.5)
    d_keys = jnp.einsum(
        "skgqt,sqkgd->stkd", d_scores, queries, preferred_element_type=jnp.float32
    ) * HEAD ** (-0.5)
    d_q32, d_k32, query_gain_grad, key_gain_grad = pull_heads(
        (d_queries.reshape(seq_count, length, HEADS, HEAD), d_keys)
    )
    d_query = d_q32.astype(jnp.bfloat16)
    d_key = d_k32.astype(jnp.bfloat16)
    w_query_grad = lax.psum_scatter(
        column_term(normed_in, d_query).astype(jnp.bfloat16),
        "shard",
        scatter_dimension=0,
        tiled=True,
    ).astype(jnp.float32)
    w_key_grad = lax.psum_scatter(
        column_term(normed_in, d_key).astype(jnp.bfloat16), "shard", scatter_dimension=0, tiled=True
    ).astype(jnp.float32)
    w_value_grad = lax.psum_scatter(
        column_term(normed_in, d_value).astype(jnp.bfloat16),
        "shard",
        scatter_dimension=0,
        tiled=True,
    ).astype(jnp.float32)
    d_normed = (
        back_product(d_query, full_q) + back_product(d_key, full_k) + back_product(d_value, full_v)
    )
    d_input_norm, attn_gain_grad = pull_first(d_normed)
    input_grad = (d_hidden + d_input_norm).astype(jnp.bfloat16)
    w_query_grad, w_key_grad, w_value_grad, w_out_grad, w_gate_grad, w_up_grad, w_down_grad = (
        lax.psum(w_query_grad.astype(jnp.bfloat16), "replica").astype(jnp.float32),
        lax.psum(w_key_grad.astype(jnp.bfloat16), "replica").astype(jnp.float32),
        lax.psum(w_value_grad.astype(jnp.bfloat16), "replica").astype(jnp.float32),
        lax.psum(w_out_grad.astype(jnp.bfloat16), "replica").astype(jnp.float32),
        lax.psum(w_gate_grad.astype(jnp.bfloat16), "replica").astype(jnp.float32),
        lax.psum(w_up_grad.astype(jnp.bfloat16), "replica").astype(jnp.float32),
        lax.psum(w_down_grad.astype(jnp.bfloat16), "replica").astype(jnp.float32),
    )
    attn_gain_grad, query_gain_grad, key_gain_grad, mlp_gain_grad = lax.psum(
        (attn_gain_grad, query_gain_grad, key_gain_grad, mlp_gain_grad), ("shard", "replica")
    )
    return (
        activations,
        input_grad,
        attn_gain_grad,
        w_query_grad,
        w_key_grad,
        w_value_grad,
        query_gain_grad,
        key_gain_grad,
        w_out_grad,
        mlp_gain_grad,
        w_gate_grad,
        w_up_grad,
        w_down_grad,
    )


def solution(mesh):
    placed = (
        P(("shard", "replica"), None),
        P(("shard", "replica"), None),
        P(),
        P("shard", None),
        P("shard", None),
        P("shard", None),
        P(),
        P(),
        P("shard", None),
        P(),
        P("shard", None),
        P("shard", None),
        P("shard", None),
        P(("shard", "replica"), None),
    )
    return jax.shard_map(
        body,
        mesh=mesh,
        in_specs=placed,
        out_specs=(
            P(("shard", "replica"), None),
            P(("shard", "replica"), None),
            P(),
            P("shard", None),
            P("shard", None),
            P("shard", None),
            P(),
            P(),
            P("shard", None),
            P(),
            P("shard", None),
            P("shard", None),
            P("shard", None),
        ),
        check_vma=False,
    )
```

profile of v0, /device:TPU:0, one launch (start us, length us, event | category | flops | bytes accessed | tf_op | source)
XLA Modules:
  0.0 1376.4 jit_solution(3234706879759538743)
XLA Ops:
  14.4 43.8 %all-gather.8.cloned.1.call-done = bf16[1024,1024]{1,0:T(8,128)(2,1)} async-done(((bf16[256,1024]{1,0:T(8,128)(2,1)}), bf16[1024,1024]{1,0:T(8,128)(2,1)}) %all-gather.8.cloned.1.call-update) | async-done | bytes 2097168 | tf_op jit(solution)/shard_map/all_gather | solution.py:97
  58.3 2.4 fusion.34
  61.5 43.0 %all-gather.10.cloned.1.call-done = bf16[1024,1024]{1,0:T(8,128)(2,1)} async-done(((bf16[256,1024]{1,0:T(8,128)(2,1)}), bf16[1024,1024]{1,0:T(8,128)(2,1)}) %all-gather.10.cloned.1.call-update) | async-done | bytes 2097168 | tf_op jit(solution)/shard_map/all_gather | solution.py:96
  104.5 2.3 convolution_bitcast_fusion.1
  107.9 1.3 fusion.48
  109.1 76.5 %all-gather.12.cloned.1.call-done = bf16[1024,2048]{1,0:T(8,128)(2,1)} async-done(((bf16[256,2048]{1,0:T(8,128)(2,1)}), bf16[1024,2048]{1,0:T(8,128)(2,1)}) %all-gather.12.cloned.1.call-update) | async-done | bytes 4194320 | tf_op jit(solution)/shard_map/all_gather | solution.py:95
  185.6 3.5 convolution_bitcast_fusion
  190.8 1.3 fusion.57
  192.9 1.5 fusion.18
  196.4 1.5 fusion.5
  199.8 2.2 fusion.20
  202.1 64.3 %all-gather.14.cloned.1.call-done = bf16[2048,1024]{1,0:T(8,128)(2,1)} async-done(((bf16[512,1024]{1,0:T(8,128)(2,1)}), bf16[2048,1024]{1,0:T(8,128)(2,1)}) %all-gather.14.cloned.1.call-update) | async-done | bytes 4194320 | tf_op jit(solution)/shard_map/all_gather | solution.py:98
  266.3 3.9 multiply_reduce_fusion.5
  271.5 110.2 %all-gather.18.cloned.1.call-done = bf16[1024,3072]{1,0:T(8,128)(2,1)} async-done(((bf16[256,3072]{1,0:T(8,128)(2,1)}), bf16[1024,3072]{1,0:T(8,128)(2,1)}) %all-gather.18.cloned.1.call-update) | async-done | bytes 6291472 | tf_op jit(solution)/shard_map/all_gather | solution.py:100
  381.7 6.2 fusion.76
  387.9 108.8 %all-gather.16.cloned.1.call-done = bf16[1024,3072]{1,0:T(8,128)(2,1)} async-done(((bf16[256,3072]{1,0:T(8,128)(2,1)}), bf16[1024,3072]{1,0:T(8,128)(2,1)}) %all-gather.16.cloned.1.call-update) | async-done | bytes 6291472 | tf_op jit(solution)/shard_map/all_gather | solution.py:99
  496.7 6.2 fusion.75
  503.0 108.9 %all-gather.20.cloned.1.call-done = bf16[3072,1024]{1,0:T(8,128)(2,1)} async-done(((bf16[768,1024]{1,0:T(8,128)(2,1)}), bf16[3072,1024]{1,0:T(8,128)(2,1)}) %all-gather.20.cloned.1.call-update) | async-done | bytes 6291472 | tf_op jit(solution)/shard_map/all_gather | solution.py:101
  611.9 9.0 multiply_convert_fusion
  621.0 2.0 fusion.77
  623.1 5.8 multiply_reduce_fusion.1
  630.3 2.3 convolution_convert_fusion.5
  632.6 2.3 copy.174
  634.9 3.8 fusion.29
  639.5 2.2 convolution_convert_fusion.6
  642.1 4.3 fusion
  646.5 1.3 fusion.11
  650.6 1.1 multiply_reduce_fusion.2
  651.8 1.7 fusion.38
  653.5 2.0 copy.151
  655.5 3.2 convolution_convert_fusion.7
  658.8 4.8 convolution_convert_fusion.3
  663.8 2.7 convolution_multiply_fusion
  666.5 1.5 fusion.74
  668.0 3.7 copy.172
  671.7 3.7 copy.173
  675.4 2.7 multiply_add_fusion.1
  678.1 1.8 multiply_reduce_fusion
  680.3 4.0 fusion.10
  685.3 3.5 convolution_convert_fusion.4
  688.8 1.3 copy-done.23
  690.3 4.5 convolution_convert_fusion
  694.8 1.3 copy-done.33
  696.2 4.4 convolution_convert_fusion.1
  700.7 1.3 copy-done.31
  702.0 4.5 convolution_convert_fusion.2
  706.8 23.3 %reduce-scatter.10.cloned.1.call-done = bf16[256,1024]{1,0:T(8,128)(2,1)} async-done(((bf16[1024,1024]{1,0:T(8,128)(2,1)}), bf16[256,1024]{1,0:T(8,128)(2,1)}) %reduce-scatter.10.cloned.1.call-update) | async-done | bytes 524304 | tf_op jit(solution)/shard_map/reduce_scatter | solution.py:224
  730.1 78.3 %reduce-scatter.14.cloned.1.call-done = bf16[512,1024]{1,0:T(8,128)(2,1)} async-done(((bf16[2048,1024]{1,0:T(8,128)(2,1)}), bf16[512,1024]{1,0:T(8,128)(2,1)}) %reduce-scatter.14.cloned.1.call-update) | async-done | bytes 1048592 | tf_op jit(solution)/shard_map/reduce_scatter | solution.py:184
  808.4 79.7 %reduce-scatter.8.cloned.1.call-done = bf16[256,2048]{1,0:T(8,128)(2,1)} async-done(((bf16[1024,2048]{1,0:T(8,128)(2,1)}), bf16[256,2048]{1,0:T(8,128)(2,1)}) %reduce-scatter.8.cloned.1.call-update) | async-done | bytes 1048592 | tf_op jit(solution)/shard_map/reduce_scatter | solution.py:218
  888.1 113.4 %reduce-scatter.20.cloned.1.call-done = bf16[768,1024]{1,0:T(8,128)(2,1)} async-done(((bf16[3072,1024]{1,0:T(8,128)(2,1)}), bf16[768,1024]{1,0:T(8,128)(2,1)}) %reduce-scatter.20.cloned.1.call-update) | async-done | bytes 1572880 | tf_op jit(solution)/shard_map/reduce_scatter | solution.py:161
  1001.5 113.6 %reduce-scatter.18.cloned.1.call-done = bf16[256,3072]{1,0:T(8,128)(2,1)} async-done(((bf16[1024,3072]{1,0:T(8,128)(2,1)}), bf16[256,3072]{1,0:T(8,128)(2,1)}) %reduce-scatter.18.cloned.1.call-update) | async-done | bytes 1572880 | tf_op jit(solution)/shard_map/reduce_scatter | solution.py:177
  1115.1 113.5 %reduce-scatter.16.cloned.1.call-done = bf16[256,3072]{1,0:T(8,128)(2,1)} async-done(((bf16[1024,3072]{1,0:T(8,128)(2,1)}), bf16[256,3072]{1,0:T(8,128)(2,1)}) %reduce-scatter.16.cloned.1.call-update) | async-done | bytes 1572880 | tf_op jit(solution)/shard_map/reduce_scatter | solution.py:171
  1228.6 1.2 copy-done.19
  1229.8 3.6 fusion.44
  1236.1 41.8 %all-reduce.4 = (f32[1024]{0:T(1024)}, f32[128]{0:T(128)}, f32[128]{0:T(128)}, f32[1024]{0:T(1024)}) all-reduce(f32[1024]{0:T(1024)S(1)} %get-tuple-element.19, f32[128]{0:T(128)S(1)} %get-tuple-element.13, f32[128]{0:T(128)S(1)} %copy-done.64, f32[1024]{0:T(1024)S(1)} %copy-done.63), channel_id=1, replica_groups=mesh['shard'=4,'replica'=8] {'shard','replica'}, use_global_device_ids=true, to_apply=%region_14.15 | all-reduce | flops 2304 | bytes 18432 | tf_op jit(solution)/shard_map/psum | solution.py:247
  1278.0 1.1 fusion.40
  1279.8 6.0 fusion.28
  1285.9 71.0 %all-reduce.8.cloned.1.call-done = (bf16[256,2048]{1,0:T(8,128)(2,1)}, bf16[256,1024]{1,0:T(8,128)(2,1)}, bf16[256,1024]{1,0:T(8,128)(2,1)}, bf16[512,1024]{1,0:...) async-done(((bf16[256,2048]{1,0:T(8,128)(2,1)}, bf16[256,1024]{1,0:T(8,128)(2,1)}, bf16[256,1024]{1,0:T(8,128)(2,1)}, ...) | async-done | bytes 7864336 | tf_op jit(solution)/shard_map/psum | solution.py:239
  1356.9 2.9 convert_element_type.183
  1359.7 1.1 convert_element_type.185
  1361.9 1.6 convert_element_type.189
  1363.5 2.0 convert_element_type.191
  1365.5 2.0 convert_element_type.193
  1367.6 2.1 convert_element_type.195
  (203 shorter events, 28.5 us)
Async XLA Ops:
  7.2 51.1 %all-gather.8.cloned.1.call-start = ((), (), s32[]{:S(2)}) async-start(), calls=%async_computation.7 | async-start | bytes 2621440 | tf_op jit(solution)/shard_map/all_gather | solution.py:97
  7.9 96.6 %all-gather.10.cloned.1.call-start = ((), (), s32[]{:S(2)}) async-start(), calls=%async_computation.8 | async-start | bytes 2621440 | tf_op jit(solution)/shard_map/all_gather | solution.py:96
  8.7 176.9 %all-gather.12.cloned.1.call-start = ((), (), s32[]{:S(2)}) async-start(), calls=%async_computation.9 | async-start | bytes 5242880 | tf_op jit(solution)/shard_map/all_gather | solution.py:95
  9.4 256.9 %all-gather.14.cloned.1.call-start = ((), (), s32[]{:S(2)}) async-start(), calls=%async_computation.10 | async-start | bytes 5242880 | tf_op jit(solution)/shard_map/all_gather | solution.py:98
  10.0 2.0 copy-start.51
  10.0 2.9 copy-start.2
  10.0 371.7 %all-gather.18.cloned.1.call-start = ((), (), s32[]{:S(2)}) async-start(), calls=%async_computation.12 | async-start | bytes 7864320 | tf_op jit(solution)/shard_map/all_gather | solution.py:100
  10.6 47.7 %copy-start.43 = (f32[1024]{0:T(1024)S(1)}, f32[1024]{0:T(1024)}, u32[]{:S(2)}) copy-start(f32[1024]{0:T(1024)} %param.16) | copy-start | bytes 12292
  10.6 486.1 %all-gather.16.cloned.1.call-start = ((), (), s32[]{:S(2)}) async-start(), calls=%async_computation.11 | async-start | bytes 7864320 | tf_op jit(solution)/shard_map/all_gather | solution.py:99
  11.2 600.7 %all-gather.20.cloned.1.call-start = ((), (), s32[]{:S(2)}) async-start(), calls=%async_computation.13 | async-start | bytes 7864320 | tf_op jit(solution)/shard_map/all_gather | solution.py:101
  11.9 694.9 %reduce-scatter.12.cloned.1.call-start = ((), (), s32[]{:S(2)}) async-start(), calls=%async_computation.16 | async-start | bytes 2621440 | tf_op jit(solution)/shard_map/reduce_scatter | solution.py:227
  13.0 48.5 %copy-start.54 = (f32[256]{0:T(256)}, f32[256]{0:T(256)S(1)}, u32[]{:S(2)}) copy-start(f32[256]{0:T(256)S(1)} %fusion.41) | copy-start | bytes 3076
  107.1 2.0 copy-start.3
  107.5 1.6 copy-start.47
  109.1 86.7 %copy-start.15 = (bf16[256,8,64]{2,0,1:T(8,128)(2,1)}, bf16[256,8,64]{2,0,1:T(8,128)(2,1)S(1)}, u32[]{:S(2)}) copy-start(bf16[256,8,64]{2,0,1:T(8,128)(2,1)S(1)} %get-tuple-element.43) | copy-start | bytes 786436
  195.6 2.3 copy-start.8
  195.8 2.0 copy-start.10
  197.9 2.0 copy-start
  197.9 2.0 copy-start.45
  197.9 2.0 copy-start.42
  266.3 5.0 copy-start.52
  611.9 9.1 copy-start.65
  620.9 2.1 copy-start.30
  621.0 2.1 copy-start.32
  621.0 2.1 copy-start.21
  621.0 2.1 copy-start.53
  621.0 2.1 copy-start.57
  623.1 5.9 copy-start.62
  623.1 5.9 copy-start.26
  623.1 7.2 copy-start.66
  641.6 88.5 %reduce-scatter.10.cloned.1.call-start = ((), (), s32[]{:S(2)}) async-start(), calls=%async_computation.15 | async-start | bytes 2621440 | tf_op jit(solution)/shard_map/reduce_scatter | solution.py:224
  642.1 4.4 copy-start.1
  642.1 4.4 copy-start.39
  642.1 4.4 copy-start.46
  642.1 4.4 copy-start.50
  646.5 1.5 copy-start.11
  649.9 1.9 copy-start.48
  658.7 149.6 %reduce-scatter.14.cloned.1.call-start = ((), (), s32[]{:S(2)}) async-start(), calls=%async_computation.17 | async-start | bytes 5242880 | tf_op jit(solution)/shard_map/reduce_scatter | solution.py:184
  663.6 224.5 %reduce-scatter.8.cloned.1.call-start = ((), (), s32[]{:S(2)}) async-start(), calls=%async_computation.14 | async-start | bytes 5242880 | tf_op jit(solution)/shard_map/reduce_scatter | solution.py:218
  675.4 2.7 copy-start.58
  678.1 1.9 copy-start.6
  678.1 2.0 copy-start.7
  678.1 2.0 copy-start.44
  688.7 1.4 copy-start.23
  688.7 1.5 copy-start.27
  688.8 312.7 %reduce-scatter.20.cloned.1.call-start = ((), (), s32[]{:S(2)}) async-start(), calls=%async_computation.20 | async-start | bytes 7864320 | tf_op jit(solution)/shard_map/reduce_scatter | solution.py:161
  694.8 1.4 copy-start.33
  694.8 420.3 %reduce-scatter.18.cloned.1.call-start = ((), (), s32[]{:S(2)}) async-start(), calls=%async_computation.19 | async-start | bytes 7864320 | tf_op jit(solution)/shard_map/reduce_scatter | solution.py:177
  700.6 1.4 copy-start.31
  700.6 528.0 %reduce-scatter.16.cloned.1.call-start = ((), (), s32[]{:S(2)}) async-start(), calls=%async_computation.18 | async-start | bytes 7864320 | tf_op jit(solution)/shard_map/reduce_scatter | solution.py:171
  706.5 650.3 %all-reduce.8.cloned.1.call-start = ((), (), s32[]{:S(2)}) async-start(), calls=%async_computation.21 | async-start | bytes 15728640 | tf_op jit(solution)/shard_map/psum | solution.py:239
  1229.8 3.6 copy-start.14
  1229.8 3.6 copy-start.17
  1233.5 1.6 copy-start.25
  1233.5 1.7 copy-start.29
  1235.1 42.8 %copy-start.55 = (f32[256]{0:T(256)S(1)}, f32[256]{0:T(256)}, u32[]{:S(2)}) copy-start(f32[256]{0:T(256)} %copy-done.54) | copy-start | bytes 3076
  1235.1 42.8 %copy-start.13 = (f32[256,1024]{1,0:T(8,128)S(1)}, f32[256,1024]{1,0:T(8,128)}, u32[]{:S(2)}) copy-start(f32[256,1024]{1,0:T(8,128)} %copy-done.12) | copy-start | bytes 3145732
  1277.9 1.9 copy-start.24
  1356.9 2.9 copy-start.41
  1356.9 4.0 copy-start.40
  1359.7 2.2 copy-start.37
  1360.8 2.7 copy-start.36
  1363.5 2.0 copy-start.35
  1365.5 2.0 copy-start.34
  (18 other events, 18.4 us)
Sparse Core Ops, SparseCore 0:
  9.6 48.6 all-gather.7
  59.8 44.6 all-gather.9
  106.1 79.4 all-gather.11
  187.0 79.2 all-gather.13
  267.8 113.8 all-gather.17
  383.1 113.5 all-gather.15
  498.3 113.5 all-gather.19
  641.8 42.0 reduce-scatter.11
  686.9 43.1 reduce-scatter.9
  732.2 76.0 reduce-scatter.13
  810.8 77.2 reduce-scatter.7
  890.2 111.2 reduce-scatter.19
  1003.8 111.2 reduce-scatter.17
  1117.3 111.2 reduce-scatter.15
  1232.6 124.2 all-reduce.7
where the time goes:
time: 1380 us
  waiting for transfers between devices  1150 us (83%)
  matrix products  97.6 us (7%)
  blocking collectives  41.8 us (3%)
  other arithmetic  36.8 us (3%)
  local copies, waits for them, and re-layouts  31.2 us (2%)
  between operations  14.9 us (1%)
    reduce_scatter x1, waiting for transfers between devices, body(): lax.psum_scatter(column_term(normed_mid, d_up).astype(jnp.bfloat16), 'sha...  114 us
    reduce_scatter x1, waiting for transfers between devices, body(): lax.psum_scatter(column_term(normed_mid, d_gate).astype(jnp.bfloat16), 's...  113 us
    reduce_scatter x1, waiting for transfers between devices, body(): lax.psum_scatter(column_term(product, cotangent).astype(jnp.bfloat16), 's...  113 us
    all_gather x1, waiting for transfers between devices, body(): lax.all_gather(w_up, 'shard', axis=0, tiled=True)  110 us
    all_gather x1, waiting for transfers between devices, body(): lax.all_gather(w_down, 'shard', axis=0, tiled=True)  109 us
    all_gather x1, waiting for transfers between devices, body(): lax.all_gather(w_gate, 'shard', axis=0, tiled=True)  109 us
    reduce_scatter x1, waiting for transfers between devices, body(): lax.psum_scatter(column_term(normed_in, d_query).astype(jnp.bfloat16), 's...  79.7 us
    reduce_scatter x1, waiting for transfers between devices, body(): lax.psum_scatter(column_term(mixed, d_hidden_low).astype(jnp.bfloat16), '...  78.3 us
  transfers between devices with their start and end apart: 15, of which 14 were waited for; matrix products, arithmetic and copies ran while one was open for 8% of the time, Pallas kernels for 0%

commit v1 on v0

v1 whole, which is shorter than its diff:
```python
import jax
import jax.numpy as jnp
from jax import lax
from jax.sharding import Mesh
from jax.sharding import PartitionSpec as P

HEADS = 16
KV_HEADS = 8
HEAD = 128
GROUP = HEADS // KV_HEADS

EPS = 1e-06
ROPE_BASE = 1000000.0
MASKED = -1e30
SCALE = HEAD ** (-0.5)
BF = jnp.bfloat16
F32 = jnp.float32
SWAP = [(0, 1), (1, 0)]


def dot(a, b):
    return jnp.dot(a, b, preferred_element_type=F32)


def dot_nt(a, b):
    return lax.dot_general(a, b, (((1,), (1,)), ((), ())), preferred_element_type=F32)


def dot_tn(a, b):
    return lax.dot_general(a, b, (((0,), (0,)), ((), ())), preferred_element_type=F32)


def swap(a, axis):
    return lax.ppermute(a, axis, SWAP)


class Plane:
    def __init__(self, ny, nx):
        self.ny, self.nx, self.n = ny, nx, ny * nx
        self.square = ny == 2 and nx == 2
        self.axes = ("y", "x")

    def index(self):
        return lax.axis_index("y") * self.nx + lax.axis_index("x")

    def gather(self, a):
        if not self.square:
            g = lax.all_gather(a, self.axes, axis=0, tiled=False)
            return [g[i] for i in range(self.n)]
        half = a.shape[0] // 32 * 16
        ax, ay = swap(a, "x"), swap(a, "y")
        d0, d1 = swap(ay[:half], "x"), swap(ax[half:], "y")
        return [a, ax, ay, jnp.concatenate([d0, d1], 0)]

    def scatter(self, blocks):
        if not self.square:
            s = jnp.concatenate(blocks, 0).astype(BF)
            return lax.psum_scatter(s, self.axes, scatter_dimension=0, tiled=True).astype(F32)
        own, bx, by, bd = blocks
        half = own.shape[0] // 2
        low = bd.astype(BF)
        fx, fy = swap(low[:half], "x"), swap(low[half:], "y")
        bx = jnp.concatenate([bx[:half].astype(BF), (bx[half:] + fy.astype(F32)).astype(BF)], 0)
        by = jnp.concatenate([(by[:half] + fx.astype(F32)).astype(BF), by[half:].astype(BF)], 0)
        rx, ry = swap(bx, "x"), swap(by, "y")
        return own + rx.astype(F32) + ry.astype(F32)

    def absolute(self, blocks):
        if not self.square:
            return blocks
        xb, yb = lax.axis_index("x") == 1, lax.axis_index("y") == 1
        a0, a1 = jnp.where(xb, blocks[1], blocks[0]), jnp.where(xb, blocks[0], blocks[1])
        a2, a3 = jnp.where(xb, blocks[3], blocks[2]), jnp.where(xb, blocks[2], blocks[3])
        return [jnp.where(yb, a2, a0), jnp.where(yb, a3, a1), jnp.where(yb, a0, a2), jnp.where(yb, a1, a3)]

    def exchange(self, a):
        if not self.square:
            return lax.all_to_all(a, self.axes, split_axis=0, concat_axis=0, tiled=True)
        t = self.index()
        pick = lambda k: lax.dynamic_index_in_dim(a, jnp.bitwise_xor(t, k), 0, keepdims=False)
        got = [
            pick(0),
            swap(pick(1), "x"),
            swap(pick(2), "y"),
            lax.ppermute(pick(3), self.axes, [(i, 3 - i) for i in range(4)]),
        ]
        return jnp.stack(self.absolute(got), 0)


def norm_parts(v):
    return lax.rsqrt(jnp.mean(v * v, axis=-1, keepdims=True) + EPS)


def norm_back(v, r, gain, d):
    dg = d * gain
    return r * (dg - v * (r * r) * jnp.mean(dg * v, axis=-1, keepdims=True))


def make_body(size, plane, halves):
    n = plane.n

    def body(tokens, segment_ids, attn_gain, w_query, w_key, w_value, query_gain, key_gain,
             w_out, mlp_gain, w_gate, w_up, w_down, cotangent):
        t = plane.index()
        c = lax.axis_index("c") if halves else 0
        parts = 2 if halves else 1
        rows, width = tokens.shape
        length = segment_ids.shape[1]
        assert rows == length
        kv_local = KV_HEADS // n // parts

        def cols(w):
            per = w.shape[1] // n
            h = per // parts
            return lax.dynamic_slice_in_dim(w, t * per + c * h, h, axis=1)

        def row_piece(w):
            q = w.shape[0] // parts // n
            return lax.dynamic_slice_in_dim(w, c * (n * q) + t * q, q, axis=0)

        def both(a):
            return [a, swap(a, "c")] if halves else [a]

        qkv_piece = jnp.concatenate([cols(w_query), cols(w_key), cols(w_value)], 1)
        wqkv = both(lax.all_gather(qkv_piece, "shard", axis=0, tiled=True))
        out_rows, down_rows = w_out.shape[0] // parts // n, w_down.shape[0] // parts // n
        od_piece = jnp.concatenate([row_piece(w_out), row_piece(w_down)], 0)
        od = lax.all_gather(od_piece, "shard", axis=0, tiled=False)
        gu_piece = jnp.concatenate([cols(w_gate), cols(w_up)], 1)
        wgu = both(lax.all_gather(gu_piece, "shard", axis=0, tiled=True))
        od = plane.exchange(od)
        od = both(od)
        wo = [w[:, :out_rows].reshape(n * out_rows, width) for w in od]
        wd = [w[:, out_rows:].reshape(n * down_rows, width) for w in od]

        seg_rows = jnp.pad(segment_ids.astype(BF), ((0, 15), (0, width - length)))
        ext = plane.gather(jnp.concatenate([tokens, seg_rows], 0))
        x_all = jnp.concatenate([b[:rows] for b in ext], 0)
        segs = jnp.stack([b[rows, :length] for b in ext], 0).astype(jnp.int32)
        cot_all = jnp.concatenate(plane.gather(cotangent), 0)
        x32 = x_all.astype(F32)
        r_in = norm_parts(x32)
        normed_in = (x32 * r_in * attn_gain).astype(BF)

        idx = jnp.arange(length, dtype=jnp.int32)
        start = jnp.sum((segs[:, None, :] < segs[:, :, None]).astype(jnp.int32), axis=-1)
        pos = idx[None, :] - start
        freqs = ROPE_BASE ** (-2.0 * jnp.arange(HEAD // 2, dtype=F32) / HEAD)
        ang = pos.astype(F32)[:, :, None] * freqs
        cos, sin = jnp.cos(ang)[:, :, None], jnp.sin(ang)[:, :, None]
        mask = (idx[None, :] <= idx[:, None])[None] & (segs[:, :, None] == segs[:, None, :])

        def rot(u):
            u1, u2 = u[..., : HEAD // 2], u[..., HEAD // 2 :]
            return jnp.concatenate([u1 * cos - u2 * sin, u2 * cos + u1 * sin], -1)

        def rot_back(u):
            u1, u2 = u[..., : HEAD // 2], u[..., HEAD // 2 :]
            return jnp.concatenate([u1 * cos + u2 * sin, u2 * cos - u1 * sin], -1)

        nq = kv_local * GROUP
        kept, mixed, partial = [], [], 0.0
        for h in range(parts):
            lin = dot(normed_in, wqkv[h])
            q = lin[:, : nq * HEAD].reshape(n, length, nq, HEAD)
            k = lin[:, nq * HEAD : (nq + kv_local) * HEAD].reshape(n, length, kv_local, HEAD)
            v = lin[:, (nq + kv_local) * HEAD :].astype(BF).reshape(n, length, kv_local, HEAD)
            rq, rk = norm_parts(q), norm_parts(k)
            qr = rot(q * rq * query_gain).astype(BF).reshape(n, length, kv_local, GROUP, HEAD)
            kr = rot(k * rk * key_gain).astype(BF)
            s = jnp.einsum("sqkgd,stkd->skgqt", qr, kr, preferred_element_type=F32)
            s = jnp.where(mask[:, None, None], s * SCALE, MASKED)
            e = jnp.exp(s - jnp.max(s, axis=-1, keepdims=True))
            p = e / jnp.sum(e, axis=-1, keepdims=True)
            m = jnp.einsum("skgqt,stkd->sqkgd", p.astype(BF), v, preferred_element_type=F32)
            m = m.astype(BF).reshape(n * length, nq * HEAD)
            kept.append((q, k, v, rq, rk, qr, kr, p))
            mixed.append(m)
            partial = partial + dot(m, wo[h])

        split = lambda a: [a[i * rows : (i + 1) * rows] for i in range(n)]
        hidden = tokens.astype(F32) + plane.scatter(split(partial))
        r_mid = norm_parts(hidden)
        normed_mid = jnp.concatenate(plane.gather((hidden * r_mid * mlp_gain).astype(BF)), 0)

        ff = wd[0].shape[0]
        partial, d_mid, gu_terms, down_terms = 0.0, 0.0, [], []
        for h in range(parts):
            gu = dot(normed_mid, wgu[h])
            gate, up = gu[:, :ff], gu[:, ff:]
            sg = jax.nn.sigmoid(gate)
            act = gate * sg
            product = (act * up).astype(BF)
            partial = partial + dot(product, wd[h])
            dp = dot_nt(cot_all, wd[h])
            d_up = (dp * act).astype(BF)
            d_gate = (dp * up * (sg + act * (1.0 - sg))).astype(BF)
            dgu = jnp.concatenate([d_gate, d_up], 1)
            d_mid = d_mid + dot_nt(dgu, wgu[h])
            gu_terms.append(dot_tn(normed_mid, dgu))
            down_terms.append(dot_tn(product, cot_all))
        d_mid = plane.scatter(split(d_mid))
        activations = (hidden + plane.scatter(split(partial))).astype(BF)

        def owned(terms):
            if halves:
                return (terms[0] + swap(terms[1].astype(BF), "c").astype(F32)).astype(BF)
            return lax.psum(terms[0].astype(BF), "c")

        def reduce_cols(terms):
            return lax.psum_scatter(owned(terms), "shard", scatter_dimension=0, tiled=True)

        def reduce_rows(terms):
            a = owned(terms)
            a = plane.exchange(a.reshape(n, a.shape[0] // n, width))
            return lax.psum_scatter(a.reshape(-1, width), "shard", scatter_dimension=0, tiled=True)

        def spread(piece):
            got = [jnp.stack(plane.absolute(plane.gather(piece)), 0)]
            if halves:
                got.append(swap(got[0], "c"))
                first = c == 0
                got = [jnp.where(first, got[0], got[1]), jnp.where(first, got[1], got[0])]
            return jnp.stack(got, 0).astype(F32)

        down_piece = reduce_rows(down_terms)
        gu_piece = reduce_cols(gu_terms)

        dh_norm = norm_back(hidden, r_mid, mlp_gain, d_mid)
        mlp_gain_grad = jnp.sum(d_mid * hidden * r_mid, axis=0)
        d_hidden = cotangent.astype(F32) + dh_norm
        dh_low = jnp.concatenate(plane.gather(d_hidden.astype(BF)), 0)

        d_in, qkv_terms, out_terms, qg_grad, kg_grad = 0.0, [], [], 0.0, 0.0
        for h in range(parts):
            q, k, v, rq, rk, qr, kr, p = kept[h]
            out_terms.append(dot_tn(mixed[h], dh_low))
            dm = dot_nt(dh_low, wo[h]).astype(BF).reshape(n, length, kv_local, GROUP, HEAD)
            da = jnp.einsum("sqkgd,stkd->skgqt", dm, v, preferred_element_type=F32)
            dv = jnp.einsum("skgqt,sqkgd->stkd", p.astype(BF), dm, preferred_element_type=F32)
            ds = (p * (da - jnp.sum(p * da, axis=-1, keepdims=True))).astype(BF)
            dq = SCALE * jnp.einsum("skgqt,stkd->sqkgd", ds, kr, preferred_element_type=F32)
            dk = SCALE * jnp.einsum("skgqt,sqkgd->stkd", ds, qr, preferred_element_type=F32)
            dq = rot_back(dq.reshape(n, length, nq, HEAD))
            dk = rot_back(dk)
            qg_grad = qg_grad + jnp.sum(dq * q * rq, axis=(0, 1, 2))
            kg_grad = kg_grad + jnp.sum(dk * k * rk, axis=(0, 1, 2))
            dq = norm_back(q, rq, query_gain, dq).astype(BF)
            dk = norm_back(k, rk, key_gain, dk).astype(BF)
            flat = lambda a: a.reshape(n * length, -1)
            dqkv = jnp.concatenate([flat(dq), flat(dk), flat(dv.astype(BF))], 1)
            qkv_terms.append(dot_tn(normed_in, dqkv))
            d_in = d_in + dot_nt(dqkv, wqkv[h])
        out_piece = reduce_rows(out_terms)
        qkv_piece = reduce_cols(qkv_terms)
        attn_gain_grad = jnp.sum(d_in * (x32 * r_in), axis=0)
        d_in = plane.scatter(split(d_in))
        x_own = tokens.astype(F32)
        input_grad = (d_hidden + norm_back(x_own, norm_parts(x_own), attn_gain, d_in)).astype(BF)

        gains = lax.psum(
            jnp.concatenate([attn_gain_grad, mlp_gain_grad, qg_grad, kg_grad]),
            ("shard", "y", "x", "c"),
        )
        cuts = [width, 2 * width, 2 * width + HEAD]
        attn_gain_grad, mlp_gain_grad, qg_grad, kg_grad = jnp.split(gains, cuts)

        def place_cols(a):
            return a.transpose(2, 1, 0, 3).reshape(a.shape[2], -1)

        qkv = spread(qkv_piece)
        gu = spread(gu_piece)
        a, b = nq * HEAD, (nq + kv_local) * HEAD
        return (
            activations,
            input_grad,
            attn_gain_grad,
            place_cols(qkv[..., :a]),
            place_cols(qkv[..., a:b]),
            place_cols(qkv[..., b:]),
            qg_grad,
            kg_grad,
            spread(out_piece).reshape(-1, width),
            mlp_gain_grad,
            place_cols(gu[..., :ff]),
            place_cols(gu[..., ff:]),
            spread(down_piece).reshape(-1, width),
        )

    return body


def solution(mesh):
    size, replicas = mesh.shape["shard"], mesh.shape["replica"]
    ny, nx = replicas // 4, 2
    assert size == ny * nx
    plane = Plane(ny, nx)
    fine = Mesh(mesh.devices.reshape(size, ny, nx, 2), ("shard", "y", "x", "c"))
    halves = KV_HEADS % (2 * plane.n) == 0
    every = P(("shard", "y", "x", "c"), None)
    shard, copy = P("shard", None), P()
    return jax.shard_map(
        make_body(size, plane, halves),
        mesh=fine,
        in_specs=(every, every, copy, shard, shard, shard, copy, copy, shard, copy, shard, shard, shard, every),
        out_specs=(every, every, copy, shard, shard, shard, copy, copy, shard, copy, shard, shard, shard),
        check_vma=False,
    )
```

time: 1380 us -> 549 us (0.40)
  waiting for transfers between devices: 1150 us -> 141 us
  local copies, waits for them, and re-layouts: 31.2 us -> 106 us
  starting transfers between devices: 1.38 us -> 67.1 us
  other arithmetic: 36.8 us -> 82 us
  matrix products: 97.6 us -> 78.6 us
    all_gather x7 -> x3, waiting for transfers between devices: 555 us -> 22 us  [the longest x1 22 us: body(): od = lax.all_gather(od_piece, 'shard', axis=0, tiled=False)]
    reduce_scatter x7 -> x4, waiting for transfers between devices: 522 us -> 0.06 us  [the longest x2 0.04 us: reduce_rows(): lax.psum_scatter(a.reshape(-1, width), 'shard', scatter_dimension=0, tile...]
    ppermute x0 -> x68, waiting for transfers between devices: none -> 119 us  [the longest x65 105 us: swap(): return lax.ppermute(a, axis, SWAP)]
    psum x1 -> x0, waiting for transfers between devices: 71 us -> none  [body(): lax.psum(w_query_grad.astype(jnp.bfloat16), 'replica').astype(jnp.float32)]
    ppermute x0 -> x68, starting transfers between devices: none -> 66.4 us  [the longest x65 61.9 us: swap(): return lax.ppermute(a, axis, SWAP)]
    dot_general x27 -> x36, matrix products: 97.6 us -> 78.6 us  [the longest x8 23.6 us: dot_nt(): lax.dot_general(a, b, (((1,), (1,)), ((), ())), preferred_element_type=F32)]
    slice x1 -> x33, local copies, waits for them, and re-layouts: 0.19 us -> 16.7 us  [the longest x16 6.31 us: gather(): d0, d1 = (swap(ay[:half], 'x'), swap(ax[half:], 'y'))]
    another operation x4 -> x23, other arithmetic: 2.59 us -> 19 us  [the longest x8 5.88 us: spread(): got = [jnp.stack(plane.absolute(plane.gather(piece)), 0)]]
  transfers between devices with their start and end apart: 15 -> 75, of which waited for: 14 -> 39; matrix products, arithmetic and copies ran while one was open for 8% -> 41% of each run, Pallas kernels for 0% -> 0%
where the time goes in v1:
time: 549 us; the launch traced here: 539 us
  waiting for transfers between devices  141 us (26%)
  local copies, waits for them, and re-layouts  106 us (19%)
  other arithmetic  82 us (15%)
  matrix products  78.6 us (14%)
  starting transfers between devices  67.1 us (12%)
  blocking collectives  47.7 us (9%)
  between operations  16.4 us (3%)
    ppermute x65, waiting for transfers between devices, swap(): return lax.ppermute(a, axis, SWAP)  105 us
    ppermute x65, starting transfers between devices, swap(): return lax.ppermute(a, axis, SWAP)  61.9 us
    psum x1, blocking collectives, body(): lax.psum(jnp.concatenate([attn_gain_grad, mlp_gain_grad, qg_grad, kg_grad...  47.7 us
    unnamed x259, local copies, waits for them, and re-layouts  34.8 us
    dot_general x8, matrix products, dot_nt(): lax.dot_general(a, b, (((1,), (1,)), ((), ())), preferred_element_type=F32)  23.6 us
    all_gather x1, waiting for transfers between devices, body(): od = lax.all_gather(od_piece, 'shard', axis=0, tiled=False)  22 us
    dot_general x8, matrix products, dot_tn(): lax.dot_general(a, b, (((0,), (0,)), ((), ())), preferred_element_type=F32)  21.8 us
    dot_general x8, matrix products, dot(): return jnp.dot(a, b, preferred_element_type=F32)  16.4 us
  transfers between devices with their start and end apart: 75, of which 39 were waited for; matrix products, arithmetic and copies ran while one was open for 41% of the time, Pallas kernels for 0%

profile of v1, /device:TPU:0, one launch (start us, length us, event | category | flops | bytes accessed | tf_op | source)
XLA Modules:
  0.0 539.0 jit_solution(18039428215532744723)
XLA Ops:
  12.6 2.9 collective-permute-start
  18.0 10.3 %collective-permute-done = bf16[272,1024]{1,0:T(8,128)(2,1)S(1)} collective-permute-done((bf16[272,1024]{1,0:T(8,128)(2,1)}, bf16[272,1024]{1,0:T(8,128)(2,1)S(1)}, u32[]{:S(2)}, u32[]{:S(2)}) %collective-permute-start) | collective-permute-done | bytes 557088 | tf_op jit(solution)/shard_map/ppermute | solution.py:34
  33.4 3.3 collective-permute-done.3
  36.7 2.3 collective-permute-done.2
  42.2 3.0 multiply_cosine_fusion
  45.3 2.6 fusion.141
  53.2 22.0 %all-gather.9.cloned.1.call-done = bf16[640,1024]{1,0:T(8,128)(2,1)} async-done(((bf16[160,1024]{1,0:T(8,128)(2,1)}), bf16[640,1024]{1,0:T(8,128)(2,1)}) %all-gather.9.cloned.1.call-update) | async-done | bytes 1310736 | tf_op jit(solution)/shard_map/all_gather | solution.py:128
  76.4 2.4 collective-permute-start.4
  81.8 6.3 %collective-permute-done.4 = bf16[160,1024]{1,0:T(8,128)(2,1)S(1)} collective-permute-done((bf16[160,1024]{1,0:T(8,128)(2,1)S(1)}, bf16[160,1024]{1,0:T(8,128)(2,1)S(1)}, u32[]{:S(2)}, u32[]{:S(2)}) %collective-permute-start.4) | collective-permute-done | bytes 327712 | tf_op jit(solution)/shard_map/ppermute | solution.py:85
  88.1 5.2 collective-permute-done.5
  97.9 2.6 fusion.139
  106.2 3.4 fusion.114
  119.0 2.2 fusion.158
  129.0 2.8 fusion.159
  137.4 4.4 collective-permute-done.9
  148.9 10.7 %collective-permute-done.12 = bf16[256,1024]{1,0:T(8,128)(2,1)S(1)} collective-permute-done((bf16[256,1024]{1,0:T(8,128)(2,1)S(1)}, bf16[256,1024]{1,0:T(8,128)(2,1)S(1)}, u32[]{:S(2)}, u32[]{:S(2)}) %collective-permute-start.12) | collective-permute-done | bytes 524320 | tf_op jit(solution)/shard_map/ppermute | solution.py:34
  164.6 6.2 %collective-permute-done.23 = bf16[256,1024]{1,0:T(8,128)(2,1)S(1)} collective-permute-done((bf16[256,1024]{1,0:T(8,128)(2,1)S(1)}, bf16[256,1024]{1,0:T(8,128)(2,1)S(1)}, u32[]{:S(2)}, u32[]{:S(2)}) %collective-permute-start.23) | collective-permute-done | bytes 524320 | tf_op jit(solution)/shard_map/ppermute | solution.py:34
  176.7 3.4 collective-permute-done.24
  184.0 2.1 collective-permute-done.25
  194.2 4.0 collective-permute-done.16
  200.1 3.1 multiply_convert_fusion.3
  205.1 3.1 multiply_convert_fusion.1
  210.2 2.0 fusion.160
  231.4 2.9 convolution_convert_fusion.2
  234.3 3.4 collective-permute-done.29
  237.8 2.4 collective-permute-done.27
  240.2 6.8 %collective-permute-done.21 = bf16[256,1024]{1,0:T(8,128)(2,1)} collective-permute-done((bf16[256,1024]{1,0:T(8,128)(2,1)}, bf16[256,1024]{1,0:T(8,128)(2,1)}, u32[]{:S(2)}, u32[]{:S(2)}) %collective-permute-start.21) | collective-permute-done | bytes 524320 | tf_op jit(solution)/shard_map/ppermute | solution.py:34
  247.4 3.5 multiply_reduce_fusion
  251.0 3.4 constant_dynamic-update-slice_fusion.14
  256.6 2.6 add_convert_fusion.2
  268.5 4.8 collective-permute-done.60
  288.9 3.3 convolution_convert_fusion.7
  295.7 2.2 copy.298
  297.9 2.6 fusion.6
  317.4 2.4 fusion.88
  320.7 2.1 multiply_reduce_fusion.7
  324.0 3.3 multiply_add_fusion
  327.3 2.1 multiply_reduce_fusion.1
  332.2 3.2 multiply_convert_fusion.7
  341.3 3.6 convolution_convert_fusion.1
  350.2 3.3 collective-permute-done.45
  363.0 3.8 add_convert_fusion.1
  367.0 3.6 convolution_convert_fusion
  372.1 7.4 %fusion.3 = (f32[1024]{0:T(1024)S(1)}, bf16[1024,1024]{1,0:T(8,128)(2,1)S(1)}, f32[1024,1024]{1,0:T(8,128)}) fusion(f32[1024]{0:T(1024)S(1)} %add_rsqrt_fusion.4, bf16[144,1024]{1,0:T(8,128)(2,1)S(1)} %copy-done.93, bf16[128,1024]{1,0:T(8,128)(2,1)} %collective-permute-done.2, bf16[256,1024]{1,0:T(8,128)(2,1)S(1)} %copy-done.65, ...), kind=kOutput, calls=%fused_computation.5 | convolution fusion | flops 1092615168 | bytes 14721024 | tf_op jit(solution)/shard_map/dot_general | solution.py:26
  381.5 3.0 add_convert_fusion
  384.5 3.8 collective-permute-done.34
  392.4 47.7 %psum.7 = f32[2304]{0:T(1024)S(1)} all-reduce(f32[2304]{0:T(1024)S(1)} %pad_maximum_fusion.45), channel_id=1, replica_groups=mesh['shard'=4,'y'=2,'x'=2,'c'=2] {'shard','y','x','c'}, use_global_device_ids=true, to_apply=%region_28.29 | all-reduce | flops 2304 | bytes 18432 | tf_op jit(solution)/shard_map/psum | solution.py:261
  442.9 2.4 collective-permute-start.63
  445.4 4.4 collective-permute-done.63
  452.0 2.5 collective-permute-done.64
  460.1 2.2 collective-permute-done.48
  462.9 2.5 fusion.35
  466.9 2.9 collective-permute-done.51
  476.3 3.7 collective-permute-done.39
  482.2 2.2 bitcast_convert_fusion
  484.4 4.0 collective-permute-done.54
  494.1 2.1 collective-permute-done.55
  502.9 2.9 copy.301
  505.8 2.9 copy.306
  516.6 3.4 slice_bitcast_fusion
  519.9 2.4 copy.304
  522.3 2.4 copy.309
  524.7 3.6 copy.305
  528.3 3.7 copy.310
  (568 shorter events, 235.0 us)
Async XLA Ops:
  7.2 38.1 %all-gather.5.cloned.1.call-start = ((), (), s32[]{:S(2)}) async-start(), calls=%async_computation.4 | async-start | bytes 1310720 | tf_op jit(solution)/shard_map/all_gather | solution.py:125
  9.9 65.3 %all-gather.9.cloned.1.call-start = ((), (), s32[]{:S(2)}) async-start(), calls=%async_computation.10 | async-start | bytes 1638400 | tf_op jit(solution)/shard_map/all_gather | solution.py:128
  12.6 15.8 %collective-permute-start = (bf16[272,1024]{1,0:T(8,128)(2,1)}, bf16[272,1024]{1,0:T(8,128)(2,1)S(1)}, u32[]{:S(2)}, u32[]{:S(2)}) collective-permute-start(bf16[272,1024]{1,0:T(8,128)(2,1)} %fusion.77), channel_id=1, source_target_pairs={{0,2},{2,0},{1,3},{3,1},{4,6},{6,4},{5,7},{7,5},{8,10},{10,8},{9,1... | collective-permute-start | bytes 1671176 | tf_op jit(solution)/shard_map/ppermute | solution.py:34
  15.5 15.5 %collective-permute-start.1 = (bf16[272,1024]{1,0:T(8,128)(2,1)}, bf16[272,1024]{1,0:T(8,128)(2,1)S(1)}, u32[]{:S(2)}, u32[]{:S(2)}) collective-permute-start(bf16[272,1024]{1,0:T(8,128)(2,1)} %fusion.77), channel_id=1, source_target_pairs={{0,4},{4,0},{1,5},{5,1},{2,6},{6,2},{3,7},{7,3},{8,12},{12,8},{9,1... | collective-permute-start | bytes 1671176 | tf_op jit(solution)/shard_map/ppermute | solution.py:34
  28.3 8.4 %collective-permute-start.3 = (bf16[144,1024]{1,0:T(8,128)(2,1)S(1)}, bf16[144,1024]{1,0:T(8,128)(2,1)S(1)}, u32[]{:S(2)}, u32[]{:S(2)}) collective-permute-start(bf16[144,1024]{1,0:T(8,128)(2,1)S(1)} %slice.394), channel_id=1, source_target_pairs={{0,4},{4,0},{1,5},{5,1},{2,6},{6,2},{3,7},{7,3},{8,12},{12,8},{9,1... | collective-permute-start | bytes 884744 | tf_op jit(solution)/shard_map/ppermute | solution.py:34
  31.0 149.9 %all-gather.7.cloned.1.call-start = ((), (), s32[]{:S(2)}) async-start(), calls=%async_computation.5 | async-start | bytes 1966080 | tf_op jit(solution)/shard_map/all_gather | solution.py:130
  31.7 7.3 %collective-permute-start.2 = (bf16[128,1024]{1,0:T(8,128)(2,1)}, bf16[128,1024]{1,0:T(8,128)(2,1)}, u32[]{:S(2)}, u32[]{:S(2)}) collective-permute-start(bf16[128,1024]{1,0:T(8,128)(2,1)} %slice.393), channel_id=1, source_target_pairs={{0,2},{2,0},{1,3},{3,1},{4,6},{6,4},{5,7},{7,5},{8,10},{10,8},{9,1... | collective-permute-start | bytes 786440 | tf_op jit(solution)/shard_map/ppermute | solution.py:34
  49.9 48.0 %collective-permute-start.7 = (bf16[1024,512]{1,0:T(8,128)(2,1)}, bf16[1024,512]{1,0:T(8,128)(2,1)}, u32[]{:S(2)}, u32[]{:S(2)}) collective-permute-start(bf16[1024,512]{1,0:T(8,128)(2,1)} %all-gather.5.cloned.1.call-done), channel_id=1, source_target_pairs={{0,1},{1,0},{2,3},{3,2},{4,5},{5,4},{6,7},{7,6},{8,9},{9,8},{10,11... | collective-permute-start | bytes 3145736 | tf_op jit(solution)/shard_map/ppermute | solution.py:34
  76.4 11.7 %collective-permute-start.4 = (bf16[160,1024]{1,0:T(8,128)(2,1)S(1)}, bf16[160,1024]{1,0:T(8,128)(2,1)S(1)}, u32[]{:S(2)}, u32[]{:S(2)}) collective-permute-start(bf16[160,1024]{1,0:T(8,128)(2,1)S(1)} %get-tuple-element.169), channel_id=1, source_target_pairs={{0,6},{2,4},{4,2},{6,0},{1,7},{3,5},{5,3},{7,1},{8,14},{10,12},{12... | collective-permute-start | bytes 983048 | tf_op jit(solution)/shard_map/ppermute | solution.py:85
  78.9 14.4 %collective-permute-start.5 = (bf16[160,1024]{1,0:T(8,128)(2,1)S(1)}, bf16[160,1024]{1,0:T(8,128)(2,1)}, u32[]{:S(2)}, u32[]{:S(2)}) collective-permute-start(bf16[160,1024]{1,0:T(8,128)(2,1)S(1)} %get-tuple-element.168), channel_id=1, source_target_pairs={{0,4},{4,0},{1,5},{5,1},{2,6},{6,2},{3,7},{7,3},{8,12},{12,8},{9,1... | collective-permute-start | bytes 983048 | tf_op jit(solution)/shard_map/ppermute | solution.py:34
  79.4 13.9 %collective-permute-start.6 = (bf16[160,1024]{1,0:T(8,128)(2,1)S(1)}, bf16[160,1024]{1,0:T(8,128)(2,1)}, u32[]{:S(2)}, u32[]{:S(2)}) collective-permute-start(bf16[160,1024]{1,0:T(8,128)(2,1)S(1)} %get-tuple-element.167), channel_id=1, source_target_pairs={{0,2},{2,0},{1,3},{3,1},{4,6},{6,4},{5,7},{7,5},{8,10},{10,8},{9,1... | collective-permute-start | bytes 983048 | tf_op jit(solution)/shard_map/ppermute | solution.py:34
  97.9 30.0 %collective-permute-start.8 = (bf16[4,160,1024]{2,1,0:T(8,128)(2,1)}, bf16[4,160,1024]{2,1,0:T(8,128)(2,1)}, u32[]{:S(2)}, u32[]{:S(2)}) collective-permute-start(bf16[4,160,1024]{2,1,0:T(8,128)(2,1)} %pad_maximum_fusion.5), channel_id=1, source_target_pairs={{0,1},{1,0},{2,3},{3,2},{4,5},{5,4},{6,7},{7,6},{8,9},{9,8},{10,11... | collective-permute-start | bytes 3932168 | tf_op jit(solution)/shard_map/ppermute | solution.py:34
  132.8 9.0 %collective-permute-start.9 = (bf16[128,1024]{1,0:T(8,128)(2,1)}, bf16[128,1024]{1,0:T(8,128)(2,1)}, u32[]{:S(2)}, u32[]{:S(2)}) collective-permute-start(bf16[128,1024]{1,0:T(8,128)(2,1)} %get-tuple-element.148), channel_id=1, source_target_pairs={{0,4},{4,0},{1,5},{5,1},{2,6},{6,2},{3,7},{7,3},{8,12},{12,8},{9,1... | collective-permute-start | bytes 786440 | tf_op jit(solution)/shard_map/ppermute | solution.py:34
  134.2 8.8 %collective-permute-start.11 = (bf16[128,1024]{1,0:T(8,128)(2,1)}, bf16[128,1024]{1,0:T(8,128)(2,1)}, u32[]{:S(2)}, u32[]{:S(2)}) collective-permute-start(bf16[128,1024]{1,0:T(8,128)(2,1)} %get-tuple-element.147), channel_id=1, source_target_pairs={{0,2},{2,0},{1,3},{3,1},{4,6},{6,4},{5,7},{7,5},{8,10},{10,8},{9,1... | collective-permute-start | bytes 786440 | tf_op jit(solution)/shard_map/ppermute | solution.py:34
  136.9 306.0 %reduce-scatter.11.cloned.1.call-start = ((), (), s32[]{:S(2)}) async-start(), calls=%async_computation.9 | async-start | bytes 983040 | tf_op jit(solution)/shard_map/reduce_scatter | solution.py:216
  144.6 14.9 %collective-permute-start.12 = (bf16[256,1024]{1,0:T(8,128)(2,1)S(1)}, bf16[256,1024]{1,0:T(8,128)(2,1)S(1)}, u32[]{:S(2)}, u32[]{:S(2)}) collective-permute-start(bf16[256,1024]{1,0:T(8,128)(2,1)S(1)} %pad_maximum_fusion.21), channel_id=1, source_target_pairs={{0,4},{4,0},{1,5},{5,1},{2,6},{6,2},{3,7},{7,3},{8,12},{12,8},{9,1... | collective-permute-start | bytes 1572872 | tf_op jit(solution)/shard_map/ppermute | solution.py:34
  145.4 14.9 %collective-permute-start.10 = (bf16[256,1024]{1,0:T(8,128)(2,1)S(1)}, bf16[256,1024]{1,0:T(8,128)(2,1)S(1)}, u32[]{:S(2)}, u32[]{:S(2)}) collective-permute-start(bf16[256,1024]{1,0:T(8,128)(2,1)S(1)} %pad_maximum_fusion.20), channel_id=1, source_target_pairs={{0,2},{2,0},{1,3},{3,1},{4,6},{6,4},{5,7},{7,5},{8,10},{10,8},{9,1... | collective-permute-start | bytes 1572872 | tf_op jit(solution)/shard_map/ppermute | solution.py:34
  146.9 26.8 %collective-permute-start.22 = (bf16[256,1024]{1,0:T(8,128)(2,1)S(1)}, bf16[256,1024]{1,0:T(8,128)(2,1)S(1)}, u32[]{:S(2)}, u32[]{:S(2)}) collective-permute-start(bf16[256,1024]{1,0:T(8,128)(2,1)S(1)} %copy-done.53), channel_id=1, source_target_pairs={{0,2},{2,0},{1,3},{3,1},{4,6},{6,4},{5,7},{7,5},{8,10},{10,8},{9,1... | collective-permute-start | bytes 1572872 | tf_op jit(solution)/shard_map/ppermute | solution.py:34
  147.5 23.3 %collective-permute-start.23 = (bf16[256,1024]{1,0:T(8,128)(2,1)S(1)}, bf16[256,1024]{1,0:T(8,128)(2,1)S(1)}, u32[]{:S(2)}, u32[]{:S(2)}) collective-permute-start(bf16[256,1024]{1,0:T(8,128)(2,1)S(1)} %copy-done.53), channel_id=1, source_target_pairs={{0,4},{4,0},{1,5},{5,1},{2,6},{6,2},{3,7},{7,3},{8,12},{12,8},{9,1... | collective-permute-start | bytes 1572872 | tf_op jit(solution)/shard_map/ppermute | solution.py:34
  163.2 18.9 %collective-permute-start.14 = (bf16[256,1024]{1,0:T(8,128)(2,1)}, bf16[256,1024]{1,0:T(8,128)(2,1)}, u32[]{:S(2)}, u32[]{:S(2)}) collective-permute-start(bf16[256,1024]{1,0:T(8,128)(2,1)} %get-tuple-element.94), channel_id=1, source_target_pairs={{0,4},{4,0},{1,5},{5,1},{2,6},{6,2},{3,7},{7,3},{8,12},{12,8},{9,1... | collective-permute-start | bytes 1572872 | tf_op jit(solution)/shard_map/ppermute | solution.py:34
  170.8 9.3 %collective-permute-start.24 = (bf16[128,1024]{1,0:T(8,128)(2,1)S(1)}, bf16[128,1024]{1,0:T(8,128)(2,1)S(1)}, u32[]{:S(2)}, u32[]{:S(2)}) collective-permute-start(bf16[128,1024]{1,0:T(8,128)(2,1)S(1)} %slice.436), channel_id=1, source_target_pairs={{0,2},{2,0},{1,3},{3,1},{4,6},{6,4},{5,7},{7,5},{8,10},{10,8},{9,1... | collective-permute-start | bytes 786440 | tf_op jit(solution)/shard_map/ppermute | solution.py:34
  171.7 18.5 %collective-permute-start.13 = (bf16[256,1024]{1,0:T(8,128)(2,1)}, bf16[256,1024]{1,0:T(8,128)(2,1)}, u32[]{:S(2)}, u32[]{:S(2)}) collective-permute-start(bf16[256,1024]{1,0:T(8,128)(2,1)} %get-tuple-element.94), channel_id=1, source_target_pairs={{0,2},{2,0},{1,3},{3,1},{4,6},{6,4},{5,7},{7,5},{8,10},{10,8},{9,1... | collective-permute-start | bytes 1572872 | tf_op jit(solution)/shard_map/ppermute | solution.py:34
  174.5 11.7 %collective-permute-start.25 = (bf16[128,1024]{1,0:T(8,128)(2,1)}, bf16[128,1024]{1,0:T(8,128)(2,1)}, u32[]{:S(2)}, u32[]{:S(2)}) collective-permute-start(bf16[128,1024]{1,0:T(8,128)(2,1)} %slice.437), channel_id=1, source_target_pairs={{0,4},{4,0},{1,5},{5,1},{2,6},{6,2},{3,7},{7,3},{8,12},{12,8},{9,1... | collective-permute-start | bytes 786440 | tf_op jit(solution)/shard_map/ppermute | solution.py:34
  180.9 22.3 %collective-permute-start.17 = (bf16[1024,768]{1,0:T(8,128)(2,1)}, bf16[1024,768]{1,0:T(8,128)(2,1)S(1)}, u32[]{:S(2)}, u32[]{:S(2)}) collective-permute-start(bf16[1024,768]{1,0:T(8,128)(2,1)} %all-gather.7.cloned.1.call-done), channel_id=1, source_target_pairs={{0,1},{1,0},{2,3},{3,2},{4,5},{5,4},{6,7},{7,6},{8,9},{9,8},{10,11... | collective-permute-start | bytes 4718600 | tf_op jit(solution)/shard_map/ppermute | solution.py:34
  183.1 11.0 %collective-permute-start.15 = (bf16[128,1024]{1,0:T(8,128)(2,1)S(1)}, bf16[128,1024]{1,0:T(8,128)(2,1)S(1)}, u32[]{:S(2)}, u32[]{:S(2)}) collective-permute-start(bf16[128,1024]{1,0:T(8,128)(2,1)S(1)} %slice.421), channel_id=1, source_target_pairs={{0,2},{2,0},{1,3},{3,1},{4,6},{6,4},{5,7},{7,5},{8,10},{10,8},{9,1... | collective-permute-start | bytes 786440 | tf_op jit(solution)/shard_map/ppermute | solution.py:34
  212.3 8.5 %collective-permute-start.26 = (bf16[128,1024]{1,0:T(8,128)(2,1)S(1)}, bf16[128,1024]{1,0:T(8,128)(2,1)S(1)}, u32[]{:S(2)}, u32[]{:S(2)}) collective-permute-start(bf16[128,1024]{1,0:T(8,128)(2,1)S(1)} %get-tuple-element.140), channel_id=1, source_target_pairs={{0,4},{4,0},{1,5},{5,1},{2,6},{6,2},{3,7},{7,3},{8,12},{12,8},{9,1... | collective-permute-start | bytes 786440 | tf_op jit(solution)/shard_map/ppermute | solution.py:34
  212.9 8.5 %collective-permute-start.28 = (bf16[128,1024]{1,0:T(8,128)(2,1)S(1)}, bf16[128,1024]{1,0:T(8,128)(2,1)S(1)}, u32[]{:S(2)}, u32[]{:S(2)}) collective-permute-start(bf16[128,1024]{1,0:T(8,128)(2,1)S(1)} %get-tuple-element.139), channel_id=1, source_target_pairs={{0,2},{2,0},{1,3},{3,1},{4,6},{6,4},{5,7},{7,5},{8,10},{10,8},{9,1... | collective-permute-start | bytes 786440 | tf_op jit(solution)/shard_map/ppermute | solution.py:34
  217.0 9.4 %collective-permute-start.18 = (bf16[128,1024]{1,0:T(8,128)(2,1)S(1)}, bf16[128,1024]{1,0:T(8,128)(2,1)S(1)}, u32[]{:S(2)}, u32[]{:S(2)}) collective-permute-start(bf16[128,1024]{1,0:T(8,128)(2,1)S(1)} %get-tuple-element.144), channel_id=1, source_target_pairs={{0,4},{4,0},{1,5},{5,1},{2,6},{6,2},{3,7},{7,3},{8,12},{12,8},{9,1... | collective-permute-start | bytes 786440 | tf_op jit(solution)/shard_map/ppermute | solution.py:34
  217.9 9.2 %collective-permute-start.20 = (bf16[128,1024]{1,0:T(8,128)(2,1)S(1)}, bf16[128,1024]{1,0:T(8,128)(2,1)S(1)}, u32[]{:S(2)}, u32[]{:S(2)}) collective-permute-start(bf16[128,1024]{1,0:T(8,128)(2,1)S(1)} %get-tuple-element.143), channel_id=1, source_target_pairs={{0,2},{2,0},{1,3},{3,1},{4,6},{6,4},{5,7},{7,5},{8,10},{10,8},{9,1... | collective-permute-start | bytes 786440 | tf_op jit(solution)/shard_map/ppermute | solution.py:34
  222.3 15.4 %collective-permute-start.29 = (bf16[256,1024]{1,0:T(8,128)(2,1)}, bf16[256,1024]{1,0:T(8,128)(2,1)}, u32[]{:S(2)}, u32[]{:S(2)}) collective-permute-start(bf16[256,1024]{1,0:T(8,128)(2,1)} %pad_maximum_fusion.25), channel_id=1, source_target_pairs={{0,4},{4,0},{1,5},{5,1},{2,6},{6,2},{3,7},{7,3},{8,12},{12,8},{9,1... | collective-permute-start | bytes 1572872 | tf_op jit(solution)/shard_map/ppermute | solution.py:34
  225.0 15.2 %collective-permute-start.27 = (bf16[256,1024]{1,0:T(8,128)(2,1)}, bf16[256,1024]{1,0:T(8,128)(2,1)}, u32[]{:S(2)}, u32[]{:S(2)}) collective-permute-start(bf16[256,1024]{1,0:T(8,128)(2,1)} %pad_maximum_fusion.24), channel_id=1, source_target_pairs={{0,2},{2,0},{1,3},{3,1},{4,6},{6,4},{5,7},{7,5},{8,10},{10,8},{9,1... | collective-permute-start | bytes 1572872 | tf_op jit(solution)/shard_map/ppermute | solution.py:34
  228.2 18.8 %collective-permute-start.21 = (bf16[256,1024]{1,0:T(8,128)(2,1)}, bf16[256,1024]{1,0:T(8,128)(2,1)}, u32[]{:S(2)}, u32[]{:S(2)}) collective-permute-start(bf16[256,1024]{1,0:T(8,128)(2,1)} %pad_maximum_fusion.23), channel_id=1, source_target_pairs={{0,4},{4,0},{1,5},{5,1},{2,6},{6,2},{3,7},{7,3},{8,12},{12,8},{9,1... | collective-permute-start | bytes 1572872 | tf_op jit(solution)/shard_map/ppermute | solution.py:34
  230.6 16.8 %collective-permute-start.19 = (bf16[256,1024]{1,0:T(8,128)(2,1)}, bf16[256,1024]{1,0:T(8,128)(2,1)}, u32[]{:S(2)}, u32[]{:S(2)}) collective-permute-start(bf16[256,1024]{1,0:T(8,128)(2,1)} %pad_maximum_fusion.22), channel_id=1, source_target_pairs={{0,2},{2,0},{1,3},{3,1},{4,6},{6,4},{5,7},{7,5},{8,10},{10,8},{9,1... | collective-permute-start | bytes 1572872 | tf_op jit(solution)/shard_map/ppermute | solution.py:34
  234.3 22.3 %collective-permute-start.59 = (bf16[384,1024]{1,0:T(8,128)(2,1)S(1)}, bf16[384,1024]{1,0:T(8,128)(2,1)S(1)}, u32[]{:S(2)}, u32[]{:S(2)}) collective-permute-start(bf16[384,1024]{1,0:T(8,128)(2,1)S(1)} %convolution_convert_fusion.2), channel_id=1, source_target_pairs={{0,1},{1,0},{2,3},{3,2},{4,5},{5,4},{6,7},{7,6},{8,9},{9,8},{10,11... | collective-permute-start | bytes 2359304 | tf_op jit(solution)/shard_map/ppermute | solution.py:34
  254.3 25.9 %collective-permute-start.30 = (bf16[256,1024]{1,0:T(8,128)(2,1)}, bf16[256,1024]{1,0:T(8,128)(2,1)}, u32[]{:S(2)}, u32[]{:S(2)}) collective-permute-start(bf16[256,1024]{1,0:T(8,128)(2,1)} %get-tuple-element.91), channel_id=1, source_target_pairs={{0,2},{2,0},{1,3},{3,1},{4,6},{6,4},{5,7},{7,5},{8,10},{10,8},{9,1... | collective-permute-start | bytes 1572872 | tf_op jit(solution)/shard_map/ppermute | solution.py:34
  255.7 20.4 %collective-permute-start.31 = (bf16[256,1024]{1,0:T(8,128)(2,1)}, bf16[256,1024]{1,0:T(8,128)(2,1)}, u32[]{:S(2)}, u32[]{:S(2)}) collective-permute-start(bf16[256,1024]{1,0:T(8,128)(2,1)} %get-tuple-element.91), channel_id=1, source_target_pairs={{0,4},{4,0},{1,5},{5,1},{2,6},{6,2},{3,7},{7,3},{8,12},{12,8},{9,1... | collective-permute-start | bytes 1572872 | tf_op jit(solution)/shard_map/ppermute | solution.py:34
  260.9 12.4 %collective-permute-start.60 = (bf16[96,1024]{1,0:T(8,128)(2,1)}, bf16[96,1024]{1,0:T(8,128)(2,1)}, u32[]{:S(2)}, u32[]{:S(2)}) collective-permute-start(bf16[96,1024]{1,0:T(8,128)(2,1)} %get-tuple-element.191), channel_id=1, source_target_pairs={{0,6},{2,4},{4,2},{6,0},{1,7},{3,5},{5,3},{7,1},{8,14},{10,12},{12... | collective-permute-start | bytes 589832 | tf_op jit(solution)/shard_map/ppermute | solution.py:85
  262.1 12.7 %collective-permute-start.61 = (bf16[96,1024]{1,0:T(8,128)(2,1)}, bf16[96,1024]{1,0:T(8,128)(2,1)}, u32[]{:S(2)}, u32[]{:S(2)}) collective-permute-start(bf16[96,1024]{1,0:T(8,128)(2,1)} %get-tuple-element.190), channel_id=1, source_target_pairs={{0,4},{4,0},{1,5},{5,1},{2,6},{6,2},{3,7},{7,3},{8,12},{12,8},{9,1... | collective-permute-start | bytes 589832 | tf_op jit(solution)/shard_map/ppermute | solution.py:34
  263.7 11.2 %collective-permute-start.62 = (bf16[96,1024]{1,0:T(8,128)(2,1)}, bf16[96,1024]{1,0:T(8,128)(2,1)}, u32[]{:S(2)}, u32[]{:S(2)}) collective-permute-start(bf16[96,1024]{1,0:T(8,128)(2,1)} %get-tuple-element.189), channel_id=1, source_target_pairs={{0,2},{2,0},{1,3},{3,1},{4,6},{6,4},{5,7},{7,5},{8,10},{10,8},{9,1... | collective-permute-start | bytes 589832 | tf_op jit(solution)/shard_map/ppermute | solution.py:34
  277.8 8.7 %collective-permute-start.32 = (bf16[128,1024]{1,0:T(8,128)(2,1)}, bf16[128,1024]{1,0:T(8,128)(2,1)}, u32[]{:S(2)}, u32[]{:S(2)}) collective-permute-start(bf16[128,1024]{1,0:T(8,128)(2,1)} %slice.445), channel_id=1, source_target_pairs={{0,2},{2,0},{1,3},{3,1},{4,6},{6,4},{5,7},{7,5},{8,10},{10,8},{9,1... | collective-permute-start | bytes 786440 | tf_op jit(solution)/shard_map/ppermute | solution.py:34
  280.1 176.8 %reduce-scatter.7.cloned.1.call-start = ((), (), s32[]{:S(2)}) async-start(), calls=%async_computation.7 | async-start | bytes 655360 | tf_op jit(solution)/shard_map/reduce_scatter | solution.py:216
  281.2 6.9 %collective-permute-start.33 = (bf16[128,1024]{1,0:T(8,128)(2,1)S(1)}, bf16[128,1024]{1,0:T(8,128)(2,1)S(1)}, u32[]{:S(2)}, u32[]{:S(2)}) collective-permute-start(bf16[128,1024]{1,0:T(8,128)(2,1)S(1)} %slice.446), channel_id=1, source_target_pairs={{0,4},{4,0},{1,5},{5,1},{2,6},{6,2},{3,7},{7,3},{8,12},{12,8},{9,1... | collective-permute-start | bytes 786440 | tf_op jit(solution)/shard_map/ppermute | solution.py:34
  332.2 13.1 %collective-permute-start.44 = (bf16[256,1024]{1,0:T(8,128)(2,1)}, bf16[256,1024]{1,0:T(8,128)(2,1)S(1)}, u32[]{:S(2)}, u32[]{:S(2)}) collective-permute-start(bf16[256,1024]{1,0:T(8,128)(2,1)} %convolution_convert_fusion.5), channel_id=1, source_target_pairs={{0,1},{1,0},{2,3},{3,2},{4,5},{5,4},{6,7},{7,6},{8,9},{9,8},{10,11... | collective-permute-start | bytes 1572872 | tf_op jit(solution)/shard_map/ppermute | solution.py:34
  344.8 17.3 %collective-permute-start.38 = (bf16[1024,512]{1,0:T(8,128)(2,1)}, bf16[1024,512]{1,0:T(8,128)(2,1)}, u32[]{:S(2)}, u32[]{:S(2)}) collective-permute-start(bf16[1024,512]{1,0:T(8,128)(2,1)} %convolution_convert_fusion.1), channel_id=1, source_target_pairs={{0,1},{1,0},{2,3},{3,2},{4,5},{5,4},{6,7},{7,6},{8,9},{9,8},{10,11... | collective-permute-start | bytes 3145736 | tf_op jit(solution)/shard_map/ppermute | solution.py:34
  346.1 7.4 %collective-permute-start.45 = (bf16[64,1024]{1,0:T(8,128)(2,1)S(1)}, bf16[64,1024]{1,0:T(8,128)(2,1)S(1)}, u32[]{:S(2)}, u32[]{:S(2)}) collective-permute-start(bf16[64,1024]{1,0:T(8,128)(2,1)S(1)} %get-tuple-element.206), channel_id=1, source_target_pairs={{0,6},{2,4},{4,2},{6,0},{1,7},{3,5},{5,3},{7,1},{8,14},{10,12},{12... | collective-permute-start | bytes 393224 | tf_op jit(solution)/shard_map/ppermute | solution.py:85
  346.9 8.0 %collective-permute-start.46 = (bf16[64,1024]{1,0:T(8,128)(2,1)S(1)}, bf16[64,1024]{1,0:T(8,128)(2,1)S(1)}, u32[]{:S(2)}, u32[]{:S(2)}) collective-permute-start(bf16[64,1024]{1,0:T(8,128)(2,1)S(1)} %get-tuple-element.205), channel_id=1, source_target_pairs={{0,4},{4,0},{1,5},{5,1},{2,6},{6,2},{3,7},{7,3},{8,12},{12,8},{9,1... | collective-permute-start | bytes 393224 | tf_op jit(solution)/shard_map/ppermute | solution.py:34
  347.9 7.0 %collective-permute-start.47 = (bf16[64,1024]{1,0:T(8,128)(2,1)S(1)}, bf16[64,1024]{1,0:T(8,128)(2,1)S(1)}, u32[]{:S(2)}, u32[]{:S(2)}) collective-permute-start(bf16[64,1024]{1,0:T(8,128)(2,1)S(1)} %get-tuple-element.204), channel_id=1, source_target_pairs={{0,2},{2,0},{1,3},{3,1},{4,6},{6,4},{5,7},{7,5},{8,10},{10,8},{9,1... | collective-permute-start | bytes 393224 | tf_op jit(solution)/shard_map/ppermute | solution.py:34
  355.8 114.9 %reduce-scatter.5.cloned.1.call-start = ((), (), s32[]{:S(2)}) async-start(), calls=%async_computation.6 | async-start | bytes 1310720 | tf_op jit(solution)/shard_map/reduce_scatter | solution.py:211
  366.8 107.2 %reduce-scatter.9.cloned.1.call-start = ((), (), s32[]{:S(2)}) async-start(), calls=%async_computation.8 | async-start | bytes 1966080 | tf_op jit(solution)/shard_map/reduce_scatter | solution.py:211
  370.6 10.9 %collective-permute-start.53 = (bf16[1024,768]{1,0:T(8,128)(2,1)S(1)}, bf16[1024,768]{1,0:T(8,128)(2,1)S(1)}, u32[]{:S(2)}, u32[]{:S(2)}) collective-permute-start(bf16[1024,768]{1,0:T(8,128)(2,1)S(1)} %convolution_convert_fusion), channel_id=1, source_target_pairs={{0,1},{1,0},{2,3},{3,2},{4,5},{5,4},{6,7},{7,6},{8,9},{9,8},{10,11... | collective-permute-start | bytes 4718600 | tf_op jit(solution)/shard_map/ppermute | solution.py:34
  379.6 8.8 %collective-permute-start.34 = (bf16[128,1024]{1,0:T(8,128)(2,1)S(1)}, bf16[128,1024]{1,0:T(8,128)(2,1)S(1)}, u32[]{:S(2)}, u32[]{:S(2)}) collective-permute-start(bf16[128,1024]{1,0:T(8,128)(2,1)S(1)} %get-tuple-element.132), channel_id=1, source_target_pairs={{0,4},{4,0},{1,5},{5,1},{2,6},{6,2},{3,7},{7,3},{8,12},{12,8},{9,1... | collective-permute-start | bytes 786440 | tf_op jit(solution)/shard_map/ppermute | solution.py:34
  380.7 8.4 %collective-permute-start.36 = (bf16[128,1024]{1,0:T(8,128)(2,1)S(1)}, bf16[128,1024]{1,0:T(8,128)(2,1)S(1)}, u32[]{:S(2)}, u32[]{:S(2)}) collective-permute-start(bf16[128,1024]{1,0:T(8,128)(2,1)S(1)} %get-tuple-element.131), channel_id=1, source_target_pairs={{0,2},{2,0},{1,3},{3,1},{4,6},{6,4},{5,7},{7,5},{8,10},{10,8},{9,1... | collective-permute-start | bytes 786440 | tf_op jit(solution)/shard_map/ppermute | solution.py:34
  390.5 50.7 %collective-permute-start.37 = (bf16[256,1024]{1,0:T(8,128)(2,1)S(1)}, bf16[256,1024]{1,0:T(8,128)(2,1)S(1)}, u32[]{:S(2)}, u32[]{:S(2)}) collective-permute-start(bf16[256,1024]{1,0:T(8,128)(2,1)S(1)} %pad_maximum_fusion.29), channel_id=1, source_target_pairs={{0,4},{4,0},{1,5},{5,1},{2,6},{6,2},{3,7},{7,3},{8,12},{12,8},{9,1... | collective-permute-start | bytes 1572872 | tf_op jit(solution)/shard_map/ppermute | solution.py:34
  391.6 49.7 %collective-permute-start.35 = (bf16[256,1024]{1,0:T(8,128)(2,1)S(1)}, bf16[256,1024]{1,0:T(8,128)(2,1)S(1)}, u32[]{:S(2)}, u32[]{:S(2)}) collective-permute-start(bf16[256,1024]{1,0:T(8,128)(2,1)S(1)} %pad_maximum_fusion.28), channel_id=1, source_target_pairs={{0,2},{2,0},{1,3},{3,1},{4,6},{6,4},{5,7},{7,5},{8,10},{10,8},{9,1... | collective-permute-start | bytes 1572872 | tf_op jit(solution)/shard_map/ppermute | solution.py:34
  458.7 14.0 %collective-permute-start.67 = (bf16[4,96,1024]{2,1,0:T(8,128)(2,1)}, bf16[4,96,1024]{2,1,0:T(8,128)(2,1)}, u32[]{:S(2)}, u32[]{:S(2)}) collective-permute-start(bf16[4,96,1024]{2,1,0:T(8,128)(2,1)} %pad_maximum_fusion.17), channel_id=1, source_target_pairs={{0,1},{1,0},{2,3},{3,2},{4,5},{5,4},{6,7},{7,6},{8,9},{9,8},{10,11... | collective-permute-start | bytes 2359304 | tf_op jit(solution)/shard_map/ppermute | solution.py:34
  470.7 27.2 %collective-permute-start.52 = (bf16[4,64,1024]{2,1,0:T(8,128)(2,1)}, bf16[4,64,1024]{2,1,0:T(8,128)(2,1)}, u32[]{:S(2)}, u32[]{:S(2)}) collective-permute-start(bf16[4,64,1024]{2,1,0:T(8,128)(2,1)} %pad_maximum_fusion.31), channel_id=1, source_target_pairs={{0,1},{1,0},{2,3},{3,2},{4,5},{5,4},{6,7},{7,6},{8,9},{9,8},{10,11... | collective-permute-start | bytes 1572872 | tf_op jit(solution)/shard_map/ppermute | solution.py:34
  470.7 9.3 %collective-permute-start.39 = (bf16[256,512]{1,0:T(8,128)(2,1)}, bf16[256,512]{1,0:T(8,128)(2,1)S(1)}, u32[]{:S(2)}, u32[]{:S(2)}) collective-permute-start(bf16[256,512]{1,0:T(8,128)(2,1)} %reduce-scatter.5.cloned.1.call-done), channel_id=1, source_target_pairs={{0,4},{4,0},{1,5},{5,1},{2,6},{6,2},{3,7},{7,3},{8,12},{12,8},{9,1... | collective-permute-start | bytes 786440 | tf_op jit(solution)/shard_map/ppermute | solution.py:34
  472.0 9.4 %collective-permute-start.41 = (bf16[256,512]{1,0:T(8,128)(2,1)}, bf16[256,512]{1,0:T(8,128)(2,1)S(1)}, u32[]{:S(2)}, u32[]{:S(2)}) collective-permute-start(bf16[256,512]{1,0:T(8,128)(2,1)} %reduce-scatter.5.cloned.1.call-done), channel_id=1, source_target_pairs={{0,2},{2,0},{1,3},{3,1},{4,6},{6,4},{5,7},{7,5},{8,10},{10,8},{9,1... | collective-permute-start | bytes 786440 | tf_op jit(solution)/shard_map/ppermute | solution.py:34
  474.0 14.4 %collective-permute-start.54 = (bf16[256,768]{1,0:T(8,128)(2,1)}, bf16[256,768]{1,0:T(8,128)(2,1)S(1)}, u32[]{:S(2)}, u32[]{:S(2)}) collective-permute-start(bf16[256,768]{1,0:T(8,128)(2,1)} %reduce-scatter.9.cloned.1.call-done), channel_id=1, source_target_pairs={{0,4},{4,0},{1,5},{5,1},{2,6},{6,2},{3,7},{7,3},{8,12},{12,8},{9,1... | collective-permute-start | bytes 1179656 | tf_op jit(solution)/shard_map/ppermute | solution.py:34
  475.4 14.4 %collective-permute-start.56 = (bf16[256,768]{1,0:T(8,128)(2,1)}, bf16[256,768]{1,0:T(8,128)(2,1)S(1)}, u32[]{:S(2)}, u32[]{:S(2)}) collective-permute-start(bf16[256,768]{1,0:T(8,128)(2,1)} %reduce-scatter.9.cloned.1.call-done), channel_id=1, source_target_pairs={{0,2},{2,0},{1,3},{3,1},{4,6},{6,4},{5,7},{7,5},{8,10},{10,8},{9,1... | collective-permute-start | bytes 1179656 | tf_op jit(solution)/shard_map/ppermute | solution.py:34
  480.0 12.6 %collective-permute-start.40 = (bf16[128,512]{1,0:T(8,128)(2,1)S(1)}, bf16[128,512]{1,0:T(8,128)(2,1)S(1)}, u32[]{:S(2)}, u32[]{:S(2)}) collective-permute-start(bf16[128,512]{1,0:T(8,128)(2,1)S(1)} %slice.462), channel_id=1, source_target_pairs={{0,2},{2,0},{1,3},{3,1},{4,6},{6,4},{5,7},{7,5},{8,10},{10,8},{9,1... | collective-permute-start | bytes 393224 | tf_op jit(solution)/shard_map/ppermute | solution.py:34
  481.5 11.2 %collective-permute-start.42 = (bf16[128,512]{1,0:T(8,128)(2,1)S(1)}, bf16[128,512]{1,0:T(8,128)(2,1)S(1)}, u32[]{:S(2)}, u32[]{:S(2)}) collective-permute-start(bf16[128,512]{1,0:T(8,128)(2,1)S(1)} %slice.463), channel_id=1, source_target_pairs={{0,4},{4,0},{1,5},{5,1},{2,6},{6,2},{3,7},{7,3},{8,12},{12,8},{9,1... | collective-permute-start | bytes 393224 | tf_op jit(solution)/shard_map/ppermute | solution.py:34
  488.4 7.7 %collective-permute-start.55 = (bf16[128,768]{1,0:T(8,128)(2,1)S(1)}, bf16[128,768]{1,0:T(8,128)(2,1)S(1)}, u32[]{:S(2)}, u32[]{:S(2)}) collective-permute-start(bf16[128,768]{1,0:T(8,128)(2,1)S(1)} %slice.467), channel_id=1, source_target_pairs={{0,2},{2,0},{1,3},{3,1},{4,6},{6,4},{5,7},{7,5},{8,10},{10,8},{9,1... | collective-permute-start | bytes 589832 | tf_op jit(solution)/shard_map/ppermute | solution.py:34
  497.9 16.5 %collective-permute-start.58 = (bf16[4,256,768]{2,1,0:T(8,128)(2,1)}, bf16[4,256,768]{2,1,0:T(8,128)(2,1)}, u32[]{:S(2)}, u32[]{:S(2)}) collective-permute-start(bf16[4,256,768]{2,1,0:T(8,128)(2,1)} %pad_maximum_fusion.3), channel_id=1, source_target_pairs={{0,1},{1,0},{2,3},{3,2},{4,5},{5,4},{6,7},{7,6},{8,9},{9,8},{10,11... | collective-permute-start | bytes 4718600 | tf_op jit(solution)/shard_map/ppermute | solution.py:34
  (130 other events, 668.0 us)
Sparse Core Ops, SparseCore 0:
  10.2 30.6 all-gather.4
  43.0 32.1 all-gather.8
  137.0 35.7 all-gather.6
  280.3 21.9 reduce-scatter.10
  355.9 20.5 reduce-scatter.6
  379.2 25.3 reduce-scatter.4
  407.6 34.8 reduce-scatter.8

commit v2 on v1

v2 whole, which is shorter than its diff:
```python
import functools
import math

import jax
import jax.numpy as jnp
from jax import lax
from jax.experimental import pallas as pl
from jax.experimental.pallas import tpu as pltpu
from jax.sharding import Mesh
from jax.sharding import PartitionSpec as P

HEADS = 16
KV_HEADS = 8
HEAD = 128
GROUP = HEADS // KV_HEADS

EPS = 1e-06
ROPE_BASE = 1000000.0
MASKED = -1e30
SCALE = HEAD ** (-0.5)
BF = jnp.bfloat16
F32 = jnp.float32
SWAP = [(0, 1), (1, 0)]
B = 256


def dot(a, b):
    return jnp.dot(a, b, preferred_element_type=F32)


def dot_nt(a, b):
    return lax.dot_general(a, b, (((1,), (1,)), ((), ())), preferred_element_type=F32)


def dot_tn(a, b):
    return lax.dot_general(a, b, (((0,), (0,)), ((), ())), preferred_element_type=F32)


def swap(a, axis):
    return lax.ppermute(a, axis, SWAP)


tie = lax.optimization_barrier


def sds(shape, dtype):
    return jax.ShapeDtypeStruct(shape, dtype)


def hbm(shape, dtype):
    return pltpu.HBM(shape, dtype)


VM = pl.BlockSpec(memory_space=pltpu.VMEM)
SM = pl.BlockSpec(memory_space=pltpu.SMEM)


def kernel_call(body, outs, args, flops=0, scalars=0, **kw):
    moved = sum(a.size * a.dtype.itemsize for a in args) + sum(math.prod(o.shape) * o.dtype.itemsize for o in outs)
    if "grid" not in kw:
        kw = dict(in_specs=[SM] * scalars + [VM] * (len(args) - scalars), out_specs=[VM] * len(outs))
    return pl.pallas_call(
        body,
        out_shape=outs,
        compiler_params=pltpu.CompilerParams(vmem_limit_bytes=44 * 1024 * 1024),
        cost_estimate=pl.CostEstimate(flops=flops, bytes_accessed=moved, transcendentals=0),
        **kw,
    )(*args)


class Plane:
    def __init__(self, ny, nx):
        self.ny, self.nx, self.n = ny, nx, ny * nx
        self.square = ny == 2 and nx == 2
        self.axes = ("y", "x")

    def index(self):
        return lax.axis_index("y") * self.nx + lax.axis_index("x")

    def place(self, t, r):
        return jnp.bitwise_xor(t, r) if self.square else r

    def gather(self, top, low):
        if not self.square:
            g, h = (lax.all_gather(a, self.axes, axis=0, tiled=False) for a in (top, low))
            return [[g[i], h[i]] for i in range(self.n)]
        ty, lx = swap(top, "y"), swap(low, "x")
        tx, ly = swap(top, "x"), swap(low, "y")
        return [[top, low], [tx, lx], [ty, ly], [swap(ty, "x"), swap(lx, "y")]]

    def gather_whole(self, a):
        if not self.square:
            g = lax.all_gather(a, self.axes, axis=0, tiled=False)
            return [g[i] for i in range(self.n)]
        return [a, swap(a, "x"), swap(a, "y"), lax.ppermute(a, self.axes, [(i, 3 - i) for i in range(4)])]

    def scatter(self, blocks):
        if not self.square:
            a = jnp.concatenate([h for b in blocks for h in b], 0)
            a = lax.psum_scatter(a, self.axes, scatter_dimension=0, tiled=True)
            return [[a[: a.shape[0] // 2]], [a[a.shape[0] // 2 :]]]
        own, bx, by, bd = blocks
        fx, fy = swap(bd[0], "x"), swap(bd[1], "y")
        xt, yl = swap(bx[0], "x"), swap(by[1], "y")
        add = lambda u, v: (u.astype(F32) + v.astype(F32)).astype(BF)
        yt, xl = swap(add(by[0], fx), "y"), swap(add(bx[1], fy), "x")
        return [[own[0], xt, yt], [own[1], xl, yl]]

    def exchange(self, slice_for):
        if not self.square:
            a = jnp.stack([slice_for(i) for i in range(self.n)], 0)
            a = lax.all_to_all(a, self.axes, split_axis=0, concat_axis=0, tiled=True)
            return [a[i] for i in range(self.n)]
        t = self.index()
        return [
            slice_for(t),
            swap(slice_for(jnp.bitwise_xor(t, 1)), "x"),
            swap(slice_for(jnp.bitwise_xor(t, 2)), "y"),
            lax.ppermute(slice_for(jnp.bitwise_xor(t, 3)), self.axes, [(i, 3 - i) for i in range(4)]),
        ]


def columns(ref, lo, count, rows):
    s = ref.shape[0]
    got = [ref[:, (lo + j) * rows : (lo + j + 1) * rows, :].reshape(s * rows, B) for j in range(count)]
    return got[0] if count == 1 else jnp.concatenate(got, 1)


def split(ref):
    return jnp.concatenate([ref[0][...], ref[1][...]], 0)


def put(halves, value):
    k = halves[0].shape[0]
    halves[0][...] = value[:k].astype(halves[0].dtype)
    halves[1][...] = value[k:].astype(halves[1].dtype)


def rsq(v):
    return lax.rsqrt(jnp.mean(v * v, axis=-1, keepdims=True) + EPS)


def norm_back(v, r, gain, d):
    dg = d * gain
    return r * (dg - v * (r * r) * jnp.mean(dg * v, axis=-1, keepdims=True))


def half_roll(u):
    return pltpu.roll(u, HEAD // 2, 1)


def prep_block(length, gain, freq, tok, cotseg, nin, cos, sin, mask):
    x = tok[...].astype(F32)
    nin[...] = (x * rsq(x) * gain[...]).astype(BF)
    row = cotseg[length : length + 16, :length].astype(F32)[:1]
    row = jnp.broadcast_to(row, (length, length))
    col = row.T
    start = jnp.sum(jnp.where(row < col, 1.0, 0.0), axis=-1, keepdims=True)
    i = lax.broadcasted_iota(jnp.int32, (length, length), 0)
    j = lax.broadcasted_iota(jnp.int32, (length, length), 1)
    mask[...] = jnp.where((j <= i) & (row == col), 1.0, 0.0)
    pos = lax.broadcasted_iota(jnp.int32, (length, HEAD), 0).astype(F32) - start
    ang = pos * freq[...]
    lane = lax.broadcasted_iota(jnp.int32, (length, HEAD), 1)
    s = jnp.sin(ang)
    cos[...] = jnp.cos(ang)
    sin[...] = jnp.where(lane < HEAD // 2, -s, s)


def soft(qr, kr, mask):
    s = jnp.where(mask, dot_nt(qr, kr) * SCALE, MASKED)
    e = jnp.exp(s - jnp.max(s, axis=-1, keepdims=True))
    return e * (1.0 / jnp.sum(e, axis=-1, keepdims=True))


def attend_block(parts, wrows, qg, kg, wa, wo, nin, cos, sin, mask, lin, vals, mixed, out0, out1):
    keep = mask[...] > 0.0
    c, s = cos[...], sin[...]
    rot = lambda u: u * c + half_roll(u) * s
    n = nin[...]
    out = None
    for h in range(parts):
        q = dot(n, columns(wa[h], 0, 1, wrows))
        kv = dot(n, columns(wa[h], 1, 1, wrows))
        k, v = kv[:, :HEAD], kv[:, HEAD:].astype(BF)
        lin[:, h * 3 * HEAD : h * 3 * HEAD + 2 * HEAD] = q
        lin[:, h * 3 * HEAD + 2 * HEAD : (h + 1) * 3 * HEAD] = k
        vals[:, h * HEAD : (h + 1) * HEAD] = v
        kr = rot(k * rsq(k) * kg[...]).astype(BF)
        for g in range(GROUP):
            qh = q[:, g * HEAD : (g + 1) * HEAD]
            p = soft(rot(qh * rsq(qh) * qg[...]).astype(BF), kr, keep)
            at = h * GROUP * HEAD + g * HEAD
            mixed[:, at : at + HEAD] = dot(p.astype(BF), v).astype(BF)
        term = dot(mixed[:, h * GROUP * HEAD : (h + 1) * GROUP * HEAD], wo[h][...])
        out = term if out is None else out + term
    put((out0, out1), out)


def mlp_block(parts, wrows, ff, wgu, wd, nm0, nm1, cotseg, product, dgu, out0, out1, dm0, dm1):
    n, ct = split((nm0, nm1)), cotseg[: 2 * nm0.shape[0], :]
    out, dm = None, None
    for h in range(parts):
        w = columns(wgu[h], 0, 2 * ff // B, wrows)
        d = wd[h][...]
        gu = dot(n, w)
        gate, up = gu[:, :ff], gu[:, ff:]
        sg = jax.nn.sigmoid(gate)
        act = gate * sg
        pr = (act * up).astype(BF)
        product[:, h * ff : (h + 1) * ff] = pr
        dp = dot_nt(ct, d)
        d_gate = (dp * up * (sg + act * (1.0 - sg))).astype(BF)
        d_up = (dp * act).astype(BF)
        at = h * 2 * ff
        dgu[:, at : at + ff] = d_gate
        dgu[:, at + ff : at + 2 * ff] = d_up
        a, b = dot(pr, d), dot_nt(dgu[:, at : at + 2 * ff], w)
        out = a if out is None else out + a
        dm = b if dm is None else dm + b
    put((out0, out1), out)
    put((dm0, dm1), dm)


def attend_back_block(parts, wrows, qg, kg, wa, wo, dh0, dh1, tok, lin, vals, cos, sin, mask, dqkv, din0, din1, gains):
    keep = mask[...] > 0.0
    c, s = cos[...], sin[...]
    rot = lambda u: u * c + half_roll(u) * s
    rot_back = lambda u: u * c - half_roll(u) * s
    d = split((dh0, dh1))
    din, qgain, kgain = None, 0.0, 0.0
    for h in range(parts):
        dm = dot_nt(d, wo[h][...]).astype(BF)
        base = h * 3 * HEAD
        k = lin[:, base + 2 * HEAD : base + 3 * HEAD]
        v = vals[:, h * HEAD : (h + 1) * HEAD]
        rk = rsq(k)
        kr = rot(k * rk * kg[...]).astype(BF)
        dk, dv = 0.0, 0.0
        at = h * 4 * HEAD
        for g in range(GROUP):
            q = lin[:, base + g * HEAD : base + (g + 1) * HEAD]
            rq = rsq(q)
            qr = rot(q * rq * qg[...]).astype(BF)
            p = soft(qr, kr, keep)
            dmh = dm[:, g * HEAD : (g + 1) * HEAD]
            da = dot_nt(dmh, v)
            dv = dv + dot_tn(p.astype(BF), dmh)
            ds = (p * (da - jnp.sum(p * da, axis=-1, keepdims=True))).astype(BF)
            dq = rot_back(dot(ds, kr) * SCALE)
            dk = dk + dot_tn(ds, qr)
            qgain = qgain + jnp.sum(dq * q * rq, axis=0, keepdims=True)
            dqkv[:, at + g * HEAD : at + (g + 1) * HEAD] = norm_back(q, rq, qg[...], dq).astype(BF)
        dk = rot_back(dk * SCALE)
        kgain = kgain + jnp.sum(dk * k * rk, axis=0, keepdims=True)
        dqkv[:, at + 2 * HEAD : at + 3 * HEAD] = norm_back(k, rk, kg[...], dk).astype(BF)
        dqkv[:, at + 3 * HEAD : at + 4 * HEAD] = dv.astype(BF)
        term = dot_nt(dqkv[:, at : at + 4 * HEAD], columns(wa[h], 0, 2, wrows))
        din = term if din is None else din + term
    put((din0, din1), din)
    x = tok[...].astype(F32)
    width = x.shape[1]
    gains[:, :width] += jnp.sum(din * (x * rsq(x)), axis=0, keepdims=True)
    gains[:, width : width + HEAD] += qgain
    gains[:, width + HEAD :] += kgain


def added(refs):
    total = refs[0][...].astype(F32)
    for r in refs[1:]:
        total = total + r[...].astype(F32)
    return total


def mid_kernel(nterms, tokens, gain, *refs):
    terms, (hidden, nm0, nm1) = refs[: 2 * nterms], refs[2 * nterms :]
    half = tokens.shape[0] // 2
    for i, nm in enumerate((nm0, nm1)):
        at = slice(i * half, (i + 1) * half)
        h = tokens[at, :].astype(F32) + added(terms[i * nterms : (i + 1) * nterms])
        hidden[at, :] = h
        nm[...] = (h * rsq(h) * gain[...]).astype(BF)


def mid_back_kernel(nterms, hidden, cot, gain, *refs):
    terms, (d_hidden, low0, low1, ggrad) = refs[: 2 * nterms], refs[2 * nterms :]
    half = hidden.shape[0] // 2
    total = 0.0
    for i, low in enumerate((low0, low1)):
        at = slice(i * half, (i + 1) * half)
        d = added(terms[i * nterms : (i + 1) * nterms])
        h = hidden[at, :]
        r = rsq(h)
        out = cot[at, :].astype(F32) + norm_back(h, r, gain[...], d)
        d_hidden[at, :] = out
        low[...] = out.astype(BF)
        total = total + jnp.sum(d * h * r, axis=0, keepdims=True)
    ggrad[...] = total


def last_kernel(nterms, tokens, d_hidden, gain, *refs):
    terms, (out,) = refs[: 2 * nterms], refs[2 * nterms :]
    half = tokens.shape[0] // 2
    for i in range(2):
        at = slice(i * half, (i + 1) * half)
        x = tokens[at, :].astype(F32)
        d = added(terms[i * nterms : (i + 1) * nterms])
        out[at, :] = (d_hidden[at, :] + norm_back(x, rsq(x), gain[...], d)).astype(BF)


def out_kernel(nterms, hidden, *refs):
    terms, (out,) = refs[: 2 * nterms], refs[2 * nterms :]
    half = hidden.shape[0] // 2
    for i in range(2):
        at = slice(i * half, (i + 1) * half)
        out[at, :] = (hidden[at, :] + added(terms[i * nterms : (i + 1) * nterms])).astype(BF)


def arrange(plane, t, blocks, cb):
    q = blocks[0].shape[0] // cb

    def body(where, *refs):
        for r, ref in enumerate(refs[:-1]):
            start = pl.multiple_of(plane.place(where[0], r) * q, 16)
            for j in range(cb):
                refs[-1][pl.ds(start, q), j * B : (j + 1) * B] = ref[j * q : (j + 1) * q, :]

    return kernel_call(body, [sds((len(blocks) * q, cb * B), BF)], [t.astype(jnp.int32)[None], *blocks], scalars=1)[0]


def grad_columns(plane, t, lhs, rhs, half, width, size, other, below=None):
    nblk = width // B
    flat_l, flat_r = sum(lhs, []), sum(rhs, [])
    nl, nr = len(flat_l), len(flat_r)
    rows = flat_l[0].shape[1] // size
    more = 0 if below is None else below[0].shape[0]

    def body(where, *refs):
        left = jnp.concatenate([r[...] for r in refs[:nl]], 0)
        right = jnp.concatenate([r[...] for r in refs[nl : nl + nr]], 0)
        rest, out = refs[nl + nr : -1], refs[-1]
        got = dot_tn(left, right)
        for j in range(nblk):
            part = got[:, j * B : (j + 1) * B]
            if other is not None:
                part = part + rest[0][0, j * rows : (j + 1) * rows, :].astype(F32)
            out[0, j * rows : (j + 1) * rows, :] = part.astype(BF)
        if more:
            z = pl.program_id(0)
            for r in range(plane.n):
                @pl.when(plane.place(where[0], r) == z)
                def _():
                    out[0, nblk * rows :, :] = rest[-plane.n + r][...]

    tall = lambda k: pl.BlockSpec((1, k, B), lambda z, w: (z, 0, 0))
    in_specs = [pl.BlockSpec((a.shape[0], rows), lambda z, w: (0, z)) for a in flat_l]
    in_specs += [pl.BlockSpec((a.shape[0], width), lambda z, w: (0, half)) for a in flat_r]
    args = flat_l + flat_r
    if other is not None:
        in_specs.append(tall(nblk * rows))
        args = args + [other]
    if more:
        in_specs += [pl.BlockSpec((more, B), lambda z, w: (0, 0))] * plane.n
        args = args + below
    tokens = sum(a.shape[0] for a in flat_l)
    out = sds((size, nblk * rows + more, B), BF)
    return pl.pallas_call(
        body,
        out_shape=out,
        grid_spec=pltpu.PrefetchScalarGridSpec(
            num_scalar_prefetch=1, grid=(size,), in_specs=in_specs, out_specs=tall(nblk * rows + more)
        ),
        compiler_params=pltpu.CompilerParams(vmem_limit_bytes=44 * 1024 * 1024),
        cost_estimate=pl.CostEstimate(
            flops=2 * tokens * rows * size * width,
            bytes_accessed=sum(a.size * 2 for a in args) + math.prod(out.shape) * 2,
            transcendentals=0,
        ),
    )(t.astype(jnp.int32)[None], *args)


def grad_rows(lhs, rhs, tokens_each, half, width, n, other):
    flat_l, flat_r = lhs, sum(rhs, [])
    nl = len(flat_l)
    cb = flat_r[0].shape[1] // B
    q = width // n

    def body(*refs):
        left = jnp.concatenate([r[...] for r in refs[:nl]], 0)
        right = jnp.concatenate([r[...] for r in refs[nl : nl + len(flat_r)]], 0)
        got = dot_tn(left, right).reshape(n, q, B)
        if other is not None:
            got = got + refs[-2][...].astype(F32)
        refs[-1][...] = got.astype(BF)

    spec = pl.BlockSpec((n, q, B), lambda j: (0, j, 0))
    in_specs = [pl.BlockSpec((a.shape[0], width), lambda j: (0, half)) for a in flat_l]
    in_specs += [pl.BlockSpec((tokens_each, B), lambda j: (0, j)) for a in flat_r]
    args = flat_l + flat_r
    if other is not None:
        in_specs.append(spec)
        args = args + [other]
    tokens = sum(a.shape[0] for a in flat_l)
    return kernel_call(
        body, [sds((n, cb * q, B), BF)], args, flops=2 * tokens * width * cb * B,
        grid=(cb,), in_specs=in_specs, out_specs=[spec],
    )[0]


def over_blocks(block, shared, per_block, outs, flops, total=False):
    flat = []
    shape = []
    for a in shared:
        shape.append(len(a) if isinstance(a, list) else None)
        flat += a if isinstance(a, list) else [a]
    nb, k, o = len(per_block), len(per_block[0]), len(outs[0])
    args = flat + sum(per_block, [])
    out_shapes = sum(outs, []) + ([total] if total else [])

    def body(*refs):
        at, head = 0, []
        for m in shape:
            head.append(refs[at] if m is None else refs[at : at + m])
            at += 1 if m is None else m
        ins, results = refs[at : at + nb * k], refs[at + nb * k :]
        tail = ()
        if total:
            results[-1][...] = jnp.zeros_like(results[-1])
            tail = (results[-1],)
        for b in range(nb):
            block(*head, *ins[b * k : (b + 1) * k], *results[b * o : (b + 1) * o], *tail)

    got = kernel_call(body, out_shapes, args, flops=flops * nb)
    return [got[b * o : (b + 1) * o] for b in range(nb)], (got[-1] if total else None)


def make_body(size, plane, halves):
    n = plane.n
    parts = 2 if halves else 1
    first, rest = [n - 1], list(range(n - 1))[::-1]

    def body(tokens, segment_ids, attn_gain, w_query, w_key, w_value, query_gain, key_gain,
             w_out, mlp_gain, w_gate, w_up, w_down, cotangent):
        t = plane.index()
        c = lax.axis_index("c") if halves else 0
        rows, width = tokens.shape
        length = segment_ids.shape[1]
        assert rows == length
        half = rows // 2
        cb = width // B
        wrows = w_query.shape[0]
        cut_a, cut_b = 2 * wrows, 2 * w_gate.shape[1] // n // parts // B * wrows
        out_rows, down_rows = w_out.shape[0] // parts // n, w_down.shape[0] // parts // n
        ff = n * down_rows
        gain_in, gain_mid = attn_gain[None, :], mlp_gain[None, :]
        qg, kg = query_gain[None, :], key_gain[None, :]
        freq = ROPE_BASE ** (-2.0 * (jnp.arange(HEAD) % (HEAD // 2)).astype(F32) / HEAD)[None, :]

        def pick(col_weights, row_weight):
            each = [w.shape[1] // n // parts for w in col_weights]
            total = sum(each)
            q = row_weight.shape[0] // parts // n
            high = total // B * wrows
            where = jnp.stack([t * parts + c, c * n + t]).astype(jnp.int32)

            def fill(_, *refs):
                a = jnp.concatenate([r[...] for r in refs[:-2]], 1)
                for j in range(total // B):
                    refs[-1][j * wrows : (j + 1) * wrows, :] = a[:, j * B : (j + 1) * B]
                for j in range(cb):
                    refs[-1][high + j * q : high + (j + 1) * q, :] = refs[-2][:, j * B : (j + 1) * B]

            return pl.pallas_call(
                fill,
                out_shape=sds((high + cb * q, B), BF),
                grid_spec=pltpu.PrefetchScalarGridSpec(
                    num_scalar_prefetch=1,
                    grid=(1,),
                    in_specs=[pl.BlockSpec((wrows, k), lambda i, at: (0, at[0])) for k in each]
                    + [pl.BlockSpec((q, width), lambda i, at: (at[1], 0))],
                    out_specs=pl.BlockSpec((high + cb * q, B), lambda i, at: (0, 0)),
                ),
            )(where, *col_weights, row_weight)

        def both(a):
            return [a, swap(a, "c")] if halves else [a]

        def rows_to_chip(got, cut):
            blocks = plane.exchange(lambda i: lax.dynamic_slice_in_dim(got, i, 1, 0)[0, cut:])
            return arrange(plane, t, blocks, cb)

        got_a = lax.all_gather(pick([w_query, w_key, w_value], w_out), "shard", axis=0, tiled=False)

        seg_rows = jnp.pad(segment_ids.astype(BF), ((0, 15), (0, width - length)))
        ext = plane.gather(tokens, jnp.concatenate([cotangent, seg_rows], 0))
        tok, cot = [b[0] for b in ext], [b[1] for b in ext]
        w_gate, w_up, w_down, tok[n - 1] = tie((w_gate, w_up, w_down, tok[n - 1]))
        piece_b = pick([w_gate, w_up], w_down)
        prep, _ = over_blocks(
            functools.partial(prep_block, length), [gain_in, freq],
            [[tok[r], cot[r]] for r in range(n)],
            [[hbm((length, width), BF), hbm((length, HEAD), F32), hbm((length, HEAD), F32), hbm((length, length), F32)]] * n,
            0,
        )
        got_a, prep, piece_b = tie((got_a, prep, piece_b))
        nin, tables = [a[0] for a in prep], [a[1:] for a in prep]
        got_b = lax.all_gather(piece_b, "shard", axis=0, tiled=False)
        wa, wo = both(got_a), both(rows_to_chip(got_a, cut_a))

        def term_types(r):
            return [sds((half, width), F32 if r == 0 and plane.square else BF)] * 2

        def run(block, shared, ins, outs, flops, order, total=None, before=lambda got: None):
            got, totals = {}, []
            for group in order:
                res, tot = over_blocks(block, shared, [ins[r] for r in group], [outs(r) for r in group], flops, total)
                got.update(zip(group, res))
                totals.append(tot)
            return [[got[r][i] for r in range(n)] for i in range(len(outs(0)))], totals

        (lin, vals, mixed, o0, o1), _ = run(
            functools.partial(attend_block, parts, wrows), [qg, kg, wa, wo],
            [[nin[r], *tables[r]] for r in range(n)],
            lambda r: [hbm((length, parts * 3 * HEAD), F32), hbm((length, parts * HEAD), BF),
                       hbm((length, parts * GROUP * HEAD), BF), *term_types(r)],
            2 * length * width * parts * 6 * HEAD, [first, rest],
        )
        terms = plane.scatter(list(zip(o0, o1)))
        nterms = len(terms[0])
        hidden, nm0, nm1 = kernel_call(
            functools.partial(mid_kernel, nterms),
            [hbm((rows, width), F32), sds((half, width), BF), sds((half, width), BF)],
            [tokens, gain_mid, *terms[0], *terms[1]],
        )
        nm = plane.gather(nm0, nm1)
        got_b, nm = tie((got_b, nm))
        wgu, wd = both(got_b), both(rows_to_chip(got_b, cut_b))

        (product, dgu, o0, o1, m0, m1), _ = run(
            functools.partial(mlp_block, parts, wrows, ff), [wgu, wd],
            [[*nm[r], cot[r]] for r in range(n)],
            lambda r: [hbm((rows, parts * ff), BF), hbm((rows, parts * 2 * ff), BF),
                       *[hbm(o.shape, o.dtype) for o in term_types(r)], *term_types(r)],
            2 * length * width * parts * 7 * ff, [first, rest],
        )
        terms_mid = plane.scatter(list(zip(m0, m1)))

        def owned(make):
            if halves:
                return make(0, swap(make(1, None), "c"))
            return lax.psum(make(0, None), "c")

        down = owned(lambda h, o: grad_rows(product, [[a] for a in cot], rows, h, ff, n, o))
        gu_other = grad_columns(plane, t, nm, [[a] for a in dgu], 1, 2 * ff, size, None) if halves else None
        terms_mid, gu_other, down = tie((terms_mid, gu_other, down))
        d_hidden, dh0, dh1, mlp_grad = kernel_call(
            functools.partial(mid_back_kernel, nterms),
            [hbm((rows, width), F32), sds((half, width), BF), sds((half, width), BF), sds((1, width), F32)],
            [hidden, cotangent, gain_mid, *terms_mid[0], *terms_mid[1]],
        )
        dh = plane.gather(dh0, dh1)

        def merged(lhs, rhs, width_, other, low):
            low = plane.exchange(lambda i: lax.dynamic_index_in_dim(low, i, 0, keepdims=False))
            if halves:
                return grad_columns(plane, t, lhs, rhs, 0, width_, size, swap(other, "c"), low)
            a = grad_columns(plane, t, lhs, rhs, 0, width_, size, None)
            return jnp.concatenate([lax.psum(a, "c"), jnp.stack(low, 0)], 1)

        grads_b = merged(nm, [[a] for a in dgu], 2 * ff, gu_other, down)
        dh[n - 1], o0, o1, grads_b = tie((dh[n - 1], o0, o1, grads_b))
        grads_b = lax.psum_scatter(grads_b.reshape(-1, B), "shard", scatter_dimension=0, tiled=True)
        terms_out = plane.scatter(list(zip(o0, o1)))

        out = owned(lambda h, o: grad_rows(mixed, dh, half, h, GROUP * HEAD, n, o))
        (dqkv, i0, i1), gains = run(
            functools.partial(attend_back_block, parts, wrows), [qg, kg, wa, wo],
            [[*dh[r], tok[r], lin[r], vals[r], *tables[r]] for r in range(n)],
            lambda r: [hbm((rows, parts * 4 * HEAD), BF), *term_types(r)],
            2 * length * width * parts * 6 * HEAD, [[0], list(range(1, n))], sds((1, width + 2 * HEAD), F32),
        )
        dqkv = [[a] for a in dqkv]
        lhs = [[a] for a in nin]
        qkv_other = grad_columns(plane, t, lhs, dqkv, 1, 4 * HEAD, size, None) if halves else None
        grads_a = merged(lhs, dqkv, 4 * HEAD, qkv_other, out)
        grads_a, grads_b, terms_out = tie((grads_a, grads_b, terms_out))
        grads_a = lax.psum_scatter(grads_a.reshape(-1, B), "shard", scatter_dimension=0, tiled=True)

        activations = kernel_call(
            functools.partial(out_kernel, nterms), [sds((rows, width), BF)],
            [hidden, *terms_out[0], *terms_out[1]],
        )[0]
        terms_in = plane.scatter(list(zip(i0, i1)))
        input_grad = kernel_call(
            functools.partial(last_kernel, nterms),
            [sds((rows, width), BF)],
            [tokens, d_hidden, gain_in, *terms_in[0], *terms_in[1]],
        )[0]

        gains = jnp.concatenate([functools.reduce(jnp.add, gains), mlp_grad], 1)
        if plane.square and size == 4:
            for axis in ("c", "x", "y"):
                gains = gains + swap(gains, axis)
            for k in (1, 2):
                gains = gains + lax.ppermute(gains, "shard", [(i, i ^ k) for i in range(4)])
        else:
            gains = lax.psum(gains, ("shard", "y", "x", "c"))
        gains = gains[0]

        def assemble(piece, outs, write):
            mine = plane.gather_whole(piece)
            got = [(r, 0, a) for r, a in enumerate(mine)]
            if halves:
                got += [(r, 1, swap(a, "c")) for r, a in enumerate(mine)]

            def body(where, *refs):
                for (r, other, _), ref in zip(got, refs):
                    core = jnp.bitwise_xor(where[1], other) if halves else 0
                    write(ref, plane.place(where[0], r), core, refs[len(got) :])

            where = jnp.stack([t, c]).astype(jnp.int32)
            return kernel_call(body, outs, [where] + [a for _, _, a in got], scalars=1)

        def write_cols(ref, j, todo, src, core):
            a = ref[j * wrows : (j + 1) * wrows, :].astype(F32)
            for lo, hi, out, per, at in todo:
                start = pl.multiple_of((src * parts + core) * per + at, HEAD)
                out[:, pl.ds(start, hi - lo)] = a[:, lo:hi]

        def write_rows(ref, base, q, src, core, out):
            start = pl.multiple_of((core * n + src) * q, 16)
            for j in range(cb):
                a = ref[base + j * q : base + (j + 1) * q, :].astype(F32)
                out[pl.ds(start, q), j * B : (j + 1) * B] = a

        def write_b(ref, src, core, outs):
            gate, up, down = outs
            for j in range(2 * ff // B):
                todo = []
                for out, lo in ((gate, 0), (up, ff)):
                    a, b = max(j * B, lo), min((j + 1) * B, lo + ff)
                    if a < b:
                        todo.append((a - j * B, b - j * B, out, ff, a - lo))
                write_cols(ref, j, todo, src, core)
            write_rows(ref, cut_b, down_rows, src, core, down)

        def write_a(ref, src, core, outs):
            q, k, v, out = outs
            write_cols(ref, 0, [(0, B, q, B, 0)], src, core)
            write_cols(ref, 1, [(0, HEAD, k, HEAD, 0), (HEAD, B, v, HEAD, 0)], src, core)
            write_rows(ref, cut_a, out_rows, src, core, out)

        like = lambda w: sds(w.shape, F32)
        gate_g, up_g, down_g = assemble(grads_b, [like(w_gate), like(w_up), like(w_down)], write_b)
        grads_a, gate_g, up_g, down_g = tie((grads_a, gate_g, up_g, down_g))
        query_g, key_g, value_g, out_g = assemble(
            grads_a, [like(w_query), like(w_key), like(w_value), like(w_out)], write_a)

        return (
            activations,
            input_grad,
            gains[:width],
            query_g,
            key_g,
            value_g,
            gains[width : width + HEAD],
            gains[width + HEAD : width + 2 * HEAD],
            out_g,
            gains[width + 2 * HEAD :],
            gate_g,
            up_g,
            down_g,
        )

    return body


def solution(mesh):
    size, replicas = mesh.shape["shard"], mesh.shape["replica"]
    ny, nx = replicas // 4, 2
    assert size == ny * nx
    plane = Plane(ny, nx)
    fine = Mesh(mesh.devices.reshape(size, ny, nx, 2), ("shard", "y", "x", "c"))
    halves = KV_HEADS % (2 * plane.n) == 0
    every = P(("shard", "y", "x", "c"), None)
    shard, copy = P("shard", None), P()
    return jax.shard_map(
        make_body(size, plane, halves),
        mesh=fine,
        in_specs=(every, every, copy, shard, shard, shard, copy, copy, shard, copy, shard, shard, shard, every),
        out_specs=(every, every, copy, shard, shard, shard, copy, copy, shard, copy, shard, shard, shard),
        check_vma=False,
    )
```

time: 549 us -> 384 us (0.70); the launches traced: 539 us -> 380 us
  Pallas kernels: 0 us -> 104 us
  other arithmetic: 82 us -> 3.38 us
  matrix products: 78.6 us -> 0 us
  local copies, waits for them, and re-layouts: 106 us -> 34.7 us
  blocking collectives: 47.7 us -> 0 us
  starting transfers between devices: 67.1 us -> 74.8 us
  waiting for transfers between devices: 141 us -> 147 us
    pallas_call x0 -> x25, Pallas kernels: none -> 104 us  [the longest x19 86.6 us: kernel_call(): pl.pallas_call(body, out_shape=outs, compiler_params=pltpu.CompilerParams...]
    dot_general x36 -> x0, matrix products: 78.6 us -> none  [the longest x8 23.6 us: dot_nt(): lax.dot_general(a, b, (((1,), (1,)), ((), ())), preferred_element_type=F32)]
    psum x1 -> x0, blocking collectives: 47.7 us -> none  [body(): lax.psum(jnp.concatenate([attn_gain_grad, mlp_gain_grad, qg_grad, kg_grad...]
    all_gather x3 -> x2, waiting for transfers between devices: 22 us -> 0.02 us  [the longest x1 0.02 us: body(): lax.all_gather(pick([w_query, w_key, w_value], w_out), 'shard', axis=0, t...]
    reduce_sum x17 -> x0, other arithmetic: 19.9 us -> none  [the longest x7 10.3 us: norm_parts(): return lax.rsqrt(jnp.mean(v * v, axis=-1, keepdims=True) + EPS)]
    another operation x23 -> x2, other arithmetic: 19 us -> 0.66 us  [the longest x1 0.59 us: pick(): where = jnp.stack([t * parts + c, c * n + t]).astype(jnp.int32)]
    ppermute x65 -> x73, waiting for transfers between devices: 105 us -> 121 us  [swap(): return lax.ppermute(a, axis, SWAP)]
    transpose x7 -> x0, local copies, waits for them, and re-layouts: 15.7 us -> none  [place_cols(): return a.transpose(2, 1, 0, 3).reshape(a.shape[2], -1)]
  transfers between devices with their start and end apart: 75 -> 85, of which waited for: 39 -> 35; matrix products, arithmetic and copies ran while one was open for 41% -> 2% of each run, Pallas kernels for 0% -> 24%
where the time goes in v2:
time: 384 us; the launch traced here: 380 us
  waiting for transfers between devices  147 us (38%)
  Pallas kernels  104 us (27%)
  starting transfers between devices  74.8 us (19%)
  local copies, waits for them, and re-layouts  34.7 us (9%)
  between operations  15.7 us (4%)
    ppermute x73, waiting for transfers between devices, swap(): return lax.ppermute(a, axis, SWAP)  121 us
    pallas_call x19, Pallas kernels, kernel_call(): pl.pallas_call(body, out_shape=outs, compiler_params=pltpu.CompilerParams...  86.6 us
    ppermute x73, starting transfers between devices, swap(): return lax.ppermute(a, axis, SWAP)  61 us
    unnamed x294, local copies, waits for them, and re-layouts  30.7 us
    ppermute x2, waiting for transfers between devices, gather_whole(): lax.ppermute(a, self.axes, [(i, 3 - i) for i in range(4)])  13.1 us
    pallas_call x4, Pallas kernels, grad_columns(): pl.pallas_call(body, out_shape=out, grid_spec=pltpu.PrefetchScalarGridSpe...  12 us
    ppermute x4, waiting for transfers between devices, exchange(): lax.ppermute(slice_for(jnp.bitwise_xor(t, 3)), self.axes, [(i, 3 - i) for...  11.2 us
  transfers between devices with their start and end apart: 85, of which 35 were waited for; matrix products, arithmetic and copies ran while one was open for 2% of the time, Pallas kernels for 24%

profile of v2, /device:TPU:0, one launch (start us, length us, event | category | flops | bytes accessed | tf_op | source)
XLA Modules:
  0.0 379.5 jit_solution(476633129496819488)
XLA Ops:
  7.8 2.6 shard_map.237
  10.6 3.0 collective-permute-start.1
  13.6 1.5 collective-permute-start.2
  15.6 10.6 %collective-permute-done.1.refs_5_.refs_9_ = bf16[272,1024]{1,0:T(8,128)(2,1)S(1)} collective-permute-done((bf16[272,1024]{1,0:T(8,128)(2,1)S(1)}, bf16[272,1024]{1,0:T(8,128)(2,1)S(1)}, u32[]{:S(2)}, u32[]{:S(2)}) %collective-permute-start.1) | collective-permute-done | bytes 557088 | tf_op jit(solution)/shard_map/ppermute | solution.py:40
  26.2 1.8 collective-permute-start.5
  30.5 12.8 %collective-permute-done.4.refs_8_.refs_24_ = bf16[256,1024]{1,0:T(8,128)(2,1)S(1)} collective-permute-done((bf16[256,1024]{1,0:T(8,128)(2,1)S(1)}, bf16[256,1024]{1,0:T(8,128)(2,1)S(1)}, u32[]{:S(2)}, u32[]{:S(2)}) %collective-permute-start.4) | collective-permute-done | bytes 524320 | tf_op jit(solution)/shard_map/ppermute | solution.py:40
  44.1 2.6 shard_map.239
  46.8 5.2 %collective-permute-done.refs_4_.refs_8_ = bf16[256,1024]{1,0:T(8,128)(2,1)} collective-permute-done((bf16[256,1024]{1,0:T(8,128)(2,1)S(1)}, bf16[256,1024]{1,0:T(8,128)(2,1)}, u32[]{:S(2)}, u32[]{:S(2)}) %collective-permute-start) | collective-permute-done | bytes 524320 | tf_op jit(solution)/shard_map/ppermute | solution.py:40
  53.4 5.7 %shard_map.238 = (bf16[256,1024]{1,0:T(8,128)(2,1)}, f32[256,128]{1,0:T(8,128)}, f32[256,128]{1,0:T(8,128)}, f32[256,256]{1,0:T(8,128)}, bf16[256,1024]{1,0:T(8,...) custom-call(f32[1,1024]{1,0:T(1,128)S(1)} %bitcast.63, ...), custom_call_target="tpu_custom_call" | custom-call | bytes 8524288 | tf_op jit(solution)/shard_map/pallas_call | solution.py:62
  62.5 1.5 collective-permute-start.8
  64.6 3.8 collective-permute-done.9.refs_3_
  68.4 2.1 collective-permute-done.8.refs_2_
  70.6 1.9 collective-permute-done.10.refs_5_
  72.7 4.0 %shard_map.242 = (f32[256,768]{1,0:T(8,128)}, bf16[256,256]{1,0:T(8,128)(2,1)}, bf16[256,512]{1,0:T(8,128)(2,1)}, bf16[128,1024]{1,0:T(8,128)(2,1)S(1)}, bf16[128,1024]{1,0:T(8,128)(2,1)S(1)}) custom-call(f32[1,128]{1,0:T(1,128)S(1)} %bitcast.65, f32[1,128]{1,0:T(1,128)S(1)} %bitcast.69, bf16[4,768,256]{2,1,0:T(8,128)(2,1)S(1)} %bitcast.53, ...), custom_call_target="tpu_custom_call" | custom-call | flops 805306368 | bytes 6947840 | tf_op jit(solution)/shard_map/pallas_call | solution.py:62
  78.9 9.4 %shard_map.241 = (f32[256,768]{1,0:T(8,128)}, bf16[256,256]{1,0:T(8,128)(2,1)}, bf16[256,512]{1,0:T(8,128)(2,1)}, bf16[128,1024]{1,0:T(8,128)(2,1)S(1)}, bf16[12...) custom-call(f32[1,128]{1,0:T(1,128)S(1)} %bitcast.66, ...), custom_call_target="tpu_custom_call" | custom-call | flops 2415919104 | bytes 12977152 | tf_op jit(solution)/shard_map/pallas_call | solution.py:62
  91.1 1.6 collective-permute-start.15
  92.7 4.9 %collective-permute-done.11.refs_1_ = bf16[128,1024]{1,0:T(8,128)(2,1)S(1)} collective-permute-done((bf16[128,1024]{1,0:T(8,128)(2,1)S(1)}, bf16[128,1024]{1,0:T(8,128)(2,1)S(1)}, u32[]{:S(2)}, u32[]{:S(2)}) %collective-permute-start.11) | collective-permute-done | bytes 262176 | tf_op jit(solution)/shard_map/ppermute | solution.py:40
  98.1 3.9 %collective-permute-done.13.refs_2_ = bf16[128,1024]{1,0:T(8,128)(2,1)S(1)} collective-permute-done((bf16[128,1024]{1,0:T(8,128)(2,1)S(1)}, bf16[128,1024]{1,0:T(8,128)(2,1)S(1)}, u32[]{:S(2)}, u32[]{:S(2)}) %collective-permute-start.13) | collective-permute-done | bytes 262176 | tf_op jit(solution)/shard_map/ppermute | solution.py:40
  108.1 4.5 %collective-permute-done.19.refs_4_ = bf16[128,1024]{1,0:T(8,128)(2,1)S(1)} collective-permute-done((bf16[128,1024]{1,0:T(8,128)(2,1)S(1)}, bf16[128,1024]{1,0:T(8,128)(2,1)S(1)}, u32[]{:S(2)}, u32[]{:S(2)}) %collective-permute-start.19) | collective-permute-done | bytes 262176 | tf_op jit(solution)/shard_map/ppermute | solution.py:40
  116.2 3.3 collective-permute-done.17.refs_7_.refs_2_
  125.2 1.6 collective-permute-start.26
  128.7 5.2 %collective-permute-done.26.refs_3_ = bf16[384,256]{1,0:T(8,128)(2,1)S(1)} collective-permute-done((bf16[384,256]{1,0:T(8,128)(2,1)S(1)}, bf16[384,256]{1,0:T(8,128)(2,1)S(1)}, u32[]{:S(2)}, u32[]{:S(2)}) %collective-permute-start.26) | collective-permute-done | bytes 196640 | tf_op jit(solution)/shard_map/ppermute | solution.py:119
  133.9 3.8 collective-permute-done.25.refs_2_
  137.9 2.2 collective-permute-done.27.refs_3_
  140.2 1.7 copy-done.113
  141.8 5.8 %shard_map.246 = (bf16[256,768]{1,0:T(8,128)(2,1)}, bf16[256,1536]{1,0:T(8,128)(2,1)}, bf16[128,1024]{1,0:T(8,128)(2,1)}, bf16[128,1024]{1,0:T(8,128)(2,1)}, bf1...) custom-call(bf16[4,1152,256]{2,1,0:T(8,128)(2,1)S(1)} %bitcast.59, ...), custom_call_target="tpu_custom_call" | custom-call | flops 2818572288 | bytes 9601024 | tf_op jit(solution)/shard_map/pallas_call | solution.py:62
  148.5 11.8 %shard_map.245 = (bf16[256,768]{1,0:T(8,128)(2,1)}, bf16[256,1536]{1,0:T(8,128)(2,1)}, bf16[128,1024]{1,0:T(8,128)(2,1)}, bf16[128,1024]{1,0:T(8,128)(2,1)}, bf1...) custom-call(bf16[4,1152,256]{2,1,0:T(8,128)(2,1)S(1)} %bitcast.60, ...), custom_call_target="tpu_custom_call" | custom-call | flops 8455716864 | bytes 17268736 | tf_op jit(solution)/shard_map/pallas_call | solution.py:62
  163.3 2.6 shard_map.248
  170.0 5.1 %collective-permute-done.31 = bf16[128,1024]{1,0:T(8,128)(2,1)S(1)} collective-permute-done((bf16[128,1024]{1,0:T(8,128)(2,1)S(1)}, bf16[128,1024]{1,0:T(8,128)(2,1)S(1)}, u32[]{:S(2)}, u32[]{:S(2)}) %collective-permute-start.31) | collective-permute-done | bytes 262176 | tf_op jit(solution)/shard_map/ppermute | solution.py:40
  176.5 3.1 shard_map.247
  179.6 2.3 shard_map.249
  181.9 4.0 %collective-permute-done.30.refs_2_ = bf16[128,1024]{1,0:T(8,128)(2,1)S(1)} collective-permute-done((bf16[128,1024]{1,0:T(8,128)(2,1)S(1)}, bf16[128,1024]{1,0:T(8,128)(2,1)S(1)}, u32[]{:S(2)}, u32[]{:S(2)}) %collective-permute-start.30) | collective-permute-done | bytes 262176 | tf_op jit(solution)/shard_map/ppermute | solution.py:40
  187.3 1.6 shard_map.250
  192.5 2.2 collective-permute-done.44.refs_16_
  195.9 4.0 %collective-permute-done.37.refs_14_.refs_8_ = bf16[128,1024]{1,0:T(8,128)(2,1)S(1)} collective-permute-done((bf16[128,1024]{1,0:T(8,128)(2,1)S(1)}, bf16[128,1024]{1,0:T(8,128)(2,1)S(1)}, u32[]{:S(2)}, u32[]{:S(2)}) %collective-permute-start.37) | collective-permute-done | bytes 262176 | tf_op jit(solution)/shard_map/ppermute | solution.py:40
  201.8 2.4 collective-permute-done.43.refs_15_
  204.3 3.3 shard_map.252
  222.2 6.3 %shard_map.251 = (bf16[256,1024]{1,0:T(8,128)(2,1)}, f32[128,1024]{1,0:T(8,128)S(1)}, f32[128,1024]{1,0:T(8,128)S(1)}, f32[1,1280]{1,0:T(1,128)S(1)}) custom-call(f32[1,128]{1,0:T(1,128)S(1)} %bitcast.67, f32[1,128]{1,0:T(1,128)S(1)} %bitcast.71, bf16[4,768,256]{2,1,0:T(8,128)(2,1)S(1)} %bitcast.55, bf16[4,768,256]{2,1,0:T(8,128)(2,1)S(1)} %collective-permute-done.6.refs_3_, ...), custom_call_target="tpu_custom_call" | custom-call | flops 805306368 | bytes 8263680 | tf_op jit(solution)/shard_map/pallas_call | solution.py:62
  231.0 2.1 shard_map.255
  233.4 19.5 %shard_map.253 = (bf16[256,1024]{1,0:T(8,128)(2,1)}, bf16[128,1024]{1,0:T(8,128)(2,1)}, bf16[128,1024]{1,0:T(8,128)(2,1)S(1)}, bf16[256,1024]{1,0:T(8,128)(2,1)}...) custom-call(f32[1,128]{1,0:T(1,128)S(1)} %bitcast.68, ...), custom_call_target="tpu_custom_call" | custom-call | flops 2415919104 | bytes 14817280 | tf_op jit(solution)/shard_map/pallas_call | solution.py:62
  256.4 2.3 shard_map.254
  261.3 2.0 shard_map.256
  263.4 1.6 collective-permute-start.49
  266.3 6.3 %collective-permute-done.53 = bf16[128,1024]{1,0:T(8,128)(2,1)S(1)} collective-permute-done((bf16[128,1024]{1,0:T(8,128)(2,1)S(1)}, bf16[128,1024]{1,0:T(8,128)(2,1)S(1)}, u32[]{:S(2)}, u32[]{:S(2)}) %collective-permute-start.53) | collective-permute-done | bytes 262176 | tf_op jit(solution)/shard_map/ppermute | solution.py:40
  276.0 2.8 collective-permute-done.47.refs_10_
  279.1 3.3 shard_map.257
  282.6 2.8 collective-permute-done.52.refs_2_
  291.3 13.1 %collective-permute-done.69.refs_3_ = bf16[1152,256]{1,0:T(8,128)(2,1)S(1)} collective-permute-done((bf16[1152,256]{1,0:T(8,128)(2,1)S(1)}, bf16[1152,256]{1,0:T(8,128)(2,1)S(1)}, u32[]{:S(2)}, u32[]{:S(2)}) %collective-permute-start.69) | collective-permute-done | bytes 589856 | tf_op jit(solution)/shard_map/ppermute | solution.py:95
  304.3 8.8 %collective-permute-done.68.refs_2_ = bf16[1152,256]{1,0:T(8,128)(2,1)S(1)} collective-permute-done((bf16[1152,256]{1,0:T(8,128)(2,1)S(1)}, bf16[1152,256]{1,0:T(8,128)(2,1)S(1)}, u32[]{:S(2)}, u32[]{:S(2)}) %collective-permute-start.68) | collective-permute-done | bytes 589856 | tf_op jit(solution)/shard_map/ppermute | solution.py:40
  314.0 3.4 collective-permute-done.63
  317.7 3.4 collective-permute-done.64
  321.1 1.9 collective-permute-start.65
  323.0 1.9 collective-permute-done.65
  325.2 1.8 collective-permute-start.56
  327.3 2.5 collective-permute-start.66
  329.8 5.0 %shard_map.260 = (f32[256,3072]{1,0:T(8,128)}, f32[256,3072]{1,0:T(8,128)}, f32[768,1024]{1,0:T(8,128)}) custom-call(s32[2]{0:T(128)S(1)} %pad_add_fusion.1.where, bf16[1152,256]{1,0:T(8,128)(2,1)S(1)} %copy-done.92, bf16[1152,256]{1,0:T(8,128)(2,1)S(1)} %collective-permute-done.67.refs_1_, bf16[1152,256]{1,0:T(8,128)(2,1)S(1)} %collective-permute-done.68.refs_2_, ...), custom_call_target="tpu_custom_call" | custom-call | bytes 14155784 | tf_op jit(solution)/shard_map/pallas_call | solution.py:62
  334.8 1.7 collective-permute-start.76
  336.5 1.7 collective-permute-start.75
  339.5 1.7 collective-permute-start.61
  342.7 16.3 %collective-permute-done.61.refs_5_ = bf16[128,1024]{1,0:T(8,128)(2,1)S(1)} collective-permute-done((bf16[128,1024]{1,0:T(8,128)(2,1)}, bf16[128,1024]{1,0:T(8,128)(2,1)S(1)}, u32[]{:S(2)}, u32[]{:S(2)}) %collective-permute-start.61) | collective-permute-done | bytes 262176 | tf_op jit(solution)/shard_map/ppermute | solution.py:40
  359.0 1.7 collective-permute-start.60
  360.6 2.7 collective-permute-done.58.refs_2_
  365.5 2.5 shard_map.259
  369.0 3.7 shard_map.261
  (455 shorter events, 92.1 us)
Async XLA Ops:
  7.2 52.1 %all-gather.5.cloned.1.call-start = ((), (), s32[]{:S(2)}) async-start(), calls=%async_computation.4 | async-start | bytes 1966080 | tf_op jit(solution)/shard_map/all_gather | solution.py:492
  10.5 113.3 %all-gather.7.cloned.1.call-start = ((), (), s32[]{:S(2)}) async-start(), calls=%async_computation.5 | async-start | bytes 2949120 | tf_op jit(solution)/shard_map/all_gather | solution.py:507
  10.6 15.6 %collective-permute-start.1 = (bf16[272,1024]{1,0:T(8,128)(2,1)S(1)}, bf16[272,1024]{1,0:T(8,128)(2,1)S(1)}, u32[]{:S(2)}, u32[]{:S(2)}) collective-permute-start(bf16[272,1024]{1,0:T(8,128)(2,1)S(1)} %fusion.1.refs_3_.refs_12_.refs_4_), channel_id=1, source_target_pairs={{0,2},{2,0},{1,3},{3,1},{4,6},{6,4},{5,7},{7,5},{8,10},{10,8},{9,1... | collective-permute-start | bytes 1671176 | tf_op jit(solution)/shard_map/ppermute | solution.py:40
  13.6 14.8 %collective-permute-start.2 = (bf16[256,1024]{1,0:T(8,128)(2,1)S(1)}, bf16[256,1024]{1,0:T(8,128)(2,1)S(1)}, u32[]{:S(2)}, u32[]{:S(2)}) collective-permute-start(bf16[256,1024]{1,0:T(8,128)(2,1)S(1)} %copy-done.5), channel_id=1, source_target_pairs={{0,4},{4,0},{1,5},{5,1},{2,6},{6,2},{3,7},{7,3},{8,12},{12,8},{9,1... | collective-permute-start | bytes 1572872 | tf_op jit(solution)/shard_map/ppermute | solution.py:40
  15.1 36.8 %collective-permute-start.3 = (bf16[272,1024]{1,0:T(8,128)(2,1)S(1)}, bf16[272,1024]{1,0:T(8,128)(2,1)S(1)}, u32[]{:S(2)}, u32[]{:S(2)}) collective-permute-start(bf16[272,1024]{1,0:T(8,128)(2,1)S(1)} %fusion.1.refs_3_.refs_12_.refs_4_), channel_id=1, source_target_pairs={{0,4},{4,0},{1,5},{5,1},{2,6},{6,2},{3,7},{7,3},{8,12},{12,8},{9,1... | collective-permute-start | bytes 1671176 | tf_op jit(solution)/shard_map/ppermute | solution.py:40
  26.2 25.7 %collective-permute-start.5 = (bf16[272,1024]{1,0:T(8,128)(2,1)S(1)}, bf16[272,1024]{1,0:T(8,128)(2,1)S(1)}, u32[]{:S(2)}, u32[]{:S(2)}) collective-permute-start(bf16[272,1024]{1,0:T(8,128)(2,1)S(1)} %collective-permute-done.1.refs_5_.refs_9_), channel_id=1, source_target_pairs={{0,4},{4,0},{1,5},{5,1},{2,6},{6,2},{3,7},{7,3},{8,12},{12,8},{9,1... | collective-permute-start | bytes 1671176 | tf_op jit(solution)/shard_map/ppermute | solution.py:40
  28.5 14.9 %collective-permute-start.4 = (bf16[256,1024]{1,0:T(8,128)(2,1)S(1)}, bf16[256,1024]{1,0:T(8,128)(2,1)S(1)}, u32[]{:S(2)}, u32[]{:S(2)}) collective-permute-start(bf16[256,1024]{1,0:T(8,128)(2,1)S(1)} %collective-permute-done.2.refs_6_.refs_16_), channel_id=1, source_target_pairs={{0,2},{2,0},{1,3},{3,1},{4,6},{6,4},{5,7},{7,5},{8,10},{10,8},{9,1... | collective-permute-start | bytes 1572872 | tf_op jit(solution)/shard_map/ppermute | solution.py:40
  29.5 22.5 %collective-permute-start = (bf16[256,1024]{1,0:T(8,128)(2,1)S(1)}, bf16[256,1024]{1,0:T(8,128)(2,1)}, u32[]{:S(2)}, u32[]{:S(2)}) collective-permute-start(bf16[256,1024]{1,0:T(8,128)(2,1)S(1)} %copy-done.5), channel_id=1, source_target_pairs={{0,2},{2,0},{1,3},{3,1},{4,6},{6,4},{5,7},{7,5},{8,10},{10,8},{9,1... | collective-permute-start | bytes 1572872 | tf_op jit(solution)/shard_map/ppermute | solution.py:40
  59.3 226.8 %reduce-scatter.3.cloned.1.call-start = ((), (), s32[]{:S(2)}) async-start(), calls=%async_computation.2 | async-start | bytes 2949120 | tf_op jit(solution)/shard_map/reduce_scatter | solution.py:572
  59.5 13.0 %collective-permute-start.6 = (bf16[4,768,256]{2,1,0:T(8,128)(2,1)}, bf16[4,768,256]{2,1,0:T(8,128)(2,1)S(1)}, u32[]{:S(2)}, u32[]{:S(2)}) collective-permute-start(bf16[4,768,256]{2,1,0:T(8,128)(2,1)} %bitcast.50), channel_id=1, source_target_pairs={{0,1},{1,0},{2,3},{3,2},{4,5},{5,4},{6,7},{7,6},{8,9},{9,8},{10,11... | collective-permute-start | bytes 4718600 | tf_op jit(solution)/shard_map/ppermute | solution.py:40
  76.7 13.6 %collective-permute-start.12 = (bf16[128,1024]{1,0:T(8,128)(2,1)S(1)}, bf16[128,1024]{1,0:T(8,128)(2,1)S(1)}, u32[]{:S(2)}, u32[]{:S(2)}) collective-permute-start(bf16[128,1024]{1,0:T(8,128)(2,1)S(1)} %get-tuple-element.203), channel_id=1, source_target_pairs={{0,2},{2,0},{1,3},{3,1},{4,6},{6,4},{5,7},{7,5},{8,10},{10,8},{9,1... | collective-permute-start | bytes 786440 | tf_op jit(solution)/shard_map/ppermute | solution.py:40
  77.6 13.5 %collective-permute-start.14 = (bf16[128,1024]{1,0:T(8,128)(2,1)S(1)}, bf16[128,1024]{1,0:T(8,128)(2,1)S(1)}, u32[]{:S(2)}, u32[]{:S(2)}) collective-permute-start(bf16[128,1024]{1,0:T(8,128)(2,1)S(1)} %get-tuple-element.206), channel_id=1, source_target_pairs={{0,4},{4,0},{1,5},{5,1},{2,6},{6,2},{3,7},{7,3},{8,12},{12,8},{9,1... | collective-permute-start | bytes 786440 | tf_op jit(solution)/shard_map/ppermute | solution.py:40
  88.4 9.2 %collective-permute-start.11 = (bf16[128,1024]{1,0:T(8,128)(2,1)S(1)}, bf16[128,1024]{1,0:T(8,128)(2,1)S(1)}, u32[]{:S(2)}, u32[]{:S(2)}) collective-permute-start(bf16[128,1024]{1,0:T(8,128)(2,1)S(1)} %get-tuple-element.197), channel_id=1, source_target_pairs={{0,2},{2,0},{1,3},{3,1},{4,6},{6,4},{5,7},{7,5},{8,10},{10,8},{9,1... | collective-permute-start | bytes 786440 | tf_op jit(solution)/shard_map/ppermute | solution.py:40
  88.9 9.2 %collective-permute-start.16 = (bf16[128,1024]{1,0:T(8,128)(2,1)S(1)}, bf16[128,1024]{1,0:T(8,128)(2,1)S(1)}, u32[]{:S(2)}, u32[]{:S(2)}) collective-permute-start(bf16[128,1024]{1,0:T(8,128)(2,1)S(1)} %get-tuple-element.207), channel_id=1, source_target_pairs={{0,4},{4,0},{1,5},{5,1},{2,6},{6,2},{3,7},{7,3},{8,12},{12,8},{9,1... | collective-permute-start | bytes 786440 | tf_op jit(solution)/shard_map/ppermute | solution.py:40
  90.4 11.6 %collective-permute-start.13 = (bf16[128,1024]{1,0:T(8,128)(2,1)S(1)}, bf16[128,1024]{1,0:T(8,128)(2,1)S(1)}, u32[]{:S(2)}, u32[]{:S(2)}) collective-permute-start(bf16[128,1024]{1,0:T(8,128)(2,1)S(1)} %add_convert_fusion.7), channel_id=1, source_target_pairs={{0,4},{4,0},{1,5},{5,1},{2,6},{6,2},{3,7},{7,3},{8,12},{12,8},{9,1... | collective-permute-start | bytes 786440 | tf_op jit(solution)/shard_map/ppermute | solution.py:40
  91.1 10.9 %collective-permute-start.15 = (bf16[128,1024]{1,0:T(8,128)(2,1)S(1)}, bf16[128,1024]{1,0:T(8,128)(2,1)S(1)}, u32[]{:S(2)}, u32[]{:S(2)}) collective-permute-start(bf16[128,1024]{1,0:T(8,128)(2,1)S(1)} %add_convert_fusion.6), channel_id=1, source_target_pairs={{0,2},{2,0},{1,3},{3,1},{4,6},{6,4},{5,7},{7,5},{8,10},{10,8},{9,1... | collective-permute-start | bytes 786440 | tf_op jit(solution)/shard_map/ppermute | solution.py:40
  103.3 9.2 %collective-permute-start.19 = (bf16[128,1024]{1,0:T(8,128)(2,1)S(1)}, bf16[128,1024]{1,0:T(8,128)(2,1)S(1)}, u32[]{:S(2)}, u32[]{:S(2)}) collective-permute-start(bf16[128,1024]{1,0:T(8,128)(2,1)S(1)} %get-tuple-element.217.refs_10_.refs_0_), channel_id=1, source_target_pairs={{0,4},{4,0},{1,5},{5,1},{2,6},{6,2},{3,7},{7,3},{8,12},{12,8},{9,1... | collective-permute-start | bytes 786440 | tf_op jit(solution)/shard_map/ppermute | solution.py:40
  104.7 10.0 %collective-permute-start.18 = (bf16[128,1024]{1,0:T(8,128)(2,1)S(1)}, bf16[128,1024]{1,0:T(8,128)(2,1)S(1)}, u32[]{:S(2)}, u32[]{:S(2)}) collective-permute-start(bf16[128,1024]{1,0:T(8,128)(2,1)S(1)} %get-tuple-element.218.refs_11_.refs_1_), channel_id=1, source_target_pairs={{0,2},{2,0},{1,3},{3,1},{4,6},{6,4},{5,7},{7,5},{8,10},{10,8},{9,1... | collective-permute-start | bytes 786440 | tf_op jit(solution)/shard_map/ppermute | solution.py:40
  105.6 14.0 %collective-permute-start.17 = (bf16[128,1024]{1,0:T(8,128)(2,1)S(1)}, bf16[128,1024]{1,0:T(8,128)(2,1)S(1)}, u32[]{:S(2)}, u32[]{:S(2)}) collective-permute-start(bf16[128,1024]{1,0:T(8,128)(2,1)S(1)} %get-tuple-element.217.refs_10_.refs_0_), channel_id=1, source_target_pairs={{0,2},{2,0},{1,3},{3,1},{4,6},{6,4},{5,7},{7,5},{8,10},{10,8},{9,1... | collective-permute-start | bytes 786440 | tf_op jit(solution)/shard_map/ppermute | solution.py:40
  106.7 13.5 %collective-permute-start.20 = (bf16[128,1024]{1,0:T(8,128)(2,1)S(1)}, bf16[128,1024]{1,0:T(8,128)(2,1)S(1)}, u32[]{:S(2)}, u32[]{:S(2)}) collective-permute-start(bf16[128,1024]{1,0:T(8,128)(2,1)S(1)} %get-tuple-element.218.refs_11_.refs_1_), channel_id=1, source_target_pairs={{0,4},{4,0},{1,5},{5,1},{2,6},{6,2},{3,7},{7,3},{8,12},{12,8},{9,1... | collective-permute-start | bytes 786440 | tf_op jit(solution)/shard_map/ppermute | solution.py:40
  112.5 9.8 %collective-permute-start.21 = (bf16[128,1024]{1,0:T(8,128)(2,1)S(1)}, bf16[128,1024]{1,0:T(8,128)(2,1)S(1)}, u32[]{:S(2)}, u32[]{:S(2)}) collective-permute-start(bf16[128,1024]{1,0:T(8,128)(2,1)S(1)} %collective-permute-done.19.refs_4_), channel_id=1, source_target_pairs={{0,2},{2,0},{1,3},{3,1},{4,6},{6,4},{5,7},{7,5},{8,10},{10,8},{9,1... | collective-permute-start | bytes 786440 | tf_op jit(solution)/shard_map/ppermute | solution.py:40
  123.8 16.4 %collective-permute-start.23 = (bf16[4,1152,256]{2,1,0:T(8,128)(2,1)}, bf16[4,1152,256]{2,1,0:T(8,128)(2,1)}, u32[]{:S(2)}, u32[]{:S(2)}) collective-permute-start(bf16[4,1152,256]{2,1,0:T(8,128)(2,1)} %bitcast.57), channel_id=1, source_target_pairs={{0,1},{1,0},{2,3},{3,2},{4,5},{5,4},{6,7},{7,6},{8,9},{9,8},{10,11... | collective-permute-start | bytes 7077896 | tf_op jit(solution)/shard_map/ppermute | solution.py:40
  126.7 10.9 %collective-permute-start.25 = (bf16[384,256]{1,0:T(8,128)(2,1)S(1)}, bf16[384,256]{1,0:T(8,128)(2,1)S(1)}, u32[]{:S(2)}, u32[]{:S(2)}) collective-permute-start(bf16[384,256]{1,0:T(8,128)(2,1)S(1)} %get-tuple-element.314), channel_id=1, source_target_pairs={{0,4},{4,0},{1,5},{5,1},{2,6},{6,2},{3,7},{7,3},{8,12},{12,8},{9,1... | collective-permute-start | bytes 589832 | tf_op jit(solution)/shard_map/ppermute | solution.py:40
  127.5 10.1 %collective-permute-start.24 = (bf16[384,256]{1,0:T(8,128)(2,1)S(1)}, bf16[384,256]{1,0:T(8,128)(2,1)S(1)}, u32[]{:S(2)}, u32[]{:S(2)}) collective-permute-start(bf16[384,256]{1,0:T(8,128)(2,1)S(1)} %get-tuple-element.315), channel_id=1, source_target_pairs={{0,2},{2,0},{1,3},{3,1},{4,6},{6,4},{5,7},{7,5},{8,10},{10,8},{9,1... | collective-permute-start | bytes 589832 | tf_op jit(solution)/shard_map/ppermute | solution.py:40
  147.6 21.7 %collective-permute-start.29 = (bf16[128,1024]{1,0:T(8,128)(2,1)S(1)}, bf16[128,1024]{1,0:T(8,128)(2,1)S(1)}, u32[]{:S(2)}, u32[]{:S(2)}) collective-permute-start(bf16[128,1024]{1,0:T(8,128)(2,1)S(1)} %get-tuple-element.224), channel_id=1, source_target_pairs={{0,2},{2,0},{1,3},{3,1},{4,6},{6,4},{5,7},{7,5},{8,10},{10,8},{9,1... | collective-permute-start | bytes 786440 | tf_op jit(solution)/shard_map/ppermute | solution.py:40
  165.9 13.7 %collective-permute-start.34 = (bf16[4,384,256]{2,1,0:T(8,128)(2,1)S(1)}, bf16[4,384,256]{2,1,0:T(8,128)(2,1)S(1)}, u32[]{:S(2)}, u32[]{:S(2)}) collective-permute-start(bf16[4,384,256]{2,1,0:T(8,128)(2,1)S(1)} %shard_map.248), channel_id=1, source_target_pairs={{0,1},{1,0},{2,3},{3,2},{4,5},{5,4},{6,7},{7,6},{8,9},{9,8},{10,11... | collective-permute-start | bytes 2359304 | tf_op jit(solution)/shard_map/ppermute | solution.py:40
  167.3 14.6 %collective-permute-start.28 = (bf16[128,1024]{1,0:T(8,128)(2,1)S(1)}, bf16[128,1024]{1,0:T(8,128)(2,1)S(1)}, u32[]{:S(2)}, u32[]{:S(2)}) collective-permute-start(bf16[128,1024]{1,0:T(8,128)(2,1)S(1)} %get-tuple-element.220), channel_id=1, source_target_pairs={{0,2},{2,0},{1,3},{3,1},{4,6},{6,4},{5,7},{7,5},{8,10},{10,8},{9,1... | collective-permute-start | bytes 786440 | tf_op jit(solution)/shard_map/ppermute | solution.py:40
  167.8 14.1 %collective-permute-start.33 = (bf16[128,1024]{1,0:T(8,128)(2,1)S(1)}, bf16[128,1024]{1,0:T(8,128)(2,1)S(1)}, u32[]{:S(2)}, u32[]{:S(2)}) collective-permute-start(bf16[128,1024]{1,0:T(8,128)(2,1)S(1)} %get-tuple-element.228), channel_id=1, source_target_pairs={{0,4},{4,0},{1,5},{5,1},{2,6},{6,2},{3,7},{7,3},{8,12},{12,8},{9,1... | collective-permute-start | bytes 786440 | tf_op jit(solution)/shard_map/ppermute | solution.py:40
  169.3 16.6 %collective-permute-start.30 = (bf16[128,1024]{1,0:T(8,128)(2,1)S(1)}, bf16[128,1024]{1,0:T(8,128)(2,1)S(1)}, u32[]{:S(2)}, u32[]{:S(2)}) collective-permute-start(bf16[128,1024]{1,0:T(8,128)(2,1)S(1)} %add_convert_fusion.5), channel_id=1, source_target_pairs={{0,4},{4,0},{1,5},{5,1},{2,6},{6,2},{3,7},{7,3},{8,12},{12,8},{9,1... | collective-permute-start | bytes 786440 | tf_op jit(solution)/shard_map/ppermute | solution.py:40
  175.2 10.7 %collective-permute-start.32 = (bf16[128,1024]{1,0:T(8,128)(2,1)S(1)}, bf16[128,1024]{1,0:T(8,128)(2,1)S(1)}, u32[]{:S(2)}, u32[]{:S(2)}) collective-permute-start(bf16[128,1024]{1,0:T(8,128)(2,1)S(1)} %add_convert_fusion.4), channel_id=1, source_target_pairs={{0,2},{2,0},{1,3},{3,1},{4,6},{6,4},{5,7},{7,5},{8,10},{10,8},{9,1... | collective-permute-start | bytes 786440 | tf_op jit(solution)/shard_map/ppermute | solution.py:40
  185.9 18.4 %collective-permute-start.41 = (bf16[4,768,256]{2,1,0:T(8,128)(2,1)S(1)}, bf16[4,768,256]{2,1,0:T(8,128)(2,1)S(1)}, u32[]{:S(2)}, u32[]{:S(2)}) collective-permute-start(bf16[4,768,256]{2,1,0:T(8,128)(2,1)S(1)} %shard_map.247), channel_id=1, source_target_pairs={{0,1},{1,0},{2,3},{3,2},{4,5},{5,4},{6,7},{7,6},{8,9},{9,8},{10,11... | collective-permute-start | bytes 4718600 | tf_op jit(solution)/shard_map/ppermute | solution.py:40
  189.0 11.0 %collective-permute-start.37 = (bf16[128,1024]{1,0:T(8,128)(2,1)S(1)}, bf16[128,1024]{1,0:T(8,128)(2,1)S(1)}, u32[]{:S(2)}, u32[]{:S(2)}) collective-permute-start(bf16[128,1024]{1,0:T(8,128)(2,1)S(1)} %get-tuple-element.243.refs_6_.refs_4_), channel_id=1, source_target_pairs={{0,4},{4,0},{1,5},{5,1},{2,6},{6,2},{3,7},{7,3},{8,12},{12,8},{9,1... | collective-permute-start | bytes 786440 | tf_op jit(solution)/shard_map/ppermute | solution.py:40
  190.4 10.8 %collective-permute-start.36 = (bf16[128,1024]{1,0:T(8,128)(2,1)S(1)}, bf16[128,1024]{1,0:T(8,128)(2,1)S(1)}, u32[]{:S(2)}, u32[]{:S(2)}) collective-permute-start(bf16[128,1024]{1,0:T(8,128)(2,1)S(1)} %get-tuple-element.244.refs_7_.refs_5_), channel_id=1, source_target_pairs={{0,2},{2,0},{1,3},{3,1},{4,6},{6,4},{5,7},{7,5},{8,10},{10,8},{9,1... | collective-permute-start | bytes 786440 | tf_op jit(solution)/shard_map/ppermute | solution.py:40
  191.2 13.0 %collective-permute-start.43 = (bf16[384,256]{1,0:T(8,128)(2,1)S(1)}, bf16[384,256]{1,0:T(8,128)(2,1)S(1)}, u32[]{:S(2)}, u32[]{:S(2)}) collective-permute-start(bf16[384,256]{1,0:T(8,128)(2,1)S(1)} %get-tuple-element.322), channel_id=1, source_target_pairs={{0,4},{4,0},{1,5},{5,1},{2,6},{6,2},{3,7},{7,3},{8,12},{12,8},{9,1... | collective-permute-start | bytes 589832 | tf_op jit(solution)/shard_map/ppermute | solution.py:40
  194.7 9.6 %collective-permute-start.42 = (bf16[384,256]{1,0:T(8,128)(2,1)S(1)}, bf16[384,256]{1,0:T(8,128)(2,1)S(1)}, u32[]{:S(2)}, u32[]{:S(2)}) collective-permute-start(bf16[384,256]{1,0:T(8,128)(2,1)S(1)} %get-tuple-element.323), channel_id=1, source_target_pairs={{0,2},{2,0},{1,3},{3,1},{4,6},{6,4},{5,7},{7,5},{8,10},{10,8},{9,1... | collective-permute-start | bytes 589832 | tf_op jit(solution)/shard_map/ppermute | solution.py:40
  199.9 9.6 %collective-permute-start.39 = (bf16[128,1024]{1,0:T(8,128)(2,1)S(1)}, bf16[128,1024]{1,0:T(8,128)(2,1)S(1)}, u32[]{:S(2)}, u32[]{:S(2)}) collective-permute-start(bf16[128,1024]{1,0:T(8,128)(2,1)S(1)} %collective-permute-done.37.refs_14_.refs_8_), channel_id=1, source_target_pairs={{0,2},{2,0},{1,3},{3,1},{4,6},{6,4},{5,7},{7,5},{8,10},{10,8},{9,1... | collective-permute-start | bytes 786440 | tf_op jit(solution)/shard_map/ppermute | solution.py:40
  211.0 123.9 %reduce-scatter.5.cloned.1.call-start = ((), (), s32[]{:S(2)}) async-start(), calls=%async_computation.3 | async-start | bytes 1966080 | tf_op jit(solution)/shard_map/reduce_scatter | solution.py:587
  211.0 19.8 %collective-permute-start.35 = (bf16[128,1024]{1,0:T(8,128)(2,1)S(1)}, bf16[128,1024]{1,0:T(8,128)(2,1)S(1)}, u32[]{:S(2)}, u32[]{:S(2)}) collective-permute-start(bf16[128,1024]{1,0:T(8,128)(2,1)S(1)} %get-tuple-element.243.refs_6_.refs_4_), channel_id=1, source_target_pairs={{0,2},{2,0},{1,3},{3,1},{4,6},{6,4},{5,7},{7,5},{8,10},{10,8},{9,1... | collective-permute-start | bytes 786440 | tf_op jit(solution)/shard_map/ppermute | solution.py:40
  211.8 19.1 %collective-permute-start.38 = (bf16[128,1024]{1,0:T(8,128)(2,1)}, bf16[128,1024]{1,0:T(8,128)(2,1)S(1)}, u32[]{:S(2)}, u32[]{:S(2)}) collective-permute-start(bf16[128,1024]{1,0:T(8,128)(2,1)} %copy-done.29), channel_id=1, source_target_pairs={{0,4},{4,0},{1,5},{5,1},{2,6},{6,2},{3,7},{7,3},{8,12},{12,8},{9,1... | collective-permute-start | bytes 786440 | tf_op jit(solution)/shard_map/ppermute | solution.py:40
  230.0 31.2 %collective-permute-start.51 = (bf16[128,1024]{1,0:T(8,128)(2,1)S(1)}, bf16[128,1024]{1,0:T(8,128)(2,1)S(1)}, u32[]{:S(2)}, u32[]{:S(2)}) collective-permute-start(bf16[128,1024]{1,0:T(8,128)(2,1)S(1)} %copy-done.146), channel_id=1, source_target_pairs={{0,2},{2,0},{1,3},{3,1},{4,6},{6,4},{5,7},{7,5},{8,10},{10,8},{9,1... | collective-permute-start | bytes 786440 | tf_op jit(solution)/shard_map/ppermute | solution.py:40
  233.1 28.2 %collective-permute-start.46 = (bf16[4,256,256]{2,1,0:T(8,128)(2,1)S(1)}, bf16[4,256,256]{2,1,0:T(8,128)(2,1)S(1)}, u32[]{:S(2)}, u32[]{:S(2)}) collective-permute-start(bf16[4,256,256]{2,1,0:T(8,128)(2,1)S(1)} %shard_map.255), channel_id=1, source_target_pairs={{0,1},{1,0},{2,3},{3,2},{4,5},{5,4},{6,7},{7,6},{8,9},{9,8},{10,11... | collective-permute-start | bytes 1572872 | tf_op jit(solution)/shard_map/ppermute | solution.py:40
  258.8 20.4 %collective-permute-start.45 = (bf16[4,512,256]{2,1,0:T(8,128)(2,1)S(1)}, bf16[4,512,256]{2,1,0:T(8,128)(2,1)S(1)}, u32[]{:S(2)}, u32[]{:S(2)}) collective-permute-start(bf16[4,512,256]{2,1,0:T(8,128)(2,1)S(1)} %shard_map.254), channel_id=1, source_target_pairs={{0,1},{1,0},{2,3},{3,2},{4,5},{5,4},{6,7},{7,6},{8,9},{9,8},{10,11... | collective-permute-start | bytes 3145736 | tf_op jit(solution)/shard_map/ppermute | solution.py:40
  259.2 23.2 %collective-permute-start.50 = (bf16[128,1024]{1,0:T(8,128)(2,1)S(1)}, bf16[128,1024]{1,0:T(8,128)(2,1)S(1)}, u32[]{:S(2)}, u32[]{:S(2)}) collective-permute-start(bf16[128,1024]{1,0:T(8,128)(2,1)S(1)} %copy-done.144), channel_id=1, source_target_pairs={{0,2},{2,0},{1,3},{3,1},{4,6},{6,4},{5,7},{7,5},{8,10},{10,8},{9,1... | collective-permute-start | bytes 786440 | tf_op jit(solution)/shard_map/ppermute | solution.py:40
  260.5 12.0 %collective-permute-start.53 = (bf16[128,1024]{1,0:T(8,128)(2,1)S(1)}, bf16[128,1024]{1,0:T(8,128)(2,1)S(1)}, u32[]{:S(2)}, u32[]{:S(2)}) collective-permute-start(bf16[128,1024]{1,0:T(8,128)(2,1)S(1)} %copy-done.145), channel_id=1, source_target_pairs={{0,4},{4,0},{1,5},{5,1},{2,6},{6,2},{3,7},{7,3},{8,12},{12,8},{9,1... | collective-permute-start | bytes 786440 | tf_op jit(solution)/shard_map/ppermute | solution.py:40
  263.4 10.0 %collective-permute-start.49 = (bf16[256,256]{1,0:T(8,128)(2,1)S(1)}, bf16[256,256]{1,0:T(8,128)(2,1)S(1)}, u32[]{:S(2)}, u32[]{:S(2)}) collective-permute-start(bf16[256,256]{1,0:T(8,128)(2,1)S(1)} %get-tuple-element.325), channel_id=1, source_target_pairs={{0,6},{2,4},{4,2},{6,0},{1,7},{3,5},{5,3},{7,1},{8,14},{10,12},{12... | collective-permute-start | bytes 393224 | tf_op jit(solution)/shard_map/ppermute | solution.py:119
  265.0 10.3 %collective-permute-start.48 = (bf16[256,256]{1,0:T(8,128)(2,1)S(1)}, bf16[256,256]{1,0:T(8,128)(2,1)S(1)}, u32[]{:S(2)}, u32[]{:S(2)}) collective-permute-start(bf16[256,256]{1,0:T(8,128)(2,1)S(1)} %get-tuple-element.326), channel_id=1, source_target_pairs={{0,4},{4,0},{1,5},{5,1},{2,6},{6,2},{3,7},{7,3},{8,12},{12,8},{9,1... | collective-permute-start | bytes 393224 | tf_op jit(solution)/shard_map/ppermute | solution.py:40
  275.2 10.1 %collective-permute-start.52 = (bf16[128,1024]{1,0:T(8,128)(2,1)S(1)}, bf16[128,1024]{1,0:T(8,128)(2,1)S(1)}, u32[]{:S(2)}, u32[]{:S(2)}) collective-permute-start(bf16[128,1024]{1,0:T(8,128)(2,1)S(1)} %add_convert_fusion.3), channel_id=1, source_target_pairs={{0,4},{4,0},{1,5},{5,1},{2,6},{6,2},{3,7},{7,3},{8,12},{12,8},{9,1... | collective-permute-start | bytes 786440 | tf_op jit(solution)/shard_map/ppermute | solution.py:40
  287.2 17.2 %collective-permute-start.69 = (bf16[1152,256]{1,0:T(8,128)(2,1)S(1)}, bf16[1152,256]{1,0:T(8,128)(2,1)S(1)}, u32[]{:S(2)}, u32[]{:S(2)}) collective-permute-start(bf16[1152,256]{1,0:T(8,128)(2,1)S(1)} %copy-done.92), channel_id=1, source_target_pairs={{0,6},{2,4},{4,2},{6,0},{1,7},{3,5},{5,3},{7,1},{8,14},{10,12},{12... | collective-permute-start | bytes 1769480 | tf_op jit(solution)/shard_map/ppermute | solution.py:95
  288.7 24.4 %collective-permute-start.68 = (bf16[1152,256]{1,0:T(8,128)(2,1)S(1)}, bf16[1152,256]{1,0:T(8,128)(2,1)S(1)}, u32[]{:S(2)}, u32[]{:S(2)}) collective-permute-start(bf16[1152,256]{1,0:T(8,128)(2,1)S(1)} %copy-done.92), channel_id=1, source_target_pairs={{0,4},{4,0},{1,5},{5,1},{2,6},{6,2},{3,7},{7,3},{8,12},{12,8},{9,1... | collective-permute-start | bytes 1769480 | tf_op jit(solution)/shard_map/ppermute | solution.py:40
  289.4 23.8 %collective-permute-start.67 = (bf16[1152,256]{1,0:T(8,128)(2,1)S(1)}, bf16[1152,256]{1,0:T(8,128)(2,1)S(1)}, u32[]{:S(2)}, u32[]{:S(2)}) collective-permute-start(bf16[1152,256]{1,0:T(8,128)(2,1)S(1)} %copy-done.92), channel_id=1, source_target_pairs={{0,2},{2,0},{1,3},{3,1},{4,6},{6,4},{5,7},{7,5},{8,10},{10,8},{9,1... | collective-permute-start | bytes 1769480 | tf_op jit(solution)/shard_map/ppermute | solution.py:40
  290.7 22.9 %collective-permute-start.62 = (f32[1,2304]{1,0:T(1,128)S(1)}, f32[1,2304]{1,0:T(1,128)S(1)}, u32[]{:S(2)}, u32[]{:S(2)}) collective-permute-start(f32[1,2304]{1,0:T(1,128)S(1)} %pad_maximum_fusion), channel_id=1, source_target_pairs={{0,1},{1,0},{2,3},{3,2},{4,5},{5,4},{6,7},{7,6},{8,9},{9,8},{10,11... | collective-permute-start | bytes 27656 | tf_op jit(solution)/shard_map/ppermute | solution.py:40
  290.8 34.4 %collective-permute-start.70 = (bf16[1152,256]{1,0:T(8,128)(2,1)S(1)}, bf16[1152,256]{1,0:T(8,128)(2,1)S(1)}, u32[]{:S(2)}, u32[]{:S(2)}) collective-permute-start(bf16[1152,256]{1,0:T(8,128)(2,1)S(1)} %copy-done.92), channel_id=1, source_target_pairs={{0,1},{1,0},{2,3},{3,2},{4,5},{5,4},{6,7},{7,6},{8,9},{9,8},{10,11... | collective-permute-start | bytes 1769480 | tf_op jit(solution)/shard_map/ppermute | solution.py:40
  304.3 22.7 %collective-permute-start.73 = (bf16[1152,256]{1,0:T(8,128)(2,1)S(1)}, bf16[1152,256]{1,0:T(8,128)(2,1)S(1)}, u32[]{:S(2)}, u32[]{:S(2)}) collective-permute-start(bf16[1152,256]{1,0:T(8,128)(2,1)S(1)} %collective-permute-done.69.refs_3_), channel_id=1, source_target_pairs={{0,1},{1,0},{2,3},{3,2},{4,5},{5,4},{6,7},{7,6},{8,9},{9,8},{10,11... | collective-permute-start | bytes 1769480 | tf_op jit(solution)/shard_map/ppermute | solution.py:40
  313.1 14.2 %collective-permute-start.72 = (bf16[1152,256]{1,0:T(8,128)(2,1)S(1)}, bf16[1152,256]{1,0:T(8,128)(2,1)S(1)}, u32[]{:S(2)}, u32[]{:S(2)}) collective-permute-start(bf16[1152,256]{1,0:T(8,128)(2,1)S(1)} %collective-permute-done.68.refs_2_), channel_id=1, source_target_pairs={{0,1},{1,0},{2,3},{3,2},{4,5},{5,4},{6,7},{7,6},{8,9},{9,8},{10,11... | collective-permute-start | bytes 1769480 | tf_op jit(solution)/shard_map/ppermute | solution.py:40
  313.2 16.6 %collective-permute-start.71 = (bf16[1152,256]{1,0:T(8,128)(2,1)S(1)}, bf16[1152,256]{1,0:T(8,128)(2,1)S(1)}, u32[]{:S(2)}, u32[]{:S(2)}) collective-permute-start(bf16[1152,256]{1,0:T(8,128)(2,1)S(1)} %collective-permute-done.67.refs_1_), channel_id=1, source_target_pairs={{0,1},{1,0},{2,3},{3,2},{4,5},{5,4},{6,7},{7,6},{8,9},{9,8},{10,11... | collective-permute-start | bytes 1769480 | tf_op jit(solution)/shard_map/ppermute | solution.py:40
  324.9 13.4 %collective-permute-start.57 = (bf16[128,1024]{1,0:T(8,128)(2,1)}, bf16[128,1024]{1,0:T(8,128)(2,1)}, u32[]{:S(2)}, u32[]{:S(2)}) collective-permute-start(bf16[128,1024]{1,0:T(8,128)(2,1)} %get-tuple-element.292), channel_id=1, source_target_pairs={{0,2},{2,0},{1,3},{3,1},{4,6},{6,4},{5,7},{7,5},{8,10},{10,8},{9,1... | collective-permute-start | bytes 786440 | tf_op jit(solution)/shard_map/ppermute | solution.py:40
  325.2 14.3 %collective-permute-start.56 = (bf16[128,1024]{1,0:T(8,128)(2,1)}, bf16[128,1024]{1,0:T(8,128)(2,1)}, u32[]{:S(2)}, u32[]{:S(2)}) collective-permute-start(bf16[128,1024]{1,0:T(8,128)(2,1)} %get-tuple-element.290), channel_id=1, source_target_pairs={{0,2},{2,0},{1,3},{3,1},{4,6},{6,4},{5,7},{7,5},{8,10},{10,8},{9,1... | collective-permute-start | bytes 786440 | tf_op jit(solution)/shard_map/ppermute | solution.py:40
  327.0 14.2 %collective-permute-start.59 = (bf16[128,1024]{1,0:T(8,128)(2,1)}, bf16[128,1024]{1,0:T(8,128)(2,1)}, u32[]{:S(2)}, u32[]{:S(2)}) collective-permute-start(bf16[128,1024]{1,0:T(8,128)(2,1)} %get-tuple-element.295), channel_id=1, source_target_pairs={{0,4},{4,0},{1,5},{5,1},{2,6},{6,2},{3,7},{7,3},{8,12},{12,8},{9,1... | collective-permute-start | bytes 786440 | tf_op jit(solution)/shard_map/ppermute | solution.py:40
  327.3 9.2 %collective-permute-start.66 = (f32[1,2304]{1,0:T(1,128)S(1)}, f32[1,2304]{1,0:T(1,128)S(1)}, u32[]{:S(2)}, u32[]{:S(2)}) collective-permute-start(f32[1,2304]{1,0:T(1,128)S(1)} %add.122), channel_id=1, source_target_pairs={{0,16},{8,24},{16,0},{24,8},{1,17},{9,25},{17,1},{25,9},{2,18},{10... | collective-permute-start | bytes 27656 | tf_op jit(solution)/shard_map/ppermute | solution.py:605
  334.8 28.5 %collective-permute-start.76 = (bf16[768,256]{1,0:T(8,128)(2,1)}, bf16[768,256]{1,0:T(8,128)(2,1)S(1)}, u32[]{:S(2)}, u32[]{:S(2)}) collective-permute-start(bf16[768,256]{1,0:T(8,128)(2,1)} %reduce-scatter.5.cloned.1.call-done.refs_0_), channel_id=1, source_target_pairs={{0,6},{2,4},{4,2},{6,0},{1,7},{3,5},{5,3},{7,1},{8,14},{10,12},{12... | collective-permute-start | bytes 1179656 | tf_op jit(solution)/shard_map/ppermute | solution.py:95
  336.5 27.3 %collective-permute-start.75 = (bf16[768,256]{1,0:T(8,128)(2,1)}, bf16[768,256]{1,0:T(8,128)(2,1)S(1)}, u32[]{:S(2)}, u32[]{:S(2)}) collective-permute-start(bf16[768,256]{1,0:T(8,128)(2,1)} %reduce-scatter.5.cloned.1.call-done.refs_0_), channel_id=1, source_target_pairs={{0,4},{4,0},{1,5},{5,1},{2,6},{6,2},{3,7},{7,3},{8,12},{12,8},{9,1... | collective-permute-start | bytes 1179656 | tf_op jit(solution)/shard_map/ppermute | solution.py:40
  338.3 25.6 %collective-permute-start.74 = (bf16[768,256]{1,0:T(8,128)(2,1)}, bf16[768,256]{1,0:T(8,128)(2,1)S(1)}, u32[]{:S(2)}, u32[]{:S(2)}) collective-permute-start(bf16[768,256]{1,0:T(8,128)(2,1)} %reduce-scatter.5.cloned.1.call-done.refs_0_), channel_id=1, source_target_pairs={{0,2},{2,0},{1,3},{3,1},{4,6},{6,4},{5,7},{7,5},{8,10},{10,8},{9,1... | collective-permute-start | bytes 1179656 | tf_op jit(solution)/shard_map/ppermute | solution.py:40
  339.5 19.5 %collective-permute-start.61 = (bf16[128,1024]{1,0:T(8,128)(2,1)}, bf16[128,1024]{1,0:T(8,128)(2,1)S(1)}, u32[]{:S(2)}, u32[]{:S(2)}) collective-permute-start(bf16[128,1024]{1,0:T(8,128)(2,1)} %copy-done.139), channel_id=1, source_target_pairs={{0,4},{4,0},{1,5},{5,1},{2,6},{6,2},{3,7},{7,3},{8,12},{12,8},{9,1... | collective-permute-start | bytes 786440 | tf_op jit(solution)/shard_map/ppermute | solution.py:40
  341.2 22.1 %collective-permute-start.58 = (bf16[128,1024]{1,0:T(8,128)(2,1)S(1)}, bf16[128,1024]{1,0:T(8,128)(2,1)S(1)}, u32[]{:S(2)}, u32[]{:S(2)}) collective-permute-start(bf16[128,1024]{1,0:T(8,128)(2,1)S(1)} %add_convert_fusion.1), channel_id=1, source_target_pairs={{0,4},{4,0},{1,5},{5,1},{2,6},{6,2},{3,7},{7,3},{8,12},{12,8},{9,1... | collective-permute-start | bytes 786440 | tf_op jit(solution)/shard_map/ppermute | solution.py:40
  (168 other events, 1530.9 us)
Sparse Core Ops, SparseCore 0:
  10.6 39.7 all-gather.4
  59.4 50.7 all-gather.6
  211.1 48.2 reduce-scatter.2
  286.2 35.5 reduce-scatter.4

commit v3 on v2

v3 whole, which is shorter than its diff:
```python
import functools
import math

import jax
import jax.numpy as jnp
from jax import lax
from jax.experimental import pallas as pl
from jax.experimental.pallas import tpu as pltpu
from jax.sharding import Mesh
from jax.sharding import PartitionSpec as P

HEADS = 16
KV_HEADS = 8
HEAD = 128
GROUP = HEADS // KV_HEADS

EPS = 1e-06
ROPE_BASE = 1000000.0
MASKED = -1e30
SCALE = HEAD ** (-0.5)
BF = jnp.bfloat16
F32 = jnp.float32
SWAP = [(0, 1), (1, 0)]
VMEM_LIMIT = 24 * 1024 * 1024
B = 256


def dot(a, b):
    return jnp.dot(a, b, preferred_element_type=F32)


def dot_nt(a, b):
    return lax.dot_general(a, b, (((1,), (1,)), ((), ())), preferred_element_type=F32)


def dot_tn(a, b):
    return lax.dot_general(a, b, (((0,), (0,)), ((), ())), preferred_element_type=F32)


def swap(a, axis):
    return lax.ppermute(a, axis, SWAP)


tie = lax.optimization_barrier


def stay(a):
    return pltpu.with_memory_space_constraint(a, pltpu.HBM)


def sds(shape, dtype):
    return jax.ShapeDtypeStruct(shape, dtype)


def hbm(shape, dtype):
    return pltpu.HBM(shape, dtype)


VM = pl.BlockSpec(memory_space=pltpu.VMEM)
SM = pl.BlockSpec(memory_space=pltpu.SMEM)


def kernel_call(body, outs, args, flops=0, scalars=0, **kw):
    moved = sum(a.size * a.dtype.itemsize for a in args) + sum(math.prod(o.shape) * o.dtype.itemsize for o in outs)
    if "grid" not in kw:
        kw = dict(in_specs=[SM] * scalars + [VM] * (len(args) - scalars), out_specs=[VM] * len(outs))
    return pl.pallas_call(
        body,
        out_shape=outs,
        compiler_params=pltpu.CompilerParams(vmem_limit_bytes=VMEM_LIMIT),
        cost_estimate=pl.CostEstimate(flops=flops, bytes_accessed=moved, transcendentals=0),
        **kw,
    )(*args)


class Plane:
    def __init__(self, ny, nx):
        self.ny, self.nx, self.n = ny, nx, ny * nx
        self.square = ny == 2 and nx == 2
        self.axes = ("y", "x")

    def index(self):
        return lax.axis_index("y") * self.nx + lax.axis_index("x")

    def place(self, t, r):
        return jnp.bitwise_xor(t, r) if self.square else r

    def gather(self, top, low):
        return self.gather_far(self.gather_near(top, low))

    def gather_near(self, top, low):
        if not self.square:
            g, h = (lax.all_gather(a, self.axes, axis=0, tiled=False) for a in (top, low))
            return [[g[i], h[i]] for i in range(self.n)]
        ty, lx = swap(top, "y"), swap(low, "x")
        tx, ly = swap(top, "x"), swap(low, "y")
        return [[top, low], [tx, lx], [ty, ly]]

    def gather_far(self, near, *after):
        if not self.square:
            return near
        (ty, lx), _ = tie(([near[2][0], near[1][1]], after))
        return near + [[swap(ty, "x"), swap(lx, "y")]]

    def near(self, a):
        if not self.square:
            g = lax.all_gather(a, self.axes, axis=0, tiled=False)
            return [g[i] for i in range(self.n)]
        return [a, swap(a, "x"), swap(a, "y")]

    def far(self, a, near):
        if not self.square:
            return near
        return near + [lax.ppermute(a, self.axes, [(i, 3 - i) for i in range(4)])]

    def gather_whole(self, a):
        return self.far(a, self.near(a))

    def scatter(self, blocks):
        if not self.square:
            a = lax.psum_scatter(jnp.concatenate(blocks, 0), self.axes, scatter_dimension=0, tiled=True)
            return [a]
        far = lax.ppermute(blocks[3], self.axes, [(i, 3 - i) for i in range(4)])
        return [blocks[0], swap(blocks[1], "x"), swap(blocks[2], "y"), far]

    def exchange(self, slice_for):
        if not self.square:
            a = jnp.stack([slice_for(i) for i in range(self.n)], 0)
            a = lax.all_to_all(a, self.axes, split_axis=0, concat_axis=0, tiled=True)
            return [a[i] for i in range(self.n)]
        t = self.index()
        return [
            slice_for(t),
            swap(slice_for(jnp.bitwise_xor(t, 1)), "x"),
            swap(slice_for(jnp.bitwise_xor(t, 2)), "y"),
            lax.ppermute(slice_for(jnp.bitwise_xor(t, 3)), self.axes, [(i, 3 - i) for i in range(4)]),
        ]


def columns(ref, lo, count, rows):
    s = ref.shape[0]
    got = [ref[:, (lo + j) * rows : (lo + j + 1) * rows, :].reshape(s * rows, B) for j in range(count)]
    return got[0] if count == 1 else jnp.concatenate(got, 1)


def split(ref):
    return jnp.concatenate([ref[0][...], ref[1][...]], 0)


def rsq(v):
    return lax.rsqrt(jnp.mean(v * v, axis=-1, keepdims=True) + EPS)


def norm_back(v, r, gain, d):
    dg = d * gain
    return r * (dg - v * (r * r) * jnp.mean(dg * v, axis=-1, keepdims=True))


def half_roll(u):
    return pltpu.roll(u, HEAD // 2, 1)


def token_rows(top, low):
    return jnp.concatenate([top[...], low[: top.shape[0], :]], 0).astype(F32)


def prep_block(length, gain, freq, tok0, tok1, nin, cos, sin, mask):
    half = length // 2
    x = token_rows(tok0, tok1)
    nin[...] = (x * rsq(x) * gain[...]).astype(BF)
    row = tok1[half : half + 16, :length].astype(F32)[:1]
    row = jnp.broadcast_to(row, (length, length))
    col = row.T
    start = jnp.sum(jnp.where(row < col, 1.0, 0.0), axis=-1, keepdims=True)
    i = lax.broadcasted_iota(jnp.int32, (length, length), 0)
    j = lax.broadcasted_iota(jnp.int32, (length, length), 1)
    mask[...] = jnp.where((j <= i) & (row == col), 1.0, 0.0)
    pos = lax.broadcasted_iota(jnp.int32, (length, HEAD), 0).astype(F32) - start
    ang = pos * freq[...]
    lane = lax.broadcasted_iota(jnp.int32, (length, HEAD), 1)
    s = jnp.sin(ang)
    cos[...] = jnp.cos(ang)
    sin[...] = jnp.where(lane < HEAD // 2, -s, s)


def ones(rows, value=1.0):
    return jnp.full((rows, HEAD), value, BF)


def twice(a):
    return jnp.concatenate([a, a], 1)


def head_mean(v):
    return dot(v.astype(BF), ones(HEAD, 1.0 / HEAD))


def head_rsq(v):
    return lax.rsqrt(head_mean(v * v) + EPS)


def head_back(v, r, gain, d):
    dg = d * gain
    return r * (dg - v * (r * r) * head_mean(dg * v))


def weights_of(qr, kr, keep):
    return jnp.where(keep, jnp.exp(dot_nt(qr, kr) * SCALE), 0.0)


def attend_block(parts, wrows, qg, kg, wa, wo, nin, cos, sin, mask, lin, vals, mixed, partial):
    keep = mask[...] > 0.0
    c, s = cos[...], sin[...]
    rot = lambda u: u * c + half_roll(u) * s
    n = nin[...]
    one = ones(n.shape[0])
    out = None
    for h in range(parts):
        q = dot(n, columns(wa[h], 0, 1, wrows))
        kv = dot(n, columns(wa[h], 1, 1, wrows))
        k, v = kv[:, :HEAD], kv[:, HEAD:].astype(BF)
        lin[:, h * 3 * HEAD : h * 3 * HEAD + 2 * HEAD] = q
        lin[:, h * 3 * HEAD + 2 * HEAD : (h + 1) * 3 * HEAD] = k
        vals[:, h * HEAD : (h + 1) * HEAD] = v
        kr = rot(k * head_rsq(k) * kg[...]).astype(BF)
        v1 = jnp.concatenate([v, one], 1)
        for g in range(GROUP):
            qh = q[:, g * HEAD : (g + 1) * HEAD]
            e = weights_of(rot(qh * head_rsq(qh) * qg[...]).astype(BF), kr, keep)
            m = dot(e.astype(BF), v1)
            at = h * GROUP * HEAD + g * HEAD
            mixed[:, at : at + HEAD] = (m[:, :HEAD] / m[:, HEAD:]).astype(BF)
        term = dot(mixed[:, h * GROUP * HEAD : (h + 1) * GROUP * HEAD], wo[h][...])
        out = term if out is None else out + term
    partial[...] = out.astype(partial.dtype)


def down_rows_of(ref, base, s0):
    def piece(s, lo, hi):
        return jnp.concatenate([ref[s, base + j * 192 + lo : base + j * 192 + hi, :] for j in range(2)], 1)

    return jnp.concatenate([piece(s0, 0, 128), piece(s0 + 1, 0, 128), piece(s0, 128, 192), piece(s0 + 1, 128, 192)], 0)


def mlp_block(spread, parts, wrows, ff, core, wgu, wd, nm0, nm1, cot0, cot1, product, dgu, partial, d_mid):
    n = split((nm0, nm1))
    blocks = 2 * ff // B
    width = n.shape[1]
    side = width // 2
    out, dm = {}, None
    for h in range(parts):
        w = columns(wgu[h], 0, blocks, wrows)
        if spread:
            s0 = 2 * jnp.bitwise_xor(core[0], h)
            where = [pl.multiple_of(jnp.bitwise_xor(core[0], j) * side, side) for j in range(2)]
            d = [(pl.ds(where[j], side), down_rows_of(wgu[j], blocks * wrows, s0)) for j in range(2)]
        else:
            d = [(slice(None), wd[h][...])]
        gu = dot(n, w)
        gate, up = gu[:, :ff], gu[:, ff:]
        sg = jax.nn.sigmoid(gate)
        act = gate * sg
        pr = (act * up).astype(BF)
        product[:, h * ff : (h + 1) * ff] = pr
        dp = None
        for at, rows in d:
            term = dot_nt(jnp.concatenate([cot0[:, at], cot1[:, at]], 0), rows)
            dp = term if dp is None else dp + term
        d_gate = (dp * up * (sg + act * (1.0 - sg))).astype(BF)
        d_up = (dp * act).astype(BF)
        at = h * 2 * ff
        dgu[:, at : at + ff] = d_gate
        dgu[:, at + ff : at + 2 * ff] = d_up
        for j, (_, rows) in enumerate(d):
            term = dot(pr, rows)
            out[j] = out[j] + term if j in out else term
        term = dot_nt(dgu[:, at : at + 2 * ff], w)
        dm = term if dm is None else dm + term
    for j, (at, _) in enumerate(d):
        partial[:, at] = out[j].astype(partial.dtype)
    d_mid[...] = dm.astype(d_mid.dtype)


def attend_back_block(parts, wrows, qg, kg, wa, wo, dh0, dh1, tok0, tok1, lin, vals, cos, sin, mask, dqkv, d_in, gains):
    keep = mask[...] > 0.0
    c, s = cos[...], sin[...]
    rot = lambda u: u * c + half_roll(u) * s
    rot_back = lambda u: u * c - half_roll(u) * s
    d = split((dh0, dh1))
    one = ones(d.shape[0])
    din, qgain, kgain = None, 0.0, 0.0
    for h in range(parts):
        dm = dot_nt(d, wo[h][...]).astype(BF)
        base = h * 3 * HEAD
        k = lin[:, base + 2 * HEAD : base + 3 * HEAD]
        v = vals[:, h * HEAD : (h + 1) * HEAD]
        rk = head_rsq(k)
        kr = rot(k * rk * kg[...]).astype(BF)
        ps, dss, qrs, dms = [], [], [], []
        at = h * 4 * HEAD
        for g in range(GROUP):
            q = lin[:, base + g * HEAD : base + (g + 1) * HEAD]
            rq = head_rsq(q)
            qr = rot(q * rq * qg[...]).astype(BF)
            e = weights_of(qr, kr, keep)
            p = e * twice(1.0 / dot(e.astype(BF), one))
            dmh = dm[:, g * HEAD : (g + 1) * HEAD]
            pd = p * dot_nt(dmh, v)
            ds = (pd - p * twice(dot(pd.astype(BF), one))).astype(BF)
            ps.append(p.astype(BF))
            dss.append(ds)
            qrs.append(qr)
            dms.append(dmh)
            dq = rot_back(dot(ds, kr) * SCALE)
            qgain = qgain + jnp.sum(dq * q * rq, axis=0, keepdims=True)
            dqkv[:, at + g * HEAD : at + (g + 1) * HEAD] = head_back(q, rq, qg[...], dq).astype(BF)
        dv = dot_tn(jnp.concatenate(ps, 0), jnp.concatenate(dms, 0))
        dk = rot_back(dot_tn(jnp.concatenate(dss, 0), jnp.concatenate(qrs, 0)) * SCALE)
        kgain = kgain + jnp.sum(dk * k * rk, axis=0, keepdims=True)
        dqkv[:, at + 2 * HEAD : at + 3 * HEAD] = head_back(k, rk, kg[...], dk).astype(BF)
        dqkv[:, at + 3 * HEAD : at + 4 * HEAD] = dv.astype(BF)
        term = dot_nt(dqkv[:, at : at + 4 * HEAD], columns(wa[h], 0, 2, wrows))
        din = term if din is None else din + term
    d_in[...] = din.astype(d_in.dtype)
    x = token_rows(tok0, tok1)
    width = x.shape[1]
    gains[:, :width] += jnp.sum(din * (x * rsq(x)), axis=0, keepdims=True)
    gains[:, width : width + HEAD] += qgain
    gains[:, width + HEAD :] += kgain


def added(refs):
    total = refs[0][...].astype(F32)
    for r in refs[1:]:
        total = total + r[...].astype(F32)
    return total


def mid_kernel(tokens, gain, *refs):
    terms, (hidden, nm0, nm1) = refs[:-3], refs[-3:]
    h = tokens[...].astype(F32) + added(terms)
    hidden[...] = h
    nm = (h * rsq(h) * gain[...]).astype(BF)
    nm0[...] = nm[: nm0.shape[0]]
    nm1[...] = nm[nm0.shape[0] :]


def mid_back_kernel(hidden, cot, gain, *refs):
    terms, (d_hidden, low0, low1, ggrad) = refs[:-4], refs[-4:]
    d = added(terms)
    h = hidden[...]
    r = rsq(h)
    out = cot[...].astype(F32) + norm_back(h, r, gain[...], d)
    d_hidden[...] = out
    low0[...] = out[: low0.shape[0]].astype(BF)
    low1[...] = out[low0.shape[0] :].astype(BF)
    ggrad[...] = jnp.sum(d * h * r, axis=0, keepdims=True)


def last_kernel(tokens, d_hidden, gain, *refs):
    terms, (out,) = refs[:-1], refs[-1:]
    x = tokens[...].astype(F32)
    out[...] = (d_hidden[...] + norm_back(x, rsq(x), gain[...], added(terms))).astype(BF)


def out_kernel(hidden, *refs):
    refs[-1][...] = (hidden[...] + added(refs[:-1])).astype(BF)


def arrange(plane, t, blocks, cb):
    q = blocks[0].shape[0] // cb

    def body(where, *refs):
        for r, ref in enumerate(refs[:-1]):
            start = pl.multiple_of(plane.place(where[0], r) * q, 16)
            for j in range(cb):
                refs[-1][pl.ds(start, q), j * B : (j + 1) * B] = ref[j * q : (j + 1) * q, :]

    return kernel_call(body, [sds((len(blocks) * q, cb * B), BF)], [t.astype(jnp.int32)[None], *blocks], scalars=1)[0]


def grad_columns(plane, t, lhs, rhs, half, width, size, other, below=None):
    nblk = width // B
    flat_l, flat_r = sum(lhs, []), sum(rhs, [])
    nl, nr = len(flat_l), len(flat_r)
    rows = flat_l[0].shape[1] // size
    ready = below is not None and not isinstance(below, list)
    more = 0 if below is None else below.shape[1] if ready else below[0].shape[0]

    def body(where, *refs):
        left = jnp.concatenate([r[...] for r in refs[:nl]], 0)
        right = jnp.concatenate([r[...] for r in refs[nl : nl + nr]], 0)
        rest, out = refs[nl + nr : -1], refs[-1]
        got = dot_tn(left, right)
        for j in range(nblk):
            part = got[:, j * B : (j + 1) * B]
            if other is not None:
                part = part + rest[0][0, j * rows : (j + 1) * rows, :].astype(F32)
            out[0, j * rows : (j + 1) * rows, :] = part.astype(BF)
        if ready:
            out[0, nblk * rows :, :] = rest[-1][0]
        elif more:
            z = pl.program_id(0)
            for r in range(plane.n):
                @pl.when(plane.place(where[0], r) == z)
                def _():
                    out[0, nblk * rows :, :] = rest[-plane.n + r][...]

    tall = lambda k: pl.BlockSpec((1, k, B), lambda z, w: (z, 0, 0))
    in_specs = [pl.BlockSpec((a.shape[0], rows), lambda z, w: (0, z)) for a in flat_l]
    in_specs += [pl.BlockSpec((a.shape[0], width), lambda z, w: (0, half)) for a in flat_r]
    args = flat_l + flat_r
    if other is not None:
        in_specs.append(tall(nblk * rows))
        args = args + [other]
    if ready:
        in_specs.append(tall(more))
        args = args + [below]
    elif more:
        in_specs += [pl.BlockSpec((more, B), lambda z, w: (0, 0))] * plane.n
        args = args + below
    tokens = sum(a.shape[0] for a in flat_l)
    out = sds((size, nblk * rows + more, B), BF)
    return pl.pallas_call(
        body,
        out_shape=out,
        grid_spec=pltpu.PrefetchScalarGridSpec(
            num_scalar_prefetch=1, grid=(size,), in_specs=in_specs, out_specs=tall(nblk * rows + more)
        ),
        compiler_params=pltpu.CompilerParams(vmem_limit_bytes=VMEM_LIMIT),
        cost_estimate=pl.CostEstimate(
            flops=2 * tokens * rows * size * width,
            bytes_accessed=sum(a.size * 2 for a in args) + math.prod(out.shape) * 2,
            transcendentals=0,
        ),
    )(t.astype(jnp.int32)[None], *args)


def grad_rows(lhs, rhs, tokens_each, half, width, n, other):
    flat_l, flat_r = lhs, sum(rhs, [])
    nl = len(flat_l)
    cb = flat_r[0].shape[1] // B
    q = width // n

    def body(*refs):
        left = jnp.concatenate([r[...] for r in refs[:nl]], 0)
        right = jnp.concatenate([r[...] for r in refs[nl : nl + len(flat_r)]], 0)
        got = dot_tn(left, right).reshape(n, q, B)
        if other is not None:
            got = got + refs[-2][...].astype(F32)
        refs[-1][...] = got.astype(BF)

    spec = pl.BlockSpec((n, q, B), lambda j: (0, j, 0))
    in_specs = [pl.BlockSpec((a.shape[0], width), lambda j: (0, half)) for a in flat_l]
    in_specs += [pl.BlockSpec((tokens_each, B), lambda j: (0, j)) for a in flat_r]
    args = flat_l + flat_r
    if other is not None:
        in_specs.append(spec)
        args = args + [other]
    tokens = sum(a.shape[0] for a in flat_l)
    return kernel_call(
        body, [sds((n, cb * q, B), BF)], args, flops=2 * tokens * width * cb * B,
        grid=(cb,), in_specs=in_specs, out_specs=[spec],
    )[0]


def grad_down(core, product, cot, other, size, ff):
    flat_r = sum(cot, [])
    nl, nr = len(product), len(flat_r)
    mine = other is not None

    def body(where, *refs):
        left = jnp.concatenate([r[...] for r in refs[:nl]], 0)
        right = jnp.concatenate([r[...] for r in refs[nl : nl + nr]], 0)
        out = refs[-1]
        got = dot_tn(left, right)
        for h in range(2):
            for i in range(2):
                s = 2 * jnp.bitwise_xor(where[0], h) + i
                at = h * ff
                part = jnp.concatenate(
                    [got[at + i * 128 : at + (i + 1) * 128], got[at + 256 + i * 64 : at + 256 + (i + 1) * 64]], 0)
                if mine:
                    part = part + refs[-2][s].astype(F32)
                out[s] = part.astype(BF)

    def column(j, w):
        return (0, jnp.bitwise_xor(w[0], 0 if mine else 1) * 2 + j)

    spec = pl.BlockSpec((size, 192, B), lambda j, w: (0, j, 0))
    in_specs = [pl.BlockSpec(a.shape, lambda j, w: (0, 0)) for a in product]
    in_specs += [pl.BlockSpec((a.shape[0], B), column) for a in flat_r]
    args = product + flat_r + ([other] if mine else [])
    return pl.pallas_call(
        body,
        out_shape=sds((size, 2 * 192, B), BF),
        grid_spec=pltpu.PrefetchScalarGridSpec(
            num_scalar_prefetch=1, grid=(2,), in_specs=in_specs + [spec] * mine, out_specs=spec
        ),
        compiler_params=pltpu.CompilerParams(vmem_limit_bytes=VMEM_LIMIT),
        cost_estimate=pl.CostEstimate(
            flops=2 * sum(a.size for a in product) * 512, bytes_accessed=sum(a.size * 2 for a in args), transcendentals=0
        ),
    )(core, *args)


def over_blocks(block, shared, per_block, outs, flops, total=False):
    flat = []
    shape = []
    for a in shared:
        shape.append(len(a) if isinstance(a, list) else None)
        flat += a if isinstance(a, list) else [a]
    nb, k, o = len(per_block), len(per_block[0]), len(outs[0])
    scalars = sum(1 for a in flat if a.dtype == jnp.int32)
    args = flat + sum(per_block, [])
    out_shapes = sum(outs, []) + ([total] if total else [])

    def body(*refs):
        at, head = 0, []
        for m in shape:
            head.append(refs[at] if m is None else refs[at : at + m])
            at += 1 if m is None else m
        ins, results = refs[at : at + nb * k], refs[at + nb * k :]
        tail = ()
        if total:
            results[-1][...] = jnp.zeros_like(results[-1])
            tail = (results[-1],)
        for b in range(nb):
            block(*head, *ins[b * k : (b + 1) * k], *results[b * o : (b + 1) * o], *tail)

    got = kernel_call(body, out_shapes, args, flops=flops * nb, scalars=scalars)
    return [got[b * o : (b + 1) * o] for b in range(nb)], (got[-1] if total else None)


def make_body(size, plane, halves):
    n = plane.n
    parts = 2 if halves else 1
    one_by_one = [[r] for r in (n - 1, *range(1, n - 1), 0)]
    three = [[n - 1], list(range(1, n - 1)), [0]]

    def body(tokens, segment_ids, attn_gain, w_query, w_key, w_value, query_gain, key_gain,
             w_out, mlp_gain, w_gate, w_up, w_down, cotangent):
        t = plane.index()
        c = lax.axis_index("c") if halves else 0
        rows, width = tokens.shape
        length = segment_ids.shape[1]
        assert rows == length
        half = rows // 2
        cb = width // B
        wrows = w_query.shape[0]
        cut_a, cut_b = 2 * wrows, 2 * w_gate.shape[1] // n // parts // B * wrows
        out_rows, down_rows = w_out.shape[0] // parts // n, w_down.shape[0] // parts // n
        ff = n * down_rows
        spread = plane.square and halves and size == 4 and ff == 384 and width == 1024
        core = jnp.stack([c]).astype(jnp.int32)
        gain_in, gain_mid = attn_gain[None, :], mlp_gain[None, :]
        qg, kg = query_gain[None, :], key_gain[None, :]
        freq = ROPE_BASE ** (-2.0 * (jnp.arange(HEAD) % (HEAD // 2)).astype(F32) / HEAD)[None, :]

        def pick(col_weights, row_weight):
            each = [w.shape[1] // n // parts for w in col_weights]
            total = sum(each)
            high = total // B * wrows
            q = row_weight.shape[0] // parts // n if row_weight is not None else 0
            where = jnp.stack([t * parts + c, c * n + t]).astype(jnp.int32)

            def fill(_, *refs):
                a = [r[...] for r in refs[: len(each)]]
                if a:
                    a = jnp.concatenate(a, 1)
                for j in range(total // B):
                    refs[-1][j * wrows : (j + 1) * wrows, :] = a[:, j * B : (j + 1) * B]
                for j in range(cb if q else 0):
                    refs[-1][high + j * q : high + (j + 1) * q, :] = refs[-2][:, j * B : (j + 1) * B]

            rows_of = [row_weight] if q else []
            return pl.pallas_call(
                fill,
                out_shape=sds((high + cb * q, B), BF),
                grid_spec=pltpu.PrefetchScalarGridSpec(
                    num_scalar_prefetch=1,
                    grid=(1,),
                    in_specs=[pl.BlockSpec((wrows, k), lambda i, at: (0, at[0])) for k in each]
                    + [pl.BlockSpec((q, width), lambda i, at: (at[1], 0)) for _ in rows_of],
                    out_specs=pl.BlockSpec((high + cb * q, B), lambda i, at: (0, 0)),
                ),
                compiler_params=pltpu.CompilerParams(vmem_limit_bytes=VMEM_LIMIT),
            )(where, *[pltpu.with_memory_space_constraint(w, pltpu.HBM) for w in (*col_weights, *rows_of)])

        def pick_spread():
            where = jnp.stack([t, c]).astype(jnp.int32)
            aligned = lambda i, k: lambda _, w: (0, 6 * (2 * w[1] + i) + (3 * w[0]) // 2 + k)

            def fill(w, *refs):
                odd = jnp.full((wrows, HEAD), w[0] % 2) == 1
                low = lax.broadcasted_iota(jnp.int32, (wrows, HEAD), 1) < HEAD // 2
                cols = []
                for m in range(2):
                    full, rest = [], []
                    for i in range(2):
                        w0, w1 = (refs[4 * m + 2 * i + k][...].astype(F32) for k in range(2))
                        r0, r1 = half_roll(w0), half_roll(w1)
                        full.append(jnp.where(odd, jnp.where(low, r0, r1), w0))
                        rest.append(jnp.where(odd, r1, w1) if i == 0 else jnp.where(odd, w1, r1))
                    cols += [*full, jnp.where(low, *rest)]
                out, down = refs[-1], refs[-2]
                for j, a in enumerate(cols):
                    out[j // 2 * wrows : (j // 2 + 1) * wrows, j % 2 * HEAD : (j % 2 + 1) * HEAD] = a.astype(BF)
                for j in range(2):
                    out[cut_b + j * 192 : cut_b + (j + 1) * 192, :] = down[:, j * B : (j + 1) * B]

            return pl.pallas_call(
                fill,
                out_shape=sds((cut_b + 384, B), BF),
                grid_spec=pltpu.PrefetchScalarGridSpec(
                    num_scalar_prefetch=1,
                    grid=(1,),
                    in_specs=[pl.BlockSpec((wrows, HEAD), aligned(i, k)) for _ in range(2) for i in range(2) for k in range(2)]
                    + [pl.BlockSpec((192, width // 2), lambda _, w: (w[0], w[1]))],
                    out_specs=pl.BlockSpec((cut_b + 384, B), lambda _, w: (0, 0)),
                ),
                compiler_params=pltpu.CompilerParams(vmem_limit_bytes=VMEM_LIMIT),
            )(where, *[stay(w_gate)] * 4, *[stay(w_up)] * 4, stay(w_down))

        def both(a):
            return [a, swap(a, "c")] if halves else [a]

        def rows_to_chip(got, cut):
            blocks = plane.exchange(lambda i: lax.dynamic_slice_in_dim(got, i, 1, 0)[0, cut:])
            return arrange(plane, t, blocks, cb)

        got_a = lax.all_gather(pick([w_query, w_key, w_value], w_out), "shard", axis=0, tiled=False)

        seg_rows = jnp.pad(segment_ids.astype(BF), ((0, 15), (0, width - length)))
        tok = plane.gather(tokens[:half], jnp.concatenate([tokens[half:], seg_rows], 0))
        cot_own, w_gate, w_up, w_down, tok[1], tok[n - 2] = tie((cotangent, w_gate, w_up, w_down, tok[1], tok[n - 2]))
        cot = plane.gather(cot_own[:half], cot_own[half:])
        piece_b = pick_spread() if spread else pick([w_gate, w_up], w_down)
        prep, _ = over_blocks(
            functools.partial(prep_block, length), [gain_in, freq], tok,
            [[hbm((length, width), BF), hbm((length, HEAD), F32), hbm((length, HEAD), F32), hbm((length, length), F32)]] * n,
            0,
        )
        got_a, prep, piece_b, cot = tie((got_a, prep, piece_b, cot))
        nin, tables = [a[0] for a in prep], [a[1:] for a in prep]
        got_b = lax.all_gather(piece_b, "shard", axis=0, tiled=False)
        wo = rows_to_chip(got_a, cut_a)
        wa, wo = both(got_a), both(wo)

        def term_type(r):
            return sds((rows, width), F32 if r == 0 and plane.square else BF)

        def run(block, shared, ins, outs, flops, order, total=None):
            got, totals = {}, []
            for group in order:
                mine = [ins[r] for r in group]
                res, tot = over_blocks(block, shared, mine, [outs(r) for r in group], flops, total)
                got.update(zip(group, res))
                totals.append(tot)
            return [{r: got[r][i] for r in got} for i in range(len(outs(0)))], totals

        (lin, vals, mixed, partial), _ = run(
            functools.partial(attend_block, parts, wrows), [qg, kg, wa, wo],
            [[stay(a) for a in (nin[r], *tables[r])] for r in range(n)],
            lambda r: [hbm((length, parts * 3 * HEAD), F32), hbm((length, parts * HEAD), BF),
                       hbm((length, parts * GROUP * HEAD), BF), term_type(r)],
            2 * length * width * parts * 6 * HEAD, three,
        )
        lin, vals, mixed, partial = ([a[r] for r in range(n)] for a in (lin, vals, mixed, partial))
        terms = plane.scatter(partial)
        hidden, nm0, nm1 = kernel_call(
            mid_kernel,
            [hbm((rows, width), F32), sds((half, width), BF), sds((half, width), BF)],
            [tokens, gain_mid, *terms],
        )
        nm = plane.gather(nm0, nm1)
        got_b, nm[1], nm[n - 2] = tie((got_b, nm[1], nm[n - 2]))
        wgu, wd = both(got_b), [] if spread else both(rows_to_chip(got_b, cut_b))

        (product, dgu, partial, d_mid), _ = run(
            functools.partial(mlp_block, spread, parts, wrows, ff), [core, wgu, wd],
            [[*nm[r], *[stay(a) for a in cot[r]]] for r in range(n)],
            lambda r: [sds((rows, parts * ff), BF), sds((rows, parts * 2 * ff), BF),
                       hbm((rows, width), term_type(r).dtype), term_type(r)],
            2 * length * width * parts * 7 * ff, one_by_one,
        )
        product, dgu, partial, d_mid = ([a[r] for r in range(n)] for a in (product, dgu, partial, d_mid))
        terms_mid = plane.scatter(d_mid)
        product, terms_mid[-1] = tie((product, terms_mid[-1]))

        def pair(make, between=lambda a: a):
            if halves:
                return make(0, swap(between(make(1, None)), "c"))
            return lax.psum(make(0, None), "c")

        dgu = [[a] for a in dgu]
        if spread:
            down = grad_down(core, product, cot, swap(grad_down(core, product, cot, None, size, ff), "c"), size, ff)
        else:
            down = pair(lambda h, o: grad_rows(product, cot, half, h, ff, n, o))
        terms_mid, down = tie((terms_mid, down))
        d_hidden, dh0, dh1, mlp_grad = kernel_call(
            mid_back_kernel,
            [hbm((rows, width), F32), sds((half, width), BF), sds((half, width), BF), sds((1, width), F32)],
            [hidden, cotangent, gain_mid, *terms_mid],
        )
        dh = plane.gather_near(dh0, dh1)
        dgu, _ = tie((dgu, dh0))
        gu_other = grad_columns(plane, t, nm, dgu, 1, 2 * ff, size, None) if halves else None
        dh[0], gu_other = tie((dh[0], gu_other))

        def back(order, dh):
            return run(
                functools.partial(attend_back_block, parts, wrows), [qg, kg, wa, wo],
                {r: [*dh[r], *[stay(a) for a in (*tok[r], lin[r], vals[r], *tables[r])]] for g in order for r in g},
                lambda r: [hbm((rows, parts * 4 * HEAD), BF), term_type(r)],
                2 * length * width * parts * 6 * HEAD, order, sds((1, width + 2 * HEAD), F32),
            )

        own_back, gains = back([[0]], dh)
        dh = plane.gather_far(dh, own_back)
        gu_other, own_back, dh[1:-1] = tie((gu_other, own_back, dh[1:-1]))

        def exchanged(low):
            return plane.exchange(lambda i: lax.dynamic_index_in_dim(low, i, 0, keepdims=False))

        def merged(lhs, rhs, width_, other, low):
            if halves:
                return grad_columns(plane, t, lhs, rhs, 0, width_, size, swap(other, "c"), low)
            a = grad_columns(plane, t, lhs, rhs, 0, width_, size, None)
            return jnp.concatenate([lax.psum(a, "c"), jnp.stack(low, 0)], 1)

        grads_b = merged(nm, dgu, 2 * ff, gu_other, down if spread else exchanged(down))
        partial, grads_b = tie((partial, grads_b))
        grads_b = lax.psum_scatter(grads_b.reshape(-1, B), "shard", scatter_dimension=0, tiled=True)
        terms_out = plane.scatter(partial)
        out = pair(lambda h, o: grad_rows(
            [stay(a) for a in mixed], [[stay(a) for a in b] for b in dh], half, h, GROUP * HEAD, n, o))
        far_back, more = back([[n - 1]], dh)
        dh[1:-1], far_back, out = tie((dh[1:-1], far_back, out))
        out = exchanged(out)
        near_back, last = back([[r] for r in range(1, n - 2)], dh)
        dh[n - 2], near_back, terms_out = tie((dh[n - 2], near_back, terms_out))
        near2_back, last2 = back([[n - 2]], dh)
        near_back = [{**a, **b} for a, b in zip(near_back, near2_back)]
        gains = gains + more + last + last2
        dqkv, d_in = ({**a, **b, **c} for a, b, c in zip(own_back, far_back, near_back))
        dqkv, d_in = ([a[r] for r in range(n)] for a in (dqkv, d_in))
        terms_in = plane.scatter(d_in)
        dqkv = [[a] for a in dqkv]
        lhs = [[a] for a in nin]
        dqkv, terms_in[-1] = tie((dqkv, terms_in[-1]))
        qkv_other = grad_columns(plane, t, lhs, dqkv, 1, 4 * HEAD, size, None) if halves else None
        qkv_other, terms_in[:-1] = tie((qkv_other, terms_in[:-1]))
        grads_a = merged(lhs, dqkv, 4 * HEAD, qkv_other, out)
        gains = jnp.concatenate([functools.reduce(jnp.add, gains), mlp_grad], 1)
        grads_a, grads_b, gains = tie((grads_a, grads_b, gains))
        grads_a = lax.psum_scatter(grads_a.reshape(-1, B), "shard", scatter_dimension=0, tiled=True)
        if plane.square and size == 4:
            for axis in ("c", "x", "y"):
                gains = gains + swap(gains, axis)
            gains, grads_b = tie((gains, grads_b))
            for k in (1, 2):
                gains = gains + lax.ppermute(gains, "shard", [(i, i ^ k) for i in range(4)])
        else:
            gains = lax.psum(gains, ("shard", "y", "x", "c"))
        grads_b = plane.gather_whole(grads_b)
        activations = kernel_call(
            out_kernel, [sds((rows, width), BF)], [hidden, *terms_out],
        )[0]
        grads_a, grads_b, gains = tie((grads_a, grads_b, gains))
        gains = gains[0]
        input_grad = kernel_call(
            last_kernel, [sds((rows, width), BF)], [tokens, d_hidden, gain_in, *terms_in],
        )[0]


        def assemble(mine, outs, write):
            got = [(r, 0, a) for r, a in enumerate(mine)]
            if halves:
                got += [(r, 1, swap(a, "c")) for r, a in enumerate(mine)]

            def body(where, *refs):
                for (r, other, _), ref in zip(got, refs):
                    core = jnp.bitwise_xor(where[1], other) if halves else 0
                    write(ref, plane.place(where[0], r), core, refs[len(got) :])

            if write is write_spread:
                body = lambda where, *refs: write(where, refs[: len(got)], refs[len(got) :])
            where = jnp.stack([t, c]).astype(jnp.int32)
            return kernel_call(body, outs, [where] + [a for _, _, a in got], scalars=1)

        def write_cols(ref, j, todo, src, core):
            a = ref[j * wrows : (j + 1) * wrows, :].astype(F32)
            for lo, hi, out, per, at in todo:
                start = pl.multiple_of((src * parts + core) * per + at, HEAD)
                out[:, pl.ds(start, hi - lo)] = a[:, lo:hi]

        def write_rows(ref, base, q, src, core, out):
            start = pl.multiple_of((core * n + src) * q, 16)
            for j in range(cb):
                a = ref[base + j * q : base + (j + 1) * q, :].astype(F32)
                out[pl.ds(start, q), j * B : (j + 1) * B] = a

        def write_b(ref, src, core, outs):
            gate, up, down = outs
            for j in range(2 * ff // B):
                todo = []
                for out, lo in ((gate, 0), (up, ff)):
                    a, b = max(j * B, lo), min((j + 1) * B, lo + ff)
                    if a < b:
                        todo.append((a - j * B, b - j * B, out, ff, a - lo))
                write_cols(ref, j, todo, src, core)
            write_rows(ref, cut_b, down_rows, src, core, down)

        def write_spread(where, refs, outs):
            gate, up, down = outs
            odd = jnp.full((wrows, HEAD), where[0] % 2) == 1
            low = lax.broadcasted_iota(jnp.int32, (wrows, HEAD), 1) < HEAD // 2
            for other in range(2):
                core = jnp.bitwise_xor(where[1], other)
                mine = refs[other * n : (other + 1) * n]
                for r, ref in enumerate(mine):
                    for j in range(2):
                        down[pl.ds(pl.multiple_of(plane.place(where[0], r) * 192, 64), 192),
                             pl.ds(pl.multiple_of((2 * core + j) * B, B), B)] = (
                            ref[cut_b + j * 192 : cut_b + (j + 1) * 192, :].astype(F32))
                for k in range(2):
                    one, two = mine[2 * k], mine[2 * k + 1]
                    pair_at = jnp.bitwise_xor(where[0] // 2, k)
                    for m, out in enumerate((gate, up)):
                        def block(ref, j):
                            j = 3 * m + j
                            return ref[j // 2 * wrows : (j // 2 + 1) * wrows, j % 2 * HEAD : (j % 2 + 1) * HEAD].astype(F32)

                        pairs = [(block(one, j), block(two, j)) for j in range(3)]
                        even = [jnp.where(odd, b, a) for a, b in pairs]
                        odds = [jnp.where(odd, a, b) for a, b in pairs]
                        for i in range(2):
                            at = pl.multiple_of(768 * (2 * core + i) + 384 * pair_at, HEAD)
                            rolled = half_roll(odds[i])
                            rest_even = even[2] if i == 0 else half_roll(even[2])
                            rest_odd = half_roll(odds[2]) if i == 0 else odds[2]
                            out[:, pl.ds(at, HEAD)] = even[i]
                            out[:, pl.ds(at + HEAD, HEAD)] = jnp.where(low, rest_even, rolled)
                            out[:, pl.ds(at + 2 * HEAD, HEAD)] = jnp.where(low, rolled, rest_odd)

        def write_a(ref, src, core, outs):
            q, k, v, out = outs
            write_cols(ref, 0, [(0, B, q, B, 0)], src, core)
            write_cols(ref, 1, [(0, HEAD, k, HEAD, 0), (HEAD, B, v, HEAD, 0)], src, core)
            write_rows(ref, cut_a, out_rows, src, core, out)

        like = lambda w: sds(w.shape, F32)
        gate_g, up_g, down_g = assemble(grads_b, [like(w_gate), like(w_up), like(w_down)], write_spread if spread else write_b)
        grads_a = plane.gather_whole(grads_a)
        grads_a, gate_g, up_g, down_g, activations, input_grad = tie(
            (grads_a, gate_g, up_g, down_g, activations, input_grad))
        query_g, key_g, value_g, out_g = assemble(
            grads_a, [like(w_query), like(w_key), like(w_value), like(w_out)], write_a)

        return (
            activations,
            input_grad,
            gains[:width],
            query_g,
            key_g,
            value_g,
            gains[width : width + HEAD],
            gains[width + HEAD : width + 2 * HEAD],
            out_g,
            gains[width + 2 * HEAD :],
            gate_g,
            up_g,
            down_g,
        )

    return body


def solution(mesh):
    size, replicas = mesh.shape["shard"], mesh.shape["replica"]
    ny, nx = replicas // 4, 2
    assert size == ny * nx
    plane = Plane(ny, nx)
    fine = Mesh(mesh.devices.reshape(size, ny, nx, 2), ("shard", "y", "x", "c"))
    halves = KV_HEADS % (2 * plane.n) == 0
    every = P(("shard", "y", "x", "c"), None)
    shard, copy = P("shard", None), P()
    return jax.shard_map(
        make_body(size, plane, halves),
        mesh=fine,
        in_specs=(every, every, copy, shard, shard, shard, copy, copy, shard, copy, shard, shard, shard, every),
        out_specs=(every, every, copy, shard, shard, shard, copy, copy, shard, copy, shard, shard, shard),
        check_vma=False,
    )
```

time: 384 us -> 349 us (0.909)
  waiting for transfers between devices: 147 us -> 132 us
  starting transfers between devices: 74.8 us -> 62.1 us
  local copies, waits for them, and re-layouts: 34.7 us -> 22.9 us
  Pallas kernels: 104 us -> 111 us
    ppermute x73 -> x58, starting transfers between devices: 61 us -> 47.5 us  [swap(): return lax.ppermute(a, axis, SWAP)]
    unnamed x294 -> x194, local copies, waits for them, and re-layouts: 30.7 us -> 20.4 us
    ppermute x2 -> x6, waiting for transfers between devices: 13.1 us -> 4.44 us  [the longest x2 3.56 us: far(): return near + [lax.ppermute(a, self.axes, [(i, 3 - i) for i in range(4)])]]
    pallas_call x0 -> x3, Pallas kernels: none -> 8.06 us  [the longest x2 5.21 us: grad_down(): pl.pallas_call(body, out_shape=sds((size, 2 * 192, B), BF), grid_spec=plt...]
    ppermute x73 -> x58, waiting for transfers between devices: 121 us -> 113 us  [swap(): return lax.ppermute(a, axis, SWAP)]
    ppermute x2 -> x6, starting transfers between devices: 3.16 us -> 9.14 us  [the longest x4 5.97 us: scatter(): far = lax.ppermute(blocks[3], self.axes, [(i, 3 - i) for i in range(4)])]
    ppermute x4 -> x2, starting transfers between devices: 5.97 us -> 1.39 us  [exchange(): lax.ppermute(slice_for(jnp.bitwise_xor(t, 3)), self.axes, [(i, 3 - i) for...]
    ppermute x2, waiting for transfers between devices: 1.87 us -> 6.37 us  [body(): gains = gains + lax.ppermute(gains, 'shard', [(i, i ^ k) for i in range(4)])]
  transfers between devices with their start and end apart: 85 -> 72, of which waited for: 35 -> 39; matrix products, arithmetic and copies ran while one was open for 2% -> 1% of each run, Pallas kernels for 24% -> 27%
where the time goes in v3:
time: 349 us; the launch traced here: 344 us
  waiting for transfers between devices  132 us (38%)
  Pallas kernels  111 us (32%)
  starting transfers between devices  62.1 us (18%)
  local copies, waits for them, and re-layouts  22.9 us (7%)
  between operations  15 us (4%)
    ppermute x58, waiting for transfers between devices, swap(): return lax.ppermute(a, axis, SWAP)  113 us
    pallas_call x21, Pallas kernels, kernel_call(): pl.pallas_call(body, out_shape=outs, compiler_params=pltpu.CompilerParams...  87.4 us
    ppermute x58, starting transfers between devices, swap(): return lax.ppermute(a, axis, SWAP)  47.5 us
    unnamed x194, local copies, waits for them, and re-layouts  20.4 us
    pallas_call x4, Pallas kernels, grad_columns(): pl.pallas_call(body, out_shape=out, grid_spec=pltpu.PrefetchScalarGridSpe...  13.6 us
    ppermute x2, waiting for transfers between devices, exchange(): lax.ppermute(slice_for(jnp.bitwise_xor(t, 3)), self.axes, [(i, 3 - i) for...  7.48 us
  transfers between devices with their start and end apart: 72, of which 39 were waited for; matrix products, arithmetic and copies ran while one was open for 1% of the time, Pallas kernels for 27%

profile of v3, /device:TPU:0, one launch (start us, length us, event | category | flops | bytes accessed | tf_op | source)
XLA Modules:
  0.0 343.6 jit_solution(5922962254921355348)
XLA Ops:
  7.3 2.4 shard_map.237
  9.9 3.0 collective-permute-start.3
  12.9 1.5 collective-permute-start.1
  15.0 10.5 %collective-permute-done.2.refs_6_.refs_8_ = bf16[128,1024]{1,0:T(8,128)(2,1)S(1)} collective-permute-done((bf16[128,1024]{1,0:T(8,128)(2,1)S(1)}, bf16[128,1024]{1,0:T(8,128)(2,1)S(1)}, u32[]{:S(2)}, u32[]{:S(2)}) %collective-permute-start.2) | collective-permute-done | bytes 262176 | tf_op jit(solution)/shard_map/ppermute | solution.py:41
  27.1 1.6 collective-permute-start.7
  29.6 1.7 collective-permute-start.5
  31.6 4.8 %collective-permute-done.7.refs_6_.refs_7_ = bf16[128,1024]{1,0:T(8,128)(2,1)S(1)} collective-permute-done((bf16[128,1024]{1,0:T(8,128)(2,1)S(1)}, bf16[128,1024]{1,0:T(8,128)(2,1)S(1)}, u32[]{:S(2)}, u32[]{:S(2)}) %collective-permute-start.7) | collective-permute-done | bytes 262176 | tf_op jit(solution)/shard_map/ppermute | solution.py:41
  38.4 3.6 %collective-permute-done.4.refs_8_ = bf16[128,1024]{1,0:T(8,128)(2,1)S(1)} collective-permute-done((bf16[128,1024]{1,0:T(8,128)(2,1)S(1)}, bf16[128,1024]{1,0:T(8,128)(2,1)S(1)}, u32[]{:S(2)}, u32[]{:S(2)}) %collective-permute-start.4) | collective-permute-done | bytes 262176 | tf_op jit(solution)/shard_map/ppermute | solution.py:41
  43.2 2.9 shard_map.239
  47.1 4.2 %shard_map.238 = (bf16[256,1024]{1,0:T(8,128)(2,1)}, f32[256,128]{1,0:T(8,128)}, f32[256,128]{1,0:T(8,128)}, f32[256,256]{1,0:T(8,128)}, bf16[256,1024]{1,0:T(8,...) custom-call(f32[1,1024]{1,0:T(1,128)S(1)} %bitcast.60, ...), custom_call_target="tpu_custom_call" | custom-call | bytes 6427136 | tf_op jit(solution)/shard_map/pallas_call | solution.py:67
  51.4 1.6 collective-permute-done.11.refs_6_.refs_11_
  56.7 1.5 collective-permute-start.13
  58.2 3.8 %collective-permute-done.15.refs_3_ = bf16[256,256]{1,0:T(8,128)(2,1)S(1)} collective-permute-done((bf16[256,256]{1,0:T(8,128)(2,1)S(1)}, bf16[256,256]{1,0:T(8,128)(2,1)S(1)}, u32[]{:S(2)}, u32[]{:S(2)}) %collective-permute-start.15) | collective-permute-done | bytes 131104 | tf_op jit(solution)/shard_map/ppermute | solution.py:136
  61.9 2.0 collective-permute-done.14.refs_2_
  64.1 1.9 collective-permute-done.16.refs_5_
  66.0 4.4 %shard_map.243 = (f32[256,768]{1,0:T(8,128)}, bf16[256,256]{1,0:T(8,128)(2,1)}, bf16[256,512]{1,0:T(8,128)(2,1)}, bf16[256,1024]{1,0:T(8,128)(2,1)S(1)}) custom-call(f32[1,128]{1,0:T(1,128)S(1)} %bitcast.44, f32[1,128]{1,0:T(1,128)S(1)} %bitcast.51, bf16[4,768,256]{2,1,0:T(8,128)(2,1)S(1)} %bitcast.36, ...), custom_call_target="tpu_custom_call" | custom-call | flops 805306368 | bytes 6947840 | tf_op jit(solution)/shard_map/pallas_call | solution.py:67
  71.6 7.1 %shard_map.242 = (f32[256,768]{1,0:T(8,128)}, bf16[256,256]{1,0:T(8,128)(2,1)}, bf16[256,512]{1,0:T(8,128)(2,1)}, bf16[256,1024]{1,0:T(8,128)(2,1)S(1)}, f32[256...) custom-call(f32[1,128]{1,0:T(1,128)S(1)} %bitcast.45, ...), custom_call_target="tpu_custom_call" | custom-call | flops 1610612736 | bytes 9700352 | tf_op jit(solution)/shard_map/pallas_call | solution.py:67
  81.0 4.3 %shard_map.241 = (f32[256,768]{1,0:T(8,128)}, bf16[256,256]{1,0:T(8,128)(2,1)}, bf16[256,512]{1,0:T(8,128)(2,1)}, f32[256,1024]{1,0:T(8,128)S(1)}) custom-call(f32[1,128]{1,0:T(1,128)S(1)} %bitcast.46, f32[1,128]{1,0:T(1,128)S(1)} %bitcast.53, bf16[4,768,256]{2,1,0:T(8,128)(2,1)S(1)} %bitcast.38, bf16[4,768,256]{2,1,0:T(8,128)(2,1)S(1)} %collective-permute-done.12.refs_3_, ...), custom_call_target="tpu_custom_call" | custom-call | flops 805306368 | bytes 7472128 | tf_op jit(solution)/shard_map/pallas_call | solution.py:67
  86.2 9.8 %collective-permute-done.17.refs_1_ = bf16[256,1024]{1,0:T(8,128)(2,1)S(1)} collective-permute-done((bf16[256,1024]{1,0:T(8,128)(2,1)S(1)}, bf16[256,1024]{1,0:T(8,128)(2,1)S(1)}, u32[]{:S(2)}, u32[]{:S(2)}) %collective-permute-start.17) | collective-permute-done | bytes 524320 | tf_op jit(solution)/shard_map/ppermute | solution.py:41
  102.6 4.4 %collective-permute-done.22.refs_3_.refs_4_ = bf16[128,1024]{1,0:T(8,128)(2,1)S(1)} collective-permute-done((bf16[128,1024]{1,0:T(8,128)(2,1)S(1)}, bf16[128,1024]{1,0:T(8,128)(2,1)S(1)}, u32[]{:S(2)}, u32[]{:S(2)}) %collective-permute-start.22) | collective-permute-done | bytes 262176 | tf_op jit(solution)/shard_map/ppermute | solution.py:41
  108.6 3.2 collective-permute-done.23.refs_4_.refs_5_
  114.5 7.0 %collective-permute-done.27.refs_3_.refs_6_ = bf16[128,1024]{1,0:T(8,128)(2,1)S(1)} collective-permute-done((bf16[128,1024]{1,0:T(8,128)(2,1)}, bf16[128,1024]{1,0:T(8,128)(2,1)S(1)}, u32[]{:S(2)}, u32[]{:S(2)}) %collective-permute-start.27) | collective-permute-done | bytes 262176 | tf_op jit(solution)/shard_map/ppermute | solution.py:41
  122.1 1.7 copy-done.91
  123.7 4.2 %shard_map.248 = (bf16[256,768]{1,0:T(8,128)(2,1)S(1)}, bf16[256,1536]{1,0:T(8,128)(2,1)S(1)}, bf16[256,1024]{1,0:T(8,128)(2,1)}, bf16[256,1024]{1,0:T(8,128)(2,1)S(1)}) custom-call(s32[1]{0:T(128)} %bitcast.5.refs_0_.where, bf16[4,1152,256]{2,1,0:T(8,128)(2,1)S(1)} %bitcast.63, bf16[4,1152,256]{2,1,0:T(8,128)(2,1)S(1)} %collective-permute-done.24.refs_2_, ...), custom_call_target="tpu_custom_call" | custom-call | flops 2818572288 | bytes 7995396 | tf_op jit(solution)/shard_map/pallas_call | solution.py:67
  128.0 1.8 collective-permute-start.29
  129.8 5.1 %shard_map.245 = (bf16[256,768]{1,0:T(8,128)(2,1)S(1)}, bf16[256,1536]{1,0:T(8,128)(2,1)S(1)}, f32[256,1024]{1,0:T(8,128)}, f32[256,1024]{1,0:T(8,128)S(1)}) custom-call(s32[1]{0:T(128)} %bitcast.5.refs_0_.where, bf16[4,1152,256]{2,1,0:T(8,128)(2,1)S(1)} %bitcast.64, bf16[4,1152,256]{2,1,0:T(8,128)(2,1)S(1)} %collective-permute-done.24.refs_2_, ...), custom_call_target="tpu_custom_call" | custom-call | flops 2818572288 | bytes 9043972 | tf_op jit(solution)/shard_map/pallas_call | solution.py:67
  134.9 4.1 %shard_map.247 = (bf16[256,768]{1,0:T(8,128)(2,1)S(1)}, bf16[256,1536]{1,0:T(8,128)(2,1)S(1)}, bf16[256,1024]{1,0:T(8,128)(2,1)}, bf16[256,1024]{1,0:T(8,128)(2,1)S(1)}) custom-call(s32[1]{0:T(128)} %bitcast.5.refs_0_.where, bf16[4,1152,256]{2,1,0:T(8,128)(2,1)S(1)} %bitcast.65, bf16[4,1152,256]{2,1,0:T(8,128)(2,1)S(1)} %collective-permute-done.24.refs_2_, ...), custom_call_target="tpu_custom_call" | custom-call | flops 2818572288 | bytes 7995396 | tf_op jit(solution)/shard_map/pallas_call | solution.py:67
  139.1 4.3 %shard_map.246 = (bf16[256,768]{1,0:T(8,128)(2,1)S(1)}, bf16[256,1536]{1,0:T(8,128)(2,1)S(1)}, bf16[256,1024]{1,0:T(8,128)(2,1)}, bf16[256,1024]{1,0:T(8,128)(2,1)S(1)}) custom-call(s32[1]{0:T(128)} %bitcast.5.refs_0_.where, bf16[4,1152,256]{2,1,0:T(8,128)(2,1)S(1)} %bitcast.66, bf16[4,1152,256]{2,1,0:T(8,128)(2,1)S(1)} %collective-permute-done.24.refs_2_, ...), custom_call_target="tpu_custom_call" | custom-call | flops 2818572288 | bytes 7995396 | tf_op jit(solution)/shard_map/pallas_call | solution.py:67
  143.4 2.8 shard_map.249
  148.6 2.4 shard_map.250.refs_13_
  151.0 9.7 %collective-permute-done.26.refs_2_ = bf16[256,1024]{1,0:T(8,128)(2,1)S(1)} collective-permute-done((bf16[256,1024]{1,0:T(8,128)(2,1)S(1)}, bf16[256,1024]{1,0:T(8,128)(2,1)S(1)}, u32[]{:S(2)}, u32[]{:S(2)}) %collective-permute-start.26) | collective-permute-done | bytes 524320 | tf_op jit(solution)/shard_map/ppermute | solution.py:41
  161.2 1.7 shard_map.251
  167.1 3.9 %shard_map.252 = bf16[4,768,256]{2,1,0:T(8,128)(2,1)S(1)} custom-call(s32[1]{0:T(128)} %bitcast.where, bf16[128,1024]{1,0:T(8,128)(2,1)S(1)} %get-tuple-element.258.refs_3_.refs_0_, bf16[128,1024]{1,0:T(8,128)(2,1)S(1)} %copy-done.54, bf16[128,1024]{1,0:T(8,128)(2,1)S(1)} %copy-done.58, bf16[128,1024]{1,0:T(8,128)(2,1)} %collective-permute-done.21.refs_4_.refs_3_, ...), custom_call_target="tpu_custom_call" | custom-call | flops 1610612736 | bytes 6815744 | tf_op jit(solution)/shard_map/pallas_call | solution.py:424
  171.0 6.6 %shard_map.253 = (bf16[256,1024]{1,0:T(8,128)(2,1)}, f32[256,1024]{1,0:T(8,128)S(1)}, f32[1,1280]{1,0:T(1,128)S(1)}) custom-call(f32[1,128]{1,0:T(1,128)S(1)} %bitcast.47, f32[1,128]{1,0:T(1,128)S(1)} %bitcast.54, bf16[4,768,256]{2,1,0:T(8,128)(2,1)S(1)} %bitcast.39, bf16[4,768,256]{2,1,0:T(8,128)(2,1)S(1)} %collective-permute-done.12.refs_3_, ...), custom_call_target="tpu_custom_call" | custom-call | flops 805306368 | bytes 8296448 | tf_op jit(solution)/shard_map/pallas_call | solution.py:67
  179.5 2.6 collective-permute-done.38.refs_12_
  182.1 3.8 %shard_map.258 = bf16[4,1152,256]{2,1,0:T(8,128)(2,1)S(1)} custom-call(s32[1]{0:T(128)} %bitcast.where, bf16[128,1024]{1,0:T(8,128)(2,1)S(1)} %get-tuple-element.258.refs_3_.refs_0_, bf16[128,1024]{1,0:T(8,128)(2,1)S(1)} %copy-done.54, bf16[128,1024]{1,0:T(8,128)(2,1)S(1)} %copy-done.58, bf16[128,1024]{1,0:T(8,128)(2,1)} %collective-permute-done.21.refs_4_.refs_3_, ...), custom_call_target="tpu_custom_call" | custom-call | flops 1610612736 | bytes 9961472 | tf_op jit(solution)/shard_map/pallas_call | solution.py:424
  190.1 6.5 %collective-permute-done.35.refs_6_.refs_10_ = bf16[128,1024]{1,0:T(8,128)(2,1)S(1)} collective-permute-done((bf16[128,1024]{1,0:T(8,128)(2,1)S(1)}, bf16[128,1024]{1,0:T(8,128)(2,1)S(1)}, u32[]{:S(2)}, u32[]{:S(2)}) %collective-permute-start.35) | collective-permute-done | bytes 262176 | tf_op jit(solution)/shard_map/ppermute | solution.py:41
  198.2 3.9 %shard_map.255 = bf16[4,256,256]{2,1,0:T(8,128)(2,1)S(1)} custom-call(bf16[256,512]{1,0:T(8,128)(2,1)} %get-tuple-element.320.refs_0_, bf16[256,512]{1,0:T(8,128)(2,1)} %get-tuple-element.321.refs_1_, bf16[256,512]{1,0:T(8,128)(2,1)} %get-tuple-element.322.refs_2_, bf16[256,512]{1,0:T(8,128)(2,1)} %get-tuple-element.323.refs_3_, ...), custom_call_target="tpu_custom_call" | custom-call | flops 536870912 | bytes 3670016 | tf_op jit(solution)/shard_map/pallas_call | solution.py:67
  207.7 6.6 %shard_map.254 = (bf16[256,1024]{1,0:T(8,128)(2,1)}, bf16[256,1024]{1,0:T(8,128)(2,1)S(1)}, f32[1,1280]{1,0:T(1,128)S(1)}) custom-call(f32[1,128]{1,0:T(1,128)S(1)} %bitcast.48, f32[1,128]{1,0:T(1,128)S(1)} %bitcast.55, bf16[4,768,256]{2,1,0:T(8,128)(2,1)S(1)} %bitcast.40, bf16[4,768,256]{2,1,0:T(8,128)(2,1)S(1)} %collective-permute-done.12.refs_3_, ...), custom_call_target="tpu_custom_call" | custom-call | flops 805306368 | bytes 7772160 | tf_op jit(solution)/shard_map/pallas_call | solution.py:67
  214.3 3.6 %shard_map.256 = bf16[4,256,256]{2,1,0:T(8,128)(2,1)S(1)} custom-call(bf16[256,512]{1,0:T(8,128)(2,1)} %get-tuple-element.320.refs_0_, bf16[256,512]{1,0:T(8,128)(2,1)} %get-tuple-element.321.refs_1_, bf16[256,512]{1,0:T(8,128)(2,1)} %get-tuple-element.322.refs_2_, bf16[256,512]{1,0:T(8,128)(2,1)} %get-tuple-element.323.refs_3_, ...), custom_call_target="tpu_custom_call" | custom-call | flops 536870912 | bytes 4194304 | tf_op jit(solution)/shard_map/pallas_call | solution.py:67
  217.9 1.8 collective-permute-start.42
  219.7 6.7 %shard_map.257 = (bf16[256,1024]{1,0:T(8,128)(2,1)}, bf16[256,1024]{1,0:T(8,128)(2,1)S(1)}, f32[1,1280]{1,0:T(1,128)S(1)}) custom-call(f32[1,128]{1,0:T(1,128)S(1)} %bitcast.49, f32[1,128]{1,0:T(1,128)S(1)} %bitcast.56, bf16[4,768,256]{2,1,0:T(8,128)(2,1)S(1)} %bitcast.41, bf16[4,768,256]{2,1,0:T(8,128)(2,1)S(1)} %collective-permute-done.12.refs_3_, ...), custom_call_target="tpu_custom_call" | custom-call | flops 805306368 | bytes 7772160 | tf_op jit(solution)/shard_map/pallas_call | solution.py:67
  227.2 13.0 %collective-permute-done.40.refs_2_ = bf16[256,1024]{1,0:T(8,128)(2,1)S(1)} collective-permute-done((bf16[256,1024]{1,0:T(8,128)(2,1)S(1)}, bf16[256,1024]{1,0:T(8,128)(2,1)S(1)}, u32[]{:S(2)}, u32[]{:S(2)}) %collective-permute-start.40) | collective-permute-done | bytes 524320 | tf_op jit(solution)/shard_map/ppermute | solution.py:41
  241.8 6.8 %shard_map.259 = (bf16[256,1024]{1,0:T(8,128)(2,1)}, bf16[256,1024]{1,0:T(8,128)(2,1)S(1)}, f32[1,1280]{1,0:T(1,128)S(1)}) custom-call(f32[1,128]{1,0:T(1,128)S(1)} %bitcast.50, f32[1,128]{1,0:T(1,128)S(1)} %bitcast.57, bf16[4,768,256]{2,1,0:T(8,128)(2,1)S(1)} %bitcast.42, bf16[4,768,256]{2,1,0:T(8,128)(2,1)S(1)} %collective-permute-done.12.refs_3_, ...), custom_call_target="tpu_custom_call" | custom-call | flops 805306368 | bytes 7772160 | tf_op jit(solution)/shard_map/pallas_call | solution.py:67
  251.5 2.3 shard_map.260
  253.8 4.0 %collective-permute-done.44.refs_2_ = bf16[256,1024]{1,0:T(8,128)(2,1)S(1)} collective-permute-done((bf16[256,1024]{1,0:T(8,128)(2,1)S(1)}, bf16[256,1024]{1,0:T(8,128)(2,1)S(1)}, u32[]{:S(2)}, u32[]{:S(2)}) %collective-permute-start.44) | collective-permute-done | bytes 524320 | tf_op jit(solution)/shard_map/ppermute | solution.py:41
  259.4 1.6 collective-permute-start.47
  261.0 1.7 collective-permute-start.46
  262.7 3.7 %collective-permute-done.48.refs_12_ = bf16[256,256]{1,0:T(8,128)(2,1)S(1)} collective-permute-done((bf16[256,256]{1,0:T(8,128)(2,1)S(1)}, bf16[256,256]{1,0:T(8,128)(2,1)S(1)}, u32[]{:S(2)}, u32[]{:S(2)}) %collective-permute-start.48) | collective-permute-done | bytes 131104 | tf_op jit(solution)/shard_map/ppermute | solution.py:136
  266.4 1.6 collective-permute-done.47.refs_11_
  268.2 3.6 %shard_map.261 = bf16[4,768,256]{2,1,0:T(8,128)(2,1)} custom-call(s32[1]{0:T(128)} %bitcast.where, bf16[256,1024]{1,0:T(8,128)(2,1)S(1)} %copy-done.11, bf16[256,1024]{1,0:T(8,128)(2,1)S(1)} %copy-done.12, bf16[256,1024]{1,0:T(8,128)(2,1)S(1)} %copy-done.13, bf16[256,1024]{1,0:T(8,128)(2,1)S(1)} %copy-done.14, bf16[256,1024]{1,0:T(8,128)(2,1)S(1)} %copy-done.40, ...), custom_call_target="tpu_custom_call" | custom-call | flops 1073741824 | bytes 7340032 | tf_op jit(solution)/shard_map/pallas_call | solution.py:424
  274.1 2.7 collective-permute-done.50
  278.2 2.4 collective-permute-done.51
  284.1 1.7 collective-permute-start.55
  285.8 2.6 collective-permute-done.55
  288.5 2.1 collective-permute-start.56
  290.6 3.8 %collective-permute-done.56 = f32[1,2304]{1,0:T(1,128)S(1)} collective-permute-done((f32[1,2304]{1,0:T(1,128)S(1)}, f32[1,2304]{1,0:T(1,128)S(1)}, u32[]{:S(2)}, u32[]{:S(2)}) %collective-permute-start.56) | collective-permute-done | bytes 9248 | tf_op jit(solution)/shard_map/ppermute | solution.py:764
  294.4 3.6 %collective-permute-done.54.refs_3_ = bf16[1152,256]{1,0:T(8,128)(2,1)} collective-permute-done((bf16[1152,256]{1,0:T(8,128)(2,1)S(1)}, bf16[1152,256]{1,0:T(8,128)(2,1)}, u32[]{:S(2)}, u32[]{:S(2)}) %collective-permute-start.54) | collective-permute-done | bytes 589856 | tf_op jit(solution)/shard_map/ppermute | solution.py:114
  297.9 9.2 %collective-permute-done.53.refs_2_ = bf16[1152,256]{1,0:T(8,128)(2,1)S(1)} collective-permute-done((bf16[1152,256]{1,0:T(8,128)(2,1)S(1)}, bf16[1152,256]{1,0:T(8,128)(2,1)S(1)}, u32[]{:S(2)}, u32[]{:S(2)}) %collective-permute-start.53) | collective-permute-done | bytes 589856 | tf_op jit(solution)/shard_map/ppermute | solution.py:41
  309.0 2.1 collective-permute-start.59
  311.7 1.8 collective-permute-start.57
  319.7 6.2 %shard_map.262 = (f32[256,3072]{1,0:T(8,128)}, f32[256,3072]{1,0:T(8,128)}, f32[768,1024]{1,0:T(8,128)}) custom-call(s32[2]{0:T(128)S(1)} %pad_add_fusion.1.w.where, bf16[1152,256]{1,0:T(8,128)(2,1)S(1)} %copy-done.71, bf16[1152,256]{1,0:T(8,128)(2,1)} %collective-permute-done.52.refs_1_, bf16[1152,256]{1,0:T(8,128)(2,1)S(1)} %copy-done.73, ...), custom_call_target="tpu_custom_call" | custom-call | bytes 14155784 | tf_op jit(solution)/shard_map/pallas_call | solution.py:67
  325.9 3.8 %collective-permute-done.58.refs_2_ = bf16[768,256]{1,0:T(8,128)(2,1)S(1)} collective-permute-done((bf16[768,256]{1,0:T(8,128)(2,1)}, bf16[768,256]{1,0:T(8,128)(2,1)S(1)}, u32[]{:S(2)}, u32[]{:S(2)}) %collective-permute-start.58) | collective-permute-done | bytes 393248 | tf_op jit(solution)/shard_map/ppermute | solution.py:41
  333.1 3.7 %shard_map.265 = (f32[256,2048]{1,0:T(8,128)}, f32[256,1024]{1,0:T(8,128)}, f32[256,1024]{1,0:T(8,128)}, f32[512,1024]{1,0:T(8,128)}) custom-call(s32[2]{0:T(128)S(1)} %pad_add_fusion.1.w.where, bf16[768,256]{1,0:T(8,128)(2,1)S(1)} %copy-done.86, bf16[768,256]{1,0:T(8,128)(2,1)S(1)} %collective-permute-done.57.refs_1_, ...), custom_call_target="tpu_custom_call" | custom-call | bytes 9437192 | tf_op jit(solution)/shard_map/pallas_call | solution.py:67
  (325 shorter events, 73.9 us)
Async XLA Ops:
  7.2 45.8 %all-gather.5.cloned.1.call-start = ((), (), s32[]{:S(2)}) async-start(), calls=%async_computation.4 | async-start | bytes 1966080 | tf_op jit(solution)/shard_map/all_gather | solution.py:632
  9.7 102.8 %all-gather.7.cloned.1.call-start = ((), (), s32[]{:S(2)}) async-start(), calls=%async_computation.5 | async-start | bytes 2949120 | tf_op jit(solution)/shard_map/all_gather | solution.py:646
  9.9 17.1 %collective-permute-start.3 = (bf16[144,1024]{1,0:T(8,128)(2,1)S(1)}, bf16[144,1024]{1,0:T(8,128)(2,1)S(1)}, u32[]{:S(2)}, u32[]{:S(2)}) collective-permute-start(bf16[144,1024]{1,0:T(8,128)(2,1)S(1)} %fusion.1.refs_3_.refs_9_), channel_id=1, source_target_pairs={{0,4},{4,0},{1,5},{5,1},{2,6},{6,2},{3,7},{7,3},{8,12},{12,8},{9,1... | collective-permute-start | bytes 884744 | tf_op jit(solution)/shard_map/ppermute | solution.py:41
  12.9 14.1 %collective-permute-start.1 = (bf16[144,1024]{1,0:T(8,128)(2,1)S(1)}, bf16[144,1024]{1,0:T(8,128)(2,1)S(1)}, u32[]{:S(2)}, u32[]{:S(2)}) collective-permute-start(bf16[144,1024]{1,0:T(8,128)(2,1)S(1)} %fusion.1.refs_3_.refs_9_), channel_id=1, source_target_pairs={{0,2},{2,0},{1,3},{3,1},{4,6},{6,4},{5,7},{7,5},{8,10},{10,8},{9,1... | collective-permute-start | bytes 884744 | tf_op jit(solution)/shard_map/ppermute | solution.py:41
  14.4 11.1 %collective-permute-start.2 = (bf16[128,1024]{1,0:T(8,128)(2,1)S(1)}, bf16[128,1024]{1,0:T(8,128)(2,1)S(1)}, u32[]{:S(2)}, u32[]{:S(2)}) collective-permute-start(bf16[128,1024]{1,0:T(8,128)(2,1)S(1)} %get-tuple-element.412.refs_2_.refs_8_), channel_id=1, source_target_pairs={{0,4},{4,0},{1,5},{5,1},{2,6},{6,2},{3,7},{7,3},{8,12},{12,8},{9,1... | collective-permute-start | bytes 786440 | tf_op jit(solution)/shard_map/ppermute | solution.py:41
  14.9 12.1 %collective-permute-start = (bf16[128,1024]{1,0:T(8,128)(2,1)S(1)}, bf16[128,1024]{1,0:T(8,128)(2,1)S(1)}, u32[]{:S(2)}, u32[]{:S(2)}) collective-permute-start(bf16[128,1024]{1,0:T(8,128)(2,1)S(1)} %get-tuple-element.412.refs_2_.refs_8_), channel_id=1, source_target_pairs={{0,2},{2,0},{1,3},{3,1},{4,6},{6,4},{5,7},{7,5},{8,10},{10,8},{9,1... | collective-permute-start | bytes 786440 | tf_op jit(solution)/shard_map/ppermute | solution.py:41
  27.1 9.3 %collective-permute-start.7 = (bf16[128,1024]{1,0:T(8,128)(2,1)S(1)}, bf16[128,1024]{1,0:T(8,128)(2,1)S(1)}, u32[]{:S(2)}, u32[]{:S(2)}) collective-permute-start(bf16[128,1024]{1,0:T(8,128)(2,1)S(1)} %get-tuple-element.262.refs_6_.refs_5_), channel_id=1, source_target_pairs={{0,2},{2,0},{1,3},{3,1},{4,6},{6,4},{5,7},{7,5},{8,10},{10,8},{9,1... | collective-permute-start | bytes 786440 | tf_op jit(solution)/shard_map/ppermute | solution.py:41
  28.7 9.2 %collective-permute-start.8 = (bf16[128,1024]{1,0:T(8,128)(2,1)S(1)}, bf16[128,1024]{1,0:T(8,128)(2,1)S(1)}, u32[]{:S(2)}, u32[]{:S(2)}) collective-permute-start(bf16[128,1024]{1,0:T(8,128)(2,1)S(1)} %get-tuple-element.261.refs_5_.refs_4_), channel_id=1, source_target_pairs={{0,4},{4,0},{1,5},{5,1},{2,6},{6,2},{3,7},{7,3},{8,12},{12,8},{9,1... | collective-permute-start | bytes 786440 | tf_op jit(solution)/shard_map/ppermute | solution.py:41
  29.2 12.8 %collective-permute-start.4 = (bf16[128,1024]{1,0:T(8,128)(2,1)S(1)}, bf16[128,1024]{1,0:T(8,128)(2,1)S(1)}, u32[]{:S(2)}, u32[]{:S(2)}) collective-permute-start(bf16[128,1024]{1,0:T(8,128)(2,1)S(1)} %collective-permute-done.2.refs_6_.refs_8_), channel_id=1, source_target_pairs={{0,2},{2,0},{1,3},{3,1},{4,6},{6,4},{5,7},{7,5},{8,10},{10,8},{9,1... | collective-permute-start | bytes 786440 | tf_op jit(solution)/shard_map/ppermute | solution.py:41
  29.6 16.5 %collective-permute-start.5 = (bf16[144,1024]{1,0:T(8,128)(2,1)S(1)}, bf16[144,1024]{1,0:T(8,128)(2,1)S(1)}, u32[]{:S(2)}, u32[]{:S(2)}) collective-permute-start(bf16[144,1024]{1,0:T(8,128)(2,1)S(1)} %collective-permute-done.1.refs_5_.refs_9_), channel_id=1, source_target_pairs={{0,4},{4,0},{1,5},{5,1},{2,6},{6,2},{3,7},{7,3},{8,12},{12,8},{9,1... | collective-permute-start | bytes 884744 | tf_op jit(solution)/shard_map/ppermute | solution.py:41
  31.2 20.1 %collective-permute-start.9 = (bf16[128,1024]{1,0:T(8,128)(2,1)S(1)}, bf16[128,1024]{1,0:T(8,128)(2,1)S(1)}, u32[]{:S(2)}, u32[]{:S(2)}) collective-permute-start(bf16[128,1024]{1,0:T(8,128)(2,1)S(1)} %get-tuple-element.262.refs_6_.refs_5_), channel_id=1, source_target_pairs={{0,4},{4,0},{1,5},{5,1},{2,6},{6,2},{3,7},{7,3},{8,12},{12,8},{9,1... | collective-permute-start | bytes 786440 | tf_op jit(solution)/shard_map/ppermute | solution.py:41
  36.4 14.9 %collective-permute-start.6 = (bf16[128,1024]{1,0:T(8,128)(2,1)S(1)}, bf16[128,1024]{1,0:T(8,128)(2,1)}, u32[]{:S(2)}, u32[]{:S(2)}) collective-permute-start(bf16[128,1024]{1,0:T(8,128)(2,1)S(1)} %get-tuple-element.261.refs_5_.refs_4_), channel_id=1, source_target_pairs={{0,2},{2,0},{1,3},{3,1},{4,6},{6,4},{5,7},{7,5},{8,10},{10,8},{9,1... | collective-permute-start | bytes 786440 | tf_op jit(solution)/shard_map/ppermute | solution.py:41
  37.9 13.4 %collective-permute-start.10 = (bf16[128,1024]{1,0:T(8,128)(2,1)S(1)}, bf16[128,1024]{1,0:T(8,128)(2,1)}, u32[]{:S(2)}, u32[]{:S(2)}) collective-permute-start(bf16[128,1024]{1,0:T(8,128)(2,1)S(1)} %collective-permute-done.8.refs_5_.refs_8_), channel_id=1, source_target_pairs={{0,2},{2,0},{1,3},{3,1},{4,6},{6,4},{5,7},{7,5},{8,10},{10,8},{9,1... | collective-permute-start | bytes 786440 | tf_op jit(solution)/shard_map/ppermute | solution.py:41
  42.7 10.3 %collective-permute-start.11 = (bf16[128,1024]{1,0:T(8,128)(2,1)S(1)}, bf16[128,1024]{1,0:T(8,128)(2,1)}, u32[]{:S(2)}, u32[]{:S(2)}) collective-permute-start(bf16[128,1024]{1,0:T(8,128)(2,1)S(1)} %collective-permute-done.7.refs_6_.refs_7_), channel_id=1, source_target_pairs={{0,4},{4,0},{1,5},{5,1},{2,6},{6,2},{3,7},{7,3},{8,12},{12,8},{9,1... | collective-permute-start | bytes 786440 | tf_op jit(solution)/shard_map/ppermute | solution.py:41
  53.0 218.8 %reduce-scatter.3.cloned.1.call-start = ((), (), s32[]{:S(2)}) async-start(), calls=%async_computation.2 | async-start | bytes 2949120 | tf_op jit(solution)/shard_map/reduce_scatter | solution.py:735
  53.3 12.7 %collective-permute-start.12 = (bf16[4,768,256]{2,1,0:T(8,128)(2,1)}, bf16[4,768,256]{2,1,0:T(8,128)(2,1)S(1)}, u32[]{:S(2)}, u32[]{:S(2)}) collective-permute-start(bf16[4,768,256]{2,1,0:T(8,128)(2,1)} %bitcast.34), channel_id=1, source_target_pairs={{0,1},{1,0},{2,3},{3,2},{4,5},{5,4},{6,7},{7,6},{8,9},{9,8},{10,11... | collective-permute-start | bytes 4718600 | tf_op jit(solution)/shard_map/ppermute | solution.py:41
  54.6 7.3 %collective-permute-start.15 = (bf16[256,256]{1,0:T(8,128)(2,1)S(1)}, bf16[256,256]{1,0:T(8,128)(2,1)S(1)}, u32[]{:S(2)}, u32[]{:S(2)}) collective-permute-start(bf16[256,256]{1,0:T(8,128)(2,1)S(1)} %get-tuple-element.401), channel_id=1, source_target_pairs={{0,6},{2,4},{4,2},{6,0},{1,7},{3,5},{5,3},{7,1},{8,14},{10,12},{12... | collective-permute-start | bytes 393224 | tf_op jit(solution)/shard_map/ppermute | solution.py:136
  55.7 8.3 %collective-permute-start.14 = (bf16[256,256]{1,0:T(8,128)(2,1)S(1)}, bf16[256,256]{1,0:T(8,128)(2,1)S(1)}, u32[]{:S(2)}, u32[]{:S(2)}) collective-permute-start(bf16[256,256]{1,0:T(8,128)(2,1)S(1)} %get-tuple-element.402), channel_id=1, source_target_pairs={{0,4},{4,0},{1,5},{5,1},{2,6},{6,2},{3,7},{7,3},{8,12},{12,8},{9,1... | collective-permute-start | bytes 393224 | tf_op jit(solution)/shard_map/ppermute | solution.py:41
  56.7 7.3 %collective-permute-start.13 = (bf16[256,256]{1,0:T(8,128)(2,1)S(1)}, bf16[256,256]{1,0:T(8,128)(2,1)S(1)}, u32[]{:S(2)}, u32[]{:S(2)}) collective-permute-start(bf16[256,256]{1,0:T(8,128)(2,1)S(1)} %get-tuple-element.403), channel_id=1, source_target_pairs={{0,2},{2,0},{1,3},{3,1},{4,6},{6,4},{5,7},{7,5},{8,10},{10,8},{9,1... | collective-permute-start | bytes 393224 | tf_op jit(solution)/shard_map/ppermute | solution.py:41
  70.5 15.7 %collective-permute-start.19 = (bf16[256,1024]{1,0:T(8,128)(2,1)S(1)}, bf16[256,1024]{1,0:T(8,128)(2,1)S(1)}, u32[]{:S(2)}, u32[]{:S(2)}) collective-permute-start(bf16[256,1024]{1,0:T(8,128)(2,1)S(1)} %get-tuple-element.255), channel_id=1, source_target_pairs={{0,6},{2,4},{4,2},{6,0},{1,7},{3,5},{5,3},{7,1},{8,14},{10,12},{12... | collective-permute-start | bytes 1572872 | tf_op jit(solution)/shard_map/ppermute | solution.py:123
  78.7 17.2 %collective-permute-start.17 = (bf16[256,1024]{1,0:T(8,128)(2,1)S(1)}, bf16[256,1024]{1,0:T(8,128)(2,1)S(1)}, u32[]{:S(2)}, u32[]{:S(2)}) collective-permute-start(bf16[256,1024]{1,0:T(8,128)(2,1)S(1)} %get-tuple-element.250), channel_id=1, source_target_pairs={{0,2},{2,0},{1,3},{3,1},{4,6},{6,4},{5,7},{7,5},{8,10},{10,8},{9,1... | collective-permute-start | bytes 1572872 | tf_op jit(solution)/shard_map/ppermute | solution.py:41
  79.8 16.8 %collective-permute-start.18 = (bf16[256,1024]{1,0:T(8,128)(2,1)S(1)}, bf16[256,1024]{1,0:T(8,128)(2,1)S(1)}, u32[]{:S(2)}, u32[]{:S(2)}) collective-permute-start(bf16[256,1024]{1,0:T(8,128)(2,1)S(1)} %get-tuple-element.251), channel_id=1, source_target_pairs={{0,4},{4,0},{1,5},{5,1},{2,6},{6,2},{3,7},{7,3},{8,12},{12,8},{9,1... | collective-permute-start | bytes 1572872 | tf_op jit(solution)/shard_map/ppermute | solution.py:41
  97.9 9.2 %collective-permute-start.22 = (bf16[128,1024]{1,0:T(8,128)(2,1)S(1)}, bf16[128,1024]{1,0:T(8,128)(2,1)S(1)}, u32[]{:S(2)}, u32[]{:S(2)}) collective-permute-start(bf16[128,1024]{1,0:T(8,128)(2,1)S(1)} %get-tuple-element.258.refs_3_.refs_0_), channel_id=1, source_target_pairs={{0,4},{4,0},{1,5},{5,1},{2,6},{6,2},{3,7},{7,3},{8,12},{12,8},{9,1... | collective-permute-start | bytes 786440 | tf_op jit(solution)/shard_map/ppermute | solution.py:41
  98.7 9.2 %collective-permute-start.20 = (bf16[128,1024]{1,0:T(8,128)(2,1)S(1)}, bf16[128,1024]{1,0:T(8,128)(2,1)S(1)}, u32[]{:S(2)}, u32[]{:S(2)}) collective-permute-start(bf16[128,1024]{1,0:T(8,128)(2,1)S(1)} %get-tuple-element.258.refs_3_.refs_0_), channel_id=1, source_target_pairs={{0,2},{2,0},{1,3},{3,1},{4,6},{6,4},{5,7},{7,5},{8,10},{10,8},{9,1... | collective-permute-start | bytes 786440 | tf_op jit(solution)/shard_map/ppermute | solution.py:41
  99.6 12.2 %collective-permute-start.23 = (bf16[128,1024]{1,0:T(8,128)(2,1)S(1)}, bf16[128,1024]{1,0:T(8,128)(2,1)S(1)}, u32[]{:S(2)}, u32[]{:S(2)}) collective-permute-start(bf16[128,1024]{1,0:T(8,128)(2,1)S(1)} %get-tuple-element.259.refs_4_.refs_1_), channel_id=1, source_target_pairs={{0,4},{4,0},{1,5},{5,1},{2,6},{6,2},{3,7},{7,3},{8,12},{12,8},{9,1... | collective-permute-start | bytes 786440 | tf_op jit(solution)/shard_map/ppermute | solution.py:41
  100.6 11.9 %collective-permute-start.21 = (bf16[128,1024]{1,0:T(8,128)(2,1)S(1)}, bf16[128,1024]{1,0:T(8,128)(2,1)}, u32[]{:S(2)}, u32[]{:S(2)}) collective-permute-start(bf16[128,1024]{1,0:T(8,128)(2,1)S(1)} %get-tuple-element.259.refs_4_.refs_1_), channel_id=1, source_target_pairs={{0,2},{2,0},{1,3},{3,1},{4,6},{6,4},{5,7},{7,5},{8,10},{10,8},{9,1... | collective-permute-start | bytes 786440 | tf_op jit(solution)/shard_map/ppermute | solution.py:41
  112.5 9.5 %collective-permute-start.24 = (bf16[4,1152,256]{2,1,0:T(8,128)(2,1)}, bf16[4,1152,256]{2,1,0:T(8,128)(2,1)S(1)}, u32[]{:S(2)}, u32[]{:S(2)}) collective-permute-start(bf16[4,1152,256]{2,1,0:T(8,128)(2,1)} %bitcast.62), channel_id=1, source_target_pairs={{0,1},{1,0},{2,3},{3,2},{4,5},{5,4},{6,7},{7,6},{8,9},{9,8},{10,11... | collective-permute-start | bytes 7077896 | tf_op jit(solution)/shard_map/ppermute | solution.py:41
  112.5 8.9 %collective-permute-start.27 = (bf16[128,1024]{1,0:T(8,128)(2,1)}, bf16[128,1024]{1,0:T(8,128)(2,1)S(1)}, u32[]{:S(2)}, u32[]{:S(2)}) collective-permute-start(bf16[128,1024]{1,0:T(8,128)(2,1)} %copy-done.55), channel_id=1, source_target_pairs={{0,2},{2,0},{1,3},{3,1},{4,6},{6,4},{5,7},{7,5},{8,10},{10,8},{9,1... | collective-permute-start | bytes 786440 | tf_op jit(solution)/shard_map/ppermute | solution.py:41
  113.5 8.6 %collective-permute-start.28 = (bf16[128,1024]{1,0:T(8,128)(2,1)}, bf16[128,1024]{1,0:T(8,128)(2,1)S(1)}, u32[]{:S(2)}, u32[]{:S(2)}) collective-permute-start(bf16[128,1024]{1,0:T(8,128)(2,1)} %collective-permute-done.21.refs_4_.refs_3_), channel_id=1, source_target_pairs={{0,4},{4,0},{1,5},{5,1},{2,6},{6,2},{3,7},{7,3},{8,12},{12,8},{9,1... | collective-permute-start | bytes 786440 | tf_op jit(solution)/shard_map/ppermute | solution.py:41
  128.0 15.4 %collective-permute-start.29 = (bf16[256,1024]{1,0:T(8,128)(2,1)S(1)}, bf16[256,1024]{1,0:T(8,128)(2,1)S(1)}, u32[]{:S(2)}, u32[]{:S(2)}) collective-permute-start(bf16[256,1024]{1,0:T(8,128)(2,1)S(1)} %get-tuple-element.282), channel_id=1, source_target_pairs={{0,6},{2,4},{4,2},{6,0},{1,7},{3,5},{5,3},{7,1},{8,14},{10,12},{12... | collective-permute-start | bytes 1572872 | tf_op jit(solution)/shard_map/ppermute | solution.py:123
  146.3 14.3 %collective-permute-start.26 = (bf16[256,1024]{1,0:T(8,128)(2,1)S(1)}, bf16[256,1024]{1,0:T(8,128)(2,1)S(1)}, u32[]{:S(2)}, u32[]{:S(2)}) collective-permute-start(bf16[256,1024]{1,0:T(8,128)(2,1)S(1)} %get-tuple-element.273), channel_id=1, source_target_pairs={{0,4},{4,0},{1,5},{5,1},{2,6},{6,2},{3,7},{7,3},{8,12},{12,8},{9,1... | collective-permute-start | bytes 1572872 | tf_op jit(solution)/shard_map/ppermute | solution.py:41
  147.2 14.0 %collective-permute-start.25 = (bf16[256,1024]{1,0:T(8,128)(2,1)S(1)}, bf16[256,1024]{1,0:T(8,128)(2,1)S(1)}, u32[]{:S(2)}, u32[]{:S(2)}) collective-permute-start(bf16[256,1024]{1,0:T(8,128)(2,1)S(1)} %get-tuple-element.268), channel_id=1, source_target_pairs={{0,2},{2,0},{1,3},{3,1},{4,6},{6,4},{5,7},{7,5},{8,10},{10,8},{9,1... | collective-permute-start | bytes 1572872 | tf_op jit(solution)/shard_map/ppermute | solution.py:41
  163.0 15.6 %collective-permute-start.34 = (bf16[128,1024]{1,0:T(8,128)(2,1)S(1)}, bf16[128,1024]{1,0:T(8,128)(2,1)S(1)}, u32[]{:S(2)}, u32[]{:S(2)}) collective-permute-start(bf16[128,1024]{1,0:T(8,128)(2,1)S(1)} %get-tuple-element.304.refs_7_.refs_5_), channel_id=1, source_target_pairs={{0,4},{4,0},{1,5},{5,1},{2,6},{6,2},{3,7},{7,3},{8,12},{12,8},{9,1... | collective-permute-start | bytes 786440 | tf_op jit(solution)/shard_map/ppermute | solution.py:41
  164.1 14.4 %collective-permute-start.32 = (bf16[128,1024]{1,0:T(8,128)(2,1)S(1)}, bf16[128,1024]{1,0:T(8,128)(2,1)S(1)}, u32[]{:S(2)}, u32[]{:S(2)}) collective-permute-start(bf16[128,1024]{1,0:T(8,128)(2,1)S(1)} %get-tuple-element.304.refs_7_.refs_5_), channel_id=1, source_target_pairs={{0,2},{2,0},{1,3},{3,1},{4,6},{6,4},{5,7},{7,5},{8,10},{10,8},{9,1... | collective-permute-start | bytes 786440 | tf_op jit(solution)/shard_map/ppermute | solution.py:41
  164.9 13.7 %collective-permute-start.33 = (bf16[128,1024]{1,0:T(8,128)(2,1)S(1)}, bf16[128,1024]{1,0:T(8,128)(2,1)S(1)}, u32[]{:S(2)}, u32[]{:S(2)}) collective-permute-start(bf16[128,1024]{1,0:T(8,128)(2,1)S(1)} %get-tuple-element.303.refs_6_.refs_4_), channel_id=1, source_target_pairs={{0,4},{4,0},{1,5},{5,1},{2,6},{6,2},{3,7},{7,3},{8,12},{12,8},{9,1... | collective-permute-start | bytes 786440 | tf_op jit(solution)/shard_map/ppermute | solution.py:41
  165.9 12.7 %collective-permute-start.31 = (bf16[128,1024]{1,0:T(8,128)(2,1)S(1)}, bf16[128,1024]{1,0:T(8,128)(2,1)S(1)}, u32[]{:S(2)}, u32[]{:S(2)}) collective-permute-start(bf16[128,1024]{1,0:T(8,128)(2,1)S(1)} %get-tuple-element.303.refs_6_.refs_4_), channel_id=1, source_target_pairs={{0,2},{2,0},{1,3},{3,1},{4,6},{6,4},{5,7},{7,5},{8,10},{10,8},{9,1... | collective-permute-start | bytes 786440 | tf_op jit(solution)/shard_map/ppermute | solution.py:41
  178.6 3.5 %collective-permute-start.38 = (bf16[4,768,256]{2,1,0:T(8,128)(2,1)S(1)}, bf16[4,768,256]{2,1,0:T(8,128)(2,1)S(1)}, u32[]{:S(2)}, u32[]{:S(2)}) collective-permute-start(bf16[4,768,256]{2,1,0:T(8,128)(2,1)S(1)} %shard_map.252), channel_id=1, source_target_pairs={{0,1},{1,0},{2,3},{3,2},{4,5},{5,4},{6,7},{7,6},{8,9},{9,8},{10,11... | collective-permute-start | bytes 4718600 | tf_op jit(solution)/shard_map/ppermute | solution.py:41
  187.3 120.6 %reduce-scatter.5.cloned.1.call-start = ((), (), s32[]{:S(2)}) async-start(), calls=%async_computation.3 | async-start | bytes 1966080 | tf_op jit(solution)/shard_map/reduce_scatter | solution.py:758
  188.3 8.3 %collective-permute-start.35 = (bf16[128,1024]{1,0:T(8,128)(2,1)S(1)}, bf16[128,1024]{1,0:T(8,128)(2,1)S(1)}, u32[]{:S(2)}, u32[]{:S(2)}) collective-permute-start(bf16[128,1024]{1,0:T(8,128)(2,1)S(1)} %copy-done.21), channel_id=1, source_target_pairs={{0,2},{2,0},{1,3},{3,1},{4,6},{6,4},{5,7},{7,5},{8,10},{10,8},{9,1... | collective-permute-start | bytes 786440 | tf_op jit(solution)/shard_map/ppermute | solution.py:41
  189.1 8.3 %collective-permute-start.36 = (bf16[128,1024]{1,0:T(8,128)(2,1)}, bf16[128,1024]{1,0:T(8,128)(2,1)S(1)}, u32[]{:S(2)}, u32[]{:S(2)}) collective-permute-start(bf16[128,1024]{1,0:T(8,128)(2,1)} %copy-done.23), channel_id=1, source_target_pairs={{0,4},{4,0},{1,5},{5,1},{2,6},{6,2},{3,7},{7,3},{8,12},{12,8},{9,1... | collective-permute-start | bytes 786440 | tf_op jit(solution)/shard_map/ppermute | solution.py:41
  202.1 12.2 %collective-permute-start.37 = (bf16[4,256,256]{2,1,0:T(8,128)(2,1)S(1)}, bf16[4,256,256]{2,1,0:T(8,128)(2,1)S(1)}, u32[]{:S(2)}, u32[]{:S(2)}) collective-permute-start(bf16[4,256,256]{2,1,0:T(8,128)(2,1)S(1)} %shard_map.255), channel_id=1, source_target_pairs={{0,1},{1,0},{2,3},{3,2},{4,5},{5,4},{6,7},{7,6},{8,9},{9,8},{10,11... | collective-permute-start | bytes 1572872 | tf_op jit(solution)/shard_map/ppermute | solution.py:41
  202.2 24.2 %collective-permute-start.39 = (bf16[256,1024]{1,0:T(8,128)(2,1)S(1)}, bf16[256,1024]{1,0:T(8,128)(2,1)S(1)}, u32[]{:S(2)}, u32[]{:S(2)}) collective-permute-start(bf16[256,1024]{1,0:T(8,128)(2,1)S(1)} %copy-done.96), channel_id=1, source_target_pairs={{0,2},{2,0},{1,3},{3,1},{4,6},{6,4},{5,7},{7,5},{8,10},{10,8},{9,1... | collective-permute-start | bytes 1572872 | tf_op jit(solution)/shard_map/ppermute | solution.py:41
  203.4 36.7 %collective-permute-start.40 = (bf16[256,1024]{1,0:T(8,128)(2,1)S(1)}, bf16[256,1024]{1,0:T(8,128)(2,1)S(1)}, u32[]{:S(2)}, u32[]{:S(2)}) collective-permute-start(bf16[256,1024]{1,0:T(8,128)(2,1)S(1)} %copy-done.95), channel_id=1, source_target_pairs={{0,4},{4,0},{1,5},{5,1},{2,6},{6,2},{3,7},{7,3},{8,12},{12,8},{9,1... | collective-permute-start | bytes 1572872 | tf_op jit(solution)/shard_map/ppermute | solution.py:41
  204.6 36.4 %collective-permute-start.41 = (bf16[256,1024]{1,0:T(8,128)(2,1)S(1)}, bf16[256,1024]{1,0:T(8,128)(2,1)S(1)}, u32[]{:S(2)}, u32[]{:S(2)}) collective-permute-start(bf16[256,1024]{1,0:T(8,128)(2,1)S(1)} %copy-done.94), channel_id=1, source_target_pairs={{0,6},{2,4},{4,2},{6,0},{1,7},{3,5},{5,3},{7,1},{8,14},{10,12},{12... | collective-permute-start | bytes 1572872 | tf_op jit(solution)/shard_map/ppermute | solution.py:123
  217.9 32.3 %collective-permute-start.42 = (bf16[256,1024]{1,0:T(8,128)(2,1)S(1)}, bf16[256,1024]{1,0:T(8,128)(2,1)S(1)}, u32[]{:S(2)}, u32[]{:S(2)}) collective-permute-start(bf16[256,1024]{1,0:T(8,128)(2,1)S(1)} %get-tuple-element.349), channel_id=1, source_target_pairs={{0,6},{2,4},{4,2},{6,0},{1,7},{3,5},{5,3},{7,1},{8,14},{10,12},{12... | collective-permute-start | bytes 1572872 | tf_op jit(solution)/shard_map/ppermute | solution.py:123
  248.6 9.2 %collective-permute-start.44 = (bf16[256,1024]{1,0:T(8,128)(2,1)S(1)}, bf16[256,1024]{1,0:T(8,128)(2,1)S(1)}, u32[]{:S(2)}, u32[]{:S(2)}) collective-permute-start(bf16[256,1024]{1,0:T(8,128)(2,1)S(1)} %get-tuple-element.356), channel_id=1, source_target_pairs={{0,4},{4,0},{1,5},{5,1},{2,6},{6,2},{3,7},{7,3},{8,12},{12,8},{9,1... | collective-permute-start | bytes 1572872 | tf_op jit(solution)/shard_map/ppermute | solution.py:41
  249.9 9.2 %collective-permute-start.43 = (bf16[256,1024]{1,0:T(8,128)(2,1)S(1)}, bf16[256,1024]{1,0:T(8,128)(2,1)S(1)}, u32[]{:S(2)}, u32[]{:S(2)}) collective-permute-start(bf16[256,1024]{1,0:T(8,128)(2,1)S(1)} %get-tuple-element.355), channel_id=1, source_target_pairs={{0,2},{2,0},{1,3},{3,1},{4,6},{6,4},{5,7},{7,5},{8,10},{10,8},{9,1... | collective-permute-start | bytes 1572872 | tf_op jit(solution)/shard_map/ppermute | solution.py:41
  259.1 9.1 %collective-permute-start.45 = (bf16[4,512,256]{2,1,0:T(8,128)(2,1)S(1)}, bf16[4,512,256]{2,1,0:T(8,128)(2,1)S(1)}, u32[]{:S(2)}, u32[]{:S(2)}) collective-permute-start(bf16[4,512,256]{2,1,0:T(8,128)(2,1)S(1)} %shard_map.260), channel_id=1, source_target_pairs={{0,1},{1,0},{2,3},{3,2},{4,5},{5,4},{6,7},{7,6},{8,9},{9,8},{10,11... | collective-permute-start | bytes 3145736 | tf_op jit(solution)/shard_map/ppermute | solution.py:41
  259.1 7.3 %collective-permute-start.48 = (bf16[256,256]{1,0:T(8,128)(2,1)S(1)}, bf16[256,256]{1,0:T(8,128)(2,1)S(1)}, u32[]{:S(2)}, u32[]{:S(2)}) collective-permute-start(bf16[256,256]{1,0:T(8,128)(2,1)S(1)} %get-tuple-element.405), channel_id=1, source_target_pairs={{0,6},{2,4},{4,2},{6,0},{1,7},{3,5},{5,3},{7,1},{8,14},{10,12},{12... | collective-permute-start | bytes 393224 | tf_op jit(solution)/shard_map/ppermute | solution.py:136
  259.4 8.6 %collective-permute-start.47 = (bf16[256,256]{1,0:T(8,128)(2,1)S(1)}, bf16[256,256]{1,0:T(8,128)(2,1)S(1)}, u32[]{:S(2)}, u32[]{:S(2)}) collective-permute-start(bf16[256,256]{1,0:T(8,128)(2,1)S(1)} %get-tuple-element.406), channel_id=1, source_target_pairs={{0,4},{4,0},{1,5},{5,1},{2,6},{6,2},{3,7},{7,3},{8,12},{12,8},{9,1... | collective-permute-start | bytes 393224 | tf_op jit(solution)/shard_map/ppermute | solution.py:41
  261.0 7.2 %collective-permute-start.46 = (bf16[256,256]{1,0:T(8,128)(2,1)S(1)}, bf16[256,256]{1,0:T(8,128)(2,1)S(1)}, u32[]{:S(2)}, u32[]{:S(2)}) collective-permute-start(bf16[256,256]{1,0:T(8,128)(2,1)S(1)} %get-tuple-element.407), channel_id=1, source_target_pairs={{0,2},{2,0},{1,3},{3,1},{4,6},{6,4},{5,7},{7,5},{8,10},{10,8},{9,1... | collective-permute-start | bytes 393224 | tf_op jit(solution)/shard_map/ppermute | solution.py:41
  273.1 3.7 %collective-permute-start.50 = (f32[1,2304]{1,0:T(1,128)S(1)}, f32[1,2304]{1,0:T(1,128)S(1)}, u32[]{:S(2)}, u32[]{:S(2)}) collective-permute-start(f32[1,2304]{1,0:T(1,128)S(1)} %add.82), channel_id=1, source_target_pairs={{0,2},{2,0},{1,3},{3,1},{4,6},{6,4},{5,7},{7,5},{8,10},{10,8},{9,1... | collective-permute-start | bytes 27656 | tf_op jit(solution)/shard_map/ppermute | solution.py:41
  276.8 3.7 %collective-permute-start.51 = (f32[1,2304]{1,0:T(1,128)S(1)}, f32[1,2304]{1,0:T(1,128)S(1)}, u32[]{:S(2)}, u32[]{:S(2)}) collective-permute-start(f32[1,2304]{1,0:T(1,128)S(1)} %add.83), channel_id=1, source_target_pairs={{0,4},{4,0},{1,5},{5,1},{2,6},{6,2},{3,7},{7,3},{8,12},{12,8},{9,1... | collective-permute-start | bytes 27656 | tf_op jit(solution)/shard_map/ppermute | solution.py:41
  280.6 17.3 %collective-permute-start.54 = (bf16[1152,256]{1,0:T(8,128)(2,1)S(1)}, bf16[1152,256]{1,0:T(8,128)(2,1)}, u32[]{:S(2)}, u32[]{:S(2)}) collective-permute-start(bf16[1152,256]{1,0:T(8,128)(2,1)S(1)} %copy-done.71), channel_id=1, source_target_pairs={{0,6},{2,4},{4,2},{6,0},{1,7},{3,5},{5,3},{7,1},{8,14},{10,12},{12... | collective-permute-start | bytes 1769480 | tf_op jit(solution)/shard_map/ppermute | solution.py:114
  281.6 25.5 %collective-permute-start.53 = (bf16[1152,256]{1,0:T(8,128)(2,1)S(1)}, bf16[1152,256]{1,0:T(8,128)(2,1)S(1)}, u32[]{:S(2)}, u32[]{:S(2)}) collective-permute-start(bf16[1152,256]{1,0:T(8,128)(2,1)S(1)} %copy-done.71), channel_id=1, source_target_pairs={{0,4},{4,0},{1,5},{5,1},{2,6},{6,2},{3,7},{7,3},{8,12},{12,8},{9,1... | collective-permute-start | bytes 1769480 | tf_op jit(solution)/shard_map/ppermute | solution.py:41
  283.1 24.8 %collective-permute-start.52 = (bf16[1152,256]{1,0:T(8,128)(2,1)S(1)}, bf16[1152,256]{1,0:T(8,128)(2,1)}, u32[]{:S(2)}, u32[]{:S(2)}) collective-permute-start(bf16[1152,256]{1,0:T(8,128)(2,1)S(1)} %copy-done.71), channel_id=1, source_target_pairs={{0,2},{2,0},{1,3},{3,1},{4,6},{6,4},{5,7},{7,5},{8,10},{10,8},{9,1... | collective-permute-start | bytes 1769480 | tf_op jit(solution)/shard_map/ppermute | solution.py:41
  284.1 4.3 %collective-permute-start.55 = (f32[1,2304]{1,0:T(1,128)S(1)}, f32[1,2304]{1,0:T(1,128)S(1)}, u32[]{:S(2)}, u32[]{:S(2)}) collective-permute-start(f32[1,2304]{1,0:T(1,128)S(1)} %add.84), channel_id=1, source_target_pairs={{0,8},{8,0},{16,24},{24,16},{1,9},{9,1},{17,25},{25,17},{2,10},{10... | collective-permute-start | bytes 27656 | tf_op jit(solution)/shard_map/ppermute | solution.py:764
  288.5 5.9 %collective-permute-start.56 = (f32[1,2304]{1,0:T(1,128)S(1)}, f32[1,2304]{1,0:T(1,128)S(1)}, u32[]{:S(2)}, u32[]{:S(2)}) collective-permute-start(f32[1,2304]{1,0:T(1,128)S(1)} %add.85), channel_id=1, source_target_pairs={{0,16},{8,24},{16,0},{24,8},{1,17},{9,25},{17,1},{25,9},{2,18},{10... | collective-permute-start | bytes 27656 | tf_op jit(solution)/shard_map/ppermute | solution.py:764
  308.0 3.7 %collective-permute-start.61 = (bf16[1152,256]{1,0:T(8,128)(2,1)}, bf16[1152,256]{1,0:T(8,128)(2,1)S(1)}, u32[]{:S(2)}, u32[]{:S(2)}) collective-permute-start(bf16[1152,256]{1,0:T(8,128)(2,1)} %collective-permute-done.52.refs_1_), channel_id=1, source_target_pairs={{0,1},{1,0},{2,3},{3,2},{4,5},{5,4},{6,7},{7,6},{8,9},{9,8},{10,11... | collective-permute-start | bytes 1769480 | tf_op jit(solution)/shard_map/ppermute | solution.py:41
  308.5 11.1 %collective-permute-start.62 = (bf16[1152,256]{1,0:T(8,128)(2,1)}, bf16[1152,256]{1,0:T(8,128)(2,1)S(1)}, u32[]{:S(2)}, u32[]{:S(2)}) collective-permute-start(bf16[1152,256]{1,0:T(8,128)(2,1)} %copy-done.72), channel_id=1, source_target_pairs={{0,1},{1,0},{2,3},{3,2},{4,5},{5,4},{6,7},{7,6},{8,9},{9,8},{10,11... | collective-permute-start | bytes 1769480 | tf_op jit(solution)/shard_map/ppermute | solution.py:41
  308.6 11.1 %collective-permute-start.63 = (bf16[1152,256]{1,0:T(8,128)(2,1)}, bf16[1152,256]{1,0:T(8,128)(2,1)S(1)}, u32[]{:S(2)}, u32[]{:S(2)}) collective-permute-start(bf16[1152,256]{1,0:T(8,128)(2,1)} %collective-permute-done.54.refs_3_), channel_id=1, source_target_pairs={{0,1},{1,0},{2,3},{3,2},{4,5},{5,4},{6,7},{7,6},{8,9},{9,8},{10,11... | collective-permute-start | bytes 1769480 | tf_op jit(solution)/shard_map/ppermute | solution.py:41
  309.0 16.8 %collective-permute-start.59 = (bf16[768,256]{1,0:T(8,128)(2,1)}, bf16[768,256]{1,0:T(8,128)(2,1)S(1)}, u32[]{:S(2)}, u32[]{:S(2)}) collective-permute-start(bf16[768,256]{1,0:T(8,128)(2,1)} %reduce-scatter.5.cloned.1.call-done.refs_0_), channel_id=1, source_target_pairs={{0,6},{2,4},{4,2},{6,0},{1,7},{3,5},{5,3},{7,1},{8,14},{10,12},{12... | collective-permute-start | bytes 1179656 | tf_op jit(solution)/shard_map/ppermute | solution.py:114
  311.1 18.5 %collective-permute-start.58 = (bf16[768,256]{1,0:T(8,128)(2,1)}, bf16[768,256]{1,0:T(8,128)(2,1)S(1)}, u32[]{:S(2)}, u32[]{:S(2)}) collective-permute-start(bf16[768,256]{1,0:T(8,128)(2,1)} %reduce-scatter.5.cloned.1.call-done.refs_0_), channel_id=1, source_target_pairs={{0,4},{4,0},{1,5},{5,1},{2,6},{6,2},{3,7},{7,3},{8,12},{12,8},{9,1... | collective-permute-start | bytes 1179656 | tf_op jit(solution)/shard_map/ppermute | solution.py:41
  311.7 18.0 %collective-permute-start.57 = (bf16[768,256]{1,0:T(8,128)(2,1)}, bf16[768,256]{1,0:T(8,128)(2,1)S(1)}, u32[]{:S(2)}, u32[]{:S(2)}) collective-permute-start(bf16[768,256]{1,0:T(8,128)(2,1)} %reduce-scatter.5.cloned.1.call-done.refs_0_), channel_id=1, source_target_pairs={{0,2},{2,0},{1,3},{3,1},{4,6},{6,4},{5,7},{7,5},{8,10},{10,8},{9,1... | collective-permute-start | bytes 1179656 | tf_op jit(solution)/shard_map/ppermute | solution.py:41
  (105 other events, 857.6 us)
Sparse Core Ops, SparseCore 0:
  10.2 39.7 all-gather.4
  53.1 50.2 all-gather.6
  187.5 48.1 reduce-scatter.2
  272.0 35.7 reduce-scatter.4

commit v4 on v3

--- a/solution.py
+++ b/solution.py
@@ -60,6 +60,10 @@
 SM = pl.BlockSpec(memory_space=pltpu.SMEM)
 
 
+def cost(flops, moved):
+    return pl.CostEstimate(flops=int(flops), bytes_accessed=int(moved), transcendentals=0)
+
+
 def kernel_call(body, outs, args, flops=0, scalars=0, **kw):
     moved = sum(a.size * a.dtype.itemsize for a in args) + sum(math.prod(o.shape) * o.dtype.itemsize for o in outs)
     if "grid" not in kw:
@@ -68,7 +72,7 @@
         body,
         out_shape=outs,
         compiler_params=pltpu.CompilerParams(vmem_limit_bytes=VMEM_LIMIT),
-        cost_estimate=pl.CostEstimate(flops=flops, bytes_accessed=moved, transcendentals=0),
+        cost_estimate=cost(flops, moved),
         **kw,
     )(*args)
 
@@ -113,14 +117,23 @@
             return near
         return near + [lax.ppermute(a, self.axes, [(i, 3 - i) for i in range(4)])]
 
+    def far_halves(self, near):
+        if not self.square:
+            return near
+        k = near[0].shape[0] // 2
+        return near + [jnp.concatenate([swap(near[2][:k], "x"), swap(near[1][k:], "y")], 0)]
+
     def gather_whole(self, a):
         return self.far(a, self.near(a))
 
-    def scatter(self, blocks):
+    def send_far(self, blocks):
+        return lax.ppermute(blocks[3], self.axes, [(i, 3 - i) for i in range(4)]) if self.square else blocks[-1]
+
+    def scatter(self, blocks, far=None):
         if not self.square:
             a = lax.psum_scatter(jnp.concatenate(blocks, 0), self.axes, scatter_dimension=0, tiled=True)
             return [a]
-        far = lax.ppermute(blocks[3], self.axes, [(i, 3 - i) for i in range(4)])
+        far = self.send_far(blocks) if far is None else far
         return [blocks[0], swap(blocks[1], "x"), swap(blocks[2], "y"), far]
 
     def exchange(self, slice_for):
@@ -363,6 +376,20 @@
     out[...] = (d_hidden[...] + norm_back(x, rsq(x), gain[...], added(terms))).astype(BF)
 
 
+def gain_lines(mlp_grad, parts):
+    total = parts[0][...]
+    for p in parts[1:]:
+        total = total + p[...]
+    width = mlp_grad.shape[1]
+    vectors = [total[:, :width], mlp_grad[...], total[:, width:]]
+    lines = [v[:, i : i + B] for v in vectors for i in range(0, v.shape[1], B)]
+    row = lax.broadcasted_iota(jnp.int32, (16, B), 0)
+    block = jnp.zeros((16, B), F32)
+    for i, line in enumerate(lines):
+        block = jnp.where(row == i, line, block)
+    return block
+
+
 def out_kernel(hidden, *refs):
     refs[-1][...] = (hidden[...] + added(refs[:-1])).astype(BF)
 
@@ -379,7 +406,7 @@
     return kernel_call(body, [sds((len(blocks) * q, cb * B), BF)], [t.astype(jnp.int32)[None], *blocks], scalars=1)[0]
 
 
-def grad_columns(plane, t, lhs, rhs, half, width, size, other, below=None):
+def grad_columns(plane, t, lhs, rhs, half, width, size, other, below=None, gains=()):
     nblk = width // B
     flat_l, flat_r = sum(lhs, []), sum(rhs, [])
     nl, nr = len(flat_l), len(flat_r)
@@ -390,7 +417,9 @@
     def body(where, *refs):
         left = jnp.concatenate([r[...] for r in refs[:nl]], 0)
         right = jnp.concatenate([r[...] for r in refs[nl : nl + nr]], 0)
-        rest, out = refs[nl + nr : -1], refs[-1]
+        gain_refs, rest, out = refs[nl + nr : nl + nr + ng], refs[nl + nr + ng : -1], refs[-1]
+        if ng:
+            out[0, nblk * rows + more :, :] = gain_lines(gain_refs[0], gain_refs[1:]).astype(BF)
         got = dot_tn(left, right)
         for j in range(nblk):
             part = got[:, j * B : (j + 1) * B]
@@ -398,18 +427,21 @@
                 part = part + rest[0][0, j * rows : (j + 1) * rows, :].astype(F32)
             out[0, j * rows : (j + 1) * rows, :] = part.astype(BF)
         if ready:
-            out[0, nblk * rows :, :] = rest[-1][0]
+            out[0, nblk * rows : nblk * rows + more, :] = rest[-1][0]
         elif more:
             z = pl.program_id(0)
             for r in range(plane.n):
                 @pl.when(plane.place(where[0], r) == z)
                 def _():
-                    out[0, nblk * rows :, :] = rest[-plane.n + r][...]
-
+                    out[0, nblk * rows : nblk * rows + more, :] = rest[-plane.n + r][...]
+
+    ng = len(gains)
+    tail = 16 if ng else 0
     tall = lambda k: pl.BlockSpec((1, k, B), lambda z, w: (z, 0, 0))
     in_specs = [pl.BlockSpec((a.shape[0], rows), lambda z, w: (0, z)) for a in flat_l]
     in_specs += [pl.BlockSpec((a.shape[0], width), lambda z, w: (0, half)) for a in flat_r]
-    args = flat_l + flat_r
+    in_specs += [pl.BlockSpec(a.shape, lambda z, w: (0, 0)) for a in gains]
+    args = flat_l + flat_r + list(gains)
     if other is not None:
         in_specs.append(tall(nblk * rows))
         args = args + [other]
@@ -420,18 +452,16 @@
         in_specs += [pl.BlockSpec((more, B), lambda z, w: (0, 0))] * plane.n
         args = args + below
     tokens = sum(a.shape[0] for a in flat_l)
-    out = sds((size, nblk * rows + more, B), BF)
+    out = sds((size, nblk * rows + more + tail, B), BF)
     return pl.pallas_call(
         body,
         out_shape=out,
         grid_spec=pltpu.PrefetchScalarGridSpec(
-            num_scalar_prefetch=1, grid=(size,), in_specs=in_specs, out_specs=tall(nblk * rows + more)
+            num_scalar_prefetch=1, grid=(size,), in_specs=in_specs, out_specs=tall(nblk * rows + more + tail)
         ),
         compiler_params=pltpu.CompilerParams(vmem_limit_bytes=VMEM_LIMIT),
-        cost_estimate=pl.CostEstimate(
-            flops=2 * tokens * rows * size * width,
-            bytes_accessed=sum(a.size * 2 for a in args) + math.prod(out.shape) * 2,
-            transcendentals=0,
+        cost_estimate=cost(
+            2 * tokens * rows * size * width, sum(a.size * 2 for a in args) + math.prod(out.shape) * 2
         ),
     )(t.astype(jnp.int32)[None], *args)
 
@@ -464,43 +494,58 @@
     )[0]
 
 
-def grad_down(core, product, cot, other, size, ff):
-    flat_r = sum(cot, [])
-    nl, nr = len(product), len(flat_r)
+def grad_mlp(core, nm, dgu, product, cot, other, size, ff):
     mine = other is not None
+    groups = [sum(nm, []), dgu, product, sum(cot, [])]
+    counts = [len(g) for g in groups]
+    width = groups[0][0].shape[1]
+    rows, blocks, side = width // size, 2 * ff // B, width // 2
+    low = blocks * rows
 
     def body(where, *refs):
-        left = jnp.concatenate([r[...] for r in refs[:nl]], 0)
-        right = jnp.concatenate([r[...] for r in refs[nl : nl + nr]], 0)
-        out = refs[-1]
-        got = dot_tn(left, right)
-        for h in range(2):
-            for i in range(2):
-                s = 2 * jnp.bitwise_xor(where[0], h) + i
-                at = h * ff
-                part = jnp.concatenate(
-                    [got[at + i * 128 : at + (i + 1) * 128], got[at + 256 + i * 64 : at + 256 + (i + 1) * 64]], 0)
-                if mine:
-                    part = part + refs[-2][s].astype(F32)
-                out[s] = part.astype(BF)
-
-    def column(j, w):
-        return (0, jnp.bitwise_xor(w[0], 0 if mine else 1) * 2 + j)
-
-    spec = pl.BlockSpec((size, 192, B), lambda j, w: (0, j, 0))
-    in_specs = [pl.BlockSpec(a.shape, lambda j, w: (0, 0)) for a in product]
-    in_specs += [pl.BlockSpec((a.shape[0], B), column) for a in flat_r]
-    args = product + flat_r + ([other] if mine else [])
+        at, parts = 0, []
+        for k in counts:
+            parts.append(refs[at : at + k])
+            at += k
+        rest, out = refs[at:-1], refs[-1]
+
+        def add(part, s, lo):
+            hi = lo + part.shape[0]
+            if mine:
+                part = part + rest[0][s, lo:hi, :].astype(F32)
+            out[s, lo:hi, :] = part.astype(BF)
+
+        lefts, rights, prods, cots = parts
+        right = jnp.concatenate([r[...] for r in rights], 0)
+        for z in range(size):
+            got = dot_tn(jnp.concatenate([r[:, z * rows : (z + 1) * rows] for r in lefts], 0), right)
+            for j in range(blocks):
+                add(got[:, j * B : (j + 1) * B], z, j * rows)
+        left = jnp.concatenate([r[...] for r in prods], 0)
+        for j in range(2):
+            got = dot_tn(left, jnp.concatenate([r[:, j * B : (j + 1) * B] for r in cots], 0))
+            for h in range(2):
+                for i in range(2):
+                    s = 2 * jnp.bitwise_xor(where[0], h) + i
+                    p = h * ff
+                    part = [got[p + i * 128 : p + (i + 1) * 128], got[p + 256 + i * 64 : p + 256 + (i + 1) * 64]]
+                    add(jnp.concatenate(part, 0), s, low + j * 192)
+
+    whole_of = lambda a: pl.BlockSpec(a.shape, lambda i, w: (0,) * a.ndim)
+    in_specs = [whole_of(a) for a in groups[0]]
+    in_specs += [pl.BlockSpec((a.shape[0], 2 * ff), lambda i, w: (0, 0 if mine else 1)) for a in dgu]
+    in_specs += [whole_of(a) for a in product]
+    in_specs += [pl.BlockSpec((a.shape[0], side), lambda i, w: (0, jnp.bitwise_xor(w[0], 0 if mine else 1))) for a in groups[3]]
+    args = sum(groups, []) + ([other] if mine else [])
+    out = sds((size, low + 384, B), BF)
     return pl.pallas_call(
         body,
-        out_shape=sds((size, 2 * 192, B), BF),
+        out_shape=out,
         grid_spec=pltpu.PrefetchScalarGridSpec(
-            num_scalar_prefetch=1, grid=(2,), in_specs=in_specs + [spec] * mine, out_specs=spec
+            num_scalar_prefetch=1, grid=(1,), in_specs=in_specs + [whole_of(out)] * mine, out_specs=whole_of(out)
         ),
         compiler_params=pltpu.CompilerParams(vmem_limit_bytes=VMEM_LIMIT),
-        cost_estimate=pl.CostEstimate(
-            flops=2 * sum(a.size for a in product) * 512, bytes_accessed=sum(a.size * 2 for a in args), transcendentals=0
-        ),
+        cost_estimate=cost(6 * 1024 * width * 2 * ff, sum(a.size * 2 for a in args)),
     )(core, *args)
 
 
@@ -677,103 +722,87 @@
         got_b, nm[1], nm[n - 2] = tie((got_b, nm[1], nm[n - 2]))
         wgu, wd = both(got_b), [] if spread else both(rows_to_chip(got_b, cut_b))
 
-        (product, dgu, partial, d_mid), _ = run(
-            functools.partial(mlp_block, spread, parts, wrows, ff), [core, wgu, wd],
-            [[*nm[r], *[stay(a) for a in cot[r]]] for r in range(n)],
-            lambda r: [sds((rows, parts * ff), BF), sds((rows, parts * 2 * ff), BF),
-                       hbm((rows, width), term_type(r).dtype), term_type(r)],
-            2 * length * width * parts * 7 * ff, one_by_one,
-        )
-        product, dgu, partial, d_mid = ([a[r] for r in range(n)] for a in (product, dgu, partial, d_mid))
+        def mlp(order):
+            return run(
+                functools.partial(mlp_block, spread, parts, wrows, ff), [core, wgu, wd],
+                {r: [*nm[r], *[stay(a) for a in cot[r]]] for g in order for r in g},
+                lambda r: [sds((rows, parts * ff), BF), sds((rows, parts * 2 * ff), BF),
+                           hbm((rows, width), term_type(r).dtype), term_type(r)],
+                2 * length * width * parts * 7 * ff, order,
+            )[0]
+
+        blocks = mlp([[n - 1], list(range(1, n - 1)), [0]])
+        product, dgu, partial, d_mid = ([a[r] for r in range(n)] for a in blocks)
         terms_mid = plane.scatter(d_mid)
-        product, terms_mid[-1] = tie((product, terms_mid[-1]))
 
         def pair(make, between=lambda a: a):
             if halves:
                 return make(0, swap(between(make(1, None)), "c"))
             return lax.psum(make(0, None), "c")
 
-        dgu = [[a] for a in dgu]
-        if spread:
-            down = grad_down(core, product, cot, swap(grad_down(core, product, cot, None, size, ff), "c"), size, ff)
-        else:
-            down = pair(lambda h, o: grad_rows(product, cot, half, h, ff, n, o))
-        terms_mid, down = tie((terms_mid, down))
+        def exchanged(low):
+            return plane.exchange(lambda i: lax.dynamic_index_in_dim(low, i, 0, keepdims=False))
+
+        def merged(lhs, rhs, width_, other, low, gains=()):
+            if halves:
+                return grad_columns(plane, t, lhs, rhs, 0, width_, size, swap(other, "c"), low, gains)
+            a = grad_columns(plane, t, lhs, rhs, 0, width_, size, None)
+            return jnp.concatenate([lax.psum(a, "c"), jnp.stack(low, 0)], 1)
+
         d_hidden, dh0, dh1, mlp_grad = kernel_call(
             mid_back_kernel,
             [hbm((rows, width), F32), sds((half, width), BF), sds((half, width), BF), sds((1, width), F32)],
             [hidden, cotangent, gain_mid, *terms_mid],
         )
         dh = plane.gather_near(dh0, dh1)
-        dgu, _ = tie((dgu, dh0))
-        gu_other = grad_columns(plane, t, nm, dgu, 1, 2 * ff, size, None) if halves else None
-        dh[0], gu_other = tie((dh[0], gu_other))
+        if spread:
+            make_b = lambda other: grad_mlp(core, nm, dgu, product, cot, other, size, ff)
+            dgu, product, _ = tie((dgu, product, dh0))
+            grads_b = make_b(swap(make_b(None), "c"))
+        else:
+            dgu = [[a] for a in dgu]
+            gu_other = grad_columns(plane, t, nm, dgu, 1, 2 * ff, size, None) if halves else None
+            grads_b = merged(nm, dgu, 2 * ff, gu_other, exchanged(pair(lambda h, o: grad_rows(product, cot, half, h, ff, n, o))))
+        dh[1], dh[n - 2], grads_b, dh[0] = tie((dh[1], dh[n - 2], grads_b, dh[0]))
+        grads_b = lax.psum_scatter(grads_b.reshape(-1, B), "shard", scatter_dimension=0, tiled=True)
 
         def back(order, dh):
             return run(
                 functools.partial(attend_back_block, parts, wrows), [qg, kg, wa, wo],
-                {r: [*dh[r], *[stay(a) for a in (*tok[r], lin[r], vals[r], *tables[r])]] for g in order for r in g},
-                lambda r: [hbm((rows, parts * 4 * HEAD), BF), term_type(r)],
+                {r: [*([stay(a) for a in dh[r]] if r == 0 else dh[r]), *[stay(a) for a in (*tok[r], lin[r], vals[r], *tables[r])]]
+                 for g in order for r in g},
+                lambda r: [hbm((rows, parts * 4 * HEAD), BF), hbm((rows, width), term_type(r).dtype)],
                 2 * length * width * parts * 6 * HEAD, order, sds((1, width + 2 * HEAD), F32),
             )
 
         own_back, gains = back([[0]], dh)
-        dh = plane.gather_far(dh, own_back)
-        gu_other, own_back, dh[1:-1] = tie((gu_other, own_back, dh[1:-1]))
-
-        def exchanged(low):
-            return plane.exchange(lambda i: lax.dynamic_index_in_dim(low, i, 0, keepdims=False))
-
-        def merged(lhs, rhs, width_, other, low):
-            if halves:
-                return grad_columns(plane, t, lhs, rhs, 0, width_, size, swap(other, "c"), low)
-            a = grad_columns(plane, t, lhs, rhs, 0, width_, size, None)
-            return jnp.concatenate([lax.psum(a, "c"), jnp.stack(low, 0)], 1)
-
-        grads_b = merged(nm, dgu, 2 * ff, gu_other, down if spread else exchanged(down))
-        partial, grads_b = tie((partial, grads_b))
-        grads_b = lax.psum_scatter(grads_b.reshape(-1, B), "shard", scatter_dimension=0, tiled=True)
-        terms_out = plane.scatter(partial)
+        dh = plane.gather_far(dh)
+        dh[n - 1], own_back = tie((dh[n - 1], own_back))
         out = pair(lambda h, o: grad_rows(
             [stay(a) for a in mixed], [[stay(a) for a in b] for b in dh], half, h, GROUP * HEAD, n, o))
-        far_back, more = back([[n - 1]], dh)
-        dh[1:-1], far_back, out = tie((dh[1:-1], far_back, out))
+        dh[1:], partial, out = tie((dh[1:], partial, out))
         out = exchanged(out)
-        near_back, last = back([[r] for r in range(1, n - 2)], dh)
-        dh[n - 2], near_back, terms_out = tie((dh[n - 2], near_back, terms_out))
-        near2_back, last2 = back([[n - 2]], dh)
-        near_back = [{**a, **b} for a, b in zip(near_back, near2_back)]
-        gains = gains + more + last + last2
-        dqkv, d_in = ({**a, **b, **c} for a, b, c in zip(own_back, far_back, near_back))
-        dqkv, d_in = ([a[r] for r in range(n)] for a in (dqkv, d_in))
+        far_out = plane.send_far(partial)
+        near_back, more = back([list(range(1, n - 1))], dh)
+        dh[n - 1], out, far_out, near_back, partial = tie((dh[n - 1], out, far_out, near_back, partial))
+        terms_out = plane.scatter(partial, far_out)
+        far_back, last = back([[n - 1]], dh)
+        gains = gains + more + last
+        far_back, grads_b, terms_out = tie((far_back, grads_b, terms_out))
+        grads_b = plane.near(grads_b)
+        dqkv, d_in = ([{**a, **b, **c}[r] for r in range(n)] for a, b, c in zip(own_back, near_back, far_back))
+        dqkv = [[stay(a)] for a in dqkv]
+        lhs = [[stay(a)] for a in nin]
+        qkv_other = grad_columns(plane, t, lhs, dqkv, 1, 4 * HEAD, size, None) if halves else None
+        if halves:
+            qkv_other, grads_b = tie((qkv_other, grads_b))
+        grads_a = merged(lhs, dqkv, 4 * HEAD, qkv_other, out, [mlp_grad, *gains] if halves else [])
+        grads_b, _ = tie((grads_b, grads_a))
+        grads_b = plane.far_halves(grads_b)
+        d_in, grads_b = tie((d_in, grads_b))
+        grads_a = lax.psum_scatter(grads_a.reshape(-1, B), "shard", scatter_dimension=0, tiled=True)
         terms_in = plane.scatter(d_in)
-        dqkv = [[a] for a in dqkv]
-        lhs = [[a] for a in nin]
-        dqkv, terms_in[-1] = tie((dqkv, terms_in[-1]))
-        qkv_other = grad_columns(plane, t, lhs, dqkv, 1, 4 * HEAD, size, None) if halves else None
-        qkv_other, terms_in[:-1] = tie((qkv_other, terms_in[:-1]))
-        grads_a = merged(lhs, dqkv, 4 * HEAD, qkv_other, out)
-        gains = jnp.concatenate([functools.reduce(jnp.add, gains), mlp_grad], 1)
-        grads_a, grads_b, gains = tie((grads_a, grads_b, gains))
-        grads_a = lax.psum_scatter(grads_a.reshape(-1, B), "shard", scatter_dimension=0, tiled=True)
-        if plane.square and size == 4:
-            for axis in ("c", "x", "y"):
-                gains = gains + swap(gains, axis)
-            gains, grads_b = tie((gains, grads_b))
-            for k in (1, 2):
-                gains = gains + lax.ppermute(gains, "shard", [(i, i ^ k) for i in range(4)])
-        else:
-            gains = lax.psum(gains, ("shard", "y", "x", "c"))
-        grads_b = plane.gather_whole(grads_b)
-        activations = kernel_call(
-            out_kernel, [sds((rows, width), BF)], [hidden, *terms_out],
-        )[0]
-        grads_a, grads_b, gains = tie((grads_a, grads_b, gains))
-        gains = gains[0]
-        input_grad = kernel_call(
-            last_kernel, [sds((rows, width), BF)], [tokens, d_hidden, gain_in, *terms_in],
-        )[0]
-
+        activations = kernel_call(out_kernel, [sds((rows, width), BF)], [hidden, *terms_out])[0]
 
         def assemble(mine, outs, write):
             got = [(r, 0, a) for r, a in enumerate(mine)]
@@ -781,6 +810,8 @@
                 got += [(r, 1, swap(a, "c")) for r, a in enumerate(mine)]
 
             def body(where, *refs):
+                if len(outs) == 5:
+                    refs[-1][...] = jnp.zeros_like(refs[-1])
                 for (r, other, _), ref in zip(got, refs):
                     core = jnp.bitwise_xor(where[1], other) if halves else 0
                     write(ref, plane.place(where[0], r), core, refs[len(got) :])
@@ -846,30 +877,42 @@
                             out[:, pl.ds(at + 2 * HEAD, HEAD)] = jnp.where(low, rolled, rest_odd)
 
         def write_a(ref, src, core, outs):
-            q, k, v, out = outs
+            q, k, v, out = outs[:4]
             write_cols(ref, 0, [(0, B, q, B, 0)], src, core)
             write_cols(ref, 1, [(0, HEAD, k, HEAD, 0), (HEAD, B, v, HEAD, 0)], src, core)
             write_rows(ref, cut_a, out_rows, src, core, out)
+            if halves:
+                outs[4][...] += ref[cut_a + cb * out_rows :, :].astype(F32)
 
         like = lambda w: sds(w.shape, F32)
         gate_g, up_g, down_g = assemble(grads_b, [like(w_gate), like(w_up), like(w_down)], write_spread if spread else write_b)
-        grads_a = plane.gather_whole(grads_a)
-        grads_a, gate_g, up_g, down_g, activations, input_grad = tie(
-            (grads_a, gate_g, up_g, down_g, activations, input_grad))
-        query_g, key_g, value_g, out_g = assemble(
-            grads_a, [like(w_query), like(w_key), like(w_value), like(w_out)], write_a)
+        grads_a, gate_g, up_g, down_g, activations, terms_in = tie(
+            (grads_a, gate_g, up_g, down_g, activations, terms_in))
+        input_grad = kernel_call(
+            last_kernel, [sds((rows, width), BF)], [tokens, d_hidden, gain_in, *terms_in])[0]
+        grads_a, input_grad = tie((plane.gather_whole(grads_a), input_grad))
+        outs_a = [like(w_query), like(w_key), like(w_value), like(w_out)]
+        if halves:
+            query_g, key_g, value_g, out_g, gains = assemble(grads_a, outs_a + [sds((16, B), F32)], write_a)
+            gains = gains[: (2 * width + 2 * HEAD) // B].reshape(-1)
+            gains = [gains[:width], gains[width : 2 * width], gains[2 * width :]]
+        else:
+            query_g, key_g, value_g, out_g = assemble(grads_a, outs_a, write_a)
+            gains = functools.reduce(jnp.add, gains)
+            gains = [gains[:, :width], mlp_grad, gains[:, width:]]
+            gains = [g[0] for g in lax.psum(gains, ("shard", "y", "x", "c"))]
 
         return (
             activations,
             input_grad,
-            gains[:width],
+            gains[0],
             query_g,
             key_g,
             value_g,
-            gains[width : width + HEAD],
-            gains[width + HEAD : width + 2 * HEAD],
+            gains[2][:HEAD],
+            gains[2][HEAD:],
             out_g,
-            gains[width + 2 * HEAD :],
+            gains[1],
             gate_g,
             up_g,
             down_g,

time: 349 us -> 336 us (0.963)
  waiting for transfers between devices: 132 us -> 122 us
  starting transfers between devices: 62.1 us -> 57 us
  local copies, waits for them, and re-layouts: 22.9 us -> 27.3 us
    ppermute x6 -> x4, waiting for transfers between devices: 7.25 us -> 0.87 us  [send_far(): lax.ppermute(blocks[3], self.axes, [(i, 3 - i) for i in range(4)])]
    ppermute x58 -> x56, waiting for transfers between devices: 113 us -> 119 us  [swap(): return lax.ppermute(a, axis, SWAP)]
    ppermute x2, waiting for transfers between devices: 7.48 us -> 2.11 us  [exchange(): lax.ppermute(slice_for(jnp.bitwise_xor(t, 3)), self.axes, [(i, 3 - i) for...]
    pallas_call x4 -> x2, Pallas kernels: 13.6 us -> 9.2 us  [grad_columns(): pl.pallas_call(body, out_shape=out, grid_spec=pltpu.PrefetchScalarGridSpe...]
    unnamed x194 -> x163, local copies, waits for them, and re-layouts: 20.4 us -> 24.6 us
    ppermute x6 -> x4, starting transfers between devices: 9.78 us -> 6.17 us  [send_far(): lax.ppermute(blocks[3], self.axes, [(i, 3 - i) for i in range(4)])]
    ppermute x2 -> x1, waiting for transfers between devices: 3.56 us -> 0.01 us  [far(): return near + [lax.ppermute(a, self.axes, [(i, 3 - i) for i in range(4)])]]
    pallas_call x21 -> x19, Pallas kernels: 87.4 us -> 86 us  [kernel_call(): pl.pallas_call(body, out_shape=outs, compiler_params=pltpu.CompilerParams...]
  transfers between devices with their start and end apart: 72 -> 67, of which waited for: 39 -> 39; matrix products, arithmetic and copies ran while one was open for 1% -> 1% of each run, Pallas kernels for 27% -> 27%
where the time goes in v4:
time: 336 us; the launch traced here: 330 us
  waiting for transfers between devices  122 us (36%)
  Pallas kernels  109 us (32%)
  starting transfers between devices  57 us (17%)
  local copies, waits for them, and re-layouts  27.3 us (8%)
  between operations  14.8 us (4%)
    ppermute x56, waiting for transfers between devices, swap(): return lax.ppermute(a, axis, SWAP)  119 us
    pallas_call x19, Pallas kernels, kernel_call(): pl.pallas_call(body, out_shape=outs, compiler_params=pltpu.CompilerParams...  86 us
    ppermute x56, starting transfers between devices, swap(): return lax.ppermute(a, axis, SWAP)  47.1 us
    unnamed x163, local copies, waits for them, and re-layouts  24.6 us
    pallas_call x2, Pallas kernels, grad_columns(): pl.pallas_call(body, out_shape=out, grid_spec=pltpu.PrefetchScalarGridSpe...  9.2 us
    pallas_call x2, Pallas kernels, grad_mlp(): pl.pallas_call(body, out_shape=out, grid_spec=pltpu.PrefetchScalarGridSpe...  8.51 us
  transfers between devices with their start and end apart: 67, of which 39 were waited for; matrix products, arithmetic and copies ran while one was open for 1% of the time, Pallas kernels for 27%

profile of v4, /device:TPU:0, one launch (start us, length us, event | category | flops | bytes accessed | tf_op | source)
XLA Modules:
  0.0 330.2 jit_solution(14418151171757584421)
XLA Ops:
  7.3 2.4 shard_map.237
  9.9 3.0 collective-permute-start.1
  12.9 1.5 collective-permute-start.3
  15.0 12.0 %collective-permute-done.2.refs_6_.refs_17_ = bf16[128,1024]{1,0:T(8,128)(2,1)S(1)} collective-permute-done((bf16[128,1024]{1,0:T(8,128)(2,1)S(1)}, bf16[128,1024]{1,0:T(8,128)(2,1)S(1)}, u32[]{:S(2)}, u32[]{:S(2)}) %collective-permute-start.2) | collective-permute-done | bytes 262176 | tf_op jit(solution)/shard_map/ppermute | solution.py:41
  28.3 1.7 collective-permute-start.8
  30.0 1.5 collective-permute-start.4
  32.3 4.9 %collective-permute-done.7.refs_6_.refs_19_ = bf16[128,1024]{1,0:T(8,128)(2,1)} collective-permute-done((bf16[128,1024]{1,0:T(8,128)(2,1)S(1)}, bf16[128,1024]{1,0:T(8,128)(2,1)}, u32[]{:S(2)}, u32[]{:S(2)}) %collective-permute-start.7) | collective-permute-done | bytes 262176 | tf_op jit(solution)/shard_map/ppermute | solution.py:41
  37.2 1.5 collective-permute-start.9
  39.5 3.3 collective-permute-done.4.refs_8_
  42.8 1.5 collective-permute-start.11
  44.4 2.9 shard_map.239
  47.3 4.2 %shard_map.238 = (bf16[256,1024]{1,0:T(8,128)(2,1)}, f32[256,128]{1,0:T(8,128)}, f32[256,128]{1,0:T(8,128)}, f32[256,256]{1,0:T(8,128)}, bf16[256,1024]{1,0:T(8,...) custom-call(f32[1,1024]{1,0:T(1,128)S(1)} %bitcast.61, ...), custom_call_target="tpu_custom_call" | custom-call | bytes 6427136 | tf_op jit(solution)/shard_map/pallas_call | solution.py:71
  54.7 1.4 collective-permute-start.13
  56.2 1.5 collective-permute-start.14
  58.3 2.8 collective-permute-done.13.refs_1_
  61.1 3.4 %collective-permute-done.14.refs_2_ = bf16[256,256]{1,0:T(8,128)(2,1)S(1)} collective-permute-done((bf16[256,256]{1,0:T(8,128)(2,1)S(1)}, bf16[256,256]{1,0:T(8,128)(2,1)S(1)}, u32[]{:S(2)}, u32[]{:S(2)}) %collective-permute-start.14) | collective-permute-done | bytes 131104 | tf_op jit(solution)/shard_map/ppermute | solution.py:41
  64.6 1.9 collective-permute-done.16.refs_5_
  66.5 4.4 %shard_map.243 = (f32[256,768]{1,0:T(8,128)}, bf16[256,256]{1,0:T(8,128)(2,1)}, bf16[256,512]{1,0:T(8,128)(2,1)}, bf16[256,1024]{1,0:T(8,128)(2,1)S(1)}) custom-call(f32[1,128]{1,0:T(1,128)S(1)} %bitcast.47, f32[1,128]{1,0:T(1,128)S(1)} %bitcast.53, bf16[4,768,256]{2,1,0:T(8,128)(2,1)S(1)} %bitcast.40, ...), custom_call_target="tpu_custom_call" | custom-call | flops 805306368 | bytes 6947840 | tf_op jit(solution)/shard_map/pallas_call | solution.py:71
  70.9 1.6 collective-permute-start.19
  72.5 7.1 %shard_map.242 = (f32[256,768]{1,0:T(8,128)}, bf16[256,256]{1,0:T(8,128)(2,1)}, bf16[256,512]{1,0:T(8,128)(2,1)}, bf16[256,1024]{1,0:T(8,128)(2,1)S(1)}, f32[256...) custom-call(f32[1,128]{1,0:T(1,128)S(1)} %bitcast.48, ...), custom_call_target="tpu_custom_call" | custom-call | flops 1610612736 | bytes 9700352 | tf_op jit(solution)/shard_map/pallas_call | solution.py:71
  79.6 1.4 collective-permute-start.17
  81.5 4.3 %shard_map.241 = (f32[256,768]{1,0:T(8,128)}, bf16[256,256]{1,0:T(8,128)(2,1)}, bf16[256,512]{1,0:T(8,128)(2,1)}, f32[256,1024]{1,0:T(8,128)S(1)}) custom-call(f32[1,128]{1,0:T(1,128)S(1)} %bitcast.49, f32[1,128]{1,0:T(1,128)S(1)} %bitcast.55, bf16[4,768,256]{2,1,0:T(8,128)(2,1)S(1)} %bitcast.42, bf16[4,768,256]{2,1,0:T(8,128)(2,1)S(1)} %collective-permute-done.12.refs_3_, ...), custom_call_target="tpu_custom_call" | custom-call | flops 805306368 | bytes 7472128 | tf_op jit(solution)/shard_map/pallas_call | solution.py:71
  86.6 10.5 %collective-permute-done.17.refs_1_ = bf16[256,1024]{1,0:T(8,128)(2,1)S(1)} collective-permute-done((bf16[256,1024]{1,0:T(8,128)(2,1)S(1)}, bf16[256,1024]{1,0:T(8,128)(2,1)S(1)}, u32[]{:S(2)}, u32[]{:S(2)}) %collective-permute-start.17) | collective-permute-done | bytes 524320 | tf_op jit(solution)/shard_map/ppermute | solution.py:41
  97.2 1.3 shard_map.244
  100.5 1.4 collective-permute-start.20
  103.2 4.5 %collective-permute-done.21.refs_4_.refs_3_ = bf16[128,1024]{1,0:T(8,128)(2,1)} collective-permute-done((bf16[128,1024]{1,0:T(8,128)(2,1)S(1)}, bf16[128,1024]{1,0:T(8,128)(2,1)}, u32[]{:S(2)}, u32[]{:S(2)}) %collective-permute-start.21) | collective-permute-done | bytes 262176 | tf_op jit(solution)/shard_map/ppermute | solution.py:41
  108.9 3.4 %collective-permute-done.20.refs_3_.refs_2_ = bf16[128,1024]{1,0:T(8,128)(2,1)S(1)} collective-permute-done((bf16[128,1024]{1,0:T(8,128)(2,1)S(1)}, bf16[128,1024]{1,0:T(8,128)(2,1)S(1)}, u32[]{:S(2)}, u32[]{:S(2)}) %collective-permute-start.20) | collective-permute-done | bytes 262176 | tf_op jit(solution)/shard_map/ppermute | solution.py:41
  115.0 1.3 collective-permute-start.28
  116.3 6.6 %collective-permute-done.27.refs_3_.refs_6_ = bf16[128,1024]{1,0:T(8,128)(2,1)S(1)} collective-permute-done((bf16[128,1024]{1,0:T(8,128)(2,1)}, bf16[128,1024]{1,0:T(8,128)(2,1)S(1)}, u32[]{:S(2)}, u32[]{:S(2)}) %collective-permute-start.27) | collective-permute-done | bytes 262176 | tf_op jit(solution)/shard_map/ppermute | solution.py:41
  123.6 1.7 copy-done.64
  125.3 4.1 %shard_map.247 = (bf16[256,768]{1,0:T(8,128)(2,1)S(1)}, bf16[256,1536]{1,0:T(8,128)(2,1)S(1)}, bf16[256,1024]{1,0:T(8,128)(2,1)}, bf16[256,1024]{1,0:T(8,128)(2,1)S(1)}) custom-call(s32[1]{0:T(128)} %bitcast.5.refs_0_.where, bf16[4,1152,256]{2,1,0:T(8,128)(2,1)S(1)} %bitcast.64, bf16[4,1152,256]{2,1,0:T(8,128)(2,1)S(1)} %collective-permute-done.24.refs_2_, ...), custom_call_target="tpu_custom_call" | custom-call | flops 2818572288 | bytes 7995396 | tf_op jit(solution)/shard_map/pallas_call | solution.py:71
  129.4 1.8 collective-permute-start.29
  131.3 7.6 %shard_map.246 = (bf16[256,768]{1,0:T(8,128)(2,1)S(1)}, bf16[256,1536]{1,0:T(8,128)(2,1)S(1)}, bf16[256,1024]{1,0:T(8,128)(2,1)}, bf16[256,1024]{1,0:T(8,128)(2,...) custom-call(s32[1]{0:T(128)} %bitcast.5.refs_0_.where, ...), custom_call_target="tpu_custom_call" | custom-call | flops 5637144576 | bytes 11272196 | tf_op jit(solution)/shard_map/pallas_call | solution.py:71
  140.7 4.8 %shard_map.245 = (bf16[256,768]{1,0:T(8,128)(2,1)S(1)}, bf16[256,1536]{1,0:T(8,128)(2,1)S(1)}, f32[256,1024]{1,0:T(8,128)}, f32[256,1024]{1,0:T(8,128)S(1)}) custom-call(s32[1]{0:T(128)} %bitcast.5.refs_0_.where, bf16[4,1152,256]{2,1,0:T(8,128)(2,1)S(1)} %bitcast.66, bf16[4,1152,256]{2,1,0:T(8,128)(2,1)S(1)} %collective-permute-done.24.refs_2_, ...), custom_call_target="tpu_custom_call" | custom-call | flops 2818572288 | bytes 9043972 | tf_op jit(solution)/shard_map/pallas_call | solution.py:71
  145.6 9.2 %collective-permute-done.25.refs_1_ = bf16[256,1024]{1,0:T(8,128)(2,1)S(1)} collective-permute-done((bf16[256,1024]{1,0:T(8,128)(2,1)S(1)}, bf16[256,1024]{1,0:T(8,128)(2,1)S(1)}, u32[]{:S(2)}, u32[]{:S(2)}) %collective-permute-start.25) | collective-permute-done | bytes 524320 | tf_op jit(solution)/shard_map/ppermute | solution.py:41
  154.9 1.7 shard_map.248
  157.2 4.2 %shard_map.249 = bf16[4,1152,256]{2,1,0:T(8,128)(2,1)S(1)} custom-call(s32[1]{0:T(128)} %bitcast.5.refs_0_.where, bf16[128,1024]{1,0:T(8,128)(2,1)S(1)} %get-tuple-element.265.refs_3_.refs_0_, bf16[128,1024]{1,0:T(8,128)(2,1)S(1)} %copy-done.69, bf16[128,1024]{1,0:T(8,128)(2,1)S(1)} %copy-done.71, bf16[128,1024]{1,0:T(8,128)(2,1)} %collective-permute-done.21.refs_4_.refs_3_, ...), custom_call_target="tpu_custom_call" | custom-call | flops 4831838208 | bytes 8912896 | tf_op jit(solution)/shard_map/pallas_call | solution.py:541
  167.0 4.3 %shard_map.250 = bf16[4,1152,256]{2,1,0:T(8,128)(2,1)S(1)} custom-call(s32[1]{0:T(128)} %bitcast.5.refs_0_.where, bf16[128,1024]{1,0:T(8,128)(2,1)S(1)} %copy-done.67, bf16[128,1024]{1,0:T(8,128)(2,1)S(1)} %copy-done.69, bf16[128,1024]{1,0:T(8,128)(2,1)S(1)} %copy-done.71, bf16[128,1024]{1,0:T(8,128)(2,1)} %collective-permute-done.21.refs_4_.refs_3_, ...), custom_call_target="tpu_custom_call" | custom-call | flops 4831838208 | bytes 11272192 | tf_op jit(solution)/shard_map/pallas_call | solution.py:541
  171.3 1.4 copy-done.22
  172.7 3.3 collective-permute-done.31.refs_7_
  177.9 1.3 collective-permute-start.36
  181.3 7.5 %shard_map.251 = (bf16[256,1024]{1,0:T(8,128)(2,1)}, f32[256,1024]{1,0:T(8,128)}, f32[1,1280]{1,0:T(1,128)S(1)}) custom-call(f32[1,128]{1,0:T(1,128)S(1)} %bitcast.50, f32[1,128]{1,0:T(1,128)S(1)} %bitcast.56, bf16[4,768,256]{2,1,0:T(8,128)(2,1)S(1)} %bitcast.43, bf16[4,768,256]{2,1,0:T(8,128)(2,1)S(1)} %collective-permute-done.12.refs_3_, ...), custom_call_target="tpu_custom_call" | custom-call | flops 805306368 | bytes 8296448 | tf_op jit(solution)/shard_map/pallas_call | solution.py:71
  189.6 3.6 %shard_map.252 = bf16[4,256,256]{2,1,0:T(8,128)(2,1)S(1)} custom-call(bf16[256,512]{1,0:T(8,128)(2,1)} %get-tuple-element.323.refs_0_, bf16[256,512]{1,0:T(8,128)(2,1)} %get-tuple-element.324.refs_1_, bf16[256,512]{1,0:T(8,128)(2,1)} %get-tuple-element.325.refs_2_, bf16[256,512]{1,0:T(8,128)(2,1)} %get-tuple-element.326.refs_3_, ...), custom_call_target="tpu_custom_call" | custom-call | flops 536870912 | bytes 3670016 | tf_op jit(solution)/shard_map/pallas_call | solution.py:71
  193.4 1.9 collective-permute-done.37.refs_12_
  195.3 3.5 %shard_map.253 = bf16[4,256,256]{2,1,0:T(8,128)(2,1)S(1)} custom-call(bf16[256,512]{1,0:T(8,128)(2,1)} %get-tuple-element.323.refs_0_, bf16[256,512]{1,0:T(8,128)(2,1)} %get-tuple-element.324.refs_1_, bf16[256,512]{1,0:T(8,128)(2,1)} %get-tuple-element.325.refs_2_, bf16[256,512]{1,0:T(8,128)(2,1)} %get-tuple-element.326.refs_3_, ...), custom_call_target="tpu_custom_call" | custom-call | flops 536870912 | bytes 4194304 | tf_op jit(solution)/shard_map/pallas_call | solution.py:71
  201.1 1.3 collective-permute-start.39
  203.7 12.9 %shard_map.254 = (bf16[256,1024]{1,0:T(8,128)(2,1)}, bf16[256,1024]{1,0:T(8,128)(2,1)}, bf16[256,1024]{1,0:T(8,128)(2,1)}, bf16[256,1024]{1,0:T(8,128)(2,1)}, f32[1,1280]{1,0:T(1,128)S(1)}) custom-call(f32[1,128]{1,0:T(1,128)S(1)} %bitcast.51, f32[1,128]{1,0:T(1,128)S(1)} %bitcast.57, bf16[4,768,256]{2,1,0:T(8,128)(2,1)S(1)} %bitcast.44, ...), custom_call_target="tpu_custom_call" | custom-call | flops 1610612736 | bytes 11343872 | tf_op jit(solution)/shard_map/pallas_call | solution.py:71
  217.3 2.1 collective-permute-done.40.refs_16_
  221.9 7.4 %shard_map.255 = (bf16[256,1024]{1,0:T(8,128)(2,1)}, bf16[256,1024]{1,0:T(8,128)(2,1)}, f32[1,1280]{1,0:T(1,128)S(1)}) custom-call(f32[1,128]{1,0:T(1,128)S(1)} %bitcast.52, f32[1,128]{1,0:T(1,128)S(1)} %bitcast.58, bf16[4,768,256]{2,1,0:T(8,128)(2,1)S(1)} %bitcast.45, bf16[4,768,256]{2,1,0:T(8,128)(2,1)S(1)} %collective-permute-done.12.refs_3_, ...), custom_call_target="tpu_custom_call" | custom-call | flops 805306368 | bytes 7772160 | tf_op jit(solution)/shard_map/pallas_call | solution.py:71
  229.9 3.4 %collective-permute-done.42.refs_1_ = bf16[256,1024]{1,0:T(8,128)(2,1)S(1)} collective-permute-done((bf16[256,1024]{1,0:T(8,128)(2,1)S(1)}, bf16[256,1024]{1,0:T(8,128)(2,1)S(1)}, u32[]{:S(2)}, u32[]{:S(2)}) %collective-permute-start.42) | collective-permute-done | bytes 524320 | tf_op jit(solution)/shard_map/ppermute | solution.py:41
  236.8 4.1 %shard_map.256 = bf16[4,512,256]{2,1,0:T(8,128)(2,1)S(1)} custom-call(s32[1]{0:T(128)} %bitcast.where, bf16[256,1024]{1,0:T(8,128)(2,1)} %get-tuple-element.242.refs_6_.refs_0_, bf16[256,1024]{1,0:T(8,128)(2,1)} %get-tuple-element.243.refs_6_.refs_1_, bf16[256,1024]{1,0:T(8,128)(2,1)} %get-tuple-element.244.refs_10_.refs_2_, ...), custom_call_target="tpu_custom_call" | custom-call | flops 1073741824 | bytes 5242880 | tf_op jit(solution)/shard_map/pallas_call | solution.py:456
  240.9 7.9 %collective-permute-done.44.refs_1_ = bf16[1152,256]{1,0:T(8,128)(2,1)S(1)} collective-permute-done((bf16[1152,256]{1,0:T(8,128)(2,1)}, bf16[1152,256]{1,0:T(8,128)(2,1)S(1)}, u32[]{:S(2)}, u32[]{:S(2)}) %collective-permute-start.44) | collective-permute-done | bytes 589856 | tf_op jit(solution)/shard_map/ppermute | solution.py:41
  249.4 2.7 collective-permute-done.46.refs_12_
  252.1 5.1 %shard_map.257 = bf16[4,784,256]{2,1,0:T(8,128)(2,1)} custom-call(s32[1]{0:T(128)} %bitcast.where, bf16[256,1024]{1,0:T(8,128)(2,1)} %get-tuple-element.242.refs_6_.refs_0_, bf16[256,1024]{1,0:T(8,128)(2,1)} %get-tuple-element.243.refs_6_.refs_1_, bf16[256,1024]{1,0:T(8,128)(2,1)} %get-tuple-element.244.refs_10_.refs_2_, ...), custom_call_target="tpu_custom_call" | custom-call | flops 1073741824 | bytes 7382528 | tf_op jit(solution)/shard_map/pallas_call | solution.py:456
  259.5 7.0 %collective-permute-done.47 = bf16[576,256]{1,0:T(8,128)(2,1)S(1)} collective-permute-done((bf16[576,256]{1,0:T(8,128)(2,1)S(1)}, bf16[576,256]{1,0:T(8,128)(2,1)S(1)}, u32[]{:S(2)}, u32[]{:S(2)}) %collective-permute-start.47) | collective-permute-done | bytes 294944 | tf_op jit(solution)/shard_map/ppermute | solution.py:41
  270.5 1.6 collective-permute-start.55
  275.4 5.4 %shard_map.258 = (f32[256,3072]{1,0:T(8,128)}, f32[256,3072]{1,0:T(8,128)}, f32[768,1024]{1,0:T(8,128)}) custom-call(s32[2]{0:T(128)S(1)} %pad_add_fusion.1.w.where, bf16[1152,256]{1,0:T(8,128)(2,1)S(1)} %copy-done.34, bf16[1152,256]{1,0:T(8,128)(2,1)S(1)} %collective-permute-done.44.refs_1_, bf16[1152,256]{1,0:T(8,128)(2,1)S(1)} %collective-permute-done.45.refs_2_, ...), custom_call_target="tpu_custom_call" | custom-call | bytes 14155784 | tf_op jit(solution)/shard_map/pallas_call | solution.py:71
  280.8 2.5 collective-permute-done.53.refs_1_
  284.1 10.6 %collective-permute-done.54.refs_2_ = bf16[256,1024]{1,0:T(8,128)(2,1)S(1)} collective-permute-done((bf16[256,1024]{1,0:T(8,128)(2,1)S(1)}, bf16[256,1024]{1,0:T(8,128)(2,1)S(1)}, u32[]{:S(2)}, u32[]{:S(2)}) %collective-permute-start.54) | collective-permute-done | bytes 524320 | tf_op jit(solution)/shard_map/ppermute | solution.py:41
  298.3 1.6 collective-permute-start.58
  305.4 1.4 shard_map.260
  306.8 2.0 collective-permute-done.56.refs_1_
  308.8 6.1 %collective-permute-done.57.refs_2_ = bf16[784,256]{1,0:T(8,128)(2,1)S(1)} collective-permute-done((bf16[784,256]{1,0:T(8,128)(2,1)}, bf16[784,256]{1,0:T(8,128)(2,1)S(1)}, u32[]{:S(2)}, u32[]{:S(2)}) %collective-permute-start.57) | collective-permute-done | bytes 401440 | tf_op jit(solution)/shard_map/ppermute | solution.py:41
  318.3 3.4 %shard_map.261 = (f32[256,2048]{1,0:T(8,128)}, f32[256,1024]{1,0:T(8,128)}, f32[256,1024]{1,0:T(8,128)}, f32[512,1024]{1,0:T(8,128)}, f32[16,256]{1,0:T(8,128)S(1)}) custom-call(s32[2]{0:T(128)S(1)} %pad_add_fusion.1.w.where, bf16[784,256]{1,0:T(8,128)(2,1)S(1)} %copy-done.47, bf16[784,256]{1,0:T(8,128)(2,1)S(1)} %collective-permute-done.56.refs_1_, ...), custom_call_target="tpu_custom_call" | custom-call | bytes 9519112 | tf_op jit(solution)/shard_map/pallas_call | solution.py:71
  (275 shorter events, 65.7 us)
Async XLA Ops:
  7.2 45.9 %all-gather.5.cloned.1.call-start = ((), (), s32[]{:S(2)}) async-start(), calls=%async_computation.4 | async-start | bytes 1966080 | tf_op jit(solution)/shard_map/all_gather | solution.py:677
  9.7 104.2 %all-gather.7.cloned.1.call-start = ((), (), s32[]{:S(2)}) async-start(), calls=%async_computation.5 | async-start | bytes 2949120 | tf_op jit(solution)/shard_map/all_gather | solution.py:691
  9.9 17.1 %collective-permute-start.1 = (bf16[144,1024]{1,0:T(8,128)(2,1)S(1)}, bf16[144,1024]{1,0:T(8,128)(2,1)S(1)}, u32[]{:S(2)}, u32[]{:S(2)}) collective-permute-start(bf16[144,1024]{1,0:T(8,128)(2,1)S(1)} %fusion.1.refs_3_.refs_9_), channel_id=1, source_target_pairs={{0,2},{2,0},{1,3},{3,1},{4,6},{6,4},{5,7},{7,5},{8,10},{10,8},{9,1... | collective-permute-start | bytes 884744 | tf_op jit(solution)/shard_map/ppermute | solution.py:41
  12.9 14.1 %collective-permute-start.3 = (bf16[144,1024]{1,0:T(8,128)(2,1)S(1)}, bf16[144,1024]{1,0:T(8,128)(2,1)S(1)}, u32[]{:S(2)}, u32[]{:S(2)}) collective-permute-start(bf16[144,1024]{1,0:T(8,128)(2,1)S(1)} %fusion.1.refs_3_.refs_9_), channel_id=1, source_target_pairs={{0,4},{4,0},{1,5},{5,1},{2,6},{6,2},{3,7},{7,3},{8,12},{12,8},{9,1... | collective-permute-start | bytes 884744 | tf_op jit(solution)/shard_map/ppermute | solution.py:41
  14.4 12.6 %collective-permute-start.2 = (bf16[128,1024]{1,0:T(8,128)(2,1)S(1)}, bf16[128,1024]{1,0:T(8,128)(2,1)S(1)}, u32[]{:S(2)}, u32[]{:S(2)}) collective-permute-start(bf16[128,1024]{1,0:T(8,128)(2,1)S(1)} %get-tuple-element.426.refs_2_.refs_8_), channel_id=1, source_target_pairs={{0,4},{4,0},{1,5},{5,1},{2,6},{6,2},{3,7},{7,3},{8,12},{12,8},{9,1... | collective-permute-start | bytes 786440 | tf_op jit(solution)/shard_map/ppermute | solution.py:41
  14.9 12.1 %collective-permute-start = (bf16[128,1024]{1,0:T(8,128)(2,1)S(1)}, bf16[128,1024]{1,0:T(8,128)(2,1)S(1)}, u32[]{:S(2)}, u32[]{:S(2)}) collective-permute-start(bf16[128,1024]{1,0:T(8,128)(2,1)S(1)} %get-tuple-element.426.refs_2_.refs_8_), channel_id=1, source_target_pairs={{0,2},{2,0},{1,3},{3,1},{4,6},{6,4},{5,7},{7,5},{8,10},{10,8},{9,1... | collective-permute-start | bytes 786440 | tf_op jit(solution)/shard_map/ppermute | solution.py:41
  27.9 9.3 %collective-permute-start.7 = (bf16[128,1024]{1,0:T(8,128)(2,1)S(1)}, bf16[128,1024]{1,0:T(8,128)(2,1)}, u32[]{:S(2)}, u32[]{:S(2)}) collective-permute-start(bf16[128,1024]{1,0:T(8,128)(2,1)S(1)} %get-tuple-element.269.refs_6_.refs_17_), channel_id=1, source_target_pairs={{0,2},{2,0},{1,3},{3,1},{4,6},{6,4},{5,7},{7,5},{8,10},{10,8},{9,1... | collective-permute-start | bytes 786440 | tf_op jit(solution)/shard_map/ppermute | solution.py:41
  28.3 10.5 %collective-permute-start.8 = (bf16[128,1024]{1,0:T(8,128)(2,1)}, bf16[128,1024]{1,0:T(8,128)(2,1)}, u32[]{:S(2)}, u32[]{:S(2)}) collective-permute-start(bf16[128,1024]{1,0:T(8,128)(2,1)} %get-tuple-element.268.refs_5_.refs_16_), channel_id=1, source_target_pairs={{0,4},{4,0},{1,5},{5,1},{2,6},{6,2},{3,7},{7,3},{8,12},{12,8},{9,1... | collective-permute-start | bytes 786440 | tf_op jit(solution)/shard_map/ppermute | solution.py:41
  30.0 12.8 %collective-permute-start.4 = (bf16[128,1024]{1,0:T(8,128)(2,1)S(1)}, bf16[128,1024]{1,0:T(8,128)(2,1)S(1)}, u32[]{:S(2)}, u32[]{:S(2)}) collective-permute-start(bf16[128,1024]{1,0:T(8,128)(2,1)S(1)} %collective-permute-done.2.refs_6_.refs_17_), channel_id=1, source_target_pairs={{0,2},{2,0},{1,3},{3,1},{4,6},{6,4},{5,7},{7,5},{8,10},{10,8},{9,1... | collective-permute-start | bytes 786440 | tf_op jit(solution)/shard_map/ppermute | solution.py:41
  31.4 15.8 %collective-permute-start.5 = (bf16[144,1024]{1,0:T(8,128)(2,1)S(1)}, bf16[144,1024]{1,0:T(8,128)(2,1)S(1)}, u32[]{:S(2)}, u32[]{:S(2)}) collective-permute-start(bf16[144,1024]{1,0:T(8,128)(2,1)S(1)} %collective-permute-done.1.refs_5_.refs_9_), channel_id=1, source_target_pairs={{0,4},{4,0},{1,5},{5,1},{2,6},{6,2},{3,7},{7,3},{8,12},{12,8},{9,1... | collective-permute-start | bytes 884744 | tf_op jit(solution)/shard_map/ppermute | solution.py:41
  32.0 19.6 %collective-permute-start.6 = (bf16[128,1024]{1,0:T(8,128)(2,1)}, bf16[128,1024]{1,0:T(8,128)(2,1)}, u32[]{:S(2)}, u32[]{:S(2)}) collective-permute-start(bf16[128,1024]{1,0:T(8,128)(2,1)} %get-tuple-element.268.refs_5_.refs_16_), channel_id=1, source_target_pairs={{0,2},{2,0},{1,3},{3,1},{4,6},{6,4},{5,7},{7,5},{8,10},{10,8},{9,1... | collective-permute-start | bytes 786440 | tf_op jit(solution)/shard_map/ppermute | solution.py:41
  37.2 14.3 %collective-permute-start.9 = (bf16[128,1024]{1,0:T(8,128)(2,1)S(1)}, bf16[128,1024]{1,0:T(8,128)(2,1)}, u32[]{:S(2)}, u32[]{:S(2)}) collective-permute-start(bf16[128,1024]{1,0:T(8,128)(2,1)S(1)} %get-tuple-element.269.refs_6_.refs_17_), channel_id=1, source_target_pairs={{0,4},{4,0},{1,5},{5,1},{2,6},{6,2},{3,7},{7,3},{8,12},{12,8},{9,1... | collective-permute-start | bytes 786440 | tf_op jit(solution)/shard_map/ppermute | solution.py:41
  38.8 13.0 %collective-permute-start.10 = (bf16[128,1024]{1,0:T(8,128)(2,1)}, bf16[128,1024]{1,0:T(8,128)(2,1)}, u32[]{:S(2)}, u32[]{:S(2)}) collective-permute-start(bf16[128,1024]{1,0:T(8,128)(2,1)} %collective-permute-done.8.refs_9_.refs_20_), channel_id=1, source_target_pairs={{0,2},{2,0},{1,3},{3,1},{4,6},{6,4},{5,7},{7,5},{8,10},{10,8},{9,1... | collective-permute-start | bytes 786440 | tf_op jit(solution)/shard_map/ppermute | solution.py:41
  42.8 10.4 %collective-permute-start.11 = (bf16[128,1024]{1,0:T(8,128)(2,1)}, bf16[128,1024]{1,0:T(8,128)(2,1)}, u32[]{:S(2)}, u32[]{:S(2)}) collective-permute-start(bf16[128,1024]{1,0:T(8,128)(2,1)} %collective-permute-done.7.refs_6_.refs_19_), channel_id=1, source_target_pairs={{0,4},{4,0},{1,5},{5,1},{2,6},{6,2},{3,7},{7,3},{8,12},{12,8},{9,1... | collective-permute-start | bytes 786440 | tf_op jit(solution)/shard_map/ppermute | solution.py:41
  53.2 181.7 %reduce-scatter.3.cloned.1.call-start = ((), (), s32[]{:S(2)}) async-start(), calls=%async_computation.2 | async-start | bytes 2949120 | tf_op jit(solution)/shard_map/reduce_scatter | solution.py:767
  53.4 13.1 %collective-permute-start.12 = (bf16[4,768,256]{2,1,0:T(8,128)(2,1)}, bf16[4,768,256]{2,1,0:T(8,128)(2,1)S(1)}, u32[]{:S(2)}, u32[]{:S(2)}) collective-permute-start(bf16[4,768,256]{2,1,0:T(8,128)(2,1)} %bitcast.38), channel_id=1, source_target_pairs={{0,1},{1,0},{2,3},{3,2},{4,5},{5,4},{6,7},{7,6},{8,9},{9,8},{10,11... | collective-permute-start | bytes 4718600 | tf_op jit(solution)/shard_map/ppermute | solution.py:41
  54.7 6.3 %collective-permute-start.13 = (bf16[256,256]{1,0:T(8,128)(2,1)S(1)}, bf16[256,256]{1,0:T(8,128)(2,1)S(1)}, u32[]{:S(2)}, u32[]{:S(2)}) collective-permute-start(bf16[256,256]{1,0:T(8,128)(2,1)S(1)} %get-tuple-element.417), channel_id=1, source_target_pairs={{0,2},{2,0},{1,3},{3,1},{4,6},{6,4},{5,7},{7,5},{8,10},{10,8},{9,1... | collective-permute-start | bytes 393224 | tf_op jit(solution)/shard_map/ppermute | solution.py:41
  56.2 8.3 %collective-permute-start.14 = (bf16[256,256]{1,0:T(8,128)(2,1)S(1)}, bf16[256,256]{1,0:T(8,128)(2,1)S(1)}, u32[]{:S(2)}, u32[]{:S(2)}) collective-permute-start(bf16[256,256]{1,0:T(8,128)(2,1)S(1)} %get-tuple-element.416), channel_id=1, source_target_pairs={{0,4},{4,0},{1,5},{5,1},{2,6},{6,2},{3,7},{7,3},{8,12},{12,8},{9,1... | collective-permute-start | bytes 393224 | tf_op jit(solution)/shard_map/ppermute | solution.py:41
  57.7 6.8 %collective-permute-start.15 = (bf16[256,256]{1,0:T(8,128)(2,1)S(1)}, bf16[256,256]{1,0:T(8,128)(2,1)S(1)}, u32[]{:S(2)}, u32[]{:S(2)}) collective-permute-start(bf16[256,256]{1,0:T(8,128)(2,1)S(1)} %get-tuple-element.415), channel_id=1, source_target_pairs={{0,6},{2,4},{4,2},{6,0},{1,7},{3,5},{5,3},{7,1},{8,14},{10,12},{12... | collective-permute-start | bytes 393224 | tf_op jit(solution)/shard_map/ppermute | solution.py:149
  70.9 15.7 %collective-permute-start.19 = (bf16[256,1024]{1,0:T(8,128)(2,1)S(1)}, bf16[256,1024]{1,0:T(8,128)(2,1)S(1)}, u32[]{:S(2)}, u32[]{:S(2)}) collective-permute-start(bf16[256,1024]{1,0:T(8,128)(2,1)S(1)} %get-tuple-element.262), channel_id=1, source_target_pairs={{0,6},{2,4},{4,2},{6,0},{1,7},{3,5},{5,3},{7,1},{8,14},{10,12},{12... | collective-permute-start | bytes 1572872 | tf_op jit(solution)/shard_map/ppermute | solution.py:130
  79.6 17.6 %collective-permute-start.17 = (bf16[256,1024]{1,0:T(8,128)(2,1)S(1)}, bf16[256,1024]{1,0:T(8,128)(2,1)S(1)}, u32[]{:S(2)}, u32[]{:S(2)}) collective-permute-start(bf16[256,1024]{1,0:T(8,128)(2,1)S(1)} %get-tuple-element.257), channel_id=1, source_target_pairs={{0,2},{2,0},{1,3},{3,1},{4,6},{6,4},{5,7},{7,5},{8,10},{10,8},{9,1... | collective-permute-start | bytes 1572872 | tf_op jit(solution)/shard_map/ppermute | solution.py:41
  81.0 16.1 %collective-permute-start.18 = (bf16[256,1024]{1,0:T(8,128)(2,1)S(1)}, bf16[256,1024]{1,0:T(8,128)(2,1)S(1)}, u32[]{:S(2)}, u32[]{:S(2)}) collective-permute-start(bf16[256,1024]{1,0:T(8,128)(2,1)S(1)} %get-tuple-element.258), channel_id=1, source_target_pairs={{0,4},{4,0},{1,5},{5,1},{2,6},{6,2},{3,7},{7,3},{8,12},{12,8},{9,1... | collective-permute-start | bytes 1572872 | tf_op jit(solution)/shard_map/ppermute | solution.py:41
  98.5 9.3 %collective-permute-start.21 = (bf16[128,1024]{1,0:T(8,128)(2,1)S(1)}, bf16[128,1024]{1,0:T(8,128)(2,1)}, u32[]{:S(2)}, u32[]{:S(2)}) collective-permute-start(bf16[128,1024]{1,0:T(8,128)(2,1)S(1)} %get-tuple-element.266.refs_4_.refs_1_), channel_id=1, source_target_pairs={{0,2},{2,0},{1,3},{3,1},{4,6},{6,4},{5,7},{7,5},{8,10},{10,8},{9,1... | collective-permute-start | bytes 786440 | tf_op jit(solution)/shard_map/ppermute | solution.py:41
  99.6 9.3 %collective-permute-start.22 = (bf16[128,1024]{1,0:T(8,128)(2,1)S(1)}, bf16[128,1024]{1,0:T(8,128)(2,1)}, u32[]{:S(2)}, u32[]{:S(2)}) collective-permute-start(bf16[128,1024]{1,0:T(8,128)(2,1)S(1)} %get-tuple-element.265.refs_3_.refs_0_), channel_id=1, source_target_pairs={{0,4},{4,0},{1,5},{5,1},{2,6},{6,2},{3,7},{7,3},{8,12},{12,8},{9,1... | collective-permute-start | bytes 786440 | tf_op jit(solution)/shard_map/ppermute | solution.py:41
  100.5 11.8 %collective-permute-start.20 = (bf16[128,1024]{1,0:T(8,128)(2,1)S(1)}, bf16[128,1024]{1,0:T(8,128)(2,1)S(1)}, u32[]{:S(2)}, u32[]{:S(2)}) collective-permute-start(bf16[128,1024]{1,0:T(8,128)(2,1)S(1)} %get-tuple-element.265.refs_3_.refs_0_), channel_id=1, source_target_pairs={{0,2},{2,0},{1,3},{3,1},{4,6},{6,4},{5,7},{7,5},{8,10},{10,8},{9,1... | collective-permute-start | bytes 786440 | tf_op jit(solution)/shard_map/ppermute | solution.py:41
  101.9 11.4 %collective-permute-start.23 = (bf16[128,1024]{1,0:T(8,128)(2,1)S(1)}, bf16[128,1024]{1,0:T(8,128)(2,1)S(1)}, u32[]{:S(2)}, u32[]{:S(2)}) collective-permute-start(bf16[128,1024]{1,0:T(8,128)(2,1)S(1)} %get-tuple-element.266.refs_4_.refs_1_), channel_id=1, source_target_pairs={{0,4},{4,0},{1,5},{5,1},{2,6},{6,2},{3,7},{7,3},{8,12},{12,8},{9,1... | collective-permute-start | bytes 786440 | tf_op jit(solution)/shard_map/ppermute | solution.py:41
  114.0 9.6 %collective-permute-start.24 = (bf16[4,1152,256]{2,1,0:T(8,128)(2,1)}, bf16[4,1152,256]{2,1,0:T(8,128)(2,1)S(1)}, u32[]{:S(2)}, u32[]{:S(2)}) collective-permute-start(bf16[4,1152,256]{2,1,0:T(8,128)(2,1)} %bitcast.63), channel_id=1, source_target_pairs={{0,1},{1,0},{2,3},{3,2},{4,5},{5,4},{6,7},{7,6},{8,9},{9,8},{10,11... | collective-permute-start | bytes 7077896 | tf_op jit(solution)/shard_map/ppermute | solution.py:41
  114.0 8.9 %collective-permute-start.27 = (bf16[128,1024]{1,0:T(8,128)(2,1)}, bf16[128,1024]{1,0:T(8,128)(2,1)S(1)}, u32[]{:S(2)}, u32[]{:S(2)}) collective-permute-start(bf16[128,1024]{1,0:T(8,128)(2,1)} %collective-permute-done.22.refs_7_.refs_4_), channel_id=1, source_target_pairs={{0,2},{2,0},{1,3},{3,1},{4,6},{6,4},{5,7},{7,5},{8,10},{10,8},{9,1... | collective-permute-start | bytes 786440 | tf_op jit(solution)/shard_map/ppermute | solution.py:41
  115.0 8.6 %collective-permute-start.28 = (bf16[128,1024]{1,0:T(8,128)(2,1)}, bf16[128,1024]{1,0:T(8,128)(2,1)S(1)}, u32[]{:S(2)}, u32[]{:S(2)}) collective-permute-start(bf16[128,1024]{1,0:T(8,128)(2,1)} %collective-permute-done.21.refs_4_.refs_3_), channel_id=1, source_target_pairs={{0,4},{4,0},{1,5},{5,1},{2,6},{6,2},{3,7},{7,3},{8,12},{12,8},{9,1... | collective-permute-start | bytes 786440 | tf_op jit(solution)/shard_map/ppermute | solution.py:41
  129.4 16.1 %collective-permute-start.29 = (bf16[256,1024]{1,0:T(8,128)(2,1)S(1)}, bf16[256,1024]{1,0:T(8,128)(2,1)S(1)}, u32[]{:S(2)}, u32[]{:S(2)}) collective-permute-start(bf16[256,1024]{1,0:T(8,128)(2,1)S(1)} %get-tuple-element.285), channel_id=1, source_target_pairs={{0,6},{2,4},{4,2},{6,0},{1,7},{3,5},{5,3},{7,1},{8,14},{10,12},{12... | collective-permute-start | bytes 1572872 | tf_op jit(solution)/shard_map/ppermute | solution.py:130
  138.9 15.8 %collective-permute-start.25 = (bf16[256,1024]{1,0:T(8,128)(2,1)S(1)}, bf16[256,1024]{1,0:T(8,128)(2,1)S(1)}, u32[]{:S(2)}, u32[]{:S(2)}) collective-permute-start(bf16[256,1024]{1,0:T(8,128)(2,1)S(1)} %get-tuple-element.279), channel_id=1, source_target_pairs={{0,2},{2,0},{1,3},{3,1},{4,6},{6,4},{5,7},{7,5},{8,10},{10,8},{9,1... | collective-permute-start | bytes 1572872 | tf_op jit(solution)/shard_map/ppermute | solution.py:41
  140.0 14.8 %collective-permute-start.26 = (bf16[256,1024]{1,0:T(8,128)(2,1)S(1)}, bf16[256,1024]{1,0:T(8,128)(2,1)S(1)}, u32[]{:S(2)}, u32[]{:S(2)}) collective-permute-start(bf16[256,1024]{1,0:T(8,128)(2,1)S(1)} %get-tuple-element.280), channel_id=1, source_target_pairs={{0,4},{4,0},{1,5},{5,1},{2,6},{6,2},{3,7},{7,3},{8,12},{12,8},{9,1... | collective-permute-start | bytes 1572872 | tf_op jit(solution)/shard_map/ppermute | solution.py:41
  161.4 4.6 %collective-permute-start.34 = (bf16[4,1152,256]{2,1,0:T(8,128)(2,1)S(1)}, bf16[4,1152,256]{2,1,0:T(8,128)(2,1)S(1)}, u32[]{:S(2)}, u32[]{:S(2)}) collective-permute-start(bf16[4,1152,256]{2,1,0:T(8,128)(2,1)S(1)} %shard_map.249), channel_id=1, source_target_pairs={{0,1},{1,0},{2,3},{3,2},{4,5},{5,4},{6,7},{7,6},{8,9},{9,8},{10,11... | collective-permute-start | bytes 7077896 | tf_op jit(solution)/shard_map/ppermute | solution.py:41
  161.5 11.2 %collective-permute-start.30 = (bf16[128,1024]{1,0:T(8,128)(2,1)S(1)}, bf16[128,1024]{1,0:T(8,128)(2,1)S(1)}, u32[]{:S(2)}, u32[]{:S(2)}) collective-permute-start(bf16[128,1024]{1,0:T(8,128)(2,1)S(1)} %get-tuple-element.308.refs_6_.refs_4_), channel_id=1, source_target_pairs={{0,2},{2,0},{1,3},{3,1},{4,6},{6,4},{5,7},{7,5},{8,10},{10,8},{9,1... | collective-permute-start | bytes 786440 | tf_op jit(solution)/shard_map/ppermute | solution.py:41
  162.6 13.3 %collective-permute-start.32 = (bf16[128,1024]{1,0:T(8,128)(2,1)S(1)}, bf16[128,1024]{1,0:T(8,128)(2,1)}, u32[]{:S(2)}, u32[]{:S(2)}) collective-permute-start(bf16[128,1024]{1,0:T(8,128)(2,1)S(1)} %get-tuple-element.308.refs_6_.refs_4_), channel_id=1, source_target_pairs={{0,4},{4,0},{1,5},{5,1},{2,6},{6,2},{3,7},{7,3},{8,12},{12,8},{9,1... | collective-permute-start | bytes 786440 | tf_op jit(solution)/shard_map/ppermute | solution.py:41
  163.9 12.1 %collective-permute-start.31 = (bf16[128,1024]{1,0:T(8,128)(2,1)S(1)}, bf16[128,1024]{1,0:T(8,128)(2,1)}, u32[]{:S(2)}, u32[]{:S(2)}) collective-permute-start(bf16[128,1024]{1,0:T(8,128)(2,1)S(1)} %get-tuple-element.309.refs_7_.refs_5_), channel_id=1, source_target_pairs={{0,2},{2,0},{1,3},{3,1},{4,6},{6,4},{5,7},{7,5},{8,10},{10,8},{9,1... | collective-permute-start | bytes 786440 | tf_op jit(solution)/shard_map/ppermute | solution.py:41
  164.9 11.8 %collective-permute-start.33 = (bf16[128,1024]{1,0:T(8,128)(2,1)S(1)}, bf16[128,1024]{1,0:T(8,128)(2,1)}, u32[]{:S(2)}, u32[]{:S(2)}) collective-permute-start(bf16[128,1024]{1,0:T(8,128)(2,1)S(1)} %get-tuple-element.309.refs_7_.refs_5_), channel_id=1, source_target_pairs={{0,4},{4,0},{1,5},{5,1},{2,6},{6,2},{3,7},{7,3},{8,12},{12,8},{9,1... | collective-permute-start | bytes 786440 | tf_op jit(solution)/shard_map/ppermute | solution.py:41
  176.7 119.6 %reduce-scatter.5.cloned.1.call-start = ((), (), s32[]{:S(2)}) async-start(), calls=%async_computation.3 | async-start | bytes 2007040 | tf_op jit(solution)/shard_map/reduce_scatter | solution.py:803
  176.8 12.0 %collective-permute-start.35 = (bf16[128,1024]{1,0:T(8,128)(2,1)}, bf16[128,1024]{1,0:T(8,128)(2,1)S(1)}, u32[]{:S(2)}, u32[]{:S(2)}) collective-permute-start(bf16[128,1024]{1,0:T(8,128)(2,1)} %collective-permute-done.32.refs_8_.refs_15_), channel_id=1, source_target_pairs={{0,2},{2,0},{1,3},{3,1},{4,6},{6,4},{5,7},{7,5},{8,10},{10,8},{9,1... | collective-permute-start | bytes 786440 | tf_op jit(solution)/shard_map/ppermute | solution.py:41
  177.9 10.9 %collective-permute-start.36 = (bf16[128,1024]{1,0:T(8,128)(2,1)}, bf16[128,1024]{1,0:T(8,128)(2,1)S(1)}, u32[]{:S(2)}, u32[]{:S(2)}) collective-permute-start(bf16[128,1024]{1,0:T(8,128)(2,1)} %collective-permute-done.31.refs_7_), channel_id=1, source_target_pairs={{0,4},{4,0},{1,5},{5,1},{2,6},{6,2},{3,7},{7,3},{8,12},{12,8},{9,1... | collective-permute-start | bytes 786440 | tf_op jit(solution)/shard_map/ppermute | solution.py:41
  198.8 21.3 %collective-permute-start.41 = (bf16[256,1024]{1,0:T(8,128)(2,1)S(1)}, bf16[256,1024]{1,0:T(8,128)(2,1)S(1)}, u32[]{:S(2)}, u32[]{:S(2)}) collective-permute-start(bf16[256,1024]{1,0:T(8,128)(2,1)S(1)} %copy-done.77), channel_id=1, source_target_pairs={{0,6},{2,4},{4,2},{6,0},{1,7},{3,5},{5,3},{7,1},{8,14},{10,12},{12... | collective-permute-start | bytes 1572872 | tf_op jit(solution)/shard_map/ppermute | solution.py:130
  200.1 17.1 %collective-permute-start.38 = (bf16[256,256]{1,0:T(8,128)(2,1)S(1)}, bf16[256,256]{1,0:T(8,128)(2,1)S(1)}, u32[]{:S(2)}, u32[]{:S(2)}) collective-permute-start(bf16[256,256]{1,0:T(8,128)(2,1)S(1)} %get-tuple-element.421), channel_id=1, source_target_pairs={{0,2},{2,0},{1,3},{3,1},{4,6},{6,4},{5,7},{7,5},{8,10},{10,8},{9,1... | collective-permute-start | bytes 393224 | tf_op jit(solution)/shard_map/ppermute | solution.py:41
  201.1 16.2 %collective-permute-start.39 = (bf16[256,256]{1,0:T(8,128)(2,1)S(1)}, bf16[256,256]{1,0:T(8,128)(2,1)S(1)}, u32[]{:S(2)}, u32[]{:S(2)}) collective-permute-start(bf16[256,256]{1,0:T(8,128)(2,1)S(1)} %get-tuple-element.420), channel_id=1, source_target_pairs={{0,4},{4,0},{1,5},{5,1},{2,6},{6,2},{3,7},{7,3},{8,12},{12,8},{9,1... | collective-permute-start | bytes 393224 | tf_op jit(solution)/shard_map/ppermute | solution.py:41
  202.5 16.9 %collective-permute-start.40 = (bf16[256,256]{1,0:T(8,128)(2,1)S(1)}, bf16[256,256]{1,0:T(8,128)(2,1)S(1)}, u32[]{:S(2)}, u32[]{:S(2)}) collective-permute-start(bf16[256,256]{1,0:T(8,128)(2,1)S(1)} %get-tuple-element.419), channel_id=1, source_target_pairs={{0,6},{2,4},{4,2},{6,0},{1,7},{3,5},{5,3},{7,1},{8,14},{10,12},{12... | collective-permute-start | bytes 393224 | tf_op jit(solution)/shard_map/ppermute | solution.py:149
  220.1 13.2 %collective-permute-start.42 = (bf16[256,1024]{1,0:T(8,128)(2,1)S(1)}, bf16[256,1024]{1,0:T(8,128)(2,1)S(1)}, u32[]{:S(2)}, u32[]{:S(2)}) collective-permute-start(bf16[256,1024]{1,0:T(8,128)(2,1)S(1)} %copy-done.76), channel_id=1, source_target_pairs={{0,2},{2,0},{1,3},{3,1},{4,6},{6,4},{5,7},{7,5},{8,10},{10,8},{9,1... | collective-permute-start | bytes 1572872 | tf_op jit(solution)/shard_map/ppermute | solution.py:41
  221.1 13.0 %collective-permute-start.43 = (bf16[256,1024]{1,0:T(8,128)(2,1)S(1)}, bf16[256,1024]{1,0:T(8,128)(2,1)S(1)}, u32[]{:S(2)}, u32[]{:S(2)}) collective-permute-start(bf16[256,1024]{1,0:T(8,128)(2,1)S(1)} %copy-done.75), channel_id=1, source_target_pairs={{0,4},{4,0},{1,5},{5,1},{2,6},{6,2},{3,7},{7,3},{8,12},{12,8},{9,1... | collective-permute-start | bytes 1572872 | tf_op jit(solution)/shard_map/ppermute | solution.py:41
  234.9 13.9 %collective-permute-start.44 = (bf16[1152,256]{1,0:T(8,128)(2,1)}, bf16[1152,256]{1,0:T(8,128)(2,1)S(1)}, u32[]{:S(2)}, u32[]{:S(2)}) collective-permute-start(bf16[1152,256]{1,0:T(8,128)(2,1)} %reduce-scatter.3.cloned.1.call-done.refs_0_), channel_id=1, source_target_pairs={{0,2},{2,0},{1,3},{3,1},{4,6},{6,4},{5,7},{7,5},{8,10},{10,8},{9,1... | collective-permute-start | bytes 1769480 | tf_op jit(solution)/shard_map/ppermute | solution.py:41
  235.9 13.5 %collective-permute-start.45 = (bf16[1152,256]{1,0:T(8,128)(2,1)}, bf16[1152,256]{1,0:T(8,128)(2,1)S(1)}, u32[]{:S(2)}, u32[]{:S(2)}) collective-permute-start(bf16[1152,256]{1,0:T(8,128)(2,1)} %reduce-scatter.3.cloned.1.call-done.refs_0_), channel_id=1, source_target_pairs={{0,4},{4,0},{1,5},{5,1},{2,6},{6,2},{3,7},{7,3},{8,12},{12,8},{9,1... | collective-permute-start | bytes 1769480 | tf_op jit(solution)/shard_map/ppermute | solution.py:41
  249.4 2.7 collective-permute-start.46
  257.4 9.1 %collective-permute-start.47 = (bf16[576,256]{1,0:T(8,128)(2,1)S(1)}, bf16[576,256]{1,0:T(8,128)(2,1)S(1)}, u32[]{:S(2)}, u32[]{:S(2)}) collective-permute-start(bf16[576,256]{1,0:T(8,128)(2,1)S(1)} %slice.70), channel_id=1, source_target_pairs={{0,2},{2,0},{1,3},{3,1},{4,6},{6,4},{5,7},{7,5},{8,10},{10,8},{9,1... | collective-permute-start | bytes 884744 | tf_op jit(solution)/shard_map/ppermute | solution.py:41
  258.6 8.8 %collective-permute-start.48 = (bf16[576,256]{1,0:T(8,128)(2,1)S(1)}, bf16[576,256]{1,0:T(8,128)(2,1)S(1)}, u32[]{:S(2)}, u32[]{:S(2)}) collective-permute-start(bf16[576,256]{1,0:T(8,128)(2,1)S(1)} %slice.71), channel_id=1, source_target_pairs={{0,4},{4,0},{1,5},{5,1},{2,6},{6,2},{3,7},{7,3},{8,12},{12,8},{9,1... | collective-permute-start | bytes 884744 | tf_op jit(solution)/shard_map/ppermute | solution.py:41
  267.5 2.1 collective-permute-start.49
  267.5 2.9 collective-permute-start.50
  268.0 7.3 %collective-permute-start.51 = (bf16[1152,256]{1,0:T(8,128)(2,1)S(1)}, bf16[1152,256]{1,0:T(8,128)(2,1)S(1)}, u32[]{:S(2)}, u32[]{:S(2)}) collective-permute-start(bf16[1152,256]{1,0:T(8,128)(2,1)S(1)} %collective-permute-done.45.refs_2_), channel_id=1, source_target_pairs={{0,1},{1,0},{2,3},{3,2},{4,5},{5,4},{6,7},{7,6},{8,9},{9,8},{10,11... | collective-permute-start | bytes 1769480 | tf_op jit(solution)/shard_map/ppermute | solution.py:41
  268.1 7.3 %collective-permute-start.52 = (bf16[1152,256]{1,0:T(8,128)(2,1)S(1)}, bf16[1152,256]{1,0:T(8,128)(2,1)S(1)}, u32[]{:S(2)}, u32[]{:S(2)}) collective-permute-start(bf16[1152,256]{1,0:T(8,128)(2,1)S(1)} %pad_maximum_fusion.refs_3_), channel_id=1, source_target_pairs={{0,1},{1,0},{2,3},{3,2},{4,5},{5,4},{6,7},{7,6},{8,9},{9,8},{10,11... | collective-permute-start | bytes 1769480 | tf_op jit(solution)/shard_map/ppermute | solution.py:41
  268.6 14.8 %collective-permute-start.53 = (bf16[256,1024]{1,0:T(8,128)(2,1)S(1)}, bf16[256,1024]{1,0:T(8,128)(2,1)S(1)}, u32[]{:S(2)}, u32[]{:S(2)}) collective-permute-start(bf16[256,1024]{1,0:T(8,128)(2,1)S(1)} %copy-done.79), channel_id=1, source_target_pairs={{0,2},{2,0},{1,3},{3,1},{4,6},{6,4},{5,7},{7,5},{8,10},{10,8},{9,1... | collective-permute-start | bytes 1572872 | tf_op jit(solution)/shard_map/ppermute | solution.py:41
  269.5 25.2 %collective-permute-start.54 = (bf16[256,1024]{1,0:T(8,128)(2,1)S(1)}, bf16[256,1024]{1,0:T(8,128)(2,1)S(1)}, u32[]{:S(2)}, u32[]{:S(2)}) collective-permute-start(bf16[256,1024]{1,0:T(8,128)(2,1)S(1)} %copy-done.78), channel_id=1, source_target_pairs={{0,4},{4,0},{1,5},{5,1},{2,6},{6,2},{3,7},{7,3},{8,12},{12,8},{9,1... | collective-permute-start | bytes 1572872 | tf_op jit(solution)/shard_map/ppermute | solution.py:41
  270.5 25.0 %collective-permute-start.55 = (bf16[256,1024]{1,0:T(8,128)(2,1)}, bf16[256,1024]{1,0:T(8,128)(2,1)S(1)}, u32[]{:S(2)}, u32[]{:S(2)}) collective-permute-start(bf16[256,1024]{1,0:T(8,128)(2,1)} %get-tuple-element.394), channel_id=1, source_target_pairs={{0,6},{2,4},{4,2},{6,0},{1,7},{3,5},{5,3},{7,1},{8,14},{10,12},{12... | collective-permute-start | bytes 1572872 | tf_op jit(solution)/shard_map/ppermute | solution.py:130
  296.3 12.4 %collective-permute-start.56 = (bf16[784,256]{1,0:T(8,128)(2,1)}, bf16[784,256]{1,0:T(8,128)(2,1)S(1)}, u32[]{:S(2)}, u32[]{:S(2)}) collective-permute-start(bf16[784,256]{1,0:T(8,128)(2,1)} %reduce-scatter.5.cloned.1.call-done.refs_0_), channel_id=1, source_target_pairs={{0,2},{2,0},{1,3},{3,1},{4,6},{6,4},{5,7},{7,5},{8,10},{10,8},{9,1... | collective-permute-start | bytes 1204232 | tf_op jit(solution)/shard_map/ppermute | solution.py:41
  297.2 17.7 %collective-permute-start.57 = (bf16[784,256]{1,0:T(8,128)(2,1)}, bf16[784,256]{1,0:T(8,128)(2,1)S(1)}, u32[]{:S(2)}, u32[]{:S(2)}) collective-permute-start(bf16[784,256]{1,0:T(8,128)(2,1)} %reduce-scatter.5.cloned.1.call-done.refs_0_), channel_id=1, source_target_pairs={{0,4},{4,0},{1,5},{5,1},{2,6},{6,2},{3,7},{7,3},{8,12},{12,8},{9,1... | collective-permute-start | bytes 1204232 | tf_op jit(solution)/shard_map/ppermute | solution.py:41
  298.3 16.6 %collective-permute-start.58 = (bf16[784,256]{1,0:T(8,128)(2,1)}, bf16[784,256]{1,0:T(8,128)(2,1)S(1)}, u32[]{:S(2)}, u32[]{:S(2)}) collective-permute-start(bf16[784,256]{1,0:T(8,128)(2,1)} %reduce-scatter.5.cloned.1.call-done.refs_0_), channel_id=1, source_target_pairs={{0,6},{2,4},{4,2},{6,0},{1,7},{3,5},{5,3},{7,1},{8,14},{10,12},{12... | collective-permute-start | bytes 1204232 | tf_op jit(solution)/shard_map/ppermute | solution.py:118
  314.9 2.3 collective-permute-start.60
  315.4 2.4 collective-permute-start.61
  315.5 2.9 collective-permute-start.62
  (83 other events, 838.0 us)
Sparse Core Ops, SparseCore 0:
  10.2 39.7 all-gather.4
  53.3 51.5 all-gather.6
  176.9 48.5 reduce-scatter.2
  257.4 35.8 reduce-scatter.4

commit v5 on v4

--- a/solution.py
+++ b/solution.py
@@ -128,6 +128,9 @@
 
     def send_far(self, blocks):
         return lax.ppermute(blocks[3], self.axes, [(i, 3 - i) for i in range(4)]) if self.square else blocks[-1]
+
+    def send_near(self, blocks):
+        return [swap(blocks[1], "x"), swap(blocks[2], "y")] if self.square else []
 
     def scatter(self, blocks, far=None):
         if not self.square:
@@ -406,6 +409,16 @@
     return kernel_call(body, [sds((len(blocks) * q, cb * B), BF)], [t.astype(jnp.int32)[None], *blocks], scalars=1)[0]
 
 
+def arrange_rows(plane, t, blocks):
+    q, width = blocks[0].shape
+
+    def body(where, *refs):
+        for r, ref in enumerate(refs[:-1]):
+            refs[-1][pl.ds(pl.multiple_of(plane.place(where[0], r) * q, 16), q), :] = ref[...]
+
+    return kernel_call(body, [sds((len(blocks) * q, width), BF)], [t.astype(jnp.int32)[None], *blocks], scalars=1)[0]
+
+
 def grad_columns(plane, t, lhs, rhs, half, width, size, other, below=None, gains=()):
     nblk = width // B
     flat_l, flat_r = sum(lhs, []), sum(rhs, [])
@@ -697,7 +710,7 @@
 
         def run(block, shared, ins, outs, flops, order, total=None):
             got, totals = {}, []
-            for group in order:
+            for group in [g[i : i + 2] for g in order for i in range(0, len(g), 2)]:
                 mine = [ins[r] for r in group]
                 res, tot = over_blocks(block, shared, mine, [outs(r) for r in group], flops, total)
                 got.update(zip(group, res))
@@ -719,7 +732,7 @@
             [tokens, gain_mid, *terms],
         )
         nm = plane.gather(nm0, nm1)
-        got_b, nm[1], nm[n - 2] = tie((got_b, nm[1], nm[n - 2]))
+        got_b, nm[1][1], nm[n - 2][0] = tie((got_b, nm[1][1], nm[n - 2][0]))
         wgu, wd = both(got_b), [] if spread else both(rows_to_chip(got_b, cut_b))
 
         def mlp(order):
@@ -731,7 +744,7 @@
                 2 * length * width * parts * 7 * ff, order,
             )[0]
 
-        blocks = mlp([[n - 1], list(range(1, n - 1)), [0]])
+        blocks = mlp([[0], [n - 1], list(range(1, n - 1))])
         product, dgu, partial, d_mid = ([a[r] for r in range(n)] for a in blocks)
         terms_mid = plane.scatter(d_mid)
 
@@ -749,6 +762,11 @@
             a = grad_columns(plane, t, lhs, rhs, 0, width_, size, None)
             return jnp.concatenate([lax.psum(a, "c"), jnp.stack(low, 0)], 1)
 
+        if spread:
+            make_b = lambda other: grad_mlp(core, nm, dgu, product, cot, other, size, ff)
+            product, terms_mid[-1] = tie((product, terms_mid[-1]))
+            other_b = make_b(None)
+            terms_mid, other_b = tie((terms_mid, other_b))
         d_hidden, dh0, dh1, mlp_grad = kernel_call(
             mid_back_kernel,
             [hbm((rows, width), F32), sds((half, width), BF), sds((half, width), BF), sds((1, width), F32)],
@@ -756,9 +774,7 @@
         )
         dh = plane.gather_near(dh0, dh1)
         if spread:
-            make_b = lambda other: grad_mlp(core, nm, dgu, product, cot, other, size, ff)
-            dgu, product, _ = tie((dgu, product, dh0))
-            grads_b = make_b(swap(make_b(None), "c"))
+            grads_b = make_b(swap(other_b, "c"))
         else:
             dgu = [[a] for a in dgu]
             gu_other = grad_columns(plane, t, nm, dgu, 1, 2 * ff, size, None) if halves else None
@@ -768,8 +784,8 @@
 
         def back(order, dh):
             return run(
-                functools.partial(attend_back_block, parts, wrows), [qg, kg, wa, wo],
-                {r: [*([stay(a) for a in dh[r]] if r == 0 else dh[r]), *[stay(a) for a in (*tok[r], lin[r], vals[r], *tables[r])]]
+                functools.partial(attend_back_block, parts, wrows), [qg, kg, wa, [stay(a) for a in wo]],
+                {r: [*[stay(a) for a in dh[r]], *[stay(a) for a in (*tok[r], lin[r], vals[r], *tables[r])]]
                  for g in order for r in g},
                 lambda r: [hbm((rows, parts * 4 * HEAD), BF), hbm((rows, width), term_type(r).dtype)],
                 2 * length * width * parts * 6 * HEAD, order, sds((1, width + 2 * HEAD), F32),
@@ -777,31 +793,44 @@
 
         own_back, gains = back([[0]], dh)
         dh = plane.gather_far(dh)
-        dh[n - 1], own_back = tie((dh[n - 1], own_back))
+        dh[n - 1], own_back, partial = tie((dh[n - 1], own_back, partial))
+        near_out = plane.send_near(partial)
         out = pair(lambda h, o: grad_rows(
             [stay(a) for a in mixed], [[stay(a) for a in b] for b in dh], half, h, GROUP * HEAD, n, o))
-        dh[1:], partial, out = tie((dh[1:], partial, out))
+        dh[1:], partial, out, near_out = tie((dh[1:], partial, out, near_out))
         out = exchanged(out)
         far_out = plane.send_far(partial)
         near_back, more = back([list(range(1, n - 1))], dh)
         dh[n - 1], out, far_out, near_back, partial = tie((dh[n - 1], out, far_out, near_back, partial))
-        terms_out = plane.scatter(partial, far_out)
+        terms_out = [partial[0], *near_out, far_out] if plane.square else plane.scatter(partial)
+        near_in = plane.send_near(near_back[1])
+        separate = plane.square and halves and size == n
+        if separate:
+            dh[n - 1], out = tie((dh[n - 1], arrange_rows(plane, t, out)))
+            out = lax.psum_scatter(out, "shard", scatter_dimension=0, tiled=True)
         far_back, last = back([[n - 1]], dh)
         gains = gains + more + last
-        far_back, grads_b, terms_out = tie((far_back, grads_b, terms_out))
+        far_back, grads_b, terms_out, near_in = tie((far_back, grads_b, terms_out, near_in))
         grads_b = plane.near(grads_b)
         dqkv, d_in = ([{**a, **b, **c}[r] for r in range(n)] for a, b, c in zip(own_back, near_back, far_back))
         dqkv = [[stay(a)] for a in dqkv]
         lhs = [[stay(a)] for a in nin]
         qkv_other = grad_columns(plane, t, lhs, dqkv, 1, 4 * HEAD, size, None) if halves else None
         if halves:
-            qkv_other, grads_b = tie((qkv_other, grads_b))
-        grads_a = merged(lhs, dqkv, 4 * HEAD, qkv_other, out, [mlp_grad, *gains] if halves else [])
-        grads_b, _ = tie((grads_b, grads_a))
-        grads_b = plane.far_halves(grads_b)
-        d_in, grads_b = tie((d_in, grads_b))
+            qkv_other, grads_b, out = tie((qkv_other, grads_b, out))
+        if separate:
+            grads_a = merged(lhs, dqkv, 4 * HEAD, qkv_other, None, [mlp_grad, *gains])
+            grads_b, grads_a = tie((grads_b, grads_a))
+            grads_b = plane.far_halves(grads_b)
+            d_in[n - 1], grads_b = tie((d_in[n - 1], grads_b))
+            terms_in = [d_in[0], *near_in, plane.send_far(d_in)]
+        else:
+            grads_a = merged(lhs, dqkv, 4 * HEAD, qkv_other, out)
+            grads_b = plane.far_halves(grads_b)
+            terms_in = plane.scatter(d_in)
         grads_a = lax.psum_scatter(grads_a.reshape(-1, B), "shard", scatter_dimension=0, tiled=True)
-        terms_in = plane.scatter(d_in)
+        if separate:
+            grads_a = jnp.concatenate([grads_a, out], 0)
         activations = kernel_call(out_kernel, [sds((rows, width), BF)], [hidden, *terms_out])[0]
 
         def assemble(mine, outs, write):
@@ -810,11 +839,20 @@
                 got += [(r, 1, swap(a, "c")) for r, a in enumerate(mine)]
 
             def body(where, *refs):
-                if len(outs) == 5:
-                    refs[-1][...] = jnp.zeros_like(refs[-1])
+                total = 0.0
                 for (r, other, _), ref in zip(got, refs):
                     core = jnp.bitwise_xor(where[1], other) if halves else 0
-                    write(ref, plane.place(where[0], r), core, refs[len(got) :])
+                    lines = write(ref, plane.place(where[0], r), core, refs[len(got) :])
+                    total = total + lines if separate and write is write_a else total
+                if separate and write is write_a:
+                    i = 0
+                    for out in refs[len(got) + 4 :]:
+                        for j in range(0, out.shape[1], B):
+                            k = min(B, out.shape[1])
+                            at = 0 if out.shape[1] > HEAD else HEAD * (i % 2)
+                            line = i if out.shape[1] > HEAD else 2 * width // B
+                            out[:, j : j + k] = total[line : line + 1, at : at + k]
+                            i += 1
 
             if write is write_spread:
                 body = lambda where, *refs: write(where, refs[: len(got)], refs[len(got) :])
@@ -880,9 +918,8 @@
             q, k, v, out = outs[:4]
             write_cols(ref, 0, [(0, B, q, B, 0)], src, core)
             write_cols(ref, 1, [(0, HEAD, k, HEAD, 0), (HEAD, B, v, HEAD, 0)], src, core)
-            write_rows(ref, cut_a, out_rows, src, core, out)
-            if halves:
-                outs[4][...] += ref[cut_a + cb * out_rows :, :].astype(F32)
+            write_rows(ref, cut_a + (16 if separate else 0), out_rows, src, core, out)
+            return ref[cut_a : cut_a + 16, :].astype(F32)
 
         like = lambda w: sds(w.shape, F32)
         gate_g, up_g, down_g = assemble(grads_b, [like(w_gate), like(w_up), like(w_down)], write_spread if spread else write_b)
@@ -892,14 +929,14 @@
             last_kernel, [sds((rows, width), BF)], [tokens, d_hidden, gain_in, *terms_in])[0]
         grads_a, input_grad = tie((plane.gather_whole(grads_a), input_grad))
         outs_a = [like(w_query), like(w_key), like(w_value), like(w_out)]
-        if halves:
-            query_g, key_g, value_g, out_g, gains = assemble(grads_a, outs_a + [sds((16, B), F32)], write_a)
-            gains = gains[: (2 * width + 2 * HEAD) // B].reshape(-1)
-            gains = [gains[:width], gains[width : 2 * width], gains[2 * width :]]
+        if separate:
+            gain_outs = [sds((1, k), F32) for k in (width, width, HEAD, HEAD)]
+            query_g, key_g, value_g, out_g, *gains = assemble(grads_a, outs_a + gain_outs, write_a)
+            gains = [g[0] for g in gains]
         else:
             query_g, key_g, value_g, out_g = assemble(grads_a, outs_a, write_a)
             gains = functools.reduce(jnp.add, gains)
-            gains = [gains[:, :width], mlp_grad, gains[:, width:]]
+            gains = [gains[:, :width], mlp_grad, gains[:, width : width + HEAD], gains[:, width + HEAD :]]
             gains = [g[0] for g in lax.psum(gains, ("shard", "y", "x", "c"))]
 
         return (
@@ -909,8 +946,8 @@
             query_g,
             key_g,
             value_g,
-            gains[2][:HEAD],
-            gains[2][HEAD:],
+            gains[2],
+            gains[3],
             out_g,
             gains[1],
             gate_g,

time: 336 us -> 321 us (0.955)
  local copies, waits for them, and re-layouts: 27.3 us -> 17.7 us
  waiting for transfers between devices: 122 us -> 114 us
    ppermute x56, waiting for transfers between devices: 119 us -> 103 us  [swap(): return lax.ppermute(a, axis, SWAP)]
    unnamed x163 -> x112, local copies, waits for them, and re-layouts: 24.6 us -> 13.5 us
    reduce_scatter x0 -> x1, waiting for transfers between devices: none -> 5.5 us  [body(): out = lax.psum_scatter(out, 'shard', scatter_dimension=0, tiled=True)]
    pallas_call x19 -> x20, Pallas kernels: 86 us -> 89.3 us  [kernel_call(): pl.pallas_call(body, out_shape=outs, compiler_params=pltpu.CompilerParams...]
  transfers between devices with their start and end apart: 67 -> 68, of which waited for: 39 -> 37; matrix products, arithmetic and copies ran while one was open for 1% -> 2% of each run, Pallas kernels for 27% -> 32%
where the time goes in v5:
time: 321 us; the launch traced here: 316 us
  waiting for transfers between devices  114 us (36%)
  Pallas kernels  112 us (35%)
  starting transfers between devices  56.3 us (18%)
  local copies, waits for them, and re-layouts  17.7 us (6%)
  between operations  14.7 us (5%)
    ppermute x56, waiting for transfers between devices, swap(): return lax.ppermute(a, axis, SWAP)  103 us
    pallas_call x20, Pallas kernels, kernel_call(): pl.pallas_call(body, out_shape=outs, compiler_params=pltpu.CompilerParams...  89.3 us
    ppermute x56, starting transfers between devices, swap(): return lax.ppermute(a, axis, SWAP)  47.5 us
    unnamed x112, local copies, waits for them, and re-layouts  13.5 us
    pallas_call x2, Pallas kernels, grad_columns(): pl.pallas_call(body, out_shape=out, grid_spec=pltpu.PrefetchScalarGridSpe...  9.04 us
    pallas_call x2, Pallas kernels, grad_mlp(): pl.pallas_call(body, out_shape=out, grid_spec=pltpu.PrefetchScalarGridSpe...  8.49 us
  transfers between devices with their start and end apart: 68, of which 37 were waited for; matrix products, arithmetic and copies ran while one was open for 2% of the time, Pallas kernels for 32%

profile of v5, /device:TPU:0, one launch (start us, length us, event | category | flops | bytes accessed | tf_op | source)
XLA Modules:
  0.0 315.8 jit_solution(8529535392265736605)
XLA Ops:
  7.3 2.4 shard_map.237
  9.9 3.0 collective-permute-start.1
  12.9 1.5 collective-permute-start.3
  15.0 12.0 %collective-permute-done.2.refs_6_.refs_17_ = bf16[128,1024]{1,0:T(8,128)(2,1)S(1)} collective-permute-done((bf16[128,1024]{1,0:T(8,128)(2,1)S(1)}, bf16[128,1024]{1,0:T(8,128)(2,1)S(1)}, u32[]{:S(2)}, u32[]{:S(2)}) %collective-permute-start.2) | collective-permute-done | bytes 262176 | tf_op jit(solution)/shard_map/ppermute | solution.py:41
  28.2 1.7 collective-permute-start.8
  29.9 1.5 collective-permute-start.4
  32.3 4.9 %collective-permute-done.7.refs_6_.refs_19_ = bf16[128,1024]{1,0:T(8,128)(2,1)} collective-permute-done((bf16[128,1024]{1,0:T(8,128)(2,1)S(1)}, bf16[128,1024]{1,0:T(8,128)(2,1)}, u32[]{:S(2)}, u32[]{:S(2)}) %collective-permute-start.7) | collective-permute-done | bytes 262176 | tf_op jit(solution)/shard_map/ppermute | solution.py:41
  37.2 1.5 collective-permute-start.9
  39.5 3.3 %collective-permute-done.4.refs_8_ = bf16[128,1024]{1,0:T(8,128)(2,1)S(1)} collective-permute-done((bf16[128,1024]{1,0:T(8,128)(2,1)S(1)}, bf16[128,1024]{1,0:T(8,128)(2,1)S(1)}, u32[]{:S(2)}, u32[]{:S(2)}) %collective-permute-start.4) | collective-permute-done | bytes 262176 | tf_op jit(solution)/shard_map/ppermute | solution.py:41
  42.7 1.5 collective-permute-start.11
  44.3 2.9 shard_map.239
  47.3 4.2 %shard_map.238 = (bf16[256,1024]{1,0:T(8,128)(2,1)}, f32[256,128]{1,0:T(8,128)}, f32[256,128]{1,0:T(8,128)}, f32[256,256]{1,0:T(8,128)}, bf16[256,1024]{1,0:T(8,...) custom-call(f32[1,1024]{1,0:T(1,128)S(1)} %bitcast.55, ...), custom_call_target="tpu_custom_call" | custom-call | bytes 6427136 | tf_op jit(solution)/shard_map/pallas_call | solution.py:71
  51.8 1.3 collective-permute-done.11.refs_6_.refs_23_
  54.7 1.4 collective-permute-start.13
  56.1 1.5 collective-permute-start.14
  58.3 2.8 collective-permute-done.13.refs_1_
  61.0 3.4 %collective-permute-done.14.refs_2_ = bf16[256,256]{1,0:T(8,128)(2,1)S(1)} collective-permute-done((bf16[256,256]{1,0:T(8,128)(2,1)S(1)}, bf16[256,256]{1,0:T(8,128)(2,1)S(1)}, u32[]{:S(2)}, u32[]{:S(2)}) %collective-permute-start.14) | collective-permute-done | bytes 131104 | tf_op jit(solution)/shard_map/ppermute | solution.py:41
  64.6 1.9 collective-permute-done.16.refs_5_
  66.5 4.4 %shard_map.243 = (f32[256,768]{1,0:T(8,128)}, bf16[256,256]{1,0:T(8,128)(2,1)}, bf16[256,512]{1,0:T(8,128)(2,1)}, bf16[256,1024]{1,0:T(8,128)(2,1)S(1)}) custom-call(f32[1,128]{1,0:T(1,128)S(1)} %bitcast.41, f32[1,128]{1,0:T(1,128)S(1)} %bitcast.47, bf16[4,768,256]{2,1,0:T(8,128)(2,1)S(1)} %bitcast.34, ...), custom_call_target="tpu_custom_call" | custom-call | flops 805306368 | bytes 6947840 | tf_op jit(solution)/shard_map/pallas_call | solution.py:71
  70.9 1.6 collective-permute-start.19
  72.5 7.1 %shard_map.242 = (f32[256,768]{1,0:T(8,128)}, bf16[256,256]{1,0:T(8,128)(2,1)}, bf16[256,512]{1,0:T(8,128)(2,1)}, bf16[256,1024]{1,0:T(8,128)(2,1)S(1)}, f32[256...) custom-call(f32[1,128]{1,0:T(1,128)S(1)} %bitcast.42, ...), custom_call_target="tpu_custom_call" | custom-call | flops 1610612736 | bytes 9700352 | tf_op jit(solution)/shard_map/pallas_call | solution.py:71
  79.6 1.4 collective-permute-start.17
  81.5 4.3 %shard_map.241 = (f32[256,768]{1,0:T(8,128)}, bf16[256,256]{1,0:T(8,128)(2,1)}, bf16[256,512]{1,0:T(8,128)(2,1)}, f32[256,1024]{1,0:T(8,128)S(1)}) custom-call(f32[1,128]{1,0:T(1,128)S(1)} %bitcast.43, f32[1,128]{1,0:T(1,128)S(1)} %bitcast.49, bf16[4,768,256]{2,1,0:T(8,128)(2,1)S(1)} %bitcast.36, bf16[4,768,256]{2,1,0:T(8,128)(2,1)S(1)} %collective-permute-done.12.refs_3_, ...), custom_call_target="tpu_custom_call" | custom-call | flops 805306368 | bytes 7472128 | tf_op jit(solution)/shard_map/pallas_call | solution.py:71
  86.6 10.5 %collective-permute-done.17.refs_1_ = bf16[256,1024]{1,0:T(8,128)(2,1)S(1)} collective-permute-done((bf16[256,1024]{1,0:T(8,128)(2,1)S(1)}, bf16[256,1024]{1,0:T(8,128)(2,1)S(1)}, u32[]{:S(2)}, u32[]{:S(2)}) %collective-permute-start.17) | collective-permute-done | bytes 524320 | tf_op jit(solution)/shard_map/ppermute | solution.py:41
  97.1 1.3 shard_map.244
  100.6 6.1 %collective-permute-done.20.refs_4_.refs_3_ = bf16[128,1024]{1,0:T(8,128)(2,1)S(1)} collective-permute-done((bf16[128,1024]{1,0:T(8,128)(2,1)S(1)}, bf16[128,1024]{1,0:T(8,128)(2,1)S(1)}, u32[]{:S(2)}, u32[]{:S(2)}) %collective-permute-start.20) | collective-permute-done | bytes 262176 | tf_op jit(solution)/shard_map/ppermute | solution.py:41
  108.7 1.3 collective-permute-start.28
  111.8 5.3 %collective-permute-done.27.refs_3_.refs_6_ = bf16[128,1024]{1,0:T(8,128)(2,1)S(1)} collective-permute-done((bf16[128,1024]{1,0:T(8,128)(2,1)}, bf16[128,1024]{1,0:T(8,128)(2,1)S(1)}, u32[]{:S(2)}, u32[]{:S(2)}) %collective-permute-start.27) | collective-permute-done | bytes 262176 | tf_op jit(solution)/shard_map/ppermute | solution.py:41
  118.1 1.7 copy-done.38
  119.7 4.2 %shard_map.247 = (bf16[256,768]{1,0:T(8,128)(2,1)S(1)}, bf16[256,1536]{1,0:T(8,128)(2,1)S(1)}, bf16[256,1024]{1,0:T(8,128)(2,1)}, bf16[256,1024]{1,0:T(8,128)(2,1)S(1)}) custom-call(s32[1]{0:T(128)} %bitcast.5.refs_0_.where, bf16[4,1152,256]{2,1,0:T(8,128)(2,1)S(1)} %bitcast.58, bf16[4,1152,256]{2,1,0:T(8,128)(2,1)S(1)} %collective-permute-done.22.refs_2_, ...), custom_call_target="tpu_custom_call" | custom-call | flops 2818572288 | bytes 7995396 | tf_op jit(solution)/shard_map/pallas_call | solution.py:71
  124.0 1.8 collective-permute-start.29
  125.8 7.6 %shard_map.246 = (bf16[256,768]{1,0:T(8,128)(2,1)S(1)}, bf16[256,1536]{1,0:T(8,128)(2,1)S(1)}, bf16[256,1024]{1,0:T(8,128)(2,1)}, bf16[256,1024]{1,0:T(8,128)(2,...) custom-call(s32[1]{0:T(128)} %bitcast.5.refs_0_.where, ...), custom_call_target="tpu_custom_call" | custom-call | flops 5637144576 | bytes 11272196 | tf_op jit(solution)/shard_map/pallas_call | solution.py:71
  135.2 4.8 %shard_map.245 = (bf16[256,768]{1,0:T(8,128)(2,1)S(1)}, bf16[256,1536]{1,0:T(8,128)(2,1)S(1)}, f32[256,1024]{1,0:T(8,128)}, f32[256,1024]{1,0:T(8,128)S(1)}) custom-call(s32[1]{0:T(128)} %bitcast.5.refs_0_.where, bf16[4,1152,256]{2,1,0:T(8,128)(2,1)S(1)} %bitcast.60, bf16[4,1152,256]{2,1,0:T(8,128)(2,1)S(1)} %collective-permute-done.22.refs_2_, ...), custom_call_target="tpu_custom_call" | custom-call | flops 2818572288 | bytes 9043972 | tf_op jit(solution)/shard_map/pallas_call | solution.py:71
  140.1 4.2 %shard_map.248 = bf16[4,1152,256]{2,1,0:T(8,128)(2,1)S(1)} custom-call(s32[1]{0:T(128)} %bitcast.5.refs_0_.where, bf16[128,1024]{1,0:T(8,128)(2,1)S(1)} %get-tuple-element.275.refs_3_.refs_0_, bf16[128,1024]{1,0:T(8,128)(2,1)S(1)} %copy-done.41, bf16[128,1024]{1,0:T(8,128)(2,1)S(1)} %collective-permute-done.23.refs_3_.refs_2_, ...), custom_call_target="tpu_custom_call" | custom-call | flops 4831838208 | bytes 8912896 | tf_op jit(solution)/shard_map/pallas_call | solution.py:554
  144.3 4.2 %collective-permute-done.25.refs_1_ = bf16[256,1024]{1,0:T(8,128)(2,1)S(1)} collective-permute-done((bf16[256,1024]{1,0:T(8,128)(2,1)S(1)}, bf16[256,1024]{1,0:T(8,128)(2,1)S(1)}, u32[]{:S(2)}, u32[]{:S(2)}) %collective-permute-start.25) | collective-permute-done | bytes 524320 | tf_op jit(solution)/shard_map/ppermute | solution.py:41
  148.8 1.7 shard_map.249
  154.6 4.3 %shard_map.250 = bf16[4,1152,256]{2,1,0:T(8,128)(2,1)S(1)} custom-call(s32[1]{0:T(128)} %bitcast.5.refs_0_.where, bf16[128,1024]{1,0:T(8,128)(2,1)S(1)} %get-tuple-element.275.refs_3_.refs_0_, bf16[128,1024]{1,0:T(8,128)(2,1)S(1)} %copy-done.41, bf16[128,1024]{1,0:T(8,128)(2,1)S(1)} %collective-permute-done.23.refs_3_.refs_2_, ...), custom_call_target="tpu_custom_call" | custom-call | flops 4831838208 | bytes 11272192 | tf_op jit(solution)/shard_map/pallas_call | solution.py:554
  158.9 1.4 copy-done.12
  160.3 4.5 %collective-permute-done.31.refs_7_ = bf16[128,1024]{1,0:T(8,128)(2,1)S(1)} collective-permute-done((bf16[128,1024]{1,0:T(8,128)(2,1)S(1)}, bf16[128,1024]{1,0:T(8,128)(2,1)S(1)}, u32[]{:S(2)}, u32[]{:S(2)}) %collective-permute-start.31) | collective-permute-done | bytes 262176 | tf_op jit(solution)/shard_map/ppermute | solution.py:41
  169.5 7.8 %shard_map.251 = (bf16[256,1024]{1,0:T(8,128)(2,1)}, f32[256,1024]{1,0:T(8,128)}, f32[1,1280]{1,0:T(1,128)S(1)}) custom-call(f32[1,128]{1,0:T(1,128)S(1)} %bitcast.44, f32[1,128]{1,0:T(1,128)S(1)} %bitcast.50, bf16[4,768,256]{2,1,0:T(8,128)(2,1)S(1)} %bitcast.37, bf16[4,768,256]{2,1,0:T(8,128)(2,1)S(1)} %collective-permute-done.12.refs_3_, ...), custom_call_target="tpu_custom_call" | custom-call | flops 805306368 | bytes 8296448 | tf_op jit(solution)/shard_map/pallas_call | solution.py:71
  178.1 3.6 %shard_map.252 = bf16[4,256,256]{2,1,0:T(8,128)(2,1)S(1)} custom-call(bf16[256,512]{1,0:T(8,128)(2,1)} %get-tuple-element.336.refs_0_, bf16[256,512]{1,0:T(8,128)(2,1)} %get-tuple-element.337.refs_1_, bf16[256,512]{1,0:T(8,128)(2,1)} %get-tuple-element.338.refs_2_, bf16[256,512]{1,0:T(8,128)(2,1)} %get-tuple-element.339.refs_3_, ...), custom_call_target="tpu_custom_call" | custom-call | flops 536870912 | bytes 3670016 | tf_op jit(solution)/shard_map/pallas_call | solution.py:71
  183.7 3.6 %shard_map.253 = bf16[4,256,256]{2,1,0:T(8,128)(2,1)S(1)} custom-call(bf16[256,512]{1,0:T(8,128)(2,1)} %get-tuple-element.336.refs_0_, bf16[256,512]{1,0:T(8,128)(2,1)} %get-tuple-element.337.refs_1_, bf16[256,512]{1,0:T(8,128)(2,1)} %get-tuple-element.338.refs_2_, bf16[256,512]{1,0:T(8,128)(2,1)} %get-tuple-element.339.refs_3_, ...), custom_call_target="tpu_custom_call" | custom-call | flops 536870912 | bytes 4194304 | tf_op jit(solution)/shard_map/pallas_call | solution.py:71
  187.3 8.9 %collective-permute-done.38.refs_1_ = bf16[256,1024]{1,0:T(8,128)(2,1)S(1)} collective-permute-done((bf16[256,1024]{1,0:T(8,128)(2,1)S(1)}, bf16[256,1024]{1,0:T(8,128)(2,1)S(1)}, u32[]{:S(2)}, u32[]{:S(2)}) %collective-permute-start.38) | collective-permute-done | bytes 524320 | tf_op jit(solution)/shard_map/ppermute | solution.py:41
  199.3 1.3 collective-permute-start.41
  201.8 13.2 %shard_map.254 = (bf16[256,1024]{1,0:T(8,128)(2,1)}, bf16[256,1024]{1,0:T(8,128)(2,1)}, bf16[256,1024]{1,0:T(8,128)(2,1)}, bf16[256,1024]{1,0:T(8,128)(2,1)}, f32[1,1280]{1,0:T(1,128)S(1)}) custom-call(f32[1,128]{1,0:T(1,128)S(1)} %bitcast.45, f32[1,128]{1,0:T(1,128)S(1)} %bitcast.51, bf16[4,768,256]{2,1,0:T(8,128)(2,1)S(1)} %bitcast.38, ...), custom_call_target="tpu_custom_call" | custom-call | flops 1610612736 | bytes 11343872 | tf_op jit(solution)/shard_map/pallas_call | solution.py:71
  215.3 1.4 collective-permute-done.42.refs_3_
  220.5 7.6 %shard_map.256 = (bf16[256,1024]{1,0:T(8,128)(2,1)}, bf16[256,1024]{1,0:T(8,128)(2,1)}, f32[1,1280]{1,0:T(1,128)S(1)}) custom-call(f32[1,128]{1,0:T(1,128)S(1)} %bitcast.46, f32[1,128]{1,0:T(1,128)S(1)} %bitcast.52, bf16[4,768,256]{2,1,0:T(8,128)(2,1)S(1)} %bitcast.39, bf16[4,768,256]{2,1,0:T(8,128)(2,1)S(1)} %collective-permute-done.12.refs_3_, ...), custom_call_target="tpu_custom_call" | custom-call | flops 805306368 | bytes 7772160 | tf_op jit(solution)/shard_map/pallas_call | solution.py:71
  228.0 2.3 collective-permute-done.44.refs_1_
  232.8 4.1 %shard_map.257 = bf16[4,512,256]{2,1,0:T(8,128)(2,1)S(1)} custom-call(s32[1]{0:T(128)} %bitcast.where, bf16[256,1024]{1,0:T(8,128)(2,1)} %get-tuple-element.251.refs_6_.refs_0_, bf16[256,1024]{1,0:T(8,128)(2,1)} %get-tuple-element.252.refs_6_.refs_1_, bf16[256,1024]{1,0:T(8,128)(2,1)} %get-tuple-element.253.refs_10_.refs_2_, ...), custom_call_target="tpu_custom_call" | custom-call | flops 1073741824 | bytes 5242880 | tf_op jit(solution)/shard_map/pallas_call | solution.py:469
  236.9 5.5 %reduce-scatter.6.cloned.1.call-done = bf16[256,256]{1,0:T(8,128)(2,1)} async-done(((bf16[1024,256]{1,0:T(8,128)(2,1)}), bf16[256,256]{1,0:T(8,128)(2,1)}) %reduce-scatter.6.cloned.1.call-update) | async-done | bytes 131088 | tf_op jit(solution)/shard_map/reduce_scatter | solution.py:810
  242.4 1.5 collective-permute-done.46.refs_1_
  244.7 2.7 collective-permute-done.48.refs_12_
  247.3 4.9 %shard_map.258 = bf16[4,528,256]{2,1,0:T(8,128)(2,1)} custom-call(s32[1]{0:T(128)} %bitcast.where, bf16[256,1024]{1,0:T(8,128)(2,1)} %get-tuple-element.251.refs_6_.refs_0_, bf16[256,1024]{1,0:T(8,128)(2,1)} %get-tuple-element.252.refs_6_.refs_1_, bf16[256,1024]{1,0:T(8,128)(2,1)} %get-tuple-element.253.refs_10_.refs_2_, ...), custom_call_target="tpu_custom_call" | custom-call | flops 1073741824 | bytes 6333952 | tf_op jit(solution)/shard_map/pallas_call | solution.py:469
  256.4 6.2 %collective-permute-done.49 = bf16[576,256]{1,0:T(8,128)(2,1)S(1)} collective-permute-done((bf16[576,256]{1,0:T(8,128)(2,1)S(1)}, bf16[576,256]{1,0:T(8,128)(2,1)S(1)}, u32[]{:S(2)}, u32[]{:S(2)}) %collective-permute-start.49) | collective-permute-done | bytes 294944 | tf_op jit(solution)/shard_map/ppermute | solution.py:41
  262.6 1.7 collective-permute-done.50
  265.4 1.3 collective-permute-start.55
  271.0 6.2 %shard_map.259 = (f32[256,3072]{1,0:T(8,128)}, f32[256,3072]{1,0:T(8,128)}, f32[768,1024]{1,0:T(8,128)}) custom-call(s32[2]{0:T(128)S(1)} %pad_add_fusion.1.w.where, bf16[1152,256]{1,0:T(8,128)(2,1)S(1)} %copy-done.25, bf16[1152,256]{1,0:T(8,128)(2,1)} %collective-permute-done.46.refs_1_, bf16[1152,256]{1,0:T(8,128)(2,1)} %collective-permute-done.47.refs_2_, ...), custom_call_target="tpu_custom_call" | custom-call | bytes 14155784 | tf_op jit(solution)/shard_map/pallas_call | solution.py:71
  277.2 3.0 reduce-scatter.8.cloned.1.call-done
  281.2 1.5 collective-permute-start.56
  282.7 1.5 collective-permute-start.57
  287.2 2.8 shard_map.261
  289.9 3.5 %collective-permute-done.56.refs_1_ = bf16[784,256]{1,0:T(8,128)(2,1)S(1)} collective-permute-done((bf16[784,256]{1,0:T(8,128)(2,1)S(1)}, bf16[784,256]{1,0:T(8,128)(2,1)S(1)}, u32[]{:S(2)}, u32[]{:S(2)}) %collective-permute-start.56) | collective-permute-done | bytes 401440 | tf_op jit(solution)/shard_map/ppermute | solution.py:41
  293.4 8.4 %collective-permute-done.57.refs_2_ = bf16[784,256]{1,0:T(8,128)(2,1)S(1)} collective-permute-done((bf16[784,256]{1,0:T(8,128)(2,1)S(1)}, bf16[784,256]{1,0:T(8,128)(2,1)S(1)}, u32[]{:S(2)}, u32[]{:S(2)}) %collective-permute-start.57) | collective-permute-done | bytes 401440 | tf_op jit(solution)/shard_map/ppermute | solution.py:41
  305.3 3.7 %shard_map.262 = (f32[256,2048]{1,0:T(8,128)}, f32[256,1024]{1,0:T(8,128)}, f32[256,1024]{1,0:T(8,128)}, f32[512,1024]{1,0:T(8,128)}, f32[1,1024]{1,0:T(1,128)},...) custom-call(s32[2]{0:T(128)S(1)} %pad_add_fusion.1.w.where, ...), custom_call_target="tpu_custom_call" | custom-call | bytes 9511944 | tf_op jit(solution)/shard_map/pallas_call | solution.py:71
  (228 shorter events, 56.6 us)
Async XLA Ops:
  7.2 45.9 %all-gather.5.cloned.1.call-start = ((), (), s32[]{:S(2)}) async-start(), calls=%async_computation.6 | async-start | bytes 1966080 | tf_op jit(solution)/shard_map/all_gather | solution.py:690
  9.7 98.0 %all-gather.7.cloned.1.call-start = ((), (), s32[]{:S(2)}) async-start(), calls=%async_computation.7 | async-start | bytes 2949120 | tf_op jit(solution)/shard_map/all_gather | solution.py:704
  9.9 17.1 %collective-permute-start.1 = (bf16[144,1024]{1,0:T(8,128)(2,1)S(1)}, bf16[144,1024]{1,0:T(8,128)(2,1)S(1)}, u32[]{:S(2)}, u32[]{:S(2)}) collective-permute-start(bf16[144,1024]{1,0:T(8,128)(2,1)S(1)} %fusion.1.refs_3_.refs_9_), channel_id=1, source_target_pairs={{0,2},{2,0},{1,3},{3,1},{4,6},{6,4},{5,7},{7,5},{8,10},{10,8},{9,1... | collective-permute-start | bytes 884744 | tf_op jit(solution)/shard_map/ppermute | solution.py:41
  12.9 14.1 %collective-permute-start.3 = (bf16[144,1024]{1,0:T(8,128)(2,1)S(1)}, bf16[144,1024]{1,0:T(8,128)(2,1)S(1)}, u32[]{:S(2)}, u32[]{:S(2)}) collective-permute-start(bf16[144,1024]{1,0:T(8,128)(2,1)S(1)} %fusion.1.refs_3_.refs_9_), channel_id=1, source_target_pairs={{0,4},{4,0},{1,5},{5,1},{2,6},{6,2},{3,7},{7,3},{8,12},{12,8},{9,1... | collective-permute-start | bytes 884744 | tf_op jit(solution)/shard_map/ppermute | solution.py:41
  14.4 12.6 %collective-permute-start.2 = (bf16[128,1024]{1,0:T(8,128)(2,1)S(1)}, bf16[128,1024]{1,0:T(8,128)(2,1)S(1)}, u32[]{:S(2)}, u32[]{:S(2)}) collective-permute-start(bf16[128,1024]{1,0:T(8,128)(2,1)S(1)} %get-tuple-element.444.refs_2_.refs_8_), channel_id=1, source_target_pairs={{0,4},{4,0},{1,5},{5,1},{2,6},{6,2},{3,7},{7,3},{8,12},{12,8},{9,1... | collective-permute-start | bytes 786440 | tf_op jit(solution)/shard_map/ppermute | solution.py:41
  14.9 12.1 %collective-permute-start = (bf16[128,1024]{1,0:T(8,128)(2,1)S(1)}, bf16[128,1024]{1,0:T(8,128)(2,1)S(1)}, u32[]{:S(2)}, u32[]{:S(2)}) collective-permute-start(bf16[128,1024]{1,0:T(8,128)(2,1)S(1)} %get-tuple-element.444.refs_2_.refs_8_), channel_id=1, source_target_pairs={{0,2},{2,0},{1,3},{3,1},{4,6},{6,4},{5,7},{7,5},{8,10},{10,8},{9,1... | collective-permute-start | bytes 786440 | tf_op jit(solution)/shard_map/ppermute | solution.py:41
  27.9 9.3 %collective-permute-start.7 = (bf16[128,1024]{1,0:T(8,128)(2,1)S(1)}, bf16[128,1024]{1,0:T(8,128)(2,1)}, u32[]{:S(2)}, u32[]{:S(2)}) collective-permute-start(bf16[128,1024]{1,0:T(8,128)(2,1)S(1)} %get-tuple-element.278.refs_6_.refs_17_), channel_id=1, source_target_pairs={{0,2},{2,0},{1,3},{3,1},{4,6},{6,4},{5,7},{7,5},{8,10},{10,8},{9,1... | collective-permute-start | bytes 786440 | tf_op jit(solution)/shard_map/ppermute | solution.py:41
  28.2 10.5 %collective-permute-start.8 = (bf16[128,1024]{1,0:T(8,128)(2,1)}, bf16[128,1024]{1,0:T(8,128)(2,1)}, u32[]{:S(2)}, u32[]{:S(2)}) collective-permute-start(bf16[128,1024]{1,0:T(8,128)(2,1)} %get-tuple-element.277.refs_5_.refs_16_), channel_id=1, source_target_pairs={{0,4},{4,0},{1,5},{5,1},{2,6},{6,2},{3,7},{7,3},{8,12},{12,8},{9,1... | collective-permute-start | bytes 786440 | tf_op jit(solution)/shard_map/ppermute | solution.py:41
  29.9 12.8 %collective-permute-start.4 = (bf16[128,1024]{1,0:T(8,128)(2,1)S(1)}, bf16[128,1024]{1,0:T(8,128)(2,1)S(1)}, u32[]{:S(2)}, u32[]{:S(2)}) collective-permute-start(bf16[128,1024]{1,0:T(8,128)(2,1)S(1)} %collective-permute-done.2.refs_6_.refs_17_), channel_id=1, source_target_pairs={{0,2},{2,0},{1,3},{3,1},{4,6},{6,4},{5,7},{7,5},{8,10},{10,8},{9,1... | collective-permute-start | bytes 786440 | tf_op jit(solution)/shard_map/ppermute | solution.py:41
  31.4 15.8 %collective-permute-start.5 = (bf16[144,1024]{1,0:T(8,128)(2,1)S(1)}, bf16[144,1024]{1,0:T(8,128)(2,1)S(1)}, u32[]{:S(2)}, u32[]{:S(2)}) collective-permute-start(bf16[144,1024]{1,0:T(8,128)(2,1)S(1)} %collective-permute-done.1.refs_5_.refs_9_), channel_id=1, source_target_pairs={{0,4},{4,0},{1,5},{5,1},{2,6},{6,2},{3,7},{7,3},{8,12},{12,8},{9,1... | collective-permute-start | bytes 884744 | tf_op jit(solution)/shard_map/ppermute | solution.py:41
  31.9 19.6 %collective-permute-start.6 = (bf16[128,1024]{1,0:T(8,128)(2,1)}, bf16[128,1024]{1,0:T(8,128)(2,1)}, u32[]{:S(2)}, u32[]{:S(2)}) collective-permute-start(bf16[128,1024]{1,0:T(8,128)(2,1)} %get-tuple-element.277.refs_5_.refs_16_), channel_id=1, source_target_pairs={{0,2},{2,0},{1,3},{3,1},{4,6},{6,4},{5,7},{7,5},{8,10},{10,8},{9,1... | collective-permute-start | bytes 786440 | tf_op jit(solution)/shard_map/ppermute | solution.py:41
  37.2 14.3 %collective-permute-start.9 = (bf16[128,1024]{1,0:T(8,128)(2,1)S(1)}, bf16[128,1024]{1,0:T(8,128)(2,1)}, u32[]{:S(2)}, u32[]{:S(2)}) collective-permute-start(bf16[128,1024]{1,0:T(8,128)(2,1)S(1)} %get-tuple-element.278.refs_6_.refs_17_), channel_id=1, source_target_pairs={{0,4},{4,0},{1,5},{5,1},{2,6},{6,2},{3,7},{7,3},{8,12},{12,8},{9,1... | collective-permute-start | bytes 786440 | tf_op jit(solution)/shard_map/ppermute | solution.py:41
  38.7 13.0 %collective-permute-start.10 = (bf16[128,1024]{1,0:T(8,128)(2,1)}, bf16[128,1024]{1,0:T(8,128)(2,1)}, u32[]{:S(2)}, u32[]{:S(2)}) collective-permute-start(bf16[128,1024]{1,0:T(8,128)(2,1)} %collective-permute-done.8.refs_9_.refs_20_), channel_id=1, source_target_pairs={{0,2},{2,0},{1,3},{3,1},{4,6},{6,4},{5,7},{7,5},{8,10},{10,8},{9,1... | collective-permute-start | bytes 786440 | tf_op jit(solution)/shard_map/ppermute | solution.py:41
  42.7 10.4 %collective-permute-start.11 = (bf16[128,1024]{1,0:T(8,128)(2,1)}, bf16[128,1024]{1,0:T(8,128)(2,1)}, u32[]{:S(2)}, u32[]{:S(2)}) collective-permute-start(bf16[128,1024]{1,0:T(8,128)(2,1)} %collective-permute-done.7.refs_6_.refs_19_), channel_id=1, source_target_pairs={{0,4},{4,0},{1,5},{5,1},{2,6},{6,2},{3,7},{7,3},{8,12},{12,8},{9,1... | collective-permute-start | bytes 786440 | tf_op jit(solution)/shard_map/ppermute | solution.py:41
  53.1 177.8 %reduce-scatter.4.cloned.1.call-start = ((), (), s32[]{:S(2)}) async-start(), calls=%async_computation.3 | async-start | bytes 2949120 | tf_op jit(solution)/shard_map/reduce_scatter | solution.py:783
  53.4 13.1 %collective-permute-start.12 = (bf16[4,768,256]{2,1,0:T(8,128)(2,1)}, bf16[4,768,256]{2,1,0:T(8,128)(2,1)S(1)}, u32[]{:S(2)}, u32[]{:S(2)}) collective-permute-start(bf16[4,768,256]{2,1,0:T(8,128)(2,1)} %bitcast.32), channel_id=1, source_target_pairs={{0,1},{1,0},{2,3},{3,2},{4,5},{5,4},{6,7},{7,6},{8,9},{9,8},{10,11... | collective-permute-start | bytes 4718600 | tf_op jit(solution)/shard_map/ppermute | solution.py:41
  54.7 6.3 %collective-permute-start.13 = (bf16[256,256]{1,0:T(8,128)(2,1)S(1)}, bf16[256,256]{1,0:T(8,128)(2,1)S(1)}, u32[]{:S(2)}, u32[]{:S(2)}) collective-permute-start(bf16[256,256]{1,0:T(8,128)(2,1)S(1)} %get-tuple-element.435), channel_id=1, source_target_pairs={{0,2},{2,0},{1,3},{3,1},{4,6},{6,4},{5,7},{7,5},{8,10},{10,8},{9,1... | collective-permute-start | bytes 393224 | tf_op jit(solution)/shard_map/ppermute | solution.py:41
  56.1 8.3 %collective-permute-start.14 = (bf16[256,256]{1,0:T(8,128)(2,1)S(1)}, bf16[256,256]{1,0:T(8,128)(2,1)S(1)}, u32[]{:S(2)}, u32[]{:S(2)}) collective-permute-start(bf16[256,256]{1,0:T(8,128)(2,1)S(1)} %get-tuple-element.434), channel_id=1, source_target_pairs={{0,4},{4,0},{1,5},{5,1},{2,6},{6,2},{3,7},{7,3},{8,12},{12,8},{9,1... | collective-permute-start | bytes 393224 | tf_op jit(solution)/shard_map/ppermute | solution.py:41
  57.6 6.8 %collective-permute-start.15 = (bf16[256,256]{1,0:T(8,128)(2,1)S(1)}, bf16[256,256]{1,0:T(8,128)(2,1)S(1)}, u32[]{:S(2)}, u32[]{:S(2)}) collective-permute-start(bf16[256,256]{1,0:T(8,128)(2,1)S(1)} %get-tuple-element.433), channel_id=1, source_target_pairs={{0,6},{2,4},{4,2},{6,0},{1,7},{3,5},{5,3},{7,1},{8,14},{10,12},{12... | collective-permute-start | bytes 393224 | tf_op jit(solution)/shard_map/ppermute | solution.py:152
  70.9 15.7 %collective-permute-start.19 = (bf16[256,1024]{1,0:T(8,128)(2,1)S(1)}, bf16[256,1024]{1,0:T(8,128)(2,1)S(1)}, u32[]{:S(2)}, u32[]{:S(2)}) collective-permute-start(bf16[256,1024]{1,0:T(8,128)(2,1)S(1)} %get-tuple-element.271), channel_id=1, source_target_pairs={{0,6},{2,4},{4,2},{6,0},{1,7},{3,5},{5,3},{7,1},{8,14},{10,12},{12... | collective-permute-start | bytes 1572872 | tf_op jit(solution)/shard_map/ppermute | solution.py:130
  79.6 17.6 %collective-permute-start.17 = (bf16[256,1024]{1,0:T(8,128)(2,1)S(1)}, bf16[256,1024]{1,0:T(8,128)(2,1)S(1)}, u32[]{:S(2)}, u32[]{:S(2)}) collective-permute-start(bf16[256,1024]{1,0:T(8,128)(2,1)S(1)} %get-tuple-element.266), channel_id=1, source_target_pairs={{0,2},{2,0},{1,3},{3,1},{4,6},{6,4},{5,7},{7,5},{8,10},{10,8},{9,1... | collective-permute-start | bytes 1572872 | tf_op jit(solution)/shard_map/ppermute | solution.py:41
  81.0 16.1 %collective-permute-start.18 = (bf16[256,1024]{1,0:T(8,128)(2,1)S(1)}, bf16[256,1024]{1,0:T(8,128)(2,1)S(1)}, u32[]{:S(2)}, u32[]{:S(2)}) collective-permute-start(bf16[256,1024]{1,0:T(8,128)(2,1)S(1)} %get-tuple-element.267), channel_id=1, source_target_pairs={{0,4},{4,0},{1,5},{5,1},{2,6},{6,2},{3,7},{7,3},{8,12},{12,8},{9,1... | collective-permute-start | bytes 1572872 | tf_op jit(solution)/shard_map/ppermute | solution.py:41
  98.4 8.2 %collective-permute-start.20 = (bf16[128,1024]{1,0:T(8,128)(2,1)S(1)}, bf16[128,1024]{1,0:T(8,128)(2,1)S(1)}, u32[]{:S(2)}, u32[]{:S(2)}) collective-permute-start(bf16[128,1024]{1,0:T(8,128)(2,1)S(1)} %get-tuple-element.274.refs_4_.refs_1_), channel_id=1, source_target_pairs={{0,2},{2,0},{1,3},{3,1},{4,6},{6,4},{5,7},{7,5},{8,10},{10,8},{9,1... | collective-permute-start | bytes 786440 | tf_op jit(solution)/shard_map/ppermute | solution.py:41
  99.6 8.2 %collective-permute-start.21 = (bf16[128,1024]{1,0:T(8,128)(2,1)S(1)}, bf16[128,1024]{1,0:T(8,128)(2,1)}, u32[]{:S(2)}, u32[]{:S(2)}) collective-permute-start(bf16[128,1024]{1,0:T(8,128)(2,1)S(1)} %get-tuple-element.275.refs_3_.refs_0_), channel_id=1, source_target_pairs={{0,4},{4,0},{1,5},{5,1},{2,6},{6,2},{3,7},{7,3},{8,12},{12,8},{9,1... | collective-permute-start | bytes 786440 | tf_op jit(solution)/shard_map/ppermute | solution.py:41
  107.7 10.3 %collective-permute-start.22 = (bf16[4,1152,256]{2,1,0:T(8,128)(2,1)}, bf16[4,1152,256]{2,1,0:T(8,128)(2,1)S(1)}, u32[]{:S(2)}, u32[]{:S(2)}) collective-permute-start(bf16[4,1152,256]{2,1,0:T(8,128)(2,1)} %bitcast.57), channel_id=1, source_target_pairs={{0,1},{1,0},{2,3},{3,2},{4,5},{5,4},{6,7},{7,6},{8,9},{9,8},{10,11... | collective-permute-start | bytes 7077896 | tf_op jit(solution)/shard_map/ppermute | solution.py:41
  107.7 9.3 %collective-permute-start.27 = (bf16[128,1024]{1,0:T(8,128)(2,1)}, bf16[128,1024]{1,0:T(8,128)(2,1)S(1)}, u32[]{:S(2)}, u32[]{:S(2)}) collective-permute-start(bf16[128,1024]{1,0:T(8,128)(2,1)} %collective-permute-done.21.refs_7_.refs_4_), channel_id=1, source_target_pairs={{0,2},{2,0},{1,3},{3,1},{4,6},{6,4},{5,7},{7,5},{8,10},{10,8},{9,1... | collective-permute-start | bytes 786440 | tf_op jit(solution)/shard_map/ppermute | solution.py:41
  108.7 9.4 %collective-permute-start.28 = (bf16[128,1024]{1,0:T(8,128)(2,1)}, bf16[128,1024]{1,0:T(8,128)(2,1)S(1)}, u32[]{:S(2)}, u32[]{:S(2)}) collective-permute-start(bf16[128,1024]{1,0:T(8,128)(2,1)} %copy-done.42), channel_id=1, source_target_pairs={{0,4},{4,0},{1,5},{5,1},{2,6},{6,2},{3,7},{7,3},{8,12},{12,8},{9,1... | collective-permute-start | bytes 786440 | tf_op jit(solution)/shard_map/ppermute | solution.py:41
  110.1 15.7 %collective-permute-start.23 = (bf16[128,1024]{1,0:T(8,128)(2,1)S(1)}, bf16[128,1024]{1,0:T(8,128)(2,1)S(1)}, u32[]{:S(2)}, u32[]{:S(2)}) collective-permute-start(bf16[128,1024]{1,0:T(8,128)(2,1)S(1)} %get-tuple-element.275.refs_3_.refs_0_), channel_id=1, source_target_pairs={{0,2},{2,0},{1,3},{3,1},{4,6},{6,4},{5,7},{7,5},{8,10},{10,8},{9,1... | collective-permute-start | bytes 786440 | tf_op jit(solution)/shard_map/ppermute | solution.py:41
  111.0 14.8 %collective-permute-start.24 = (bf16[128,1024]{1,0:T(8,128)(2,1)}, bf16[128,1024]{1,0:T(8,128)(2,1)S(1)}, u32[]{:S(2)}, u32[]{:S(2)}) collective-permute-start(bf16[128,1024]{1,0:T(8,128)(2,1)} %copy-done.40), channel_id=1, source_target_pairs={{0,4},{4,0},{1,5},{5,1},{2,6},{6,2},{3,7},{7,3},{8,12},{12,8},{9,1... | collective-permute-start | bytes 786440 | tf_op jit(solution)/shard_map/ppermute | solution.py:41
  124.0 16.1 %collective-permute-start.29 = (bf16[256,1024]{1,0:T(8,128)(2,1)S(1)}, bf16[256,1024]{1,0:T(8,128)(2,1)S(1)}, u32[]{:S(2)}, u32[]{:S(2)}) collective-permute-start(bf16[256,1024]{1,0:T(8,128)(2,1)S(1)} %get-tuple-element.296), channel_id=1, source_target_pairs={{0,6},{2,4},{4,2},{6,0},{1,7},{3,5},{5,3},{7,1},{8,14},{10,12},{12... | collective-permute-start | bytes 1572872 | tf_op jit(solution)/shard_map/ppermute | solution.py:130
  133.4 15.1 %collective-permute-start.25 = (bf16[256,1024]{1,0:T(8,128)(2,1)S(1)}, bf16[256,1024]{1,0:T(8,128)(2,1)S(1)}, u32[]{:S(2)}, u32[]{:S(2)}) collective-permute-start(bf16[256,1024]{1,0:T(8,128)(2,1)S(1)} %get-tuple-element.286), channel_id=1, source_target_pairs={{0,2},{2,0},{1,3},{3,1},{4,6},{6,4},{5,7},{7,5},{8,10},{10,8},{9,1... | collective-permute-start | bytes 1572872 | tf_op jit(solution)/shard_map/ppermute | solution.py:41
  134.6 14.2 %collective-permute-start.26 = (bf16[256,1024]{1,0:T(8,128)(2,1)S(1)}, bf16[256,1024]{1,0:T(8,128)(2,1)S(1)}, u32[]{:S(2)}, u32[]{:S(2)}) collective-permute-start(bf16[256,1024]{1,0:T(8,128)(2,1)S(1)} %get-tuple-element.287), channel_id=1, source_target_pairs={{0,4},{4,0},{1,5},{5,1},{2,6},{6,2},{3,7},{7,3},{8,12},{12,8},{9,1... | collective-permute-start | bytes 1572872 | tf_op jit(solution)/shard_map/ppermute | solution.py:41
  148.8 5.8 %collective-permute-start.34 = (bf16[4,1152,256]{2,1,0:T(8,128)(2,1)S(1)}, bf16[4,1152,256]{2,1,0:T(8,128)(2,1)S(1)}, u32[]{:S(2)}, u32[]{:S(2)}) collective-permute-start(bf16[4,1152,256]{2,1,0:T(8,128)(2,1)S(1)} %shard_map.248), channel_id=1, source_target_pairs={{0,1},{1,0},{2,3},{3,2},{4,5},{5,4},{6,7},{7,6},{8,9},{9,8},{10,11... | collective-permute-start | bytes 7077896 | tf_op jit(solution)/shard_map/ppermute | solution.py:41
  150.5 9.8 %collective-permute-start.30 = (bf16[128,1024]{1,0:T(8,128)(2,1)S(1)}, bf16[128,1024]{1,0:T(8,128)(2,1)S(1)}, u32[]{:S(2)}, u32[]{:S(2)}) collective-permute-start(bf16[128,1024]{1,0:T(8,128)(2,1)S(1)} %get-tuple-element.317.refs_6_.refs_4_), channel_id=1, source_target_pairs={{0,2},{2,0},{1,3},{3,1},{4,6},{6,4},{5,7},{7,5},{8,10},{10,8},{9,1... | collective-permute-start | bytes 786440 | tf_op jit(solution)/shard_map/ppermute | solution.py:41
  151.5 13.3 %collective-permute-start.32 = (bf16[128,1024]{1,0:T(8,128)(2,1)S(1)}, bf16[128,1024]{1,0:T(8,128)(2,1)S(1)}, u32[]{:S(2)}, u32[]{:S(2)}) collective-permute-start(bf16[128,1024]{1,0:T(8,128)(2,1)S(1)} %get-tuple-element.317.refs_6_.refs_4_), channel_id=1, source_target_pairs={{0,4},{4,0},{1,5},{5,1},{2,6},{6,2},{3,7},{7,3},{8,12},{12,8},{9,1... | collective-permute-start | bytes 786440 | tf_op jit(solution)/shard_map/ppermute | solution.py:41
  152.7 12.1 %collective-permute-start.31 = (bf16[128,1024]{1,0:T(8,128)(2,1)S(1)}, bf16[128,1024]{1,0:T(8,128)(2,1)S(1)}, u32[]{:S(2)}, u32[]{:S(2)}) collective-permute-start(bf16[128,1024]{1,0:T(8,128)(2,1)S(1)} %get-tuple-element.318.refs_7_.refs_5_), channel_id=1, source_target_pairs={{0,2},{2,0},{1,3},{3,1},{4,6},{6,4},{5,7},{7,5},{8,10},{10,8},{9,1... | collective-permute-start | bytes 786440 | tf_op jit(solution)/shard_map/ppermute | solution.py:41
  153.8 11.8 %collective-permute-start.33 = (bf16[128,1024]{1,0:T(8,128)(2,1)S(1)}, bf16[128,1024]{1,0:T(8,128)(2,1)S(1)}, u32[]{:S(2)}, u32[]{:S(2)}) collective-permute-start(bf16[128,1024]{1,0:T(8,128)(2,1)S(1)} %get-tuple-element.318.refs_7_.refs_5_), channel_id=1, source_target_pairs={{0,4},{4,0},{1,5},{5,1},{2,6},{6,2},{3,7},{7,3},{8,12},{12,8},{9,1... | collective-permute-start | bytes 786440 | tf_op jit(solution)/shard_map/ppermute | solution.py:41
  166.4 76.0 %reduce-scatter.6.cloned.1.call-start = ((), (), s32[]{:S(2)}) async-start(), calls=%async_computation.4 | async-start | bytes 655360 | tf_op jit(solution)/shard_map/reduce_scatter | solution.py:810
  167.3 10.0 %collective-permute-start.35 = (bf16[128,1024]{1,0:T(8,128)(2,1)S(1)}, bf16[128,1024]{1,0:T(8,128)(2,1)S(1)}, u32[]{:S(2)}, u32[]{:S(2)}) collective-permute-start(bf16[128,1024]{1,0:T(8,128)(2,1)S(1)} %copy-done.46), channel_id=1, source_target_pairs={{0,2},{2,0},{1,3},{3,1},{4,6},{6,4},{5,7},{7,5},{8,10},{10,8},{9,1... | collective-permute-start | bytes 786440 | tf_op jit(solution)/shard_map/ppermute | solution.py:41
  168.3 9.0 %collective-permute-start.36 = (bf16[128,1024]{1,0:T(8,128)(2,1)}, bf16[128,1024]{1,0:T(8,128)(2,1)S(1)}, u32[]{:S(2)}, u32[]{:S(2)}) collective-permute-start(bf16[128,1024]{1,0:T(8,128)(2,1)} %copy-done.47), channel_id=1, source_target_pairs={{0,4},{4,0},{1,5},{5,1},{2,6},{6,2},{3,7},{7,3},{8,12},{12,8},{9,1... | collective-permute-start | bytes 786440 | tf_op jit(solution)/shard_map/ppermute | solution.py:41
  181.8 14.3 %collective-permute-start.38 = (bf16[256,1024]{1,0:T(8,128)(2,1)S(1)}, bf16[256,1024]{1,0:T(8,128)(2,1)S(1)}, u32[]{:S(2)}, u32[]{:S(2)}) collective-permute-start(bf16[256,1024]{1,0:T(8,128)(2,1)S(1)} %copy-done.55), channel_id=1, source_target_pairs={{0,2},{2,0},{1,3},{3,1},{4,6},{6,4},{5,7},{7,5},{8,10},{10,8},{9,1... | collective-permute-start | bytes 1572872 | tf_op jit(solution)/shard_map/ppermute | solution.py:41
  183.0 14.0 %collective-permute-start.39 = (bf16[256,1024]{1,0:T(8,128)(2,1)S(1)}, bf16[256,1024]{1,0:T(8,128)(2,1)S(1)}, u32[]{:S(2)}, u32[]{:S(2)}) collective-permute-start(bf16[256,1024]{1,0:T(8,128)(2,1)S(1)} %copy-done.54), channel_id=1, source_target_pairs={{0,4},{4,0},{1,5},{5,1},{2,6},{6,2},{3,7},{7,3},{8,12},{12,8},{9,1... | collective-permute-start | bytes 1572872 | tf_op jit(solution)/shard_map/ppermute | solution.py:41
  196.9 19.8 %collective-permute-start.43 = (bf16[256,1024]{1,0:T(8,128)(2,1)S(1)}, bf16[256,1024]{1,0:T(8,128)(2,1)S(1)}, u32[]{:S(2)}, u32[]{:S(2)}) collective-permute-start(bf16[256,1024]{1,0:T(8,128)(2,1)S(1)} %copy-done.53), channel_id=1, source_target_pairs={{0,6},{2,4},{4,2},{6,0},{1,7},{3,5},{5,3},{7,1},{8,14},{10,12},{12... | collective-permute-start | bytes 1572872 | tf_op jit(solution)/shard_map/ppermute | solution.py:130
  198.2 16.7 %collective-permute-start.40 = (bf16[256,256]{1,0:T(8,128)(2,1)S(1)}, bf16[256,256]{1,0:T(8,128)(2,1)S(1)}, u32[]{:S(2)}, u32[]{:S(2)}) collective-permute-start(bf16[256,256]{1,0:T(8,128)(2,1)S(1)} %get-tuple-element.439), channel_id=1, source_target_pairs={{0,2},{2,0},{1,3},{3,1},{4,6},{6,4},{5,7},{7,5},{8,10},{10,8},{9,1... | collective-permute-start | bytes 393224 | tf_op jit(solution)/shard_map/ppermute | solution.py:41
  199.3 16.1 %collective-permute-start.41 = (bf16[256,256]{1,0:T(8,128)(2,1)S(1)}, bf16[256,256]{1,0:T(8,128)(2,1)S(1)}, u32[]{:S(2)}, u32[]{:S(2)}) collective-permute-start(bf16[256,256]{1,0:T(8,128)(2,1)S(1)} %get-tuple-element.438), channel_id=1, source_target_pairs={{0,4},{4,0},{1,5},{5,1},{2,6},{6,2},{3,7},{7,3},{8,12},{12,8},{9,1... | collective-permute-start | bytes 393224 | tf_op jit(solution)/shard_map/ppermute | solution.py:41
  200.5 16.2 %collective-permute-start.42 = (bf16[256,256]{1,0:T(8,128)(2,1)S(1)}, bf16[256,256]{1,0:T(8,128)(2,1)S(1)}, u32[]{:S(2)}, u32[]{:S(2)}) collective-permute-start(bf16[256,256]{1,0:T(8,128)(2,1)S(1)} %get-tuple-element.437), channel_id=1, source_target_pairs={{0,6},{2,4},{4,2},{6,0},{1,7},{3,5},{5,3},{7,1},{8,14},{10,12},{12... | collective-permute-start | bytes 393224 | tf_op jit(solution)/shard_map/ppermute | solution.py:152
  217.6 12.7 %collective-permute-start.44 = (bf16[256,1024]{1,0:T(8,128)(2,1)}, bf16[256,1024]{1,0:T(8,128)(2,1)}, u32[]{:S(2)}, u32[]{:S(2)}) collective-permute-start(bf16[256,1024]{1,0:T(8,128)(2,1)} %get-tuple-element.376), channel_id=1, source_target_pairs={{0,2},{2,0},{1,3},{3,1},{4,6},{6,4},{5,7},{7,5},{8,10},{10,8},{9,1... | collective-permute-start | bytes 1572872 | tf_op jit(solution)/shard_map/ppermute | solution.py:41
  218.5 12.4 %collective-permute-start.45 = (bf16[256,1024]{1,0:T(8,128)(2,1)}, bf16[256,1024]{1,0:T(8,128)(2,1)}, u32[]{:S(2)}, u32[]{:S(2)}) collective-permute-start(bf16[256,1024]{1,0:T(8,128)(2,1)} %get-tuple-element.377), channel_id=1, source_target_pairs={{0,4},{4,0},{1,5},{5,1},{2,6},{6,2},{3,7},{7,3},{8,12},{12,8},{9,1... | collective-permute-start | bytes 1572872 | tf_op jit(solution)/shard_map/ppermute | solution.py:41
  220.2 60.0 %reduce-scatter.8.cloned.1.call-start = ((), (), s32[]{:S(2)}) async-start(), calls=%async_computation.5 | async-start | bytes 1351680 | tf_op jit(solution)/shard_map/reduce_scatter | solution.py:831
  231.0 12.9 %collective-permute-start.46 = (bf16[1152,256]{1,0:T(8,128)(2,1)}, bf16[1152,256]{1,0:T(8,128)(2,1)}, u32[]{:S(2)}, u32[]{:S(2)}) collective-permute-start(bf16[1152,256]{1,0:T(8,128)(2,1)} %reduce-scatter.4.cloned.1.call-done.refs_0_), channel_id=1, source_target_pairs={{0,2},{2,0},{1,3},{3,1},{4,6},{6,4},{5,7},{7,5},{8,10},{10,8},{9,1... | collective-permute-start | bytes 1769480 | tf_op jit(solution)/shard_map/ppermute | solution.py:41
  232.0 12.6 %collective-permute-start.47 = (bf16[1152,256]{1,0:T(8,128)(2,1)}, bf16[1152,256]{1,0:T(8,128)(2,1)}, u32[]{:S(2)}, u32[]{:S(2)}) collective-permute-start(bf16[1152,256]{1,0:T(8,128)(2,1)} %reduce-scatter.4.cloned.1.call-done.refs_0_), channel_id=1, source_target_pairs={{0,4},{4,0},{1,5},{5,1},{2,6},{6,2},{3,7},{7,3},{8,12},{12,8},{9,1... | collective-permute-start | bytes 1769480 | tf_op jit(solution)/shard_map/ppermute | solution.py:41
  244.7 2.7 collective-permute-start.48
  253.4 9.1 %collective-permute-start.49 = (bf16[576,256]{1,0:T(8,128)(2,1)S(1)}, bf16[576,256]{1,0:T(8,128)(2,1)S(1)}, u32[]{:S(2)}, u32[]{:S(2)}) collective-permute-start(bf16[576,256]{1,0:T(8,128)(2,1)S(1)} %slice.38), channel_id=1, source_target_pairs={{0,2},{2,0},{1,3},{3,1},{4,6},{6,4},{5,7},{7,5},{8,10},{10,8},{9,1... | collective-permute-start | bytes 884744 | tf_op jit(solution)/shard_map/ppermute | solution.py:41
  255.5 8.8 %collective-permute-start.50 = (bf16[576,256]{1,0:T(8,128)(2,1)S(1)}, bf16[576,256]{1,0:T(8,128)(2,1)S(1)}, u32[]{:S(2)}, u32[]{:S(2)}) collective-permute-start(bf16[576,256]{1,0:T(8,128)(2,1)S(1)} %slice.39), channel_id=1, source_target_pairs={{0,4},{4,0},{1,5},{5,1},{2,6},{6,2},{3,7},{7,3},{8,12},{12,8},{9,1... | collective-permute-start | bytes 884744 | tf_op jit(solution)/shard_map/ppermute | solution.py:41
  264.3 6.6 %collective-permute-start.51 = (bf16[1152,256]{1,0:T(8,128)(2,1)}, bf16[1152,256]{1,0:T(8,128)(2,1)S(1)}, u32[]{:S(2)}, u32[]{:S(2)}) collective-permute-start(bf16[1152,256]{1,0:T(8,128)(2,1)} %reduce-scatter.4.cloned.1.call-done.refs_0_), channel_id=1, source_target_pairs={{0,1},{1,0},{2,3},{3,2},{4,5},{5,4},{6,7},{7,6},{8,9},{9,8},{10,11... | collective-permute-start | bytes 1769480 | tf_op jit(solution)/shard_map/ppermute | solution.py:41
  264.4 6.5 %collective-permute-start.52 = (bf16[1152,256]{1,0:T(8,128)(2,1)}, bf16[1152,256]{1,0:T(8,128)(2,1)S(1)}, u32[]{:S(2)}, u32[]{:S(2)}) collective-permute-start(bf16[1152,256]{1,0:T(8,128)(2,1)} %collective-permute-done.46.refs_1_), channel_id=1, source_target_pairs={{0,1},{1,0},{2,3},{3,2},{4,5},{5,4},{6,7},{7,6},{8,9},{9,8},{10,11... | collective-permute-start | bytes 1769480 | tf_op jit(solution)/shard_map/ppermute | solution.py:41
  264.9 6.0 %collective-permute-start.53 = (bf16[1152,256]{1,0:T(8,128)(2,1)}, bf16[1152,256]{1,0:T(8,128)(2,1)S(1)}, u32[]{:S(2)}, u32[]{:S(2)}) collective-permute-start(bf16[1152,256]{1,0:T(8,128)(2,1)} %collective-permute-done.47.refs_2_), channel_id=1, source_target_pairs={{0,1},{1,0},{2,3},{3,2},{4,5},{5,4},{6,7},{7,6},{8,9},{9,8},{10,11... | collective-permute-start | bytes 1769480 | tf_op jit(solution)/shard_map/ppermute | solution.py:41
  265.0 6.0 %collective-permute-start.54 = (bf16[1152,256]{1,0:T(8,128)(2,1)S(1)}, bf16[1152,256]{1,0:T(8,128)(2,1)S(1)}, u32[]{:S(2)}, u32[]{:S(2)}) collective-permute-start(bf16[1152,256]{1,0:T(8,128)(2,1)S(1)} %pad_maximum_fusion.refs_3_), channel_id=1, source_target_pairs={{0,1},{1,0},{2,3},{3,2},{4,5},{5,4},{6,7},{7,6},{8,9},{9,8},{10,11... | collective-permute-start | bytes 1769480 | tf_op jit(solution)/shard_map/ppermute | solution.py:41
  265.4 15.7 %collective-permute-start.55 = (bf16[256,1024]{1,0:T(8,128)(2,1)}, bf16[256,1024]{1,0:T(8,128)(2,1)}, u32[]{:S(2)}, u32[]{:S(2)}) collective-permute-start(bf16[256,1024]{1,0:T(8,128)(2,1)} %get-tuple-element.409), channel_id=1, source_target_pairs={{0,6},{2,4},{4,2},{6,0},{1,7},{3,5},{5,3},{7,1},{8,14},{10,12},{12... | collective-permute-start | bytes 1572872 | tf_op jit(solution)/shard_map/ppermute | solution.py:130
  281.2 12.3 %collective-permute-start.56 = (bf16[784,256]{1,0:T(8,128)(2,1)S(1)}, bf16[784,256]{1,0:T(8,128)(2,1)S(1)}, u32[]{:S(2)}, u32[]{:S(2)}) collective-permute-start(bf16[784,256]{1,0:T(8,128)(2,1)S(1)} %pad_maximum_fusion.1.refs_0_), channel_id=1, source_target_pairs={{0,2},{2,0},{1,3},{3,1},{4,6},{6,4},{5,7},{7,5},{8,10},{10,8},{9,1... | collective-permute-start | bytes 1204232 | tf_op jit(solution)/shard_map/ppermute | solution.py:41
  282.7 19.2 %collective-permute-start.57 = (bf16[784,256]{1,0:T(8,128)(2,1)S(1)}, bf16[784,256]{1,0:T(8,128)(2,1)S(1)}, u32[]{:S(2)}, u32[]{:S(2)}) collective-permute-start(bf16[784,256]{1,0:T(8,128)(2,1)S(1)} %pad_maximum_fusion.1.refs_0_), channel_id=1, source_target_pairs={{0,4},{4,0},{1,5},{5,1},{2,6},{6,2},{3,7},{7,3},{8,12},{12,8},{9,1... | collective-permute-start | bytes 1204232 | tf_op jit(solution)/shard_map/ppermute | solution.py:41
  284.2 17.7 %collective-permute-start.58 = (bf16[784,256]{1,0:T(8,128)(2,1)S(1)}, bf16[784,256]{1,0:T(8,128)(2,1)S(1)}, u32[]{:S(2)}, u32[]{:S(2)}) collective-permute-start(bf16[784,256]{1,0:T(8,128)(2,1)S(1)} %pad_maximum_fusion.1.refs_0_), channel_id=1, source_target_pairs={{0,6},{2,4},{4,2},{6,0},{1,7},{3,5},{5,3},{7,1},{8,14},{10,12},{12... | collective-permute-start | bytes 1204232 | tf_op jit(solution)/shard_map/ppermute | solution.py:118
  302.4 2.4 collective-permute-start.61
  302.4 2.9 collective-permute-start.62
  (60 other events, 554.4 us)
Sparse Core Ops, SparseCore 0:
  10.2 39.7 all-gather.4
  53.3 51.5 all-gather.6
  166.5 48.5 reduce-scatter.3
  220.3 22.0 reduce-scatter.5
  252.4 27.6 reduce-scatter.7

commit v6 on v5

--- a/solution.py
+++ b/solution.py
@@ -120,7 +120,7 @@
     def far_halves(self, near):
         if not self.square:
             return near
-        k = near[0].shape[0] // 2
+        k = near[0].shape[0] // 32 * 16
         return near + [jnp.concatenate([swap(near[2][:k], "x"), swap(near[1][k:], "y")], 0)]
 
     def gather_whole(self, a):
@@ -224,10 +224,23 @@
     return jnp.where(keep, jnp.exp(dot_nt(qr, kr) * SCALE), 0.0)
 
 
+def heads_below(a):
+    return jnp.concatenate([a[:, g * HEAD : (g + 1) * HEAD] for g in range(GROUP)], 0)
+
+
+def heads_beside(a):
+    rows = a.shape[0] // GROUP
+    return jnp.concatenate([a[g * rows : (g + 1) * rows] for g in range(GROUP)], 1)
+
+
+def repeat(a):
+    return jnp.concatenate([a] * GROUP, 0)
+
+
 def attend_block(parts, wrows, qg, kg, wa, wo, nin, cos, sin, mask, lin, vals, mixed, partial):
-    keep = mask[...] > 0.0
+    keep = repeat(mask[...]) > 0.0
     c, s = cos[...], sin[...]
-    rot = lambda u: u * c + half_roll(u) * s
+    c2, s2 = repeat(c), repeat(s)
     n = nin[...]
     one = ones(n.shape[0])
     out = None
@@ -238,15 +251,15 @@
         lin[:, h * 3 * HEAD : h * 3 * HEAD + 2 * HEAD] = q
         lin[:, h * 3 * HEAD + 2 * HEAD : (h + 1) * 3 * HEAD] = k
         vals[:, h * HEAD : (h + 1) * HEAD] = v
-        kr = rot(k * head_rsq(k) * kg[...]).astype(BF)
-        v1 = jnp.concatenate([v, one], 1)
-        for g in range(GROUP):
-            qh = q[:, g * HEAD : (g + 1) * HEAD]
-            e = weights_of(rot(qh * head_rsq(qh) * qg[...]).astype(BF), kr, keep)
-            m = dot(e.astype(BF), v1)
-            at = h * GROUP * HEAD + g * HEAD
-            mixed[:, at : at + HEAD] = (m[:, :HEAD] / m[:, HEAD:]).astype(BF)
-        term = dot(mixed[:, h * GROUP * HEAD : (h + 1) * GROUP * HEAD], wo[h][...])
+        kn = k * head_rsq(k) * kg[...]
+        kr = (kn * c + half_roll(kn) * s).astype(BF)
+        q = heads_below(q)
+        qn = q * head_rsq(q) * qg[...]
+        e = weights_of((qn * c2 + half_roll(qn) * s2).astype(BF), kr, keep)
+        m = dot(e.astype(BF), jnp.concatenate([v, one], 1))
+        m = heads_beside((m[:, :HEAD] / m[:, HEAD:]).astype(BF))
+        mixed[:, h * GROUP * HEAD : (h + 1) * GROUP * HEAD] = m
+        term = dot(m, wo[h][...])
         out = term if out is None else out + term
     partial[...] = out.astype(partial.dtype)
 
@@ -298,44 +311,40 @@
 
 
 def attend_back_block(parts, wrows, qg, kg, wa, wo, dh0, dh1, tok0, tok1, lin, vals, cos, sin, mask, dqkv, d_in, gains):
-    keep = mask[...] > 0.0
+    keep = repeat(mask[...]) > 0.0
     c, s = cos[...], sin[...]
-    rot = lambda u: u * c + half_roll(u) * s
-    rot_back = lambda u: u * c - half_roll(u) * s
+    c2, s2 = repeat(c), repeat(s)
     d = split((dh0, dh1))
     one = ones(d.shape[0])
     din, qgain, kgain = None, 0.0, 0.0
     for h in range(parts):
-        dm = dot_nt(d, wo[h][...]).astype(BF)
+        dm = heads_below(dot_nt(d, wo[h][...]).astype(BF))
         base = h * 3 * HEAD
         k = lin[:, base + 2 * HEAD : base + 3 * HEAD]
         v = vals[:, h * HEAD : (h + 1) * HEAD]
         rk = head_rsq(k)
-        kr = rot(k * rk * kg[...]).astype(BF)
-        ps, dss, qrs, dms = [], [], [], []
-        at = h * 4 * HEAD
-        for g in range(GROUP):
-            q = lin[:, base + g * HEAD : base + (g + 1) * HEAD]
-            rq = head_rsq(q)
-            qr = rot(q * rq * qg[...]).astype(BF)
-            e = weights_of(qr, kr, keep)
-            p = e * twice(1.0 / dot(e.astype(BF), one))
-            dmh = dm[:, g * HEAD : (g + 1) * HEAD]
-            pd = p * dot_nt(dmh, v)
-            ds = (pd - p * twice(dot(pd.astype(BF), one))).astype(BF)
-            ps.append(p.astype(BF))
-            dss.append(ds)
-            qrs.append(qr)
-            dms.append(dmh)
-            dq = rot_back(dot(ds, kr) * SCALE)
-            qgain = qgain + jnp.sum(dq * q * rq, axis=0, keepdims=True)
-            dqkv[:, at + g * HEAD : at + (g + 1) * HEAD] = head_back(q, rq, qg[...], dq).astype(BF)
-        dv = dot_tn(jnp.concatenate(ps, 0), jnp.concatenate(dms, 0))
-        dk = rot_back(dot_tn(jnp.concatenate(dss, 0), jnp.concatenate(qrs, 0)) * SCALE)
+        kn = k * rk * kg[...]
+        kr = (kn * c + half_roll(kn) * s).astype(BF)
+        q = heads_below(lin[:, base : base + GROUP * HEAD])
+        rq = head_rsq(q)
+        qn = q * rq * qg[...]
+        qr = (qn * c2 + half_roll(qn) * s2).astype(BF)
+        e = weights_of(qr, kr, keep)
+        p = e * twice(1.0 / dot(e.astype(BF), one))
+        pd = p * dot_nt(dm, v)
+        ds = (pd - p * twice(dot(pd.astype(BF), one))).astype(BF)
+        dq = dot(ds, kr) * SCALE
+        dk = dot_tn(ds, qr) * SCALE
+        dv = dot_tn(p.astype(BF), dm)
+        dq = dq * c2 - half_roll(dq) * s2
+        dk = dk * c - half_roll(dk) * s
+        qgain = qgain + jnp.sum(dq * q * rq, axis=0, keepdims=True)
         kgain = kgain + jnp.sum(dk * k * rk, axis=0, keepdims=True)
-        dqkv[:, at + 2 * HEAD : at + 3 * HEAD] = head_back(k, rk, kg[...], dk).astype(BF)
-        dqkv[:, at + 3 * HEAD : at + 4 * HEAD] = dv.astype(BF)
-        term = dot_nt(dqkv[:, at : at + 4 * HEAD], columns(wa[h], 0, 2, wrows))
+        dq = heads_beside(head_back(q, rq, qg[...], dq).astype(BF))
+        dk = head_back(k, rk, kg[...], dk).astype(BF)
+        both = jnp.concatenate([dq, dk, dv.astype(BF)], 1)
+        dqkv[:, h * 4 * HEAD : (h + 1) * 4 * HEAD] = both
+        term = dot_nt(both, columns(wa[h], 0, 2, wrows))
         din = term if din is None else din + term
     d_in[...] = din.astype(d_in.dtype)
     x = token_rows(tok0, tok1)
@@ -507,6 +516,29 @@
     )[0]
 
 
+def grad_rows_twice(lhs, rhs, tokens_each, width, n):
+    flat_r = sum(rhs, [])
+    nl = len(lhs)
+    cb = flat_r[0].shape[1] // B
+    q = width // n
+
+    def body(*refs):
+        left = jnp.concatenate([r[...] for r in refs[:nl]], 0)
+        right = jnp.concatenate([r[...] for r in refs[nl : nl + len(flat_r)]], 0)
+        got = dot_tn(left, right).astype(BF)
+        for h in range(2):
+            refs[h - 2][...] = got[h * width : (h + 1) * width].reshape(n, q, B)
+
+    spec = pl.BlockSpec((n, q, B), lambda j: (0, j, 0))
+    in_specs = [pl.BlockSpec(a.shape, lambda j: (0, 0)) for a in lhs]
+    in_specs += [pl.BlockSpec((tokens_each, B), lambda j: (0, j)) for a in flat_r]
+    tokens = sum(a.shape[0] for a in lhs)
+    return kernel_call(
+        body, [sds((n, cb * q, B), BF)] * 2, lhs + flat_r, flops=4 * tokens * width * cb * B,
+        grid=(cb,), in_specs=in_specs, out_specs=[spec] * 2,
+    )
+
+
 def grad_mlp(core, nm, dgu, product, cot, other, size, ff):
     mine = other is not None
     groups = [sum(nm, []), dgu, product, sum(cot, [])]
@@ -795,13 +827,18 @@
         dh = plane.gather_far(dh)
         dh[n - 1], own_back, partial = tie((dh[n - 1], own_back, partial))
         near_out = plane.send_near(partial)
-        out = pair(lambda h, o: grad_rows(
-            [stay(a) for a in mixed], [[stay(a) for a in b] for b in dh], half, h, GROUP * HEAD, n, o))
-        dh[1:], partial, out, near_out = tie((dh[1:], partial, out, near_out))
+        if halves:
+            out, other = grad_rows_twice(
+                [stay(a) for a in mixed], [[stay(a) for a in b] for b in dh], half, GROUP * HEAD, n)
+            out = (out.astype(F32) + swap(other, "c").astype(F32)).astype(BF)
+        else:
+            out = pair(lambda h, o: grad_rows(mixed, dh, half, h, GROUP * HEAD, n, o))
+        dh[1:], partial, out = tie((dh[1:], partial, out))
         out = exchanged(out)
         far_out = plane.send_far(partial)
         near_back, more = back([list(range(1, n - 1))], dh)
-        dh[n - 1], out, far_out, near_back, partial = tie((dh[n - 1], out, far_out, near_back, partial))
+        dh[n - 1], out, far_out, near_back, partial, near_out = tie(
+            (dh[n - 1], out, far_out, near_back, partial, near_out))
         terms_out = [partial[0], *near_out, far_out] if plane.square else plane.scatter(partial)
         near_in = plane.send_near(near_back[1])
         separate = plane.square and halves and size == n
@@ -927,7 +964,7 @@
             (grads_a, gate_g, up_g, down_g, activations, terms_in))
         input_grad = kernel_call(
             last_kernel, [sds((rows, width), BF)], [tokens, d_hidden, gain_in, *terms_in])[0]
-        grads_a, input_grad = tie((plane.gather_whole(grads_a), input_grad))
+        grads_a, input_grad = tie((plane.far_halves(plane.near(grads_a)), input_grad))
         outs_a = [like(w_query), like(w_key), like(w_value), like(w_out)]
         if separate:
             gain_outs = [sds((1, k), F32) for k in (width, width, HEAD, HEAD)]

time: 321 us -> 316 us (0.984)
  Pallas kernels: 112 us -> 100 us
  waiting for transfers between devices: 114 us -> 121 us
  local copies, waits for them, and re-layouts: 17.7 us -> 13.8 us
  starting transfers between devices: 56.3 us -> 59.8 us
    pallas_call x20 -> x19, Pallas kernels: 89.3 us -> 77 us  [kernel_call(): pl.pallas_call(body, out_shape=outs, compiler_params=pltpu.CompilerParams...]
    reduce_scatter x1, waiting for transfers between devices: 2.96 us -> 7.57 us  [body(): lax.psum_scatter(grads_a.reshape(-1, B), 'shard', scatter_dimension=0, ti...]
    ppermute x56 -> x58, starting transfers between devices: 47.5 us -> 51.1 us  [swap(): return lax.ppermute(a, axis, SWAP)]
    unnamed x112 -> x96, local copies, waits for them, and re-layouts: 13.5 us -> 11.4 us
    ppermute x56 -> x58, waiting for transfers between devices: 103 us -> 104 us  [swap(): return lax.ppermute(a, axis, SWAP)]
  transfers between devices with their start and end apart: 68 -> 69, of which waited for: 37 -> 37; matrix products, arithmetic and copies ran while one was open for 2% -> 1% of each run, Pallas kernels for 32% -> 29%
where the time goes in v6:
time: 316 us; the launch traced here: 311 us
  waiting for transfers between devices  121 us (38%)
  Pallas kernels  100 us (32%)
  starting transfers between devices  59.8 us (19%)
  between operations  14.6 us (5%)
  local copies, waits for them, and re-layouts  13.8 us (4%)
    ppermute x58, waiting for transfers between devices, swap(): return lax.ppermute(a, axis, SWAP)  104 us
    pallas_call x19, Pallas kernels, kernel_call(): pl.pallas_call(body, out_shape=outs, compiler_params=pltpu.CompilerParams...  77 us
    ppermute x58, starting transfers between devices, swap(): return lax.ppermute(a, axis, SWAP)  51.1 us
    unnamed x96, local copies, waits for them, and re-layouts  11.4 us
    pallas_call x2, Pallas kernels, grad_columns(): pl.pallas_call(body, out_shape=out, grid_spec=pltpu.PrefetchScalarGridSpe...  9.03 us
    pallas_call x2, Pallas kernels, grad_mlp(): pl.pallas_call(body, out_shape=out, grid_spec=pltpu.PrefetchScalarGridSpe...  8.91 us
    reduce_scatter x1, waiting for transfers between devices, body(): lax.psum_scatter(grads_a.reshape(-1, B), 'shard', scatter_dimension=0, ti...  7.57 us
  transfers between devices with their start and end apart: 69, of which 37 were waited for; matrix products, arithmetic and copies ran while one was open for 1% of the time, Pallas kernels for 29%

profile of v6, /device:TPU:0, one launch (start us, length us, event | category | flops | bytes accessed | tf_op | source)
XLA Modules:
  0.0 310.9 jit_solution(18384060538300168731)
XLA Ops:
  7.3 2.4 shard_map.237
  9.9 3.0 collective-permute-start.1
  12.9 1.5 collective-permute-start.3
  15.0 12.0 %collective-permute-done.2.refs_6_.refs_17_ = bf16[128,1024]{1,0:T(8,128)(2,1)S(1)} collective-permute-done((bf16[128,1024]{1,0:T(8,128)(2,1)S(1)}, bf16[128,1024]{1,0:T(8,128)(2,1)S(1)}, u32[]{:S(2)}, u32[]{:S(2)}) %collective-permute-start.2) | collective-permute-done | bytes 262176 | tf_op jit(solution)/shard_map/ppermute | solution.py:41
  28.4 1.7 collective-permute-start.8
  30.1 1.5 collective-permute-start.4
  32.4 5.1 %collective-permute-done.7.refs_6_.refs_19_ = bf16[128,1024]{1,0:T(8,128)(2,1)} collective-permute-done((bf16[128,1024]{1,0:T(8,128)(2,1)}, bf16[128,1024]{1,0:T(8,128)(2,1)}, u32[]{:S(2)}, u32[]{:S(2)}) %collective-permute-start.7) | collective-permute-done | bytes 262176 | tf_op jit(solution)/shard_map/ppermute | solution.py:41
  37.6 1.5 collective-permute-start.9
  39.6 3.5 %collective-permute-done.4.refs_8_ = bf16[128,1024]{1,0:T(8,128)(2,1)S(1)} collective-permute-done((bf16[128,1024]{1,0:T(8,128)(2,1)S(1)}, bf16[128,1024]{1,0:T(8,128)(2,1)S(1)}, u32[]{:S(2)}, u32[]{:S(2)}) %collective-permute-start.4) | collective-permute-done | bytes 262176 | tf_op jit(solution)/shard_map/ppermute | solution.py:41
  43.1 1.5 collective-permute-start.11
  44.7 2.9 shard_map.239
  47.6 4.2 %shard_map.238 = (bf16[256,1024]{1,0:T(8,128)(2,1)}, f32[256,128]{1,0:T(8,128)}, f32[256,128]{1,0:T(8,128)}, f32[256,256]{1,0:T(8,128)}, bf16[256,1024]{1,0:T(8,...) custom-call(f32[1,1024]{1,0:T(1,128)S(1)} %bitcast.55, ...), custom_call_target="tpu_custom_call" | custom-call | bytes 6427136 | tf_op jit(solution)/shard_map/pallas_call | solution.py:71
  56.2 1.5 collective-permute-start.14
  58.4 2.8 collective-permute-done.13.refs_1_
  61.1 3.4 %collective-permute-done.14.refs_2_ = bf16[256,256]{1,0:T(8,128)(2,1)S(1)} collective-permute-done((bf16[256,256]{1,0:T(8,128)(2,1)S(1)}, bf16[256,256]{1,0:T(8,128)(2,1)S(1)}, u32[]{:S(2)}, u32[]{:S(2)}) %collective-permute-start.14) | collective-permute-done | bytes 131104 | tf_op jit(solution)/shard_map/ppermute | solution.py:41
  64.7 1.9 collective-permute-done.16.refs_5_
  66.6 4.0 %shard_map.243 = (f32[256,768]{1,0:T(8,128)}, bf16[256,256]{1,0:T(8,128)(2,1)}, bf16[256,512]{1,0:T(8,128)(2,1)}, bf16[256,1024]{1,0:T(8,128)(2,1)S(1)}) custom-call(f32[1,128]{1,0:T(1,128)S(1)} %bitcast.41, f32[1,128]{1,0:T(1,128)S(1)} %bitcast.47, bf16[4,768,256]{2,1,0:T(8,128)(2,1)S(1)} %bitcast.34, ...), custom_call_target="tpu_custom_call" | custom-call | flops 805306368 | bytes 6947840 | tf_op jit(solution)/shard_map/pallas_call | solution.py:71
  70.6 1.5 collective-permute-start.19
  72.2 6.3 %shard_map.242 = (f32[256,768]{1,0:T(8,128)}, bf16[256,256]{1,0:T(8,128)(2,1)}, bf16[256,512]{1,0:T(8,128)(2,1)}, bf16[256,1024]{1,0:T(8,128)(2,1)S(1)}, f32[256...) custom-call(f32[1,128]{1,0:T(1,128)S(1)} %bitcast.42, ...), custom_call_target="tpu_custom_call" | custom-call | flops 1610612736 | bytes 9700352 | tf_op jit(solution)/shard_map/pallas_call | solution.py:71
  78.5 1.4 collective-permute-start.17
  80.5 3.9 %shard_map.241 = (f32[256,768]{1,0:T(8,128)}, bf16[256,256]{1,0:T(8,128)(2,1)}, bf16[256,512]{1,0:T(8,128)(2,1)}, f32[256,1024]{1,0:T(8,128)S(1)}) custom-call(f32[1,128]{1,0:T(1,128)S(1)} %bitcast.43, f32[1,128]{1,0:T(1,128)S(1)} %bitcast.49, bf16[4,768,256]{2,1,0:T(8,128)(2,1)S(1)} %bitcast.36, bf16[4,768,256]{2,1,0:T(8,128)(2,1)S(1)} %collective-permute-done.12.refs_3_, ...), custom_call_target="tpu_custom_call" | custom-call | flops 805306368 | bytes 7472128 | tf_op jit(solution)/shard_map/pallas_call | solution.py:71
  84.4 2.0 collective-permute-done.19.refs_3_
  86.4 10.5 %collective-permute-done.17.refs_1_ = bf16[256,1024]{1,0:T(8,128)(2,1)S(1)} collective-permute-done((bf16[256,1024]{1,0:T(8,128)(2,1)S(1)}, bf16[256,1024]{1,0:T(8,128)(2,1)S(1)}, u32[]{:S(2)}, u32[]{:S(2)}) %collective-permute-start.17) | collective-permute-done | bytes 524320 | tf_op jit(solution)/shard_map/ppermute | solution.py:41
  96.9 1.4 shard_map.244
  100.3 6.6 %collective-permute-done.20.refs_4_.refs_3_ = bf16[128,1024]{1,0:T(8,128)(2,1)} collective-permute-done((bf16[128,1024]{1,0:T(8,128)(2,1)}, bf16[128,1024]{1,0:T(8,128)(2,1)}, u32[]{:S(2)}, u32[]{:S(2)}) %collective-permute-start.20) | collective-permute-done | bytes 262176 | tf_op jit(solution)/shard_map/ppermute | solution.py:41
  108.4 1.5 collective-permute-start.28
  111.6 5.3 %collective-permute-done.27.refs_3_.refs_6_ = bf16[128,1024]{1,0:T(8,128)(2,1)S(1)} collective-permute-done((bf16[128,1024]{1,0:T(8,128)(2,1)}, bf16[128,1024]{1,0:T(8,128)(2,1)S(1)}, u32[]{:S(2)}, u32[]{:S(2)}) %collective-permute-start.27) | collective-permute-done | bytes 262176 | tf_op jit(solution)/shard_map/ppermute | solution.py:41
  117.7 1.7 copy-done.36
  119.4 4.1 %shard_map.247 = (bf16[256,768]{1,0:T(8,128)(2,1)S(1)}, bf16[256,1536]{1,0:T(8,128)(2,1)S(1)}, bf16[256,1024]{1,0:T(8,128)(2,1)}, bf16[256,1024]{1,0:T(8,128)(2,1)S(1)}) custom-call(s32[1]{0:T(128)} %bitcast.5.refs_0_.where, bf16[4,1152,256]{2,1,0:T(8,128)(2,1)S(1)} %bitcast.58, bf16[4,1152,256]{2,1,0:T(8,128)(2,1)S(1)} %collective-permute-done.22.refs_2_, ...), custom_call_target="tpu_custom_call" | custom-call | flops 2818572288 | bytes 7995396 | tf_op jit(solution)/shard_map/pallas_call | solution.py:71
  123.5 1.6 collective-permute-start.29
  125.1 7.5 %shard_map.246 = (bf16[256,768]{1,0:T(8,128)(2,1)S(1)}, bf16[256,1536]{1,0:T(8,128)(2,1)S(1)}, bf16[256,1024]{1,0:T(8,128)(2,1)}, bf16[256,1024]{1,0:T(8,128)(2,...) custom-call(s32[1]{0:T(128)} %bitcast.5.refs_0_.where, ...), custom_call_target="tpu_custom_call" | custom-call | flops 5637144576 | bytes 11272196 | tf_op jit(solution)/shard_map/pallas_call | solution.py:71
  132.5 1.5 collective-permute-start.25
  134.5 4.9 %shard_map.245 = (bf16[256,768]{1,0:T(8,128)(2,1)S(1)}, bf16[256,1536]{1,0:T(8,128)(2,1)S(1)}, f32[256,1024]{1,0:T(8,128)}, f32[256,1024]{1,0:T(8,128)S(1)}) custom-call(s32[1]{0:T(128)} %bitcast.5.refs_0_.where, bf16[4,1152,256]{2,1,0:T(8,128)(2,1)S(1)} %bitcast.60, bf16[4,1152,256]{2,1,0:T(8,128)(2,1)S(1)} %collective-permute-done.22.refs_2_, ...), custom_call_target="tpu_custom_call" | custom-call | flops 2818572288 | bytes 9043972 | tf_op jit(solution)/shard_map/pallas_call | solution.py:71
  139.5 4.3 %shard_map.248 = bf16[4,1152,256]{2,1,0:T(8,128)(2,1)S(1)} custom-call(s32[1]{0:T(128)} %bitcast.5.refs_0_.where, bf16[128,1024]{1,0:T(8,128)(2,1)S(1)} %get-tuple-element.277.refs_3_.refs_0_, bf16[128,1024]{1,0:T(8,128)(2,1)} %get-tuple-element.276.refs_4_.refs_1_, bf16[128,1024]{1,0:T(8,128)(2,1)S(1)} %collective-permute-done.23.refs_3_.refs_2_, ...), custom_call_target="tpu_custom_call" | custom-call | flops 4831838208 | bytes 8912896 | tf_op jit(solution)/shard_map/pallas_call | solution.py:586
  143.7 4.5 %collective-permute-done.25.refs_1_ = bf16[256,1024]{1,0:T(8,128)(2,1)S(1)} collective-permute-done((bf16[256,1024]{1,0:T(8,128)(2,1)S(1)}, bf16[256,1024]{1,0:T(8,128)(2,1)S(1)}, u32[]{:S(2)}, u32[]{:S(2)}) %collective-permute-start.25) | collective-permute-done | bytes 524320 | tf_op jit(solution)/shard_map/ppermute | solution.py:41
  148.3 1.7 shard_map.249
  152.1 1.4 collective-permute-start.31
  154.1 4.6 %shard_map.250 = bf16[4,1152,256]{2,1,0:T(8,128)(2,1)S(1)} custom-call(s32[1]{0:T(128)} %bitcast.5.refs_0_.where, bf16[128,1024]{1,0:T(8,128)(2,1)S(1)} %copy-done.38, bf16[128,1024]{1,0:T(8,128)(2,1)} %get-tuple-element.276.refs_4_.refs_1_, bf16[128,1024]{1,0:T(8,128)(2,1)S(1)} %collective-permute-done.23.refs_3_.refs_2_, ...), custom_call_target="tpu_custom_call" | custom-call | flops 4831838208 | bytes 11272192 | tf_op jit(solution)/shard_map/pallas_call | solution.py:586
  160.1 4.3 %collective-permute-done.31.refs_7_ = bf16[128,1024]{1,0:T(8,128)(2,1)} collective-permute-done((bf16[128,1024]{1,0:T(8,128)(2,1)S(1)}, bf16[128,1024]{1,0:T(8,128)(2,1)}, u32[]{:S(2)}, u32[]{:S(2)}) %collective-permute-start.31) | collective-permute-done | bytes 262176 | tf_op jit(solution)/shard_map/ppermute | solution.py:41
  166.9 1.4 collective-permute-start.36
  168.4 6.0 %shard_map.251 = (bf16[256,1024]{1,0:T(8,128)(2,1)}, f32[256,1024]{1,0:T(8,128)}, f32[1,1280]{1,0:T(1,128)S(1)}) custom-call(f32[1,128]{1,0:T(1,128)S(1)} %bitcast.44, f32[1,128]{1,0:T(1,128)S(1)} %bitcast.50, bf16[4,768,256]{2,1,0:T(8,128)(2,1)S(1)} %bitcast.37, bf16[4,768,256]{2,1,0:T(8,128)(2,1)S(1)} %collective-permute-done.12.refs_3_, ...), custom_call_target="tpu_custom_call" | custom-call | flops 805306368 | bytes 8296448 | tf_op jit(solution)/shard_map/pallas_call | solution.py:71
  175.3 4.3 %shard_map.252 = (bf16[4,256,256]{2,1,0:T(8,128)(2,1)S(1)}, bf16[4,256,256]{2,1,0:T(8,128)(2,1)S(1)}) custom-call(bf16[256,512]{1,0:T(8,128)(2,1)} %get-tuple-element.338.refs_0_, bf16[256,512]{1,0:T(8,128)(2,1)} %get-tuple-element.339.refs_1_, bf16[256,512]{1,0:T(8,128)(2,1)} %get-tuple-element.340.refs_2_, bf16[256,512]{1,0:T(8,128)(2,1)} %get-tuple-element.341.refs_3_, ...), custom_call_target="tpu_custom_call" | custom-call | flops 1073741824 | bytes 4194304 | tf_op jit(solution)/shard_map/pallas_call | solution.py:71
  181.9 1.5 collective-permute-start.41
  185.5 8.9 %collective-permute-done.42.refs_1_ = bf16[256,1024]{1,0:T(8,128)(2,1)S(1)} collective-permute-done((bf16[256,1024]{1,0:T(8,128)(2,1)S(1)}, bf16[256,1024]{1,0:T(8,128)(2,1)S(1)}, u32[]{:S(2)}, u32[]{:S(2)}) %collective-permute-start.42) | collective-permute-done | bytes 524320 | tf_op jit(solution)/shard_map/ppermute | solution.py:41
  195.2 1.5 collective-permute-start.40
  196.7 9.8 %shard_map.253 = (bf16[256,1024]{1,0:T(8,128)(2,1)}, bf16[256,1024]{1,0:T(8,128)(2,1)}, bf16[256,1024]{1,0:T(8,128)(2,1)}, bf16[256,1024]{1,0:T(8,128)(2,1)}, f32[1,1280]{1,0:T(1,128)S(1)}) custom-call(f32[1,128]{1,0:T(1,128)S(1)} %bitcast.45, f32[1,128]{1,0:T(1,128)S(1)} %bitcast.51, bf16[4,768,256]{2,1,0:T(8,128)(2,1)S(1)} %bitcast.38, ...), custom_call_target="tpu_custom_call" | custom-call | flops 1610612736 | bytes 11343872 | tf_op jit(solution)/shard_map/pallas_call | solution.py:71
  209.2 2.4 collective-permute-done.40.refs_3_
  215.8 5.8 %shard_map.255 = (bf16[256,1024]{1,0:T(8,128)(2,1)}, bf16[256,1024]{1,0:T(8,128)(2,1)}, f32[1,1280]{1,0:T(1,128)S(1)}) custom-call(f32[1,128]{1,0:T(1,128)S(1)} %bitcast.46, f32[1,128]{1,0:T(1,128)S(1)} %bitcast.52, bf16[4,768,256]{2,1,0:T(8,128)(2,1)S(1)} %bitcast.39, bf16[4,768,256]{2,1,0:T(8,128)(2,1)S(1)} %collective-permute-done.12.refs_3_, ...), custom_call_target="tpu_custom_call" | custom-call | flops 805306368 | bytes 7772160 | tf_op jit(solution)/shard_map/pallas_call | solution.py:71
  221.6 4.6 %collective-permute-done.44.refs_1_ = bf16[256,1024]{1,0:T(8,128)(2,1)} collective-permute-done((bf16[256,1024]{1,0:T(8,128)(2,1)}, bf16[256,1024]{1,0:T(8,128)(2,1)}, u32[]{:S(2)}, u32[]{:S(2)}) %collective-permute-start.44) | collective-permute-done | bytes 524320 | tf_op jit(solution)/shard_map/ppermute | solution.py:41
  228.7 4.1 %shard_map.256 = bf16[4,512,256]{2,1,0:T(8,128)(2,1)S(1)} custom-call(s32[1]{0:T(128)} %bitcast.where, bf16[256,1024]{1,0:T(8,128)(2,1)} %get-tuple-element.253.refs_6_.refs_0_, bf16[256,1024]{1,0:T(8,128)(2,1)} %get-tuple-element.254.refs_6_.refs_1_, bf16[256,1024]{1,0:T(8,128)(2,1)} %get-tuple-element.255.refs_10_.refs_2_, ...), custom_call_target="tpu_custom_call" | custom-call | flops 1073741824 | bytes 5242880 | tf_op jit(solution)/shard_map/pallas_call | solution.py:478
  232.8 5.1 %reduce-scatter.6.cloned.1.call-done = bf16[256,256]{1,0:T(8,128)(2,1)} async-done(((bf16[1024,256]{1,0:T(8,128)(2,1)}), bf16[256,256]{1,0:T(8,128)(2,1)}) %reduce-scatter.6.cloned.1.call-update) | async-done | bytes 131088 | tf_op jit(solution)/shard_map/reduce_scatter | solution.py:847
  238.0 2.5 collective-permute-done.46.refs_1_
  241.6 2.7 collective-permute-done.48.refs_12_
  244.2 4.9 %shard_map.257 = bf16[4,528,256]{2,1,0:T(8,128)(2,1)} custom-call(s32[1]{0:T(128)} %bitcast.where, bf16[256,1024]{1,0:T(8,128)(2,1)} %get-tuple-element.253.refs_6_.refs_0_, bf16[256,1024]{1,0:T(8,128)(2,1)} %get-tuple-element.254.refs_6_.refs_1_, bf16[256,1024]{1,0:T(8,128)(2,1)} %get-tuple-element.255.refs_10_.refs_2_, ...), custom_call_target="tpu_custom_call" | custom-call | flops 1073741824 | bytes 6333952 | tf_op jit(solution)/shard_map/pallas_call | solution.py:478
  250.9 7.5 %collective-permute-done.49 = bf16[576,256]{1,0:T(8,128)(2,1)S(1)} collective-permute-done((bf16[576,256]{1,0:T(8,128)(2,1)S(1)}, bf16[576,256]{1,0:T(8,128)(2,1)S(1)}, u32[]{:S(2)}, u32[]{:S(2)}) %collective-permute-start.49) | collective-permute-done | bytes 294944 | tf_op jit(solution)/shard_map/ppermute | solution.py:41
  263.7 5.4 %shard_map.258 = (f32[256,3072]{1,0:T(8,128)}, f32[256,3072]{1,0:T(8,128)}, f32[768,1024]{1,0:T(8,128)}) custom-call(s32[2]{0:T(128)S(1)} %pad_add_fusion.1.w.where, bf16[1152,256]{1,0:T(8,128)(2,1)S(1)} %copy-done.23, bf16[1152,256]{1,0:T(8,128)(2,1)S(1)} %collective-permute-done.46.refs_1_, bf16[1152,256]{1,0:T(8,128)(2,1)S(1)} %collective-permute-done.47.refs_2_, ...), custom_call_target="tpu_custom_call" | custom-call | bytes 14155784 | tf_op jit(solution)/shard_map/pallas_call | solution.py:71
  269.1 7.6 %reduce-scatter.8.cloned.1.call-done = bf16[528,256]{1,0:T(8,128)(2,1)} async-done(((bf16[2112,256]{1,0:T(8,128)(2,1)}), bf16[528,256]{1,0:T(8,128)(2,1)}) %reduce-scatter.8.cloned.1.call-update) | async-done | bytes 270352 | tf_op jit(solution)/shard_map/reduce_scatter | solution.py:868
  277.6 1.5 collective-permute-start.56
  279.2 1.5 collective-permute-start.57
  280.7 7.9 %collective-permute-done.56.refs_1_ = bf16[784,256]{1,0:T(8,128)(2,1)S(1)} collective-permute-done((bf16[784,256]{1,0:T(8,128)(2,1)S(1)}, bf16[784,256]{1,0:T(8,128)(2,1)S(1)}, u32[]{:S(2)}, u32[]{:S(2)}) %collective-permute-start.56) | collective-permute-done | bytes 401440 | tf_op jit(solution)/shard_map/ppermute | solution.py:41
  288.6 1.5 collective-permute-start.59
  290.2 1.5 collective-permute-start.58
  294.2 2.8 shard_map.260
  300.5 3.7 %shard_map.261 = (f32[256,2048]{1,0:T(8,128)}, f32[256,1024]{1,0:T(8,128)}, f32[256,1024]{1,0:T(8,128)}, f32[512,1024]{1,0:T(8,128)}, f32[1,1024]{1,0:T(1,128)},...) custom-call(s32[2]{0:T(128)S(1)} %pad_add_fusion.1.w.where, ...), custom_call_target="tpu_custom_call" | custom-call | bytes 9511944 | tf_op jit(solution)/shard_map/pallas_call | solution.py:71
  (217 shorter events, 53.0 us)
Async XLA Ops:
  7.2 46.0 %all-gather.5.cloned.1.call-start = ((), (), s32[]{:S(2)}) async-start(), calls=%async_computation.6 | async-start | bytes 1966080 | tf_op jit(solution)/shard_map/all_gather | solution.py:722
  9.7 97.8 %all-gather.7.cloned.1.call-start = ((), (), s32[]{:S(2)}) async-start(), calls=%async_computation.7 | async-start | bytes 2949120 | tf_op jit(solution)/shard_map/all_gather | solution.py:736
  9.9 17.1 %collective-permute-start.1 = (bf16[144,1024]{1,0:T(8,128)(2,1)S(1)}, bf16[144,1024]{1,0:T(8,128)(2,1)S(1)}, u32[]{:S(2)}, u32[]{:S(2)}) collective-permute-start(bf16[144,1024]{1,0:T(8,128)(2,1)S(1)} %fusion.1.refs_3_.refs_9_), channel_id=1, source_target_pairs={{0,2},{2,0},{1,3},{3,1},{4,6},{6,4},{5,7},{7,5},{8,10},{10,8},{9,1... | collective-permute-start | bytes 884744 | tf_op jit(solution)/shard_map/ppermute | solution.py:41
  12.9 14.1 %collective-permute-start.3 = (bf16[144,1024]{1,0:T(8,128)(2,1)S(1)}, bf16[144,1024]{1,0:T(8,128)(2,1)S(1)}, u32[]{:S(2)}, u32[]{:S(2)}) collective-permute-start(bf16[144,1024]{1,0:T(8,128)(2,1)S(1)} %fusion.1.refs_3_.refs_9_), channel_id=1, source_target_pairs={{0,4},{4,0},{1,5},{5,1},{2,6},{6,2},{3,7},{7,3},{8,12},{12,8},{9,1... | collective-permute-start | bytes 884744 | tf_op jit(solution)/shard_map/ppermute | solution.py:41
  14.4 12.6 %collective-permute-start.2 = (bf16[128,1024]{1,0:T(8,128)(2,1)S(1)}, bf16[128,1024]{1,0:T(8,128)(2,1)S(1)}, u32[]{:S(2)}, u32[]{:S(2)}) collective-permute-start(bf16[128,1024]{1,0:T(8,128)(2,1)S(1)} %get-tuple-element.448.refs_2_.refs_8_), channel_id=1, source_target_pairs={{0,4},{4,0},{1,5},{5,1},{2,6},{6,2},{3,7},{7,3},{8,12},{12,8},{9,1... | collective-permute-start | bytes 786440 | tf_op jit(solution)/shard_map/ppermute | solution.py:41
  14.9 12.1 %collective-permute-start = (bf16[128,1024]{1,0:T(8,128)(2,1)S(1)}, bf16[128,1024]{1,0:T(8,128)(2,1)S(1)}, u32[]{:S(2)}, u32[]{:S(2)}) collective-permute-start(bf16[128,1024]{1,0:T(8,128)(2,1)S(1)} %get-tuple-element.448.refs_2_.refs_8_), channel_id=1, source_target_pairs={{0,2},{2,0},{1,3},{3,1},{4,6},{6,4},{5,7},{7,5},{8,10},{10,8},{9,1... | collective-permute-start | bytes 786440 | tf_op jit(solution)/shard_map/ppermute | solution.py:41
  28.0 9.6 %collective-permute-start.7 = (bf16[128,1024]{1,0:T(8,128)(2,1)}, bf16[128,1024]{1,0:T(8,128)(2,1)}, u32[]{:S(2)}, u32[]{:S(2)}) collective-permute-start(bf16[128,1024]{1,0:T(8,128)(2,1)} %get-tuple-element.280.refs_6_.refs_17_), channel_id=1, source_target_pairs={{0,2},{2,0},{1,3},{3,1},{4,6},{6,4},{5,7},{7,5},{8,10},{10,8},{9,1... | collective-permute-start | bytes 786440 | tf_op jit(solution)/shard_map/ppermute | solution.py:41
  28.4 10.7 %collective-permute-start.8 = (bf16[128,1024]{1,0:T(8,128)(2,1)}, bf16[128,1024]{1,0:T(8,128)(2,1)}, u32[]{:S(2)}, u32[]{:S(2)}) collective-permute-start(bf16[128,1024]{1,0:T(8,128)(2,1)} %get-tuple-element.279.refs_5_.refs_16_), channel_id=1, source_target_pairs={{0,4},{4,0},{1,5},{5,1},{2,6},{6,2},{3,7},{7,3},{8,12},{12,8},{9,1... | collective-permute-start | bytes 786440 | tf_op jit(solution)/shard_map/ppermute | solution.py:41
  30.1 13.0 %collective-permute-start.4 = (bf16[128,1024]{1,0:T(8,128)(2,1)S(1)}, bf16[128,1024]{1,0:T(8,128)(2,1)S(1)}, u32[]{:S(2)}, u32[]{:S(2)}) collective-permute-start(bf16[128,1024]{1,0:T(8,128)(2,1)S(1)} %collective-permute-done.2.refs_6_.refs_17_), channel_id=1, source_target_pairs={{0,2},{2,0},{1,3},{3,1},{4,6},{6,4},{5,7},{7,5},{8,10},{10,8},{9,1... | collective-permute-start | bytes 786440 | tf_op jit(solution)/shard_map/ppermute | solution.py:41
  31.5 16.0 %collective-permute-start.5 = (bf16[144,1024]{1,0:T(8,128)(2,1)S(1)}, bf16[144,1024]{1,0:T(8,128)(2,1)S(1)}, u32[]{:S(2)}, u32[]{:S(2)}) collective-permute-start(bf16[144,1024]{1,0:T(8,128)(2,1)S(1)} %collective-permute-done.1.refs_5_.refs_9_), channel_id=1, source_target_pairs={{0,4},{4,0},{1,5},{5,1},{2,6},{6,2},{3,7},{7,3},{8,12},{12,8},{9,1... | collective-permute-start | bytes 884744 | tf_op jit(solution)/shard_map/ppermute | solution.py:41
  32.1 19.8 %collective-permute-start.6 = (bf16[128,1024]{1,0:T(8,128)(2,1)}, bf16[128,1024]{1,0:T(8,128)(2,1)}, u32[]{:S(2)}, u32[]{:S(2)}) collective-permute-start(bf16[128,1024]{1,0:T(8,128)(2,1)} %get-tuple-element.279.refs_5_.refs_16_), channel_id=1, source_target_pairs={{0,2},{2,0},{1,3},{3,1},{4,6},{6,4},{5,7},{7,5},{8,10},{10,8},{9,1... | collective-permute-start | bytes 786440 | tf_op jit(solution)/shard_map/ppermute | solution.py:41
  37.6 14.3 %collective-permute-start.9 = (bf16[128,1024]{1,0:T(8,128)(2,1)}, bf16[128,1024]{1,0:T(8,128)(2,1)}, u32[]{:S(2)}, u32[]{:S(2)}) collective-permute-start(bf16[128,1024]{1,0:T(8,128)(2,1)} %get-tuple-element.280.refs_6_.refs_17_), channel_id=1, source_target_pairs={{0,4},{4,0},{1,5},{5,1},{2,6},{6,2},{3,7},{7,3},{8,12},{12,8},{9,1... | collective-permute-start | bytes 786440 | tf_op jit(solution)/shard_map/ppermute | solution.py:41
  39.1 13.0 %collective-permute-start.10 = (bf16[128,1024]{1,0:T(8,128)(2,1)}, bf16[128,1024]{1,0:T(8,128)(2,1)}, u32[]{:S(2)}, u32[]{:S(2)}) collective-permute-start(bf16[128,1024]{1,0:T(8,128)(2,1)} %collective-permute-done.8.refs_9_.refs_20_), channel_id=1, source_target_pairs={{0,2},{2,0},{1,3},{3,1},{4,6},{6,4},{5,7},{7,5},{8,10},{10,8},{9,1... | collective-permute-start | bytes 786440 | tf_op jit(solution)/shard_map/ppermute | solution.py:41
  43.1 10.2 %collective-permute-start.11 = (bf16[128,1024]{1,0:T(8,128)(2,1)}, bf16[128,1024]{1,0:T(8,128)(2,1)}, u32[]{:S(2)}, u32[]{:S(2)}) collective-permute-start(bf16[128,1024]{1,0:T(8,128)(2,1)} %collective-permute-done.7.refs_6_.refs_19_), channel_id=1, source_target_pairs={{0,4},{4,0},{1,5},{5,1},{2,6},{6,2},{3,7},{7,3},{8,12},{12,8},{9,1... | collective-permute-start | bytes 786440 | tf_op jit(solution)/shard_map/ppermute | solution.py:41
  53.3 173.4 %reduce-scatter.4.cloned.1.call-start = ((), (), s32[]{:S(2)}) async-start(), calls=%async_computation.3 | async-start | bytes 2949120 | tf_op jit(solution)/shard_map/reduce_scatter | solution.py:815
  53.5 13.1 %collective-permute-start.12 = (bf16[4,768,256]{2,1,0:T(8,128)(2,1)}, bf16[4,768,256]{2,1,0:T(8,128)(2,1)S(1)}, u32[]{:S(2)}, u32[]{:S(2)}) collective-permute-start(bf16[4,768,256]{2,1,0:T(8,128)(2,1)} %bitcast.32), channel_id=1, source_target_pairs={{0,1},{1,0},{2,3},{3,2},{4,5},{5,4},{6,7},{7,6},{8,9},{9,8},{10,11... | collective-permute-start | bytes 4718600 | tf_op jit(solution)/shard_map/ppermute | solution.py:41
  54.8 6.3 %collective-permute-start.13 = (bf16[256,256]{1,0:T(8,128)(2,1)S(1)}, bf16[256,256]{1,0:T(8,128)(2,1)S(1)}, u32[]{:S(2)}, u32[]{:S(2)}) collective-permute-start(bf16[256,256]{1,0:T(8,128)(2,1)S(1)} %get-tuple-element.439), channel_id=1, source_target_pairs={{0,2},{2,0},{1,3},{3,1},{4,6},{6,4},{5,7},{7,5},{8,10},{10,8},{9,1... | collective-permute-start | bytes 393224 | tf_op jit(solution)/shard_map/ppermute | solution.py:41
  56.2 8.3 %collective-permute-start.14 = (bf16[256,256]{1,0:T(8,128)(2,1)S(1)}, bf16[256,256]{1,0:T(8,128)(2,1)S(1)}, u32[]{:S(2)}, u32[]{:S(2)}) collective-permute-start(bf16[256,256]{1,0:T(8,128)(2,1)S(1)} %get-tuple-element.438), channel_id=1, source_target_pairs={{0,4},{4,0},{1,5},{5,1},{2,6},{6,2},{3,7},{7,3},{8,12},{12,8},{9,1... | collective-permute-start | bytes 393224 | tf_op jit(solution)/shard_map/ppermute | solution.py:41
  57.8 6.8 %collective-permute-start.15 = (bf16[256,256]{1,0:T(8,128)(2,1)S(1)}, bf16[256,256]{1,0:T(8,128)(2,1)S(1)}, u32[]{:S(2)}, u32[]{:S(2)}) collective-permute-start(bf16[256,256]{1,0:T(8,128)(2,1)S(1)} %get-tuple-element.437), channel_id=1, source_target_pairs={{0,6},{2,4},{4,2},{6,0},{1,7},{3,5},{5,3},{7,1},{8,14},{10,12},{12... | collective-permute-start | bytes 393224 | tf_op jit(solution)/shard_map/ppermute | solution.py:152
  70.6 15.7 %collective-permute-start.19 = (bf16[256,1024]{1,0:T(8,128)(2,1)S(1)}, bf16[256,1024]{1,0:T(8,128)(2,1)S(1)}, u32[]{:S(2)}, u32[]{:S(2)}) collective-permute-start(bf16[256,1024]{1,0:T(8,128)(2,1)S(1)} %get-tuple-element.273), channel_id=1, source_target_pairs={{0,6},{2,4},{4,2},{6,0},{1,7},{3,5},{5,3},{7,1},{8,14},{10,12},{12... | collective-permute-start | bytes 1572872 | tf_op jit(solution)/shard_map/ppermute | solution.py:130
  78.5 18.4 %collective-permute-start.17 = (bf16[256,1024]{1,0:T(8,128)(2,1)S(1)}, bf16[256,1024]{1,0:T(8,128)(2,1)S(1)}, u32[]{:S(2)}, u32[]{:S(2)}) collective-permute-start(bf16[256,1024]{1,0:T(8,128)(2,1)S(1)} %get-tuple-element.268), channel_id=1, source_target_pairs={{0,2},{2,0},{1,3},{3,1},{4,6},{6,4},{5,7},{7,5},{8,10},{10,8},{9,1... | collective-permute-start | bytes 1572872 | tf_op jit(solution)/shard_map/ppermute | solution.py:41
  79.9 16.9 %collective-permute-start.18 = (bf16[256,1024]{1,0:T(8,128)(2,1)S(1)}, bf16[256,1024]{1,0:T(8,128)(2,1)S(1)}, u32[]{:S(2)}, u32[]{:S(2)}) collective-permute-start(bf16[256,1024]{1,0:T(8,128)(2,1)S(1)} %get-tuple-element.269), channel_id=1, source_target_pairs={{0,4},{4,0},{1,5},{5,1},{2,6},{6,2},{3,7},{7,3},{8,12},{12,8},{9,1... | collective-permute-start | bytes 1572872 | tf_op jit(solution)/shard_map/ppermute | solution.py:41
  98.3 8.5 %collective-permute-start.20 = (bf16[128,1024]{1,0:T(8,128)(2,1)}, bf16[128,1024]{1,0:T(8,128)(2,1)}, u32[]{:S(2)}, u32[]{:S(2)}) collective-permute-start(bf16[128,1024]{1,0:T(8,128)(2,1)} %get-tuple-element.276.refs_4_.refs_1_), channel_id=1, source_target_pairs={{0,2},{2,0},{1,3},{3,1},{4,6},{6,4},{5,7},{7,5},{8,10},{10,8},{9,1... | collective-permute-start | bytes 786440 | tf_op jit(solution)/shard_map/ppermute | solution.py:41
  99.4 8.2 %collective-permute-start.21 = (bf16[128,1024]{1,0:T(8,128)(2,1)S(1)}, bf16[128,1024]{1,0:T(8,128)(2,1)}, u32[]{:S(2)}, u32[]{:S(2)}) collective-permute-start(bf16[128,1024]{1,0:T(8,128)(2,1)S(1)} %get-tuple-element.277.refs_3_.refs_0_), channel_id=1, source_target_pairs={{0,4},{4,0},{1,5},{5,1},{2,6},{6,2},{3,7},{7,3},{8,12},{12,8},{9,1... | collective-permute-start | bytes 786440 | tf_op jit(solution)/shard_map/ppermute | solution.py:41
  107.6 10.2 %collective-permute-start.22 = (bf16[4,1152,256]{2,1,0:T(8,128)(2,1)}, bf16[4,1152,256]{2,1,0:T(8,128)(2,1)S(1)}, u32[]{:S(2)}, u32[]{:S(2)}) collective-permute-start(bf16[4,1152,256]{2,1,0:T(8,128)(2,1)} %bitcast.57), channel_id=1, source_target_pairs={{0,1},{1,0},{2,3},{3,2},{4,5},{5,4},{6,7},{7,6},{8,9},{9,8},{10,11... | collective-permute-start | bytes 7077896 | tf_op jit(solution)/shard_map/ppermute | solution.py:41
  107.6 9.3 %collective-permute-start.27 = (bf16[128,1024]{1,0:T(8,128)(2,1)}, bf16[128,1024]{1,0:T(8,128)(2,1)S(1)}, u32[]{:S(2)}, u32[]{:S(2)}) collective-permute-start(bf16[128,1024]{1,0:T(8,128)(2,1)} %collective-permute-done.21.refs_7_.refs_4_), channel_id=1, source_target_pairs={{0,2},{2,0},{1,3},{3,1},{4,6},{6,4},{5,7},{7,5},{8,10},{10,8},{9,1... | collective-permute-start | bytes 786440 | tf_op jit(solution)/shard_map/ppermute | solution.py:41
  108.4 9.4 %collective-permute-start.28 = (bf16[128,1024]{1,0:T(8,128)(2,1)}, bf16[128,1024]{1,0:T(8,128)(2,1)S(1)}, u32[]{:S(2)}, u32[]{:S(2)}) collective-permute-start(bf16[128,1024]{1,0:T(8,128)(2,1)} %collective-permute-done.20.refs_4_.refs_3_), channel_id=1, source_target_pairs={{0,4},{4,0},{1,5},{5,1},{2,6},{6,2},{3,7},{7,3},{8,12},{12,8},{9,1... | collective-permute-start | bytes 786440 | tf_op jit(solution)/shard_map/ppermute | solution.py:41
  109.9 15.2 %collective-permute-start.23 = (bf16[128,1024]{1,0:T(8,128)(2,1)S(1)}, bf16[128,1024]{1,0:T(8,128)(2,1)S(1)}, u32[]{:S(2)}, u32[]{:S(2)}) collective-permute-start(bf16[128,1024]{1,0:T(8,128)(2,1)S(1)} %get-tuple-element.277.refs_3_.refs_0_), channel_id=1, source_target_pairs={{0,2},{2,0},{1,3},{3,1},{4,6},{6,4},{5,7},{7,5},{8,10},{10,8},{9,1... | collective-permute-start | bytes 786440 | tf_op jit(solution)/shard_map/ppermute | solution.py:41
  110.5 14.6 %collective-permute-start.24 = (bf16[128,1024]{1,0:T(8,128)(2,1)}, bf16[128,1024]{1,0:T(8,128)(2,1)S(1)}, u32[]{:S(2)}, u32[]{:S(2)}) collective-permute-start(bf16[128,1024]{1,0:T(8,128)(2,1)} %get-tuple-element.276.refs_4_.refs_1_), channel_id=1, source_target_pairs={{0,4},{4,0},{1,5},{5,1},{2,6},{6,2},{3,7},{7,3},{8,12},{12,8},{9,1... | collective-permute-start | bytes 786440 | tf_op jit(solution)/shard_map/ppermute | solution.py:41
  123.5 16.0 %collective-permute-start.29 = (bf16[256,1024]{1,0:T(8,128)(2,1)S(1)}, bf16[256,1024]{1,0:T(8,128)(2,1)S(1)}, u32[]{:S(2)}, u32[]{:S(2)}) collective-permute-start(bf16[256,1024]{1,0:T(8,128)(2,1)S(1)} %get-tuple-element.298), channel_id=1, source_target_pairs={{0,6},{2,4},{4,2},{6,0},{1,7},{3,5},{5,3},{7,1},{8,14},{10,12},{12... | collective-permute-start | bytes 1572872 | tf_op jit(solution)/shard_map/ppermute | solution.py:130
  132.5 15.7 %collective-permute-start.25 = (bf16[256,1024]{1,0:T(8,128)(2,1)S(1)}, bf16[256,1024]{1,0:T(8,128)(2,1)S(1)}, u32[]{:S(2)}, u32[]{:S(2)}) collective-permute-start(bf16[256,1024]{1,0:T(8,128)(2,1)S(1)} %get-tuple-element.288), channel_id=1, source_target_pairs={{0,2},{2,0},{1,3},{3,1},{4,6},{6,4},{5,7},{7,5},{8,10},{10,8},{9,1... | collective-permute-start | bytes 1572872 | tf_op jit(solution)/shard_map/ppermute | solution.py:41
  134.0 14.2 %collective-permute-start.26 = (bf16[256,1024]{1,0:T(8,128)(2,1)S(1)}, bf16[256,1024]{1,0:T(8,128)(2,1)S(1)}, u32[]{:S(2)}, u32[]{:S(2)}) collective-permute-start(bf16[256,1024]{1,0:T(8,128)(2,1)S(1)} %get-tuple-element.289), channel_id=1, source_target_pairs={{0,4},{4,0},{1,5},{5,1},{2,6},{6,2},{3,7},{7,3},{8,12},{12,8},{9,1... | collective-permute-start | bytes 1572872 | tf_op jit(solution)/shard_map/ppermute | solution.py:41
  148.3 5.8 %collective-permute-start.34 = (bf16[4,1152,256]{2,1,0:T(8,128)(2,1)S(1)}, bf16[4,1152,256]{2,1,0:T(8,128)(2,1)S(1)}, u32[]{:S(2)}, u32[]{:S(2)}) collective-permute-start(bf16[4,1152,256]{2,1,0:T(8,128)(2,1)S(1)} %shard_map.248), channel_id=1, source_target_pairs={{0,1},{1,0},{2,3},{3,2},{4,5},{5,4},{6,7},{7,6},{8,9},{9,8},{10,11... | collective-permute-start | bytes 7077896 | tf_op jit(solution)/shard_map/ppermute | solution.py:41
  150.0 10.1 %collective-permute-start.30 = (bf16[128,1024]{1,0:T(8,128)(2,1)S(1)}, bf16[128,1024]{1,0:T(8,128)(2,1)S(1)}, u32[]{:S(2)}, u32[]{:S(2)}) collective-permute-start(bf16[128,1024]{1,0:T(8,128)(2,1)S(1)} %get-tuple-element.319.refs_6_.refs_4_), channel_id=1, source_target_pairs={{0,2},{2,0},{1,3},{3,1},{4,6},{6,4},{5,7},{7,5},{8,10},{10,8},{9,1... | collective-permute-start | bytes 786440 | tf_op jit(solution)/shard_map/ppermute | solution.py:41
  151.2 13.3 %collective-permute-start.32 = (bf16[128,1024]{1,0:T(8,128)(2,1)S(1)}, bf16[128,1024]{1,0:T(8,128)(2,1)}, u32[]{:S(2)}, u32[]{:S(2)}) collective-permute-start(bf16[128,1024]{1,0:T(8,128)(2,1)S(1)} %get-tuple-element.319.refs_6_.refs_4_), channel_id=1, source_target_pairs={{0,4},{4,0},{1,5},{5,1},{2,6},{6,2},{3,7},{7,3},{8,12},{12,8},{9,1... | collective-permute-start | bytes 786440 | tf_op jit(solution)/shard_map/ppermute | solution.py:41
  152.1 12.4 %collective-permute-start.31 = (bf16[128,1024]{1,0:T(8,128)(2,1)S(1)}, bf16[128,1024]{1,0:T(8,128)(2,1)}, u32[]{:S(2)}, u32[]{:S(2)}) collective-permute-start(bf16[128,1024]{1,0:T(8,128)(2,1)S(1)} %get-tuple-element.320.refs_7_.refs_5_), channel_id=1, source_target_pairs={{0,2},{2,0},{1,3},{3,1},{4,6},{6,4},{5,7},{7,5},{8,10},{10,8},{9,1... | collective-permute-start | bytes 786440 | tf_op jit(solution)/shard_map/ppermute | solution.py:41
  153.5 11.7 %collective-permute-start.33 = (bf16[128,1024]{1,0:T(8,128)(2,1)S(1)}, bf16[128,1024]{1,0:T(8,128)(2,1)S(1)}, u32[]{:S(2)}, u32[]{:S(2)}) collective-permute-start(bf16[128,1024]{1,0:T(8,128)(2,1)S(1)} %get-tuple-element.320.refs_7_.refs_5_), channel_id=1, source_target_pairs={{0,4},{4,0},{1,5},{5,1},{2,6},{6,2},{3,7},{7,3},{8,12},{12,8},{9,1... | collective-permute-start | bytes 786440 | tf_op jit(solution)/shard_map/ppermute | solution.py:41
  165.9 72.0 %reduce-scatter.6.cloned.1.call-start = ((), (), s32[]{:S(2)}) async-start(), calls=%async_computation.4 | async-start | bytes 655360 | tf_op jit(solution)/shard_map/reduce_scatter | solution.py:847
  166.0 8.4 %collective-permute-start.35 = (bf16[128,1024]{1,0:T(8,128)(2,1)}, bf16[128,1024]{1,0:T(8,128)(2,1)S(1)}, u32[]{:S(2)}, u32[]{:S(2)}) collective-permute-start(bf16[128,1024]{1,0:T(8,128)(2,1)} %collective-permute-done.32.refs_8_.refs_15_), channel_id=1, source_target_pairs={{0,2},{2,0},{1,3},{3,1},{4,6},{6,4},{5,7},{7,5},{8,10},{10,8},{9,1... | collective-permute-start | bytes 786440 | tf_op jit(solution)/shard_map/ppermute | solution.py:41
  166.9 7.6 %collective-permute-start.36 = (bf16[128,1024]{1,0:T(8,128)(2,1)}, bf16[128,1024]{1,0:T(8,128)(2,1)S(1)}, u32[]{:S(2)}, u32[]{:S(2)}) collective-permute-start(bf16[128,1024]{1,0:T(8,128)(2,1)} %collective-permute-done.31.refs_7_), channel_id=1, source_target_pairs={{0,4},{4,0},{1,5},{5,1},{2,6},{6,2},{3,7},{7,3},{8,12},{12,8},{9,1... | collective-permute-start | bytes 786440 | tf_op jit(solution)/shard_map/ppermute | solution.py:41
  179.6 14.8 %collective-permute-start.42 = (bf16[256,1024]{1,0:T(8,128)(2,1)S(1)}, bf16[256,1024]{1,0:T(8,128)(2,1)S(1)}, u32[]{:S(2)}, u32[]{:S(2)}) collective-permute-start(bf16[256,1024]{1,0:T(8,128)(2,1)S(1)} %copy-done.47), channel_id=1, source_target_pairs={{0,2},{2,0},{1,3},{3,1},{4,6},{6,4},{5,7},{7,5},{8,10},{10,8},{9,1... | collective-permute-start | bytes 1572872 | tf_op jit(solution)/shard_map/ppermute | solution.py:41
  180.7 26.0 %collective-permute-start.43 = (bf16[256,1024]{1,0:T(8,128)(2,1)S(1)}, bf16[256,1024]{1,0:T(8,128)(2,1)S(1)}, u32[]{:S(2)}, u32[]{:S(2)}) collective-permute-start(bf16[256,1024]{1,0:T(8,128)(2,1)S(1)} %copy-done.46), channel_id=1, source_target_pairs={{0,4},{4,0},{1,5},{5,1},{2,6},{6,2},{3,7},{7,3},{8,12},{12,8},{9,1... | collective-permute-start | bytes 1572872 | tf_op jit(solution)/shard_map/ppermute | solution.py:41
  181.9 29.7 %collective-permute-start.41 = (bf16[256,1024]{1,0:T(8,128)(2,1)S(1)}, bf16[256,1024]{1,0:T(8,128)(2,1)S(1)}, u32[]{:S(2)}, u32[]{:S(2)}) collective-permute-start(bf16[256,1024]{1,0:T(8,128)(2,1)S(1)} %copy-done.45), channel_id=1, source_target_pairs={{0,6},{2,4},{4,2},{6,0},{1,7},{3,5},{5,3},{7,1},{8,14},{10,12},{12... | collective-permute-start | bytes 1572872 | tf_op jit(solution)/shard_map/ppermute | solution.py:130
  183.4 25.1 %collective-permute-start.38 = (bf16[256,256]{1,0:T(8,128)(2,1)S(1)}, bf16[256,256]{1,0:T(8,128)(2,1)S(1)}, u32[]{:S(2)}, u32[]{:S(2)}) collective-permute-start(bf16[256,256]{1,0:T(8,128)(2,1)S(1)} %get-tuple-element.443), channel_id=1, source_target_pairs={{0,2},{2,0},{1,3},{3,1},{4,6},{6,4},{5,7},{7,5},{8,10},{10,8},{9,1... | collective-permute-start | bytes 393224 | tf_op jit(solution)/shard_map/ppermute | solution.py:41
  184.6 24.6 %collective-permute-start.39 = (bf16[256,256]{1,0:T(8,128)(2,1)S(1)}, bf16[256,256]{1,0:T(8,128)(2,1)S(1)}, u32[]{:S(2)}, u32[]{:S(2)}) collective-permute-start(bf16[256,256]{1,0:T(8,128)(2,1)S(1)} %get-tuple-element.442), channel_id=1, source_target_pairs={{0,4},{4,0},{1,5},{5,1},{2,6},{6,2},{3,7},{7,3},{8,12},{12,8},{9,1... | collective-permute-start | bytes 393224 | tf_op jit(solution)/shard_map/ppermute | solution.py:41
  195.2 16.4 %collective-permute-start.40 = (bf16[256,256]{1,0:T(8,128)(2,1)S(1)}, bf16[256,256]{1,0:T(8,128)(2,1)S(1)}, u32[]{:S(2)}, u32[]{:S(2)}) collective-permute-start(bf16[256,256]{1,0:T(8,128)(2,1)S(1)} %get-tuple-element.441), channel_id=1, source_target_pairs={{0,6},{2,4},{4,2},{6,0},{1,7},{3,5},{5,3},{7,1},{8,14},{10,12},{12... | collective-permute-start | bytes 393224 | tf_op jit(solution)/shard_map/ppermute | solution.py:152
  212.4 13.8 %collective-permute-start.44 = (bf16[256,1024]{1,0:T(8,128)(2,1)}, bf16[256,1024]{1,0:T(8,128)(2,1)}, u32[]{:S(2)}, u32[]{:S(2)}) collective-permute-start(bf16[256,1024]{1,0:T(8,128)(2,1)} %get-tuple-element.380), channel_id=1, source_target_pairs={{0,2},{2,0},{1,3},{3,1},{4,6},{6,4},{5,7},{7,5},{8,10},{10,8},{9,1... | collective-permute-start | bytes 1572872 | tf_op jit(solution)/shard_map/ppermute | solution.py:41
  213.4 13.3 %collective-permute-start.45 = (bf16[256,1024]{1,0:T(8,128)(2,1)}, bf16[256,1024]{1,0:T(8,128)(2,1)}, u32[]{:S(2)}, u32[]{:S(2)}) collective-permute-start(bf16[256,1024]{1,0:T(8,128)(2,1)} %get-tuple-element.381), channel_id=1, source_target_pairs={{0,4},{4,0},{1,5},{5,1},{2,6},{6,2},{3,7},{7,3},{8,12},{12,8},{9,1... | collective-permute-start | bytes 1572872 | tf_op jit(solution)/shard_map/ppermute | solution.py:41
  215.6 61.1 %reduce-scatter.8.cloned.1.call-start = ((), (), s32[]{:S(2)}) async-start(), calls=%async_computation.5 | async-start | bytes 1351680 | tf_op jit(solution)/shard_map/reduce_scatter | solution.py:868
  226.7 13.7 %collective-permute-start.46 = (bf16[1152,256]{1,0:T(8,128)(2,1)}, bf16[1152,256]{1,0:T(8,128)(2,1)S(1)}, u32[]{:S(2)}, u32[]{:S(2)}) collective-permute-start(bf16[1152,256]{1,0:T(8,128)(2,1)} %reduce-scatter.4.cloned.1.call-done.refs_0_), channel_id=1, source_target_pairs={{0,2},{2,0},{1,3},{3,1},{4,6},{6,4},{5,7},{7,5},{8,10},{10,8},{9,1... | collective-permute-start | bytes 1769480 | tf_op jit(solution)/shard_map/ppermute | solution.py:41
  228.0 13.6 %collective-permute-start.47 = (bf16[1152,256]{1,0:T(8,128)(2,1)}, bf16[1152,256]{1,0:T(8,128)(2,1)S(1)}, u32[]{:S(2)}, u32[]{:S(2)}) collective-permute-start(bf16[1152,256]{1,0:T(8,128)(2,1)} %reduce-scatter.4.cloned.1.call-done.refs_0_), channel_id=1, source_target_pairs={{0,4},{4,0},{1,5},{5,1},{2,6},{6,2},{3,7},{7,3},{8,12},{12,8},{9,1... | collective-permute-start | bytes 1769480 | tf_op jit(solution)/shard_map/ppermute | solution.py:41
  241.6 2.7 collective-permute-start.48
  249.3 9.1 %collective-permute-start.49 = (bf16[576,256]{1,0:T(8,128)(2,1)S(1)}, bf16[576,256]{1,0:T(8,128)(2,1)S(1)}, u32[]{:S(2)}, u32[]{:S(2)}) collective-permute-start(bf16[576,256]{1,0:T(8,128)(2,1)S(1)} %slice.44), channel_id=1, source_target_pairs={{0,2},{2,0},{1,3},{3,1},{4,6},{6,4},{5,7},{7,5},{8,10},{10,8},{9,1... | collective-permute-start | bytes 884744 | tf_op jit(solution)/shard_map/ppermute | solution.py:41
  250.0 8.8 %collective-permute-start.50 = (bf16[576,256]{1,0:T(8,128)(2,1)S(1)}, bf16[576,256]{1,0:T(8,128)(2,1)S(1)}, u32[]{:S(2)}, u32[]{:S(2)}) collective-permute-start(bf16[576,256]{1,0:T(8,128)(2,1)S(1)} %slice.45), channel_id=1, source_target_pairs={{0,4},{4,0},{1,5},{5,1},{2,6},{6,2},{3,7},{7,3},{8,12},{12,8},{9,1... | collective-permute-start | bytes 884744 | tf_op jit(solution)/shard_map/ppermute | solution.py:41
  258.8 4.8 %collective-permute-start.51 = (bf16[1152,256]{1,0:T(8,128)(2,1)S(1)}, bf16[1152,256]{1,0:T(8,128)(2,1)S(1)}, u32[]{:S(2)}, u32[]{:S(2)}) collective-permute-start(bf16[1152,256]{1,0:T(8,128)(2,1)S(1)} %copy-done.23), channel_id=1, source_target_pairs={{0,1},{1,0},{2,3},{3,2},{4,5},{5,4},{6,7},{7,6},{8,9},{9,8},{10,11... | collective-permute-start | bytes 1769480 | tf_op jit(solution)/shard_map/ppermute | solution.py:41
  258.9 4.7 %collective-permute-start.52 = (bf16[1152,256]{1,0:T(8,128)(2,1)S(1)}, bf16[1152,256]{1,0:T(8,128)(2,1)S(1)}, u32[]{:S(2)}, u32[]{:S(2)}) collective-permute-start(bf16[1152,256]{1,0:T(8,128)(2,1)S(1)} %collective-permute-done.46.refs_1_), channel_id=1, source_target_pairs={{0,1},{1,0},{2,3},{3,2},{4,5},{5,4},{6,7},{7,6},{8,9},{9,8},{10,11... | collective-permute-start | bytes 1769480 | tf_op jit(solution)/shard_map/ppermute | solution.py:41
  259.4 4.2 %collective-permute-start.53 = (bf16[1152,256]{1,0:T(8,128)(2,1)S(1)}, bf16[1152,256]{1,0:T(8,128)(2,1)S(1)}, u32[]{:S(2)}, u32[]{:S(2)}) collective-permute-start(bf16[1152,256]{1,0:T(8,128)(2,1)S(1)} %collective-permute-done.47.refs_2_), channel_id=1, source_target_pairs={{0,1},{1,0},{2,3},{3,2},{4,5},{5,4},{6,7},{7,6},{8,9},{9,8},{10,11... | collective-permute-start | bytes 1769480 | tf_op jit(solution)/shard_map/ppermute | solution.py:41
  259.5 4.2 %collective-permute-start.54 = (bf16[1152,256]{1,0:T(8,128)(2,1)S(1)}, bf16[1152,256]{1,0:T(8,128)(2,1)S(1)}, u32[]{:S(2)}, u32[]{:S(2)}) collective-permute-start(bf16[1152,256]{1,0:T(8,128)(2,1)S(1)} %pad_maximum_fusion.refs_3_), channel_id=1, source_target_pairs={{0,1},{1,0},{2,3},{3,2},{4,5},{5,4},{6,7},{7,6},{8,9},{9,8},{10,11... | collective-permute-start | bytes 1769480 | tf_op jit(solution)/shard_map/ppermute | solution.py:41
  259.9 17.7 %collective-permute-start.55 = (bf16[256,1024]{1,0:T(8,128)(2,1)}, bf16[256,1024]{1,0:T(8,128)(2,1)}, u32[]{:S(2)}, u32[]{:S(2)}) collective-permute-start(bf16[256,1024]{1,0:T(8,128)(2,1)} %get-tuple-element.413), channel_id=1, source_target_pairs={{0,6},{2,4},{4,2},{6,0},{1,7},{3,5},{5,3},{7,1},{8,14},{10,12},{12... | collective-permute-start | bytes 1572872 | tf_op jit(solution)/shard_map/ppermute | solution.py:130
  277.6 10.9 %collective-permute-start.56 = (bf16[784,256]{1,0:T(8,128)(2,1)S(1)}, bf16[784,256]{1,0:T(8,128)(2,1)S(1)}, u32[]{:S(2)}, u32[]{:S(2)}) collective-permute-start(bf16[784,256]{1,0:T(8,128)(2,1)S(1)} %pad_maximum_fusion.1.refs_0_), channel_id=1, source_target_pairs={{0,2},{2,0},{1,3},{3,1},{4,6},{6,4},{5,7},{7,5},{8,10},{10,8},{9,1... | collective-permute-start | bytes 1204232 | tf_op jit(solution)/shard_map/ppermute | solution.py:41
  279.2 11.0 %collective-permute-start.57 = (bf16[784,256]{1,0:T(8,128)(2,1)S(1)}, bf16[784,256]{1,0:T(8,128)(2,1)S(1)}, u32[]{:S(2)}, u32[]{:S(2)}) collective-permute-start(bf16[784,256]{1,0:T(8,128)(2,1)S(1)} %pad_maximum_fusion.1.refs_0_), channel_id=1, source_target_pairs={{0,4},{4,0},{1,5},{5,1},{2,6},{6,2},{3,7},{7,3},{8,12},{12,8},{9,1... | collective-permute-start | bytes 1204232 | tf_op jit(solution)/shard_map/ppermute | solution.py:41
  288.6 8.3 %collective-permute-start.59 = (bf16[400,256]{1,0:T(8,128)(2,1)S(1)}, bf16[400,256]{1,0:T(8,128)(2,1)S(1)}, u32[]{:S(2)}, u32[]{:S(2)}) collective-permute-start(bf16[400,256]{1,0:T(8,128)(2,1)S(1)} %slice.49), channel_id=1, source_target_pairs={{0,4},{4,0},{1,5},{5,1},{2,6},{6,2},{3,7},{7,3},{8,12},{12,8},{9,1... | collective-permute-start | bytes 614408 | tf_op jit(solution)/shard_map/ppermute | solution.py:41
  290.2 6.8 %collective-permute-start.58 = (bf16[384,256]{1,0:T(8,128)(2,1)S(1)}, bf16[384,256]{1,0:T(8,128)(2,1)S(1)}, u32[]{:S(2)}, u32[]{:S(2)}) collective-permute-start(bf16[384,256]{1,0:T(8,128)(2,1)S(1)} %slice.48), channel_id=1, source_target_pairs={{0,2},{2,0},{1,3},{3,1},{4,6},{6,4},{5,7},{7,5},{8,10},{10,8},{9,1... | collective-permute-start | bytes 589832 | tf_op jit(solution)/shard_map/ppermute | solution.py:41
  297.6 2.9 collective-permute-start.63
  (53 other events, 549.1 us)
Sparse Core Ops, SparseCore 0:
  10.2 39.7 all-gather.4
  53.4 51.5 all-gather.6
  166.0 48.5 reduce-scatter.3
  216.8 21.1 reduce-scatter.5
  249.3 27.2 reduce-scatter.7

commit v7 on v6

--- a/solution.py
+++ b/solution.py
@@ -963,7 +963,8 @@
         grads_a, gate_g, up_g, down_g, activations, terms_in = tie(
             (grads_a, gate_g, up_g, down_g, activations, terms_in))
         input_grad = kernel_call(
-            last_kernel, [sds((rows, width), BF)], [tokens, d_hidden, gain_in, *terms_in])[0]
+            last_kernel, [sds((rows, width), BF)],
+            [tokens, stay(d_hidden), gain_in, stay(terms_in[0]), *terms_in[1:]])[0]
         grads_a, input_grad = tie((plane.far_halves(plane.near(grads_a)), input_grad))
         outs_a = [like(w_query), like(w_key), like(w_value), like(w_out)]
         if separate:

time: 316 us -> 315 us (level)
    unnamed x96 -> x92, local copies, waits for them, and re-layouts: 11.4 us -> 9.01 us
  transfers between devices with their start and end apart: 69 -> 69, of which waited for: 37 -> 38; matrix products, arithmetic and copies ran while one was open for 1% -> 1% of each run, Pallas kernels for 29% -> 29%
where the time goes in v7:
time: 315 us; the launch traced here: 310 us
  waiting for transfers between devices  122 us (39%)
  Pallas kernels  101 us (32%)
  starting transfers between devices  59.8 us (19%)
  between operations  14.6 us (5%)
  local copies, waits for them, and re-layouts  11.3 us (4%)
    ppermute x58, waiting for transfers between devices, swap(): return lax.ppermute(a, axis, SWAP)  105 us
    pallas_call x19, Pallas kernels, kernel_call(): pl.pallas_call(body, out_shape=outs, compiler_params=pltpu.CompilerParams...  77.6 us
    ppermute x58, starting transfers between devices, swap(): return lax.ppermute(a, axis, SWAP)  51.1 us
    pallas_call x2, Pallas kernels, grad_columns(): pl.pallas_call(body, out_shape=out, grid_spec=pltpu.PrefetchScalarGridSpe...  9.03 us
    unnamed x92, local copies, waits for them, and re-layouts  9.01 us
    pallas_call x2, Pallas kernels, grad_mlp(): pl.pallas_call(body, out_shape=out, grid_spec=pltpu.PrefetchScalarGridSpe...  8.91 us
    reduce_scatter x1, waiting for transfers between devices, body(): lax.psum_scatter(grads_a.reshape(-1, B), 'shard', scatter_dimension=0, ti...  7.55 us
  transfers between devices with their start and end apart: 69, of which 38 were waited for; matrix products, arithmetic and copies ran while one was open for 1% of the time, Pallas kernels for 29%

profile of v7, /device:TPU:0, one launch (start us, length us, event | category | flops | bytes accessed | tf_op | source)
XLA Modules:
  0.0 309.9 jit_solution(3754084576386087602)
XLA Ops:
  7.3 2.4 shard_map.237
  9.9 3.0 collective-permute-start.1
  12.9 1.5 collective-permute-start.3
  15.0 12.0 %collective-permute-done.2.refs_6_.refs_17_ = bf16[128,1024]{1,0:T(8,128)(2,1)S(1)} collective-permute-done((bf16[128,1024]{1,0:T(8,128)(2,1)S(1)}, bf16[128,1024]{1,0:T(8,128)(2,1)S(1)}, u32[]{:S(2)}, u32[]{:S(2)}) %collective-permute-start.2) | collective-permute-done | bytes 262176 | tf_op jit(solution)/shard_map/ppermute | solution.py:41
  28.3 1.7 collective-permute-start.8
  30.0 1.5 collective-permute-start.4
  32.4 5.1 %collective-permute-done.7.refs_6_.refs_19_ = bf16[128,1024]{1,0:T(8,128)(2,1)} collective-permute-done((bf16[128,1024]{1,0:T(8,128)(2,1)}, bf16[128,1024]{1,0:T(8,128)(2,1)}, u32[]{:S(2)}, u32[]{:S(2)}) %collective-permute-start.7) | collective-permute-done | bytes 262176 | tf_op jit(solution)/shard_map/ppermute | solution.py:41
  37.5 1.5 collective-permute-start.9
  39.6 3.5 %collective-permute-done.4.refs_8_ = bf16[128,1024]{1,0:T(8,128)(2,1)S(1)} collective-permute-done((bf16[128,1024]{1,0:T(8,128)(2,1)S(1)}, bf16[128,1024]{1,0:T(8,128)(2,1)S(1)}, u32[]{:S(2)}, u32[]{:S(2)}) %collective-permute-start.4) | collective-permute-done | bytes 262176 | tf_op jit(solution)/shard_map/ppermute | solution.py:41
  43.0 1.5 collective-permute-start.11
  44.7 2.9 shard_map.239
  47.6 4.2 %shard_map.238 = (bf16[256,1024]{1,0:T(8,128)(2,1)}, f32[256,128]{1,0:T(8,128)}, f32[256,128]{1,0:T(8,128)}, f32[256,256]{1,0:T(8,128)}, bf16[256,1024]{1,0:T(8,...) custom-call(f32[1,1024]{1,0:T(1,128)S(1)} %bitcast.55, ...), custom_call_target="tpu_custom_call" | custom-call | bytes 6427136 | tf_op jit(solution)/shard_map/pallas_call | solution.py:71
  56.2 1.5 collective-permute-start.14
  58.4 2.8 collective-permute-done.13.refs_1_
  61.1 3.4 %collective-permute-done.14.refs_2_ = bf16[256,256]{1,0:T(8,128)(2,1)S(1)} collective-permute-done((bf16[256,256]{1,0:T(8,128)(2,1)S(1)}, bf16[256,256]{1,0:T(8,128)(2,1)S(1)}, u32[]{:S(2)}, u32[]{:S(2)}) %collective-permute-start.14) | collective-permute-done | bytes 131104 | tf_op jit(solution)/shard_map/ppermute | solution.py:41
  64.6 1.9 collective-permute-done.16.refs_5_
  66.6 4.0 %shard_map.243 = (f32[256,768]{1,0:T(8,128)}, bf16[256,256]{1,0:T(8,128)(2,1)}, bf16[256,512]{1,0:T(8,128)(2,1)}, bf16[256,1024]{1,0:T(8,128)(2,1)S(1)}) custom-call(f32[1,128]{1,0:T(1,128)S(1)} %bitcast.41, f32[1,128]{1,0:T(1,128)S(1)} %bitcast.47, bf16[4,768,256]{2,1,0:T(8,128)(2,1)S(1)} %bitcast.34, ...), custom_call_target="tpu_custom_call" | custom-call | flops 805306368 | bytes 6947840 | tf_op jit(solution)/shard_map/pallas_call | solution.py:71
  70.6 1.6 collective-permute-start.19
  72.2 6.3 %shard_map.242 = (f32[256,768]{1,0:T(8,128)}, bf16[256,256]{1,0:T(8,128)(2,1)}, bf16[256,512]{1,0:T(8,128)(2,1)}, bf16[256,1024]{1,0:T(8,128)(2,1)S(1)}, f32[256...) custom-call(f32[1,128]{1,0:T(1,128)S(1)} %bitcast.42, ...), custom_call_target="tpu_custom_call" | custom-call | flops 1610612736 | bytes 9700352 | tf_op jit(solution)/shard_map/pallas_call | solution.py:71
  78.5 1.4 collective-permute-start.17
  80.4 3.9 %shard_map.241 = (f32[256,768]{1,0:T(8,128)}, bf16[256,256]{1,0:T(8,128)(2,1)}, bf16[256,512]{1,0:T(8,128)(2,1)}, f32[256,1024]{1,0:T(8,128)S(1)}) custom-call(f32[1,128]{1,0:T(1,128)S(1)} %bitcast.43, f32[1,128]{1,0:T(1,128)S(1)} %bitcast.49, bf16[4,768,256]{2,1,0:T(8,128)(2,1)S(1)} %bitcast.36, bf16[4,768,256]{2,1,0:T(8,128)(2,1)S(1)} %collective-permute-done.12.refs_3_, ...), custom_call_target="tpu_custom_call" | custom-call | flops 805306368 | bytes 7472128 | tf_op jit(solution)/shard_map/pallas_call | solution.py:71
  84.3 2.0 collective-permute-done.19.refs_3_
  86.3 10.5 %collective-permute-done.17.refs_1_ = bf16[256,1024]{1,0:T(8,128)(2,1)S(1)} collective-permute-done((bf16[256,1024]{1,0:T(8,128)(2,1)S(1)}, bf16[256,1024]{1,0:T(8,128)(2,1)S(1)}, u32[]{:S(2)}, u32[]{:S(2)}) %collective-permute-start.17) | collective-permute-done | bytes 524320 | tf_op jit(solution)/shard_map/ppermute | solution.py:41
  100.3 6.5 %collective-permute-done.20.refs_4_.refs_3_ = bf16[128,1024]{1,0:T(8,128)(2,1)} collective-permute-done((bf16[128,1024]{1,0:T(8,128)(2,1)}, bf16[128,1024]{1,0:T(8,128)(2,1)}, u32[]{:S(2)}, u32[]{:S(2)}) %collective-permute-start.20) | collective-permute-done | bytes 262176 | tf_op jit(solution)/shard_map/ppermute | solution.py:41
  108.3 1.5 collective-permute-start.28
  111.6 5.3 %collective-permute-done.27.refs_3_.refs_6_ = bf16[128,1024]{1,0:T(8,128)(2,1)S(1)} collective-permute-done((bf16[128,1024]{1,0:T(8,128)(2,1)}, bf16[128,1024]{1,0:T(8,128)(2,1)S(1)}, u32[]{:S(2)}, u32[]{:S(2)}) %collective-permute-start.27) | collective-permute-done | bytes 262176 | tf_op jit(solution)/shard_map/ppermute | solution.py:41
  117.7 1.7 copy-done.34
  119.4 4.1 %shard_map.247 = (bf16[256,768]{1,0:T(8,128)(2,1)S(1)}, bf16[256,1536]{1,0:T(8,128)(2,1)S(1)}, bf16[256,1024]{1,0:T(8,128)(2,1)}, bf16[256,1024]{1,0:T(8,128)(2,1)S(1)}) custom-call(s32[1]{0:T(128)} %bitcast.5.refs_0_.where, bf16[4,1152,256]{2,1,0:T(8,128)(2,1)S(1)} %bitcast.58, bf16[4,1152,256]{2,1,0:T(8,128)(2,1)S(1)} %collective-permute-done.22.refs_2_, ...), custom_call_target="tpu_custom_call" | custom-call | flops 2818572288 | bytes 7995396 | tf_op jit(solution)/shard_map/pallas_call | solution.py:71
  123.4 1.6 collective-permute-start.29
  125.0 7.5 %shard_map.246 = (bf16[256,768]{1,0:T(8,128)(2,1)S(1)}, bf16[256,1536]{1,0:T(8,128)(2,1)S(1)}, bf16[256,1024]{1,0:T(8,128)(2,1)}, bf16[256,1024]{1,0:T(8,128)(2,...) custom-call(s32[1]{0:T(128)} %bitcast.5.refs_0_.where, ...), custom_call_target="tpu_custom_call" | custom-call | flops 5637144576 | bytes 11272196 | tf_op jit(solution)/shard_map/pallas_call | solution.py:71
  132.5 1.5 collective-permute-start.25
  134.5 4.9 %shard_map.245 = (bf16[256,768]{1,0:T(8,128)(2,1)S(1)}, bf16[256,1536]{1,0:T(8,128)(2,1)S(1)}, f32[256,1024]{1,0:T(8,128)}, f32[256,1024]{1,0:T(8,128)S(1)}) custom-call(s32[1]{0:T(128)} %bitcast.5.refs_0_.where, bf16[4,1152,256]{2,1,0:T(8,128)(2,1)S(1)} %bitcast.60, bf16[4,1152,256]{2,1,0:T(8,128)(2,1)S(1)} %collective-permute-done.22.refs_2_, ...), custom_call_target="tpu_custom_call" | custom-call | flops 2818572288 | bytes 9043972 | tf_op jit(solution)/shard_map/pallas_call | solution.py:71
  139.4 4.3 %shard_map.248 = bf16[4,1152,256]{2,1,0:T(8,128)(2,1)S(1)} custom-call(s32[1]{0:T(128)} %bitcast.5.refs_0_.where, bf16[128,1024]{1,0:T(8,128)(2,1)S(1)} %get-tuple-element.277.refs_3_.refs_0_, bf16[128,1024]{1,0:T(8,128)(2,1)} %get-tuple-element.276.refs_4_.refs_1_, bf16[128,1024]{1,0:T(8,128)(2,1)S(1)} %collective-permute-done.23.refs_3_.refs_2_, ...), custom_call_target="tpu_custom_call" | custom-call | flops 4831838208 | bytes 8912896 | tf_op jit(solution)/shard_map/pallas_call | solution.py:586
  143.7 4.5 %collective-permute-done.25.refs_1_ = bf16[256,1024]{1,0:T(8,128)(2,1)S(1)} collective-permute-done((bf16[256,1024]{1,0:T(8,128)(2,1)S(1)}, bf16[256,1024]{1,0:T(8,128)(2,1)S(1)}, u32[]{:S(2)}, u32[]{:S(2)}) %collective-permute-start.25) | collective-permute-done | bytes 524320 | tf_op jit(solution)/shard_map/ppermute | solution.py:41
  148.3 1.7 shard_map.249
  152.0 1.4 collective-permute-start.31
  154.0 4.6 %shard_map.250 = bf16[4,1152,256]{2,1,0:T(8,128)(2,1)S(1)} custom-call(s32[1]{0:T(128)} %bitcast.5.refs_0_.where, bf16[128,1024]{1,0:T(8,128)(2,1)S(1)} %copy-done.36, bf16[128,1024]{1,0:T(8,128)(2,1)} %get-tuple-element.276.refs_4_.refs_1_, bf16[128,1024]{1,0:T(8,128)(2,1)S(1)} %collective-permute-done.23.refs_3_.refs_2_, ...), custom_call_target="tpu_custom_call" | custom-call | flops 4831838208 | bytes 11272192 | tf_op jit(solution)/shard_map/pallas_call | solution.py:586
  160.1 4.3 %collective-permute-done.31.refs_7_ = bf16[128,1024]{1,0:T(8,128)(2,1)} collective-permute-done((bf16[128,1024]{1,0:T(8,128)(2,1)S(1)}, bf16[128,1024]{1,0:T(8,128)(2,1)}, u32[]{:S(2)}, u32[]{:S(2)}) %collective-permute-start.31) | collective-permute-done | bytes 262176 | tf_op jit(solution)/shard_map/ppermute | solution.py:41
  166.9 1.4 collective-permute-start.36
  168.3 6.1 %shard_map.251 = (bf16[256,1024]{1,0:T(8,128)(2,1)}, f32[256,1024]{1,0:T(8,128)}, f32[1,1280]{1,0:T(1,128)S(1)}) custom-call(f32[1,128]{1,0:T(1,128)S(1)} %bitcast.44, f32[1,128]{1,0:T(1,128)S(1)} %bitcast.50, bf16[4,768,256]{2,1,0:T(8,128)(2,1)S(1)} %bitcast.37, bf16[4,768,256]{2,1,0:T(8,128)(2,1)S(1)} %collective-permute-done.12.refs_3_, ...), custom_call_target="tpu_custom_call" | custom-call | flops 805306368 | bytes 8296448 | tf_op jit(solution)/shard_map/pallas_call | solution.py:71
  175.2 4.3 %shard_map.252 = (bf16[4,256,256]{2,1,0:T(8,128)(2,1)S(1)}, bf16[4,256,256]{2,1,0:T(8,128)(2,1)S(1)}) custom-call(bf16[256,512]{1,0:T(8,128)(2,1)} %get-tuple-element.338.refs_0_, bf16[256,512]{1,0:T(8,128)(2,1)} %get-tuple-element.339.refs_1_, bf16[256,512]{1,0:T(8,128)(2,1)} %get-tuple-element.340.refs_2_, bf16[256,512]{1,0:T(8,128)(2,1)} %get-tuple-element.341.refs_3_, ...), custom_call_target="tpu_custom_call" | custom-call | flops 1073741824 | bytes 4194304 | tf_op jit(solution)/shard_map/pallas_call | solution.py:71
  181.9 1.5 collective-permute-start.41
  185.5 8.9 %collective-permute-done.42.refs_1_ = bf16[256,1024]{1,0:T(8,128)(2,1)S(1)} collective-permute-done((bf16[256,1024]{1,0:T(8,128)(2,1)S(1)}, bf16[256,1024]{1,0:T(8,128)(2,1)S(1)}, u32[]{:S(2)}, u32[]{:S(2)}) %collective-permute-start.42) | collective-permute-done | bytes 524320 | tf_op jit(solution)/shard_map/ppermute | solution.py:41
  195.2 1.5 collective-permute-start.40
  196.7 9.8 %shard_map.253 = (bf16[256,1024]{1,0:T(8,128)(2,1)}, bf16[256,1024]{1,0:T(8,128)(2,1)}, bf16[256,1024]{1,0:T(8,128)(2,1)}, bf16[256,1024]{1,0:T(8,128)(2,1)}, f32[1,1280]{1,0:T(1,128)S(1)}) custom-call(f32[1,128]{1,0:T(1,128)S(1)} %bitcast.45, f32[1,128]{1,0:T(1,128)S(1)} %bitcast.51, bf16[4,768,256]{2,1,0:T(8,128)(2,1)S(1)} %bitcast.38, ...), custom_call_target="tpu_custom_call" | custom-call | flops 1610612736 | bytes 11343872 | tf_op jit(solution)/shard_map/pallas_call | solution.py:71
  209.1 2.4 collective-permute-done.40.refs_3_
  215.8 5.8 %shard_map.255 = (bf16[256,1024]{1,0:T(8,128)(2,1)}, bf16[256,1024]{1,0:T(8,128)(2,1)}, f32[1,1280]{1,0:T(1,128)S(1)}) custom-call(f32[1,128]{1,0:T(1,128)S(1)} %bitcast.46, f32[1,128]{1,0:T(1,128)S(1)} %bitcast.52, bf16[4,768,256]{2,1,0:T(8,128)(2,1)S(1)} %bitcast.39, bf16[4,768,256]{2,1,0:T(8,128)(2,1)S(1)} %collective-permute-done.12.refs_3_, ...), custom_call_target="tpu_custom_call" | custom-call | flops 805306368 | bytes 7772160 | tf_op jit(solution)/shard_map/pallas_call | solution.py:71
  221.6 4.6 %collective-permute-done.44.refs_1_ = bf16[256,1024]{1,0:T(8,128)(2,1)} collective-permute-done((bf16[256,1024]{1,0:T(8,128)(2,1)}, bf16[256,1024]{1,0:T(8,128)(2,1)}, u32[]{:S(2)}, u32[]{:S(2)}) %collective-permute-start.44) | collective-permute-done | bytes 524320 | tf_op jit(solution)/shard_map/ppermute | solution.py:41
  228.7 4.1 %shard_map.256 = bf16[4,512,256]{2,1,0:T(8,128)(2,1)S(1)} custom-call(s32[1]{0:T(128)} %bitcast.where, bf16[256,1024]{1,0:T(8,128)(2,1)} %get-tuple-element.253.refs_6_.refs_0_, bf16[256,1024]{1,0:T(8,128)(2,1)} %get-tuple-element.254.refs_6_.refs_1_, bf16[256,1024]{1,0:T(8,128)(2,1)} %get-tuple-element.255.refs_10_.refs_2_, ...), custom_call_target="tpu_custom_call" | custom-call | flops 1073741824 | bytes 5242880 | tf_op jit(solution)/shard_map/pallas_call | solution.py:478
  232.8 5.1 %reduce-scatter.6.cloned.1.call-done = bf16[256,256]{1,0:T(8,128)(2,1)} async-done(((bf16[1024,256]{1,0:T(8,128)(2,1)}), bf16[256,256]{1,0:T(8,128)(2,1)}) %reduce-scatter.6.cloned.1.call-update) | async-done | bytes 131088 | tf_op jit(solution)/shard_map/reduce_scatter | solution.py:847
  237.9 2.5 collective-permute-done.46.refs_1_
  241.6 2.7 collective-permute-done.48.refs_12_
  244.2 4.9 %shard_map.257 = bf16[4,528,256]{2,1,0:T(8,128)(2,1)} custom-call(s32[1]{0:T(128)} %bitcast.where, bf16[256,1024]{1,0:T(8,128)(2,1)} %get-tuple-element.253.refs_6_.refs_0_, bf16[256,1024]{1,0:T(8,128)(2,1)} %get-tuple-element.254.refs_6_.refs_1_, bf16[256,1024]{1,0:T(8,128)(2,1)} %get-tuple-element.255.refs_10_.refs_2_, ...), custom_call_target="tpu_custom_call" | custom-call | flops 1073741824 | bytes 6333952 | tf_op jit(solution)/shard_map/pallas_call | solution.py:478
  250.9 7.5 %collective-permute-done.49 = bf16[576,256]{1,0:T(8,128)(2,1)S(1)} collective-permute-done((bf16[576,256]{1,0:T(8,128)(2,1)S(1)}, bf16[576,256]{1,0:T(8,128)(2,1)S(1)}, u32[]{:S(2)}, u32[]{:S(2)}) %collective-permute-start.49) | collective-permute-done | bytes 294944 | tf_op jit(solution)/shard_map/ppermute | solution.py:41
  259.9 1.4 collective-permute-start.55
  263.6 5.4 %shard_map.258 = (f32[256,3072]{1,0:T(8,128)}, f32[256,3072]{1,0:T(8,128)}, f32[768,1024]{1,0:T(8,128)}) custom-call(s32[2]{0:T(128)S(1)} %pad_add_fusion.1.w.where, bf16[1152,256]{1,0:T(8,128)(2,1)S(1)} %copy-done.21, bf16[1152,256]{1,0:T(8,128)(2,1)S(1)} %collective-permute-done.46.refs_1_, bf16[1152,256]{1,0:T(8,128)(2,1)S(1)} %collective-permute-done.47.refs_2_, ...), custom_call_target="tpu_custom_call" | custom-call | bytes 14155784 | tf_op jit(solution)/shard_map/pallas_call | solution.py:71
  269.1 7.5 %reduce-scatter.8.cloned.1.call-done = bf16[528,256]{1,0:T(8,128)(2,1)} async-done(((bf16[2112,256]{1,0:T(8,128)(2,1)}), bf16[528,256]{1,0:T(8,128)(2,1)}) %reduce-scatter.8.cloned.1.call-update) | async-done | bytes 270352 | tf_op jit(solution)/shard_map/reduce_scatter | solution.py:868
  277.6 1.5 collective-permute-start.56
  279.2 1.5 collective-permute-start.57
  280.6 7.9 %collective-permute-done.56.refs_1_ = bf16[784,256]{1,0:T(8,128)(2,1)S(1)} collective-permute-done((bf16[784,256]{1,0:T(8,128)(2,1)S(1)}, bf16[784,256]{1,0:T(8,128)(2,1)S(1)}, u32[]{:S(2)}, u32[]{:S(2)}) %collective-permute-start.56) | collective-permute-done | bytes 401440 | tf_op jit(solution)/shard_map/ppermute | solution.py:41
  288.6 1.5 collective-permute-start.59
  290.1 1.5 collective-permute-start.58
  291.7 3.4 %shard_map.260 = bf16[256,1024]{1,0:T(8,128)(2,1)} custom-call(bf16[256,1024]{1,0:T(8,128)(2,1)S(1)} %copy-done.5, f32[256,1024]{1,0:T(8,128)} %get-tuple-element.416.d_hidden, f32[1,1024]{1,0:T(1,128)S(1)} %bitcast.56, f32[256,1024]{1,0:T(8,128)} %get-tuple-element.417.refs_0_, bf16[256,1024]{1,0:T(8,128)(2,1)} %collective-permute-done.44.refs_1_, ...), custom_call_target="tpu_custom_call" | custom-call | bytes 4722688 | tf_op jit(solution)/shard_map/pallas_call | solution.py:71
  299.4 3.7 %shard_map.261 = (f32[256,2048]{1,0:T(8,128)}, f32[256,1024]{1,0:T(8,128)}, f32[256,1024]{1,0:T(8,128)}, f32[512,1024]{1,0:T(8,128)}, f32[1,1024]{1,0:T(1,128)},...) custom-call(s32[2]{0:T(128)S(1)} %pad_add_fusion.1.w.where, ...), custom_call_target="tpu_custom_call" | custom-call | bytes 9511944 | tf_op jit(solution)/shard_map/pallas_call | solution.py:71
  (213 shorter events, 51.3 us)
Async XLA Ops:
  7.2 46.0 %all-gather.5.cloned.1.call-start = ((), (), s32[]{:S(2)}) async-start(), calls=%async_computation.6 | async-start | bytes 1966080 | tf_op jit(solution)/shard_map/all_gather | solution.py:722
  9.7 97.8 %all-gather.7.cloned.1.call-start = ((), (), s32[]{:S(2)}) async-start(), calls=%async_computation.7 | async-start | bytes 2949120 | tf_op jit(solution)/shard_map/all_gather | solution.py:736
  9.9 17.1 %collective-permute-start.1 = (bf16[144,1024]{1,0:T(8,128)(2,1)S(1)}, bf16[144,1024]{1,0:T(8,128)(2,1)S(1)}, u32[]{:S(2)}, u32[]{:S(2)}) collective-permute-start(bf16[144,1024]{1,0:T(8,128)(2,1)S(1)} %fusion.1.refs_3_.refs_9_), channel_id=1, source_target_pairs={{0,2},{2,0},{1,3},{3,1},{4,6},{6,4},{5,7},{7,5},{8,10},{10,8},{9,1... | collective-permute-start | bytes 884744 | tf_op jit(solution)/shard_map/ppermute | solution.py:41
  12.9 14.1 %collective-permute-start.3 = (bf16[144,1024]{1,0:T(8,128)(2,1)S(1)}, bf16[144,1024]{1,0:T(8,128)(2,1)S(1)}, u32[]{:S(2)}, u32[]{:S(2)}) collective-permute-start(bf16[144,1024]{1,0:T(8,128)(2,1)S(1)} %fusion.1.refs_3_.refs_9_), channel_id=1, source_target_pairs={{0,4},{4,0},{1,5},{5,1},{2,6},{6,2},{3,7},{7,3},{8,12},{12,8},{9,1... | collective-permute-start | bytes 884744 | tf_op jit(solution)/shard_map/ppermute | solution.py:41
  14.4 12.6 %collective-permute-start.2 = (bf16[128,1024]{1,0:T(8,128)(2,1)S(1)}, bf16[128,1024]{1,0:T(8,128)(2,1)S(1)}, u32[]{:S(2)}, u32[]{:S(2)}) collective-permute-start(bf16[128,1024]{1,0:T(8,128)(2,1)S(1)} %get-tuple-element.448.refs_2_.refs_8_), channel_id=1, source_target_pairs={{0,4},{4,0},{1,5},{5,1},{2,6},{6,2},{3,7},{7,3},{8,12},{12,8},{9,1... | collective-permute-start | bytes 786440 | tf_op jit(solution)/shard_map/ppermute | solution.py:41
  14.9 12.1 %collective-permute-start = (bf16[128,1024]{1,0:T(8,128)(2,1)S(1)}, bf16[128,1024]{1,0:T(8,128)(2,1)S(1)}, u32[]{:S(2)}, u32[]{:S(2)}) collective-permute-start(bf16[128,1024]{1,0:T(8,128)(2,1)S(1)} %get-tuple-element.448.refs_2_.refs_8_), channel_id=1, source_target_pairs={{0,2},{2,0},{1,3},{3,1},{4,6},{6,4},{5,7},{7,5},{8,10},{10,8},{9,1... | collective-permute-start | bytes 786440 | tf_op jit(solution)/shard_map/ppermute | solution.py:41
  28.0 9.6 %collective-permute-start.7 = (bf16[128,1024]{1,0:T(8,128)(2,1)}, bf16[128,1024]{1,0:T(8,128)(2,1)}, u32[]{:S(2)}, u32[]{:S(2)}) collective-permute-start(bf16[128,1024]{1,0:T(8,128)(2,1)} %get-tuple-element.280.refs_6_.refs_17_), channel_id=1, source_target_pairs={{0,2},{2,0},{1,3},{3,1},{4,6},{6,4},{5,7},{7,5},{8,10},{10,8},{9,1... | collective-permute-start | bytes 786440 | tf_op jit(solution)/shard_map/ppermute | solution.py:41
  28.3 10.7 %collective-permute-start.8 = (bf16[128,1024]{1,0:T(8,128)(2,1)}, bf16[128,1024]{1,0:T(8,128)(2,1)}, u32[]{:S(2)}, u32[]{:S(2)}) collective-permute-start(bf16[128,1024]{1,0:T(8,128)(2,1)} %get-tuple-element.279.refs_5_.refs_16_), channel_id=1, source_target_pairs={{0,4},{4,0},{1,5},{5,1},{2,6},{6,2},{3,7},{7,3},{8,12},{12,8},{9,1... | collective-permute-start | bytes 786440 | tf_op jit(solution)/shard_map/ppermute | solution.py:41
  30.0 13.0 %collective-permute-start.4 = (bf16[128,1024]{1,0:T(8,128)(2,1)S(1)}, bf16[128,1024]{1,0:T(8,128)(2,1)S(1)}, u32[]{:S(2)}, u32[]{:S(2)}) collective-permute-start(bf16[128,1024]{1,0:T(8,128)(2,1)S(1)} %collective-permute-done.2.refs_6_.refs_17_), channel_id=1, source_target_pairs={{0,2},{2,0},{1,3},{3,1},{4,6},{6,4},{5,7},{7,5},{8,10},{10,8},{9,1... | collective-permute-start | bytes 786440 | tf_op jit(solution)/shard_map/ppermute | solution.py:41
  31.5 16.0 %collective-permute-start.5 = (bf16[144,1024]{1,0:T(8,128)(2,1)S(1)}, bf16[144,1024]{1,0:T(8,128)(2,1)S(1)}, u32[]{:S(2)}, u32[]{:S(2)}) collective-permute-start(bf16[144,1024]{1,0:T(8,128)(2,1)S(1)} %collective-permute-done.1.refs_5_.refs_9_), channel_id=1, source_target_pairs={{0,4},{4,0},{1,5},{5,1},{2,6},{6,2},{3,7},{7,3},{8,12},{12,8},{9,1... | collective-permute-start | bytes 884744 | tf_op jit(solution)/shard_map/ppermute | solution.py:41
  32.0 19.8 %collective-permute-start.6 = (bf16[128,1024]{1,0:T(8,128)(2,1)}, bf16[128,1024]{1,0:T(8,128)(2,1)}, u32[]{:S(2)}, u32[]{:S(2)}) collective-permute-start(bf16[128,1024]{1,0:T(8,128)(2,1)} %get-tuple-element.279.refs_5_.refs_16_), channel_id=1, source_target_pairs={{0,2},{2,0},{1,3},{3,1},{4,6},{6,4},{5,7},{7,5},{8,10},{10,8},{9,1... | collective-permute-start | bytes 786440 | tf_op jit(solution)/shard_map/ppermute | solution.py:41
  37.5 14.3 %collective-permute-start.9 = (bf16[128,1024]{1,0:T(8,128)(2,1)}, bf16[128,1024]{1,0:T(8,128)(2,1)}, u32[]{:S(2)}, u32[]{:S(2)}) collective-permute-start(bf16[128,1024]{1,0:T(8,128)(2,1)} %get-tuple-element.280.refs_6_.refs_17_), channel_id=1, source_target_pairs={{0,4},{4,0},{1,5},{5,1},{2,6},{6,2},{3,7},{7,3},{8,12},{12,8},{9,1... | collective-permute-start | bytes 786440 | tf_op jit(solution)/shard_map/ppermute | solution.py:41
  39.1 13.0 %collective-permute-start.10 = (bf16[128,1024]{1,0:T(8,128)(2,1)}, bf16[128,1024]{1,0:T(8,128)(2,1)}, u32[]{:S(2)}, u32[]{:S(2)}) collective-permute-start(bf16[128,1024]{1,0:T(8,128)(2,1)} %collective-permute-done.8.refs_9_.refs_20_), channel_id=1, source_target_pairs={{0,2},{2,0},{1,3},{3,1},{4,6},{6,4},{5,7},{7,5},{8,10},{10,8},{9,1... | collective-permute-start | bytes 786440 | tf_op jit(solution)/shard_map/ppermute | solution.py:41
  43.0 10.2 %collective-permute-start.11 = (bf16[128,1024]{1,0:T(8,128)(2,1)}, bf16[128,1024]{1,0:T(8,128)(2,1)}, u32[]{:S(2)}, u32[]{:S(2)}) collective-permute-start(bf16[128,1024]{1,0:T(8,128)(2,1)} %collective-permute-done.7.refs_6_.refs_19_), channel_id=1, source_target_pairs={{0,4},{4,0},{1,5},{5,1},{2,6},{6,2},{3,7},{7,3},{8,12},{12,8},{9,1... | collective-permute-start | bytes 786440 | tf_op jit(solution)/shard_map/ppermute | solution.py:41
  53.2 173.4 %reduce-scatter.4.cloned.1.call-start = ((), (), s32[]{:S(2)}) async-start(), calls=%async_computation.3 | async-start | bytes 2949120 | tf_op jit(solution)/shard_map/reduce_scatter | solution.py:815
  53.4 13.1 %collective-permute-start.12 = (bf16[4,768,256]{2,1,0:T(8,128)(2,1)}, bf16[4,768,256]{2,1,0:T(8,128)(2,1)S(1)}, u32[]{:S(2)}, u32[]{:S(2)}) collective-permute-start(bf16[4,768,256]{2,1,0:T(8,128)(2,1)} %bitcast.32), channel_id=1, source_target_pairs={{0,1},{1,0},{2,3},{3,2},{4,5},{5,4},{6,7},{7,6},{8,9},{9,8},{10,11... | collective-permute-start | bytes 4718600 | tf_op jit(solution)/shard_map/ppermute | solution.py:41
  54.8 6.3 %collective-permute-start.13 = (bf16[256,256]{1,0:T(8,128)(2,1)S(1)}, bf16[256,256]{1,0:T(8,128)(2,1)S(1)}, u32[]{:S(2)}, u32[]{:S(2)}) collective-permute-start(bf16[256,256]{1,0:T(8,128)(2,1)S(1)} %get-tuple-element.439), channel_id=1, source_target_pairs={{0,2},{2,0},{1,3},{3,1},{4,6},{6,4},{5,7},{7,5},{8,10},{10,8},{9,1... | collective-permute-start | bytes 393224 | tf_op jit(solution)/shard_map/ppermute | solution.py:41
  56.2 8.3 %collective-permute-start.14 = (bf16[256,256]{1,0:T(8,128)(2,1)S(1)}, bf16[256,256]{1,0:T(8,128)(2,1)S(1)}, u32[]{:S(2)}, u32[]{:S(2)}) collective-permute-start(bf16[256,256]{1,0:T(8,128)(2,1)S(1)} %get-tuple-element.438), channel_id=1, source_target_pairs={{0,4},{4,0},{1,5},{5,1},{2,6},{6,2},{3,7},{7,3},{8,12},{12,8},{9,1... | collective-permute-start | bytes 393224 | tf_op jit(solution)/shard_map/ppermute | solution.py:41
  57.7 6.8 %collective-permute-start.15 = (bf16[256,256]{1,0:T(8,128)(2,1)S(1)}, bf16[256,256]{1,0:T(8,128)(2,1)S(1)}, u32[]{:S(2)}, u32[]{:S(2)}) collective-permute-start(bf16[256,256]{1,0:T(8,128)(2,1)S(1)} %get-tuple-element.437), channel_id=1, source_target_pairs={{0,6},{2,4},{4,2},{6,0},{1,7},{3,5},{5,3},{7,1},{8,14},{10,12},{12... | collective-permute-start | bytes 393224 | tf_op jit(solution)/shard_map/ppermute | solution.py:152
  70.6 15.7 %collective-permute-start.19 = (bf16[256,1024]{1,0:T(8,128)(2,1)S(1)}, bf16[256,1024]{1,0:T(8,128)(2,1)S(1)}, u32[]{:S(2)}, u32[]{:S(2)}) collective-permute-start(bf16[256,1024]{1,0:T(8,128)(2,1)S(1)} %get-tuple-element.273), channel_id=1, source_target_pairs={{0,6},{2,4},{4,2},{6,0},{1,7},{3,5},{5,3},{7,1},{8,14},{10,12},{12... | collective-permute-start | bytes 1572872 | tf_op jit(solution)/shard_map/ppermute | solution.py:130
  78.5 18.3 %collective-permute-start.17 = (bf16[256,1024]{1,0:T(8,128)(2,1)S(1)}, bf16[256,1024]{1,0:T(8,128)(2,1)S(1)}, u32[]{:S(2)}, u32[]{:S(2)}) collective-permute-start(bf16[256,1024]{1,0:T(8,128)(2,1)S(1)} %get-tuple-element.268), channel_id=1, source_target_pairs={{0,2},{2,0},{1,3},{3,1},{4,6},{6,4},{5,7},{7,5},{8,10},{10,8},{9,1... | collective-permute-start | bytes 1572872 | tf_op jit(solution)/shard_map/ppermute | solution.py:41
  79.9 16.9 %collective-permute-start.18 = (bf16[256,1024]{1,0:T(8,128)(2,1)S(1)}, bf16[256,1024]{1,0:T(8,128)(2,1)S(1)}, u32[]{:S(2)}, u32[]{:S(2)}) collective-permute-start(bf16[256,1024]{1,0:T(8,128)(2,1)S(1)} %get-tuple-element.269), channel_id=1, source_target_pairs={{0,4},{4,0},{1,5},{5,1},{2,6},{6,2},{3,7},{7,3},{8,12},{12,8},{9,1... | collective-permute-start | bytes 1572872 | tf_op jit(solution)/shard_map/ppermute | solution.py:41
  98.3 8.5 %collective-permute-start.20 = (bf16[128,1024]{1,0:T(8,128)(2,1)}, bf16[128,1024]{1,0:T(8,128)(2,1)}, u32[]{:S(2)}, u32[]{:S(2)}) collective-permute-start(bf16[128,1024]{1,0:T(8,128)(2,1)} %get-tuple-element.276.refs_4_.refs_1_), channel_id=1, source_target_pairs={{0,2},{2,0},{1,3},{3,1},{4,6},{6,4},{5,7},{7,5},{8,10},{10,8},{9,1... | collective-permute-start | bytes 786440 | tf_op jit(solution)/shard_map/ppermute | solution.py:41
  99.4 8.2 %collective-permute-start.21 = (bf16[128,1024]{1,0:T(8,128)(2,1)S(1)}, bf16[128,1024]{1,0:T(8,128)(2,1)}, u32[]{:S(2)}, u32[]{:S(2)}) collective-permute-start(bf16[128,1024]{1,0:T(8,128)(2,1)S(1)} %get-tuple-element.277.refs_3_.refs_0_), channel_id=1, source_target_pairs={{0,4},{4,0},{1,5},{5,1},{2,6},{6,2},{3,7},{7,3},{8,12},{12,8},{9,1... | collective-permute-start | bytes 786440 | tf_op jit(solution)/shard_map/ppermute | solution.py:41
  107.5 10.2 %collective-permute-start.22 = (bf16[4,1152,256]{2,1,0:T(8,128)(2,1)}, bf16[4,1152,256]{2,1,0:T(8,128)(2,1)S(1)}, u32[]{:S(2)}, u32[]{:S(2)}) collective-permute-start(bf16[4,1152,256]{2,1,0:T(8,128)(2,1)} %bitcast.57), channel_id=1, source_target_pairs={{0,1},{1,0},{2,3},{3,2},{4,5},{5,4},{6,7},{7,6},{8,9},{9,8},{10,11... | collective-permute-start | bytes 7077896 | tf_op jit(solution)/shard_map/ppermute | solution.py:41
  107.5 9.3 %collective-permute-start.27 = (bf16[128,1024]{1,0:T(8,128)(2,1)}, bf16[128,1024]{1,0:T(8,128)(2,1)S(1)}, u32[]{:S(2)}, u32[]{:S(2)}) collective-permute-start(bf16[128,1024]{1,0:T(8,128)(2,1)} %collective-permute-done.21.refs_7_.refs_4_), channel_id=1, source_target_pairs={{0,2},{2,0},{1,3},{3,1},{4,6},{6,4},{5,7},{7,5},{8,10},{10,8},{9,1... | collective-permute-start | bytes 786440 | tf_op jit(solution)/shard_map/ppermute | solution.py:41
  108.3 9.4 %collective-permute-start.28 = (bf16[128,1024]{1,0:T(8,128)(2,1)}, bf16[128,1024]{1,0:T(8,128)(2,1)S(1)}, u32[]{:S(2)}, u32[]{:S(2)}) collective-permute-start(bf16[128,1024]{1,0:T(8,128)(2,1)} %collective-permute-done.20.refs_4_.refs_3_), channel_id=1, source_target_pairs={{0,4},{4,0},{1,5},{5,1},{2,6},{6,2},{3,7},{7,3},{8,12},{12,8},{9,1... | collective-permute-start | bytes 786440 | tf_op jit(solution)/shard_map/ppermute | solution.py:41
  109.9 15.2 %collective-permute-start.23 = (bf16[128,1024]{1,0:T(8,128)(2,1)S(1)}, bf16[128,1024]{1,0:T(8,128)(2,1)S(1)}, u32[]{:S(2)}, u32[]{:S(2)}) collective-permute-start(bf16[128,1024]{1,0:T(8,128)(2,1)S(1)} %get-tuple-element.277.refs_3_.refs_0_), channel_id=1, source_target_pairs={{0,2},{2,0},{1,3},{3,1},{4,6},{6,4},{5,7},{7,5},{8,10},{10,8},{9,1... | collective-permute-start | bytes 786440 | tf_op jit(solution)/shard_map/ppermute | solution.py:41
  110.5 14.6 %collective-permute-start.24 = (bf16[128,1024]{1,0:T(8,128)(2,1)}, bf16[128,1024]{1,0:T(8,128)(2,1)S(1)}, u32[]{:S(2)}, u32[]{:S(2)}) collective-permute-start(bf16[128,1024]{1,0:T(8,128)(2,1)} %get-tuple-element.276.refs_4_.refs_1_), channel_id=1, source_target_pairs={{0,4},{4,0},{1,5},{5,1},{2,6},{6,2},{3,7},{7,3},{8,12},{12,8},{9,1... | collective-permute-start | bytes 786440 | tf_op jit(solution)/shard_map/ppermute | solution.py:41
  123.4 16.0 %collective-permute-start.29 = (bf16[256,1024]{1,0:T(8,128)(2,1)S(1)}, bf16[256,1024]{1,0:T(8,128)(2,1)S(1)}, u32[]{:S(2)}, u32[]{:S(2)}) collective-permute-start(bf16[256,1024]{1,0:T(8,128)(2,1)S(1)} %get-tuple-element.298), channel_id=1, source_target_pairs={{0,6},{2,4},{4,2},{6,0},{1,7},{3,5},{5,3},{7,1},{8,14},{10,12},{12... | collective-permute-start | bytes 1572872 | tf_op jit(solution)/shard_map/ppermute | solution.py:130
  132.5 15.7 %collective-permute-start.25 = (bf16[256,1024]{1,0:T(8,128)(2,1)S(1)}, bf16[256,1024]{1,0:T(8,128)(2,1)S(1)}, u32[]{:S(2)}, u32[]{:S(2)}) collective-permute-start(bf16[256,1024]{1,0:T(8,128)(2,1)S(1)} %get-tuple-element.288), channel_id=1, source_target_pairs={{0,2},{2,0},{1,3},{3,1},{4,6},{6,4},{5,7},{7,5},{8,10},{10,8},{9,1... | collective-permute-start | bytes 1572872 | tf_op jit(solution)/shard_map/ppermute | solution.py:41
  134.0 14.2 %collective-permute-start.26 = (bf16[256,1024]{1,0:T(8,128)(2,1)S(1)}, bf16[256,1024]{1,0:T(8,128)(2,1)S(1)}, u32[]{:S(2)}, u32[]{:S(2)}) collective-permute-start(bf16[256,1024]{1,0:T(8,128)(2,1)S(1)} %get-tuple-element.289), channel_id=1, source_target_pairs={{0,4},{4,0},{1,5},{5,1},{2,6},{6,2},{3,7},{7,3},{8,12},{12,8},{9,1... | collective-permute-start | bytes 1572872 | tf_op jit(solution)/shard_map/ppermute | solution.py:41
  148.2 5.8 %collective-permute-start.34 = (bf16[4,1152,256]{2,1,0:T(8,128)(2,1)S(1)}, bf16[4,1152,256]{2,1,0:T(8,128)(2,1)S(1)}, u32[]{:S(2)}, u32[]{:S(2)}) collective-permute-start(bf16[4,1152,256]{2,1,0:T(8,128)(2,1)S(1)} %shard_map.248), channel_id=1, source_target_pairs={{0,1},{1,0},{2,3},{3,2},{4,5},{5,4},{6,7},{7,6},{8,9},{9,8},{10,11... | collective-permute-start | bytes 7077896 | tf_op jit(solution)/shard_map/ppermute | solution.py:41
  150.0 10.1 %collective-permute-start.30 = (bf16[128,1024]{1,0:T(8,128)(2,1)S(1)}, bf16[128,1024]{1,0:T(8,128)(2,1)S(1)}, u32[]{:S(2)}, u32[]{:S(2)}) collective-permute-start(bf16[128,1024]{1,0:T(8,128)(2,1)S(1)} %get-tuple-element.319.refs_6_.refs_4_), channel_id=1, source_target_pairs={{0,2},{2,0},{1,3},{3,1},{4,6},{6,4},{5,7},{7,5},{8,10},{10,8},{9,1... | collective-permute-start | bytes 786440 | tf_op jit(solution)/shard_map/ppermute | solution.py:41
  151.1 13.3 %collective-permute-start.32 = (bf16[128,1024]{1,0:T(8,128)(2,1)S(1)}, bf16[128,1024]{1,0:T(8,128)(2,1)}, u32[]{:S(2)}, u32[]{:S(2)}) collective-permute-start(bf16[128,1024]{1,0:T(8,128)(2,1)S(1)} %get-tuple-element.319.refs_6_.refs_4_), channel_id=1, source_target_pairs={{0,4},{4,0},{1,5},{5,1},{2,6},{6,2},{3,7},{7,3},{8,12},{12,8},{9,1... | collective-permute-start | bytes 786440 | tf_op jit(solution)/shard_map/ppermute | solution.py:41
  152.0 12.4 %collective-permute-start.31 = (bf16[128,1024]{1,0:T(8,128)(2,1)S(1)}, bf16[128,1024]{1,0:T(8,128)(2,1)}, u32[]{:S(2)}, u32[]{:S(2)}) collective-permute-start(bf16[128,1024]{1,0:T(8,128)(2,1)S(1)} %get-tuple-element.320.refs_7_.refs_5_), channel_id=1, source_target_pairs={{0,2},{2,0},{1,3},{3,1},{4,6},{6,4},{5,7},{7,5},{8,10},{10,8},{9,1... | collective-permute-start | bytes 786440 | tf_op jit(solution)/shard_map/ppermute | solution.py:41
  153.5 11.7 %collective-permute-start.33 = (bf16[128,1024]{1,0:T(8,128)(2,1)S(1)}, bf16[128,1024]{1,0:T(8,128)(2,1)S(1)}, u32[]{:S(2)}, u32[]{:S(2)}) collective-permute-start(bf16[128,1024]{1,0:T(8,128)(2,1)S(1)} %get-tuple-element.320.refs_7_.refs_5_), channel_id=1, source_target_pairs={{0,4},{4,0},{1,5},{5,1},{2,6},{6,2},{3,7},{7,3},{8,12},{12,8},{9,1... | collective-permute-start | bytes 786440 | tf_op jit(solution)/shard_map/ppermute | solution.py:41
  165.9 72.0 %reduce-scatter.6.cloned.1.call-start = ((), (), s32[]{:S(2)}) async-start(), calls=%async_computation.4 | async-start | bytes 655360 | tf_op jit(solution)/shard_map/reduce_scatter | solution.py:847
  165.9 8.4 %collective-permute-start.35 = (bf16[128,1024]{1,0:T(8,128)(2,1)}, bf16[128,1024]{1,0:T(8,128)(2,1)S(1)}, u32[]{:S(2)}, u32[]{:S(2)}) collective-permute-start(bf16[128,1024]{1,0:T(8,128)(2,1)} %collective-permute-done.32.refs_8_.refs_15_), channel_id=1, source_target_pairs={{0,2},{2,0},{1,3},{3,1},{4,6},{6,4},{5,7},{7,5},{8,10},{10,8},{9,1... | collective-permute-start | bytes 786440 | tf_op jit(solution)/shard_map/ppermute | solution.py:41
  166.9 7.6 %collective-permute-start.36 = (bf16[128,1024]{1,0:T(8,128)(2,1)}, bf16[128,1024]{1,0:T(8,128)(2,1)S(1)}, u32[]{:S(2)}, u32[]{:S(2)}) collective-permute-start(bf16[128,1024]{1,0:T(8,128)(2,1)} %collective-permute-done.31.refs_7_), channel_id=1, source_target_pairs={{0,4},{4,0},{1,5},{5,1},{2,6},{6,2},{3,7},{7,3},{8,12},{12,8},{9,1... | collective-permute-start | bytes 786440 | tf_op jit(solution)/shard_map/ppermute | solution.py:41
  179.6 14.8 %collective-permute-start.42 = (bf16[256,1024]{1,0:T(8,128)(2,1)S(1)}, bf16[256,1024]{1,0:T(8,128)(2,1)S(1)}, u32[]{:S(2)}, u32[]{:S(2)}) collective-permute-start(bf16[256,1024]{1,0:T(8,128)(2,1)S(1)} %copy-done.45), channel_id=1, source_target_pairs={{0,2},{2,0},{1,3},{3,1},{4,6},{6,4},{5,7},{7,5},{8,10},{10,8},{9,1... | collective-permute-start | bytes 1572872 | tf_op jit(solution)/shard_map/ppermute | solution.py:41
  180.7 26.0 %collective-permute-start.43 = (bf16[256,1024]{1,0:T(8,128)(2,1)S(1)}, bf16[256,1024]{1,0:T(8,128)(2,1)S(1)}, u32[]{:S(2)}, u32[]{:S(2)}) collective-permute-start(bf16[256,1024]{1,0:T(8,128)(2,1)S(1)} %copy-done.44), channel_id=1, source_target_pairs={{0,4},{4,0},{1,5},{5,1},{2,6},{6,2},{3,7},{7,3},{8,12},{12,8},{9,1... | collective-permute-start | bytes 1572872 | tf_op jit(solution)/shard_map/ppermute | solution.py:41
  181.9 29.7 %collective-permute-start.41 = (bf16[256,1024]{1,0:T(8,128)(2,1)S(1)}, bf16[256,1024]{1,0:T(8,128)(2,1)S(1)}, u32[]{:S(2)}, u32[]{:S(2)}) collective-permute-start(bf16[256,1024]{1,0:T(8,128)(2,1)S(1)} %copy-done.43), channel_id=1, source_target_pairs={{0,6},{2,4},{4,2},{6,0},{1,7},{3,5},{5,3},{7,1},{8,14},{10,12},{12... | collective-permute-start | bytes 1572872 | tf_op jit(solution)/shard_map/ppermute | solution.py:130
  183.4 25.1 %collective-permute-start.38 = (bf16[256,256]{1,0:T(8,128)(2,1)S(1)}, bf16[256,256]{1,0:T(8,128)(2,1)S(1)}, u32[]{:S(2)}, u32[]{:S(2)}) collective-permute-start(bf16[256,256]{1,0:T(8,128)(2,1)S(1)} %get-tuple-element.443), channel_id=1, source_target_pairs={{0,2},{2,0},{1,3},{3,1},{4,6},{6,4},{5,7},{7,5},{8,10},{10,8},{9,1... | collective-permute-start | bytes 393224 | tf_op jit(solution)/shard_map/ppermute | solution.py:41
  184.6 24.6 %collective-permute-start.39 = (bf16[256,256]{1,0:T(8,128)(2,1)S(1)}, bf16[256,256]{1,0:T(8,128)(2,1)S(1)}, u32[]{:S(2)}, u32[]{:S(2)}) collective-permute-start(bf16[256,256]{1,0:T(8,128)(2,1)S(1)} %get-tuple-element.442), channel_id=1, source_target_pairs={{0,4},{4,0},{1,5},{5,1},{2,6},{6,2},{3,7},{7,3},{8,12},{12,8},{9,1... | collective-permute-start | bytes 393224 | tf_op jit(solution)/shard_map/ppermute | solution.py:41
  195.2 16.4 %collective-permute-start.40 = (bf16[256,256]{1,0:T(8,128)(2,1)S(1)}, bf16[256,256]{1,0:T(8,128)(2,1)S(1)}, u32[]{:S(2)}, u32[]{:S(2)}) collective-permute-start(bf16[256,256]{1,0:T(8,128)(2,1)S(1)} %get-tuple-element.441), channel_id=1, source_target_pairs={{0,6},{2,4},{4,2},{6,0},{1,7},{3,5},{5,3},{7,1},{8,14},{10,12},{12... | collective-permute-start | bytes 393224 | tf_op jit(solution)/shard_map/ppermute | solution.py:152
  212.4 13.8 %collective-permute-start.44 = (bf16[256,1024]{1,0:T(8,128)(2,1)}, bf16[256,1024]{1,0:T(8,128)(2,1)}, u32[]{:S(2)}, u32[]{:S(2)}) collective-permute-start(bf16[256,1024]{1,0:T(8,128)(2,1)} %get-tuple-element.380), channel_id=1, source_target_pairs={{0,2},{2,0},{1,3},{3,1},{4,6},{6,4},{5,7},{7,5},{8,10},{10,8},{9,1... | collective-permute-start | bytes 1572872 | tf_op jit(solution)/shard_map/ppermute | solution.py:41
  213.3 13.3 %collective-permute-start.45 = (bf16[256,1024]{1,0:T(8,128)(2,1)}, bf16[256,1024]{1,0:T(8,128)(2,1)}, u32[]{:S(2)}, u32[]{:S(2)}) collective-permute-start(bf16[256,1024]{1,0:T(8,128)(2,1)} %get-tuple-element.381), channel_id=1, source_target_pairs={{0,4},{4,0},{1,5},{5,1},{2,6},{6,2},{3,7},{7,3},{8,12},{12,8},{9,1... | collective-permute-start | bytes 1572872 | tf_op jit(solution)/shard_map/ppermute | solution.py:41
  215.5 61.1 %reduce-scatter.8.cloned.1.call-start = ((), (), s32[]{:S(2)}) async-start(), calls=%async_computation.5 | async-start | bytes 1351680 | tf_op jit(solution)/shard_map/reduce_scatter | solution.py:868
  226.7 13.7 %collective-permute-start.46 = (bf16[1152,256]{1,0:T(8,128)(2,1)}, bf16[1152,256]{1,0:T(8,128)(2,1)S(1)}, u32[]{:S(2)}, u32[]{:S(2)}) collective-permute-start(bf16[1152,256]{1,0:T(8,128)(2,1)} %reduce-scatter.4.cloned.1.call-done.refs_0_), channel_id=1, source_target_pairs={{0,2},{2,0},{1,3},{3,1},{4,6},{6,4},{5,7},{7,5},{8,10},{10,8},{9,1... | collective-permute-start | bytes 1769480 | tf_op jit(solution)/shard_map/ppermute | solution.py:41
  227.9 13.6 %collective-permute-start.47 = (bf16[1152,256]{1,0:T(8,128)(2,1)}, bf16[1152,256]{1,0:T(8,128)(2,1)S(1)}, u32[]{:S(2)}, u32[]{:S(2)}) collective-permute-start(bf16[1152,256]{1,0:T(8,128)(2,1)} %reduce-scatter.4.cloned.1.call-done.refs_0_), channel_id=1, source_target_pairs={{0,4},{4,0},{1,5},{5,1},{2,6},{6,2},{3,7},{7,3},{8,12},{12,8},{9,1... | collective-permute-start | bytes 1769480 | tf_op jit(solution)/shard_map/ppermute | solution.py:41
  241.5 2.7 collective-permute-start.48
  249.2 9.1 %collective-permute-start.49 = (bf16[576,256]{1,0:T(8,128)(2,1)S(1)}, bf16[576,256]{1,0:T(8,128)(2,1)S(1)}, u32[]{:S(2)}, u32[]{:S(2)}) collective-permute-start(bf16[576,256]{1,0:T(8,128)(2,1)S(1)} %slice.44), channel_id=1, source_target_pairs={{0,2},{2,0},{1,3},{3,1},{4,6},{6,4},{5,7},{7,5},{8,10},{10,8},{9,1... | collective-permute-start | bytes 884744 | tf_op jit(solution)/shard_map/ppermute | solution.py:41
  249.9 8.8 %collective-permute-start.50 = (bf16[576,256]{1,0:T(8,128)(2,1)S(1)}, bf16[576,256]{1,0:T(8,128)(2,1)S(1)}, u32[]{:S(2)}, u32[]{:S(2)}) collective-permute-start(bf16[576,256]{1,0:T(8,128)(2,1)S(1)} %slice.45), channel_id=1, source_target_pairs={{0,4},{4,0},{1,5},{5,1},{2,6},{6,2},{3,7},{7,3},{8,12},{12,8},{9,1... | collective-permute-start | bytes 884744 | tf_op jit(solution)/shard_map/ppermute | solution.py:41
  258.8 4.8 %collective-permute-start.51 = (bf16[1152,256]{1,0:T(8,128)(2,1)S(1)}, bf16[1152,256]{1,0:T(8,128)(2,1)S(1)}, u32[]{:S(2)}, u32[]{:S(2)}) collective-permute-start(bf16[1152,256]{1,0:T(8,128)(2,1)S(1)} %copy-done.21), channel_id=1, source_target_pairs={{0,1},{1,0},{2,3},{3,2},{4,5},{5,4},{6,7},{7,6},{8,9},{9,8},{10,11... | collective-permute-start | bytes 1769480 | tf_op jit(solution)/shard_map/ppermute | solution.py:41
  258.9 4.7 %collective-permute-start.52 = (bf16[1152,256]{1,0:T(8,128)(2,1)S(1)}, bf16[1152,256]{1,0:T(8,128)(2,1)S(1)}, u32[]{:S(2)}, u32[]{:S(2)}) collective-permute-start(bf16[1152,256]{1,0:T(8,128)(2,1)S(1)} %collective-permute-done.46.refs_1_), channel_id=1, source_target_pairs={{0,1},{1,0},{2,3},{3,2},{4,5},{5,4},{6,7},{7,6},{8,9},{9,8},{10,11... | collective-permute-start | bytes 1769480 | tf_op jit(solution)/shard_map/ppermute | solution.py:41
  259.4 4.2 %collective-permute-start.53 = (bf16[1152,256]{1,0:T(8,128)(2,1)S(1)}, bf16[1152,256]{1,0:T(8,128)(2,1)S(1)}, u32[]{:S(2)}, u32[]{:S(2)}) collective-permute-start(bf16[1152,256]{1,0:T(8,128)(2,1)S(1)} %collective-permute-done.47.refs_2_), channel_id=1, source_target_pairs={{0,1},{1,0},{2,3},{3,2},{4,5},{5,4},{6,7},{7,6},{8,9},{9,8},{10,11... | collective-permute-start | bytes 1769480 | tf_op jit(solution)/shard_map/ppermute | solution.py:41
  259.5 4.2 %collective-permute-start.54 = (bf16[1152,256]{1,0:T(8,128)(2,1)S(1)}, bf16[1152,256]{1,0:T(8,128)(2,1)S(1)}, u32[]{:S(2)}, u32[]{:S(2)}) collective-permute-start(bf16[1152,256]{1,0:T(8,128)(2,1)S(1)} %pad_maximum_fusion.refs_3_), channel_id=1, source_target_pairs={{0,1},{1,0},{2,3},{3,2},{4,5},{5,4},{6,7},{7,6},{8,9},{9,8},{10,11... | collective-permute-start | bytes 1769480 | tf_op jit(solution)/shard_map/ppermute | solution.py:41
  259.9 17.7 %collective-permute-start.55 = (bf16[256,1024]{1,0:T(8,128)(2,1)}, bf16[256,1024]{1,0:T(8,128)(2,1)}, u32[]{:S(2)}, u32[]{:S(2)}) collective-permute-start(bf16[256,1024]{1,0:T(8,128)(2,1)} %get-tuple-element.413), channel_id=1, source_target_pairs={{0,6},{2,4},{4,2},{6,0},{1,7},{3,5},{5,3},{7,1},{8,14},{10,12},{12... | collective-permute-start | bytes 1572872 | tf_op jit(solution)/shard_map/ppermute | solution.py:130
  277.6 10.9 %collective-permute-start.56 = (bf16[784,256]{1,0:T(8,128)(2,1)S(1)}, bf16[784,256]{1,0:T(8,128)(2,1)S(1)}, u32[]{:S(2)}, u32[]{:S(2)}) collective-permute-start(bf16[784,256]{1,0:T(8,128)(2,1)S(1)} %pad_maximum_fusion.1.refs_0_), channel_id=1, source_target_pairs={{0,2},{2,0},{1,3},{3,1},{4,6},{6,4},{5,7},{7,5},{8,10},{10,8},{9,1... | collective-permute-start | bytes 1204232 | tf_op jit(solution)/shard_map/ppermute | solution.py:41
  279.2 11.0 %collective-permute-start.57 = (bf16[784,256]{1,0:T(8,128)(2,1)S(1)}, bf16[784,256]{1,0:T(8,128)(2,1)S(1)}, u32[]{:S(2)}, u32[]{:S(2)}) collective-permute-start(bf16[784,256]{1,0:T(8,128)(2,1)S(1)} %pad_maximum_fusion.1.refs_0_), channel_id=1, source_target_pairs={{0,4},{4,0},{1,5},{5,1},{2,6},{6,2},{3,7},{7,3},{8,12},{12,8},{9,1... | collective-permute-start | bytes 1204232 | tf_op jit(solution)/shard_map/ppermute | solution.py:41
  288.6 7.3 %collective-permute-start.59 = (bf16[400,256]{1,0:T(8,128)(2,1)S(1)}, bf16[400,256]{1,0:T(8,128)(2,1)S(1)}, u32[]{:S(2)}, u32[]{:S(2)}) collective-permute-start(bf16[400,256]{1,0:T(8,128)(2,1)S(1)} %slice.49), channel_id=1, source_target_pairs={{0,4},{4,0},{1,5},{5,1},{2,6},{6,2},{3,7},{7,3},{8,12},{12,8},{9,1... | collective-permute-start | bytes 614408 | tf_op jit(solution)/shard_map/ppermute | solution.py:41
  290.1 5.7 %collective-permute-start.58 = (bf16[384,256]{1,0:T(8,128)(2,1)S(1)}, bf16[384,256]{1,0:T(8,128)(2,1)S(1)}, u32[]{:S(2)}, u32[]{:S(2)}) collective-permute-start(bf16[384,256]{1,0:T(8,128)(2,1)S(1)} %slice.48), channel_id=1, source_target_pairs={{0,2},{2,0},{1,3},{3,1},{4,6},{6,4},{5,7},{7,5},{8,10},{10,8},{9,1... | collective-permute-start | bytes 589832 | tf_op jit(solution)/shard_map/ppermute | solution.py:41
  296.6 2.9 collective-permute-start.63
  (51 other events, 546.5 us)
Sparse Core Ops, SparseCore 0:
  10.2 39.7 all-gather.4
  53.4 51.5 all-gather.6
  166.0 48.5 reduce-scatter.3
  216.8 21.1 reduce-scatter.5
  249.3 27.2 reduce-scatter.7
